TPU v7x, 512 devices: a whole 4x4x16 slice. The times are simulated.
512 devices in a mesh: seq: 128 (over y, z, x_lo), grp: 4 (over x_hi, core).
Axes of the slice: x: 4 (x_hi: 2, x_lo: 2; x = x_hi * 2 + x_lo), y: 4, z: 16, core: 2. Of those that a mesh axis runs over, the one named last changes fastest.
Arguments:
- query_main: bfloat16 [12288, 2560], P('seq', 'grp'), may hold values from -7 to 7
- key_main: bfloat16 [12288, 2560], P('seq', 'grp'), may hold values from -9 to 9
- value_main: bfloat16 [12288, 2560], P('seq', 'grp'), may hold values from -6 to 6
- query_guide: bfloat16 [12288, 1536], P('seq', 'grp'), may hold values from -7 to 7
- key_guide: bfloat16 [12288, 1536], P('seq', 'grp'), may hold values from -9 to 9
- value_guide: bfloat16 [12288, 1536], P('seq', 'grp'), may hold values from -6 to 6
- map_main: bfloat16 [2560, 64], P('grp'), may hold values from -0.47851562 to 0.47851562
- map_guide: bfloat16 [1536, 64], P('grp'), may hold values from -0.47851562 to 0.47851562
Outputs:
- guided: float32 [12288, 64], P('seq')
All inputs are finite; a program needn't handle non-finite values.
Results may differ from a plain program's by a relative error of at most 0.0065.
Values may be sent and summed in bfloat16 or wider, within the bound.
No kernel may reach another device: no remote copies, remote signals or barrier semaphores. Data moves between devices by JAX's collectives and lax.ppermute only.
A program may use at most 64 MiB of HBM per device.

v0:
```python
import math

import jax
import jax.numpy as jnp
from jax import lax
from jax.sharding import PartitionSpec as P

HD = 128


guidance = 2.5


def from_partner(value, axis, distance):
    mask = 2**distance
    pairs = [(source, source ^ mask) for source in range(lax.axis_size(axis))]
    return lax.ppermute(value, axis, pairs)


def shifted(x, axis, by):
    length = lax.axis_size(axis)
    return lax.ppermute(x, axis, [(i, (i + by) % length) for i in range(length)])


def butterfly(stacked, exchanger, sections):
    position = lax.axis_index("seq")
    for bit_index in range(sections):
        parity = position >> bit_index & 1
        is_odd = parity == 1
        layout = stacked.shape
        grouped = stacked.reshape((layout[0] >> bit_index + 1, 2, 1 << bit_index) + layout[1:])
        lower_half = grouped[:, 0]
        upper_half = grouped[:, 1]
        outgoing = jnp.where(is_odd, lower_half, upper_half)
        incoming = exchanger(outgoing, bit_index)
        lower_half = jnp.where(is_odd, incoming, lower_half)
        upper_half = jnp.where(is_odd, upper_half, incoming)
        stacked = jnp.stack([lower_half, upper_half], axis=1).reshape(layout)
    return stacked


def absorb(carry_state, queries, key_value):
    running, summed, accumulated = carry_state
    scaling = 1.0 / math.sqrt(HD)
    scores = (
        jnp.einsum("qd,kd->qk", queries, key_value[0], preferred_element_type=jnp.float32) * scaling
    )
    new_running = jnp.maximum(running, jnp.max(scores, axis=1))
    weights = jnp.exp(scores - new_running[:, None])
    shrink = jnp.exp(running - new_running)
    summed = summed * shrink + jnp.sum(weights, axis=1)
    accumulated = accumulated * shrink[:, None] + jnp.dot(
        weights.astype(jnp.bfloat16), key_value[1], preferred_element_type=jnp.float32
    )
    return (new_running, summed, accumulated)


def body(
    query_main, key_main, value_main, query_guide, key_guide, value_guide, map_main, map_guide
):
    tokens_here = query_main.shape[0]
    main_heads = query_main.shape[1] // HD
    guide_heads = query_guide.shape[1] // HD
    group_size = main_heads + guide_heads
    sections = group_size.bit_length() - 1

    def head_slots(main_part, guide_part):
        joined = jnp.concatenate([main_part, guide_part], axis=1)
        return joined.reshape(tokens_here, group_size, HD).transpose(1, 0, 2)

    stacked = jnp.stack(
        [
            head_slots(query_main, query_guide),
            head_slots(key_main, key_guide),
            head_slots(value_main, value_guide),
        ],
        axis=1,
    )

    def swap_inputs(payload, bit_index):
        return from_partner(payload, "seq", bit_index)

    arrived = butterfly(stacked, swap_inputs, sections)
    block_rows = group_size * tokens_here
    queries = arrived[:, 0].reshape(block_rows, HD)
    key_value = arrived[:, 1:].transpose(1, 0, 2, 3).reshape(2, block_rows, HD)
    carry_state = (
        jnp.full((block_rows,), -1e30, jnp.float32),
        jnp.zeros((block_rows,), jnp.float32),
        jnp.zeros((block_rows, HD), jnp.float32),
    )
    carry_state = absorb(carry_state, queries, key_value)
    turn_count = lax.axis_size("seq") // group_size

    def one_side(step_index, carry):
        state_now, ahead_block = carry
        ahead_block = shifted(ahead_block, "seq", group_size)
        return (absorb(state_now, queries, ahead_block), ahead_block)

    carry_state, ahead_block = lax.fori_loop(0, turn_count - 1, one_side, (carry_state, key_value))
    running, summed, accumulated = carry_state
    out_head = (accumulated / summed[:, None]).astype(jnp.bfloat16)

    def swap_results(payload, bit_index):
        return from_partner(payload, "seq", bit_index)

    returned = butterfly(out_head.reshape(group_size, tokens_here, HD), swap_results, sections)
    flattened = returned.transpose(1, 0, 2).reshape(tokens_here, group_size * HD)
    main_pred = jnp.dot(
        flattened[:, : main_heads * HD], map_main, preferred_element_type=jnp.float32
    )
    guide_pred = jnp.dot(
        flattened[:, main_heads * HD :], map_guide, preferred_element_type=jnp.float32
    )
    partial_sum = (1.0 - guidance) * guide_pred + guidance * main_pred
    return lax.psum(partial_sum, "grp")


def solution(mesh):
    placed = (
        P("seq", "grp"),
        P("seq", "grp"),
        P("seq", "grp"),
        P("seq", "grp"),
        P("seq", "grp"),
        P("seq", "grp"),
        P("grp", None),
        P("grp", None),
    )
    return jax.shard_map(
        body, mesh=mesh, in_specs=placed, out_specs=P("seq", None), check_vma=False
    )
```

profile of v0, /device:TPU:1, one launch (start us, length us, event | category | flops | bytes accessed | tf_op | source)
XLA Modules:
  0.0 635.9 jit_solution(10624432688270614726)
XLA Ops:
  0.0 1.0 maximum_bitcast_fusion
  1.1 1.0 maximum_bitcast_fusion.1
  2.4 3.9 collective-permute-start.1
  6.4 4.1 collective-permute-done.1
  10.7 6.1 collective-permute-start.2
  16.8 4.1 collective-permute-done.2
  21.0 6.5 %collective-permute-start.3 = (bf16[1,4,3,96,128]{4,3,2,1,0:T(8,128)(2,1)S(1)}, bf16[1,4,3,96,128]{4,3,2,1,0:T(8,128)(2,1)S(1)}, u32[]{:S(2)}, u32[]{:S(2)}) collective-permute-start(bf16[1,4,3,96,128]{4,3,2,1,0:T(8,128)(2,1)S(1)} %broadcast_select_fusion.4), channel_id=1, source_target_pairs={{0,16},{4,20},{8,24},{12,28},{16,0},{20,4},{24,8},{28,12},{32,48},... | collective-permute-start | bytes 884744 | tf_op jit(solution)/shard_map/ppermute | solution.py:17
  27.5 12.7 %collective-permute-done.3 = bf16[1,4,3,96,128]{4,3,2,1,0:T(8,128)(2,1)S(1)} collective-permute-done((bf16[1,4,3,96,128]{4,3,2,1,0:T(8,128)(2,1)S(1)}, bf16[1,4,3,96,128]{4,3,2,1,0:T(8,128)(2,1)S(1)}, u32[]{:S(2)}, u32[]{:S(2)}) %collective-permute-start.3) | collective-permute-done | bytes 294944 | tf_op jit(solution)/shard_map/ppermute | solution.py:17
  40.6 0.5 multiply_reduce_fusion.1
  41.5 0.6 convolution_add_fusion.1
  42.1 549.7 %while.16 = (s32[]{:T(128)}, f32[768]{0:T(1024)S(1)}, f32[768]{0:T(1024)S(1)}, f32[768,128]{1,0:T(8,128)S(1)}, bf16[2,768,128]{2,1,0:T(8,128)(2,1)S(1)}, /*index=5*/bf16[768,128]{1,0:T(8,128)(2,1)S(1)}, s32[]{:T(128)}) while((s32[]{:T(128)}, f32[768]{0:T(1024)S(1)}, f32[768]{0:T(1024)S(1)}, f32[768,128]{1,0:T(8,128)S(1)}, ...), condition=%wide.region_5.6_spmd, body=%wide.region_2.5_spmd.sunk | while | flops 306906624 | bytes 10864757 | solution.py:100
  42.1 8.8 %collective-permute-start = (bf16[2,768,128]{2,1,0:T(8,128)(2,1)S(1)}, bf16[2,768,128]{2,1,0:T(8,128)(2,1)S(1)}, u32[]{:S(2)}, u32[]{:S(2)}) collective-permute-start(bf16[2,768,128]{2,1,0:T(8,128)(2,1)S(1)} %get-tuple-element.132), channel_id=1, source_target_pairs={{0,32},{4,36},{8,40},{12,44},{16,48},{20,52},{24,56},{28,60},{32,6... | collective-permute-start | bytes 1179656 | tf_op jit(solution)/shard_map/while/body/eval_jaxpr/ppermute | solution.py:22
  50.9 37.4 %collective-permute-done = bf16[2,768,128]{2,1,0:T(8,128)(2,1)S(1)} collective-permute-done((bf16[2,768,128]{2,1,0:T(8,128)(2,1)S(1)}, bf16[2,768,128]{2,1,0:T(8,128)(2,1)S(1)}, u32[]{:S(2)}, u32[]{:S(2)}) %collective-permute-start) | collective-permute-done | bytes 393248 | tf_op jit(solution)/shard_map/while/body/eval_jaxpr/ppermute | solution.py:22
  89.3 0.6 convolution_add_fusion.3
  90.0 5.0 collective-permute-start
  95.0 31.2 %collective-permute-done = bf16[2,768,128]{2,1,0:T(8,128)(2,1)S(1)} collective-permute-done((bf16[2,768,128]{2,1,0:T(8,128)(2,1)S(1)}, bf16[2,768,128]{2,1,0:T(8,128)(2,1)S(1)}, u32[]{:S(2)}, u32[]{:S(2)}) %collective-permute-start) | collective-permute-done | bytes 393248 | tf_op jit(solution)/shard_map/while/body/eval_jaxpr/ppermute | solution.py:22
  127.2 0.6 convolution_add_fusion.3
  127.8 3.8 collective-permute-start
  131.7 28.6 %collective-permute-done = bf16[2,768,128]{2,1,0:T(8,128)(2,1)S(1)} collective-permute-done((bf16[2,768,128]{2,1,0:T(8,128)(2,1)S(1)}, bf16[2,768,128]{2,1,0:T(8,128)(2,1)S(1)}, u32[]{:S(2)}, u32[]{:S(2)}) %collective-permute-start) | collective-permute-done | bytes 393248 | tf_op jit(solution)/shard_map/while/body/eval_jaxpr/ppermute | solution.py:22
  161.2 0.6 convolution_add_fusion.3
  161.9 1.9 collective-permute-start
  163.8 32.5 %collective-permute-done = bf16[2,768,128]{2,1,0:T(8,128)(2,1)S(1)} collective-permute-done((bf16[2,768,128]{2,1,0:T(8,128)(2,1)S(1)}, bf16[2,768,128]{2,1,0:T(8,128)(2,1)S(1)}, u32[]{:S(2)}, u32[]{:S(2)}) %collective-permute-start) | collective-permute-done | bytes 393248 | tf_op jit(solution)/shard_map/while/body/eval_jaxpr/ppermute | solution.py:22
  197.3 0.6 convolution_add_fusion.3
  198.0 1.9 collective-permute-start
  199.9 28.7 %collective-permute-done = bf16[2,768,128]{2,1,0:T(8,128)(2,1)S(1)} collective-permute-done((bf16[2,768,128]{2,1,0:T(8,128)(2,1)S(1)}, bf16[2,768,128]{2,1,0:T(8,128)(2,1)S(1)}, u32[]{:S(2)}, u32[]{:S(2)}) %collective-permute-start) | collective-permute-done | bytes 393248 | tf_op jit(solution)/shard_map/while/body/eval_jaxpr/ppermute | solution.py:22
  229.5 0.6 convolution_add_fusion.3
  230.2 2.6 collective-permute-start
  232.8 31.0 %collective-permute-done = bf16[2,768,128]{2,1,0:T(8,128)(2,1)S(1)} collective-permute-done((bf16[2,768,128]{2,1,0:T(8,128)(2,1)S(1)}, bf16[2,768,128]{2,1,0:T(8,128)(2,1)S(1)}, u32[]{:S(2)}, u32[]{:S(2)}) %collective-permute-start) | collective-permute-done | bytes 393248 | tf_op jit(solution)/shard_map/while/body/eval_jaxpr/ppermute | solution.py:22
  264.7 0.6 convolution_add_fusion.3
  265.4 3.0 collective-permute-start
  268.4 33.2 %collective-permute-done = bf16[2,768,128]{2,1,0:T(8,128)(2,1)S(1)} collective-permute-done((bf16[2,768,128]{2,1,0:T(8,128)(2,1)S(1)}, bf16[2,768,128]{2,1,0:T(8,128)(2,1)S(1)}, u32[]{:S(2)}, u32[]{:S(2)}) %collective-permute-start) | collective-permute-done | bytes 393248 | tf_op jit(solution)/shard_map/while/body/eval_jaxpr/ppermute | solution.py:22
  302.5 0.6 convolution_add_fusion.3
  303.2 1.9 collective-permute-start
  305.1 31.8 %collective-permute-done = bf16[2,768,128]{2,1,0:T(8,128)(2,1)S(1)} collective-permute-done((bf16[2,768,128]{2,1,0:T(8,128)(2,1)S(1)}, bf16[2,768,128]{2,1,0:T(8,128)(2,1)S(1)}, u32[]{:S(2)}, u32[]{:S(2)}) %collective-permute-start) | collective-permute-done | bytes 393248 | tf_op jit(solution)/shard_map/while/body/eval_jaxpr/ppermute | solution.py:22
  337.9 0.6 convolution_add_fusion.3
  338.5 2.2 collective-permute-start
  340.7 32.4 %collective-permute-done = bf16[2,768,128]{2,1,0:T(8,128)(2,1)S(1)} collective-permute-done((bf16[2,768,128]{2,1,0:T(8,128)(2,1)S(1)}, bf16[2,768,128]{2,1,0:T(8,128)(2,1)S(1)}, u32[]{:S(2)}, u32[]{:S(2)}) %collective-permute-start) | collective-permute-done | bytes 393248 | tf_op jit(solution)/shard_map/while/body/eval_jaxpr/ppermute | solution.py:22
  374.0 0.6 convolution_add_fusion.3
  374.7 2.6 collective-permute-start
  377.3 31.2 %collective-permute-done = bf16[2,768,128]{2,1,0:T(8,128)(2,1)S(1)} collective-permute-done((bf16[2,768,128]{2,1,0:T(8,128)(2,1)S(1)}, bf16[2,768,128]{2,1,0:T(8,128)(2,1)S(1)}, u32[]{:S(2)}, u32[]{:S(2)}) %collective-permute-start) | collective-permute-done | bytes 393248 | tf_op jit(solution)/shard_map/while/body/eval_jaxpr/ppermute | solution.py:22
  409.4 0.6 convolution_add_fusion.3
  410.1 2.7 collective-permute-start
  412.8 33.1 %collective-permute-done = bf16[2,768,128]{2,1,0:T(8,128)(2,1)S(1)} collective-permute-done((bf16[2,768,128]{2,1,0:T(8,128)(2,1)S(1)}, bf16[2,768,128]{2,1,0:T(8,128)(2,1)S(1)}, u32[]{:S(2)}, u32[]{:S(2)}) %collective-permute-start) | collective-permute-done | bytes 393248 | tf_op jit(solution)/shard_map/while/body/eval_jaxpr/ppermute | solution.py:22
  446.9 0.6 convolution_add_fusion.3
  447.6 1.9 collective-permute-start
  449.5 32.0 %collective-permute-done = bf16[2,768,128]{2,1,0:T(8,128)(2,1)S(1)} collective-permute-done((bf16[2,768,128]{2,1,0:T(8,128)(2,1)S(1)}, bf16[2,768,128]{2,1,0:T(8,128)(2,1)S(1)}, u32[]{:S(2)}, u32[]{:S(2)}) %collective-permute-start) | collective-permute-done | bytes 393248 | tf_op jit(solution)/shard_map/while/body/eval_jaxpr/ppermute | solution.py:22
  482.5 0.6 convolution_add_fusion.3
  483.1 2.0 collective-permute-start
  485.1 32.4 %collective-permute-done = bf16[2,768,128]{2,1,0:T(8,128)(2,1)S(1)} collective-permute-done((bf16[2,768,128]{2,1,0:T(8,128)(2,1)S(1)}, bf16[2,768,128]{2,1,0:T(8,128)(2,1)S(1)}, u32[]{:S(2)}, u32[]{:S(2)}) %collective-permute-start) | collective-permute-done | bytes 393248 | tf_op jit(solution)/shard_map/while/body/eval_jaxpr/ppermute | solution.py:22
  518.4 0.6 convolution_add_fusion.3
  519.1 2.6 collective-permute-start
  521.7 31.3 %collective-permute-done = bf16[2,768,128]{2,1,0:T(8,128)(2,1)S(1)} collective-permute-done((bf16[2,768,128]{2,1,0:T(8,128)(2,1)S(1)}, bf16[2,768,128]{2,1,0:T(8,128)(2,1)S(1)}, u32[]{:S(2)}, u32[]{:S(2)}) %collective-permute-start) | collective-permute-done | bytes 393248 | tf_op jit(solution)/shard_map/while/body/eval_jaxpr/ppermute | solution.py:22
  554.0 0.6 convolution_add_fusion.3
  554.6 2.6 collective-permute-start
  557.2 32.9 %collective-permute-done = bf16[2,768,128]{2,1,0:T(8,128)(2,1)S(1)} collective-permute-done((bf16[2,768,128]{2,1,0:T(8,128)(2,1)S(1)}, bf16[2,768,128]{2,1,0:T(8,128)(2,1)S(1)}, u32[]{:S(2)}, u32[]{:S(2)}) %collective-permute-start) | collective-permute-done | bytes 393248 | tf_op jit(solution)/shard_map/while/body/eval_jaxpr/ppermute | solution.py:22
  590.2 0.5 multiply_reduce_fusion.3
  591.1 0.6 convolution_add_fusion.3
  592.0 3.3 collective-permute-start.4
  595.4 2.4 collective-permute-done.4
  597.8 1.9 collective-permute-start.5
  599.7 3.4 collective-permute-done.5
  603.5 12.2 %collective-permute-start.6 = (bf16[1,4,96,128]{3,1,2,0:T(4,128)(2,1)S(1)}, bf16[1,4,96,128]{3,1,2,0:T(4,128)(2,1)S(1)}, u32[]{:S(2)}, u32[]{:S(2)}) collective-permute-start(bf16[1,4,96,128]{3,1,2,0:T(4,128)(2,1)S(1)} %broadcast_select_fusion.9), channel_id=1, source_target_pairs={{0,16},{4,20},{8,24},{12,28},{16,0},{20,4},{24,8},{28,12},{32,48},... | collective-permute-start | bytes 294920 | tf_op jit(solution)/shard_map/ppermute | solution.py:17
  615.7 2.8 collective-permute-done.6
  619.2 16.8 %psum.7 = f32[96,64]{0,1:T(8,128)} all-reduce(f32[96,64]{0,1:T(8,128)S(1)} %fusion.12), channel_id=1, replica_groups=mesh['seq'=128,'grp'=4] {'grp'}, use_global_device_ids=true, to_apply=%region_6.7 | all-reduce | flops 6144 | bytes 49152 | tf_op jit(solution)/shard_map/psum | solution.py:116
  (133 shorter events, 16.2 us)
Async XLA Ops:
  0.0 619.0 %copy-start = (bf16[640,64]{0,1:T(8,128)(2,1)S(1)}, bf16[640,64]{0,1:T(8,128)(2,1)}, u32[]{:S(2)}) copy-start(bf16[640,64]{0,1:T(8,128)(2,1)} %param.16) | copy-start | bytes 245764
  0.0 2.1 copy-start.1
  0.0 2.1 copy-start.2
  2.4 8.1 %collective-permute-start.1 = (bf16[4,1,3,96,128]{4,3,0,2,1:T(8,128)(2,1)S(1)}, bf16[4,1,3,96,128]{4,3,0,2,1:T(8,128)(2,1)S(1)}, u32[]{:S(2)}, u32[]{:S(2)}) collective-permute-start(bf16[4,1,3,96,128]{4,3,0,2,1:T(8,128)(2,1)S(1)} %broadcast_select_fusion.2), channel_id=1, source_target_pairs={{0,4},{4,0},{8,12},{12,8},{16,20},{20,16},{24,28},{28,24},{32,36},... | collective-permute-start | bytes 884744 | tf_op jit(solution)/shard_map/ppermute | solution.py:17
  10.7 10.2 %collective-permute-start.2 = (bf16[2,2,3,96,128]{4,3,0,2,1:T(8,128)(2,1)S(1)}, bf16[2,2,3,96,128]{4,3,0,2,1:T(8,128)(2,1)S(1)}, u32[]{:S(2)}, u32[]{:S(2)}) collective-permute-start(bf16[2,2,3,96,128]{4,3,0,2,1:T(8,128)(2,1)S(1)} %broadcast_select_fusion.3), channel_id=1, source_target_pairs={{0,8},{4,12},{8,0},{12,4},{16,24},{20,28},{24,16},{28,20},{32,40},... | collective-permute-start | bytes 884744 | tf_op jit(solution)/shard_map/ppermute | solution.py:17
  21.0 19.2 %collective-permute-start.3 = (bf16[1,4,3,96,128]{4,3,2,1,0:T(8,128)(2,1)S(1)}, bf16[1,4,3,96,128]{4,3,2,1,0:T(8,128)(2,1)S(1)}, u32[]{:S(2)}, u32[]{:S(2)}) collective-permute-start(bf16[1,4,3,96,128]{4,3,2,1,0:T(8,128)(2,1)S(1)} %broadcast_select_fusion.4), channel_id=1, source_target_pairs={{0,16},{4,20},{8,24},{12,28},{16,0},{20,4},{24,8},{28,12},{32,48},... | collective-permute-start | bytes 884744 | tf_op jit(solution)/shard_map/ppermute | solution.py:17
  42.1 46.3 %collective-permute-start = (bf16[2,768,128]{2,1,0:T(8,128)(2,1)S(1)}, bf16[2,768,128]{2,1,0:T(8,128)(2,1)S(1)}, u32[]{:S(2)}, u32[]{:S(2)}) collective-permute-start(bf16[2,768,128]{2,1,0:T(8,128)(2,1)S(1)} %get-tuple-element.132), channel_id=1, source_target_pairs={{0,32},{4,36},{8,40},{12,44},{16,48},{20,52},{24,56},{28,60},{32,6... | collective-permute-start | bytes 1179656 | tf_op jit(solution)/shard_map/while/body/eval_jaxpr/ppermute | solution.py:22
  90.0 36.2 %collective-permute-start = (bf16[2,768,128]{2,1,0:T(8,128)(2,1)S(1)}, bf16[2,768,128]{2,1,0:T(8,128)(2,1)S(1)}, u32[]{:S(2)}, u32[]{:S(2)}) collective-permute-start(bf16[2,768,128]{2,1,0:T(8,128)(2,1)S(1)} %get-tuple-element.132), channel_id=1, source_target_pairs={{0,32},{4,36},{8,40},{12,44},{16,48},{20,52},{24,56},{28,60},{32,6... | collective-permute-start | bytes 1179656 | tf_op jit(solution)/shard_map/while/body/eval_jaxpr/ppermute | solution.py:22
  127.8 32.4 %collective-permute-start = (bf16[2,768,128]{2,1,0:T(8,128)(2,1)S(1)}, bf16[2,768,128]{2,1,0:T(8,128)(2,1)S(1)}, u32[]{:S(2)}, u32[]{:S(2)}) collective-permute-start(bf16[2,768,128]{2,1,0:T(8,128)(2,1)S(1)} %get-tuple-element.132), channel_id=1, source_target_pairs={{0,32},{4,36},{8,40},{12,44},{16,48},{20,52},{24,56},{28,60},{32,6... | collective-permute-start | bytes 1179656 | tf_op jit(solution)/shard_map/while/body/eval_jaxpr/ppermute | solution.py:22
  161.9 34.5 %collective-permute-start = (bf16[2,768,128]{2,1,0:T(8,128)(2,1)S(1)}, bf16[2,768,128]{2,1,0:T(8,128)(2,1)S(1)}, u32[]{:S(2)}, u32[]{:S(2)}) collective-permute-start(bf16[2,768,128]{2,1,0:T(8,128)(2,1)S(1)} %get-tuple-element.132), channel_id=1, source_target_pairs={{0,32},{4,36},{8,40},{12,44},{16,48},{20,52},{24,56},{28,60},{32,6... | collective-permute-start | bytes 1179656 | tf_op jit(solution)/shard_map/while/body/eval_jaxpr/ppermute | solution.py:22
  198.0 30.6 %collective-permute-start = (bf16[2,768,128]{2,1,0:T(8,128)(2,1)S(1)}, bf16[2,768,128]{2,1,0:T(8,128)(2,1)S(1)}, u32[]{:S(2)}, u32[]{:S(2)}) collective-permute-start(bf16[2,768,128]{2,1,0:T(8,128)(2,1)S(1)} %get-tuple-element.132), channel_id=1, source_target_pairs={{0,32},{4,36},{8,40},{12,44},{16,48},{20,52},{24,56},{28,60},{32,6... | collective-permute-start | bytes 1179656 | tf_op jit(solution)/shard_map/while/body/eval_jaxpr/ppermute | solution.py:22
  230.2 33.6 %collective-permute-start = (bf16[2,768,128]{2,1,0:T(8,128)(2,1)S(1)}, bf16[2,768,128]{2,1,0:T(8,128)(2,1)S(1)}, u32[]{:S(2)}, u32[]{:S(2)}) collective-permute-start(bf16[2,768,128]{2,1,0:T(8,128)(2,1)S(1)} %get-tuple-element.132), channel_id=1, source_target_pairs={{0,32},{4,36},{8,40},{12,44},{16,48},{20,52},{24,56},{28,60},{32,6... | collective-permute-start | bytes 1179656 | tf_op jit(solution)/shard_map/while/body/eval_jaxpr/ppermute | solution.py:22
  265.4 36.2 %collective-permute-start = (bf16[2,768,128]{2,1,0:T(8,128)(2,1)S(1)}, bf16[2,768,128]{2,1,0:T(8,128)(2,1)S(1)}, u32[]{:S(2)}, u32[]{:S(2)}) collective-permute-start(bf16[2,768,128]{2,1,0:T(8,128)(2,1)S(1)} %get-tuple-element.132), channel_id=1, source_target_pairs={{0,32},{4,36},{8,40},{12,44},{16,48},{20,52},{24,56},{28,60},{32,6... | collective-permute-start | bytes 1179656 | tf_op jit(solution)/shard_map/while/body/eval_jaxpr/ppermute | solution.py:22
  303.2 33.7 %collective-permute-start = (bf16[2,768,128]{2,1,0:T(8,128)(2,1)S(1)}, bf16[2,768,128]{2,1,0:T(8,128)(2,1)S(1)}, u32[]{:S(2)}, u32[]{:S(2)}) collective-permute-start(bf16[2,768,128]{2,1,0:T(8,128)(2,1)S(1)} %get-tuple-element.132), channel_id=1, source_target_pairs={{0,32},{4,36},{8,40},{12,44},{16,48},{20,52},{24,56},{28,60},{32,6... | collective-permute-start | bytes 1179656 | tf_op jit(solution)/shard_map/while/body/eval_jaxpr/ppermute | solution.py:22
  338.5 34.5 %collective-permute-start = (bf16[2,768,128]{2,1,0:T(8,128)(2,1)S(1)}, bf16[2,768,128]{2,1,0:T(8,128)(2,1)S(1)}, u32[]{:S(2)}, u32[]{:S(2)}) collective-permute-start(bf16[2,768,128]{2,1,0:T(8,128)(2,1)S(1)} %get-tuple-element.132), channel_id=1, source_target_pairs={{0,32},{4,36},{8,40},{12,44},{16,48},{20,52},{24,56},{28,60},{32,6... | collective-permute-start | bytes 1179656 | tf_op jit(solution)/shard_map/while/body/eval_jaxpr/ppermute | solution.py:22
  374.7 33.8 %collective-permute-start = (bf16[2,768,128]{2,1,0:T(8,128)(2,1)S(1)}, bf16[2,768,128]{2,1,0:T(8,128)(2,1)S(1)}, u32[]{:S(2)}, u32[]{:S(2)}) collective-permute-start(bf16[2,768,128]{2,1,0:T(8,128)(2,1)S(1)} %get-tuple-element.132), channel_id=1, source_target_pairs={{0,32},{4,36},{8,40},{12,44},{16,48},{20,52},{24,56},{28,60},{32,6... | collective-permute-start | bytes 1179656 | tf_op jit(solution)/shard_map/while/body/eval_jaxpr/ppermute | solution.py:22
  410.1 35.9 %collective-permute-start = (bf16[2,768,128]{2,1,0:T(8,128)(2,1)S(1)}, bf16[2,768,128]{2,1,0:T(8,128)(2,1)S(1)}, u32[]{:S(2)}, u32[]{:S(2)}) collective-permute-start(bf16[2,768,128]{2,1,0:T(8,128)(2,1)S(1)} %get-tuple-element.132), channel_id=1, source_target_pairs={{0,32},{4,36},{8,40},{12,44},{16,48},{20,52},{24,56},{28,60},{32,6... | collective-permute-start | bytes 1179656 | tf_op jit(solution)/shard_map/while/body/eval_jaxpr/ppermute | solution.py:22
  447.6 33.9 %collective-permute-start = (bf16[2,768,128]{2,1,0:T(8,128)(2,1)S(1)}, bf16[2,768,128]{2,1,0:T(8,128)(2,1)S(1)}, u32[]{:S(2)}, u32[]{:S(2)}) collective-permute-start(bf16[2,768,128]{2,1,0:T(8,128)(2,1)S(1)} %get-tuple-element.132), channel_id=1, source_target_pairs={{0,32},{4,36},{8,40},{12,44},{16,48},{20,52},{24,56},{28,60},{32,6... | collective-permute-start | bytes 1179656 | tf_op jit(solution)/shard_map/while/body/eval_jaxpr/ppermute | solution.py:22
  483.1 34.4 %collective-permute-start = (bf16[2,768,128]{2,1,0:T(8,128)(2,1)S(1)}, bf16[2,768,128]{2,1,0:T(8,128)(2,1)S(1)}, u32[]{:S(2)}, u32[]{:S(2)}) collective-permute-start(bf16[2,768,128]{2,1,0:T(8,128)(2,1)S(1)} %get-tuple-element.132), channel_id=1, source_target_pairs={{0,32},{4,36},{8,40},{12,44},{16,48},{20,52},{24,56},{28,60},{32,6... | collective-permute-start | bytes 1179656 | tf_op jit(solution)/shard_map/while/body/eval_jaxpr/ppermute | solution.py:22
  519.1 33.9 %collective-permute-start = (bf16[2,768,128]{2,1,0:T(8,128)(2,1)S(1)}, bf16[2,768,128]{2,1,0:T(8,128)(2,1)S(1)}, u32[]{:S(2)}, u32[]{:S(2)}) collective-permute-start(bf16[2,768,128]{2,1,0:T(8,128)(2,1)S(1)} %get-tuple-element.132), channel_id=1, source_target_pairs={{0,32},{4,36},{8,40},{12,44},{16,48},{20,52},{24,56},{28,60},{32,6... | collective-permute-start | bytes 1179656 | tf_op jit(solution)/shard_map/while/body/eval_jaxpr/ppermute | solution.py:22
  554.6 35.5 %collective-permute-start = (bf16[2,768,128]{2,1,0:T(8,128)(2,1)S(1)}, bf16[2,768,128]{2,1,0:T(8,128)(2,1)S(1)}, u32[]{:S(2)}, u32[]{:S(2)}) collective-permute-start(bf16[2,768,128]{2,1,0:T(8,128)(2,1)S(1)} %get-tuple-element.132), channel_id=1, source_target_pairs={{0,32},{4,36},{8,40},{12,44},{16,48},{20,52},{24,56},{28,60},{32,6... | collective-permute-start | bytes 1179656 | tf_op jit(solution)/shard_map/while/body/eval_jaxpr/ppermute | solution.py:22
  591.8 27.0 %copy-start.3 = (bf16[384,64]{0,1:T(8,128)(2,1)S(1)}, bf16[384,64]{0,1:T(8,128)(2,1)}, u32[]{:S(2)}) copy-start(bf16[384,64]{0,1:T(8,128)(2,1)} %param.17) | copy-start | bytes 147460
  592.0 5.8 collective-permute-start.4
  597.8 5.4 collective-permute-start.5
  603.5 15.0 %collective-permute-start.6 = (bf16[1,4,96,128]{3,1,2,0:T(4,128)(2,1)S(1)}, bf16[1,4,96,128]{3,1,2,0:T(4,128)(2,1)S(1)}, u32[]{:S(2)}, u32[]{:S(2)}) collective-permute-start(bf16[1,4,96,128]{3,1,2,0:T(4,128)(2,1)S(1)} %broadcast_select_fusion.9), channel_id=1, source_target_pairs={{0,16},{4,20},{8,24},{12,28},{16,0},{20,4},{24,8},{28,12},{32,48},... | collective-permute-start | bytes 294920 | tf_op jit(solution)/shard_map/ppermute | solution.py:17
where the time goes:
time: 637 us; the launch traced here: 636 us
  waiting for transfers between devices  509 us (80%)
  starting transfers between devices  79.6 us (12%)
  matrix products  18 us (3%)
  blocking collectives  16.8 us (3%)
  other arithmetic  10.2 us (2%)
    ppermute x15, waiting for transfers between devices, shifted(): lax.ppermute(x, axis, [(i, (i + by) % length) for i in range(length)])  480 us
    ppermute x15, starting transfers between devices, shifted(): lax.ppermute(x, axis, [(i, (i + by) % length) for i in range(length)])  45.6 us
    ppermute x6, starting transfers between devices, from_partner(): return lax.ppermute(value, axis, pairs)  34 us
    ppermute x6, waiting for transfers between devices, from_partner(): return lax.ppermute(value, axis, pairs)  29.5 us
    psum x1, blocking collectives, body(): return lax.psum(partial_sum, 'grp')  16.8 us
  transfers between devices with their start and end apart: 21, of which 21 were waited for; matrix products, arithmetic and copies ran while one was open for 0% of the time, Pallas kernels for 0%

commit v1 on v0

v1 whole, which is shorter than its diff:
```python
import functools
import math

import jax
import jax.numpy as jnp
from jax import lax
from jax.experimental import pallas as pl
from jax.experimental.pallas import tpu as pltpu
from jax.sharding import Mesh
from jax.sharding import PartitionSpec as P

HD = 128
CH = 64
guidance = 2.5
SCALE = math.log2(math.e) / math.sqrt(HD)
F32 = jnp.float32
BF16 = jnp.bfloat16
VMEM = pl.BlockSpec(memory_space=pltpu.VMEM)
MESSAGE_ROWS = CH + 16

SEQ = ("y", "zh", "z0", "xl")
GRP = ("xh", "c")
Z = ("zh", "z0")
QUERY_AXES = ("z0", "xl")


def dot_t(a, b):
    return lax.dot_general(a, b, (((1,), (1,)), ((), ())), preferred_element_type=F32)


def pack_kernel(half, main_heads, guide_heads, qm, km, vm, qg, kg, vg, q_out, kv_out):
    for h in range(main_heads + guide_heads):
        if h < main_heads:
            q, k, v, at = qm, km, vm, h * HD
        else:
            q, k, v, at = qg, kg, vg, (h - main_heads) * HD
        for b in range(2):
            rows = slice(b * half, (b + 1) * half)
            q_out[2 * h + b] = q[rows, at : at + HD]
            kv_out[2 * h + b, 0] = k[rows, at : at + HD]
            kv_out[2 * h + b, 1] = v[rows, at : at + HD]


def split_two(x):
    high = x.astype(BF16).astype(F32)
    return high, x - high


def attend_kernel(rows_at_once, q_ref, *refs):
    *kv_refs, map_ref, out_ref, sums_ref = refs
    rows = out_ref.shape[2]
    keys = kv_refs[0].shape[0] * kv_refs[0].shape[2]
    ones = jnp.ones((keys, HD), BF16)
    lane = lax.broadcasted_iota(jnp.int32, (rows_at_once, HD), 1)
    picks = lax.broadcasted_iota(jnp.int32, (16, HD), 0) == lax.broadcasted_iota(
        jnp.int32, (16, HD), 1
    )
    picks = picks.astype(F32).astype(BF16)

    def block(piece):
        return piece[:, 0].reshape(keys, HD), piece[:, 1].reshape(keys, HD)

    def weighted(queries, shift):
        total = None
        for piece in kv_refs:
            k, v = block(piece)
            scores = dot_t(queries, k) * SCALE
            if shift is not None:
                scores = scores - shift
            weights = jnp.exp2(scores).astype(BF16)
            part = jnp.dot(
                weights, jnp.concatenate([v, ones], axis=1), preferred_element_type=F32
            )
            total = part if total is None else total + part
        return total

    def highest(queries):
        top = None
        for piece in kv_refs:
            k, _ = block(piece)
            here = jnp.max(dot_t(queries, k), axis=1, keepdims=True)
            top = here if top is None else jnp.maximum(top, here)
        return jnp.ceil(top * SCALE)

    def emit(at, total, shift):
        out_ref[0, :CH, at] = dot_t(map_ref[...], total[:, :HD].astype(BF16)).astype(BF16)
        high, low = split_two(total[:, HD:])
        rest = jnp.where(lane == 0, high, jnp.where(lane == 1, low, 0.0))
        if shift is not None:
            high, low = split_two(shift)
            rest = jnp.where(lane == 2, high, jnp.where(lane == 3, low, rest))
        out_ref[0, CH:, at] = dot_t(picks, rest.astype(BF16)).astype(BF16)

    for i in range(rows // rows_at_once):
        at = slice(i * rows_at_once, (i + 1) * rows_at_once)
        total = weighted(q_ref[at, :], None)
        emit(at, total, None)
        sums_ref[at, :] = total[:, HD:]
    least = jnp.min(sums_ref[...])
    most = jnp.max(sums_ref[...])

    @pl.when(jnp.logical_not((least > 1e-20) & (most < 1e25)))
    def _():
        @pl.loop(0, rows // rows_at_once)
        def _(i):
            at = pl.ds(pl.multiple_of(i * rows_at_once, rows_at_once), rows_at_once)
            queries = q_ref[at, :]
            shift = highest(queries)
            emit(at, weighted(queries, shift), shift)


def attend(queries, key_values, map_t, rows, rows_at_once=256):
    blocks = queries.shape[0] // rows
    keys = key_values[0].shape[0] * key_values[0].shape[2] * len(key_values)
    whole = pl.BlockSpec(key_values[0].shape, lambda i: (0, 0, 0, 0))
    return pl.pallas_call(
        functools.partial(attend_kernel, rows_at_once),
        grid=(blocks,),
        in_specs=[pl.BlockSpec((rows, HD), lambda i: (i, 0))]
        + [whole] * len(key_values)
        + [pl.BlockSpec((CH, HD), lambda i: (0, 0))],
        out_specs=pl.BlockSpec((1, MESSAGE_ROWS, rows), lambda i: (i, 0, 0)),
        out_shape=jax.ShapeDtypeStruct((blocks, MESSAGE_ROWS, rows), BF16),
        scratch_shapes=[pltpu.VMEM((rows, HD), F32)],
        compiler_params=pltpu.CompilerParams(vmem_limit_bytes=40 << 20),
        cost_estimate=pl.CostEstimate(
            flops=4 * queries.shape[0] * keys * HD,
            bytes_accessed=3 << 20,
            transcendentals=queries.shape[0] * keys,
        ),
    )(queries, *key_values, map_t)


def combine_kernel(gain_ref, in_ref, out_ref):
    parts = in_ref.shape[0]
    tokens = 2 * out_ref.shape[1]
    stats = [in_ref[p, CH:, :].astype(F32) for p in range(parts)]
    shifts = [s[2:3] + s[3:4] for s in stats]
    top = functools.reduce(jnp.maximum, shifts)
    scales = [jnp.exp2(shift - top) for shift in shifts]
    summed = sum((s[0:1] + s[1:2]) * scale for s, scale in zip(stats, scales))
    velocity = sum(in_ref[p, :CH, :].astype(F32) * scale for p, scale in enumerate(scales))
    velocity = (velocity * (gain_ref[0] / summed)).T
    velocity = velocity.reshape(out_ref.shape[0], 2, tokens // 2, CH)
    out_ref[...] = jnp.concatenate([velocity[:, 0], velocity[:, 1]], axis=2).astype(BF16)


def body(
    query_main, key_main, value_main, query_guide, key_guide, value_guide, map_main, map_guide
):
    tokens_here = query_main.shape[0]
    half = tokens_here // 2
    main_heads = query_main.shape[1] // HD
    guide_heads = query_guide.shape[1] // HD
    planes = lax.axis_size(Z)
    head = lax.axis_index("zh")

    maps = jnp.concatenate([map_main, map_guide], axis=0).reshape(-1, HD, CH)
    map_t = lax.dynamic_index_in_dim(maps, head, 0, keepdims=False).T
    gain = jnp.where(head < main_heads, guidance, 1.0 - guidance).astype(F32).reshape(1)

    with jax.named_scope("pack"):
        q, kv = pl.pallas_call(
            functools.partial(pack_kernel, half, main_heads, guide_heads),
            in_specs=[VMEM] * 6,
            out_specs=[VMEM] * 2,
            out_shape=[
                jax.ShapeDtypeStruct((planes, half, HD), BF16),
                jax.ShapeDtypeStruct((planes, 2, half, HD), BF16),
            ],
        )(query_main, key_main, value_main, query_guide, key_guide, value_guide)
    with jax.named_scope("to_heads"):
        q = lax.all_to_all(q, Z, 0, 0, tiled=True)
        kv = lax.all_to_all(kv, Z, 0, 0, tiled=True)
    rows = planes * half
    with jax.named_scope("gather"):
        queries = lax.all_gather(q.reshape(rows, HD), QUERY_AXES, axis=0, tiled=True)
        around = lax.axis_size("y")
        key_values = [kv] + [
            lax.ppermute(kv, "y", [(i, (i + by) % around) for i in range(around)])
            for by in (1, around - 1, 2)
        ]
    with jax.named_scope("attend"):
        shares = attend(queries, key_values, map_t, rows)
    with jax.named_scope("combine"):
        shares = lax.all_to_all(shares, QUERY_AXES, 0, 0, tiled=True)
        velocity = pl.pallas_call(
            combine_kernel,
            in_specs=[pl.BlockSpec(memory_space=pltpu.SMEM), VMEM],
            out_specs=VMEM,
            out_shape=jax.ShapeDtypeStruct((planes, half // 2, 2 * CH), BF16),
        )(gain, shares)
    with jax.named_scope("to_tokens"):
        velocity = lax.all_to_all(velocity, Z, 0, 0, tiled=True)
        velocity = jnp.sum(
            velocity.reshape(planes // 2, half, 2 * CH).astype(F32), axis=0
        )
        everywhere = lax.all_gather(velocity, GRP, axis=0)
        velocity = jnp.sum(everywhere, axis=0)
    return velocity.reshape(2, half // 2, 2, CH).transpose(0, 2, 1, 3).reshape(tokens_here, CH)


def solution(mesh):
    fine = Mesh(mesh.devices.reshape(4, 8, 2, 2, 2, 2), SEQ + GRP)
    placed = (P(SEQ, GRP),) * 6 + (P(GRP, None),) * 2
    return jax.shard_map(
        body, mesh=fine, in_specs=placed, out_specs=P(SEQ, None), check_vma=False
    )
```

time: 637 us -> 145 us (0.23)
  waiting for transfers between devices: 509 us -> 7.41 us
  blocking collectives: 16.8 us -> 84.1 us
  starting transfers between devices: 79.6 us -> 29.6 us
  Pallas kernels: 0 us -> 21.2 us
  matrix products: 18 us -> 0 us
  other arithmetic: 10.2 us -> 0.04 us
    ppermute x21 -> x3, waiting for transfers between devices: 509 us -> 0.01 us  [body(): lax.ppermute(kv, 'y', [(i, (i + by) % around) for i in range(around)])]
    ppermute x21 -> x3, starting transfers between devices: 79.6 us -> 10.1 us  [body(): lax.ppermute(kv, 'y', [(i, (i + by) % around) for i in range(around)])]
    all_to_all x0 -> x2, blocking collectives: none -> 51.6 us  [the longest x1 33.7 us: body(): kv = lax.all_to_all(kv, Z, 0, 0, tiled=True)]
    all_gather x0 -> x2, blocking collectives: none -> 32.4 us  [the longest x1 19.3 us: body(): lax.all_gather(q.reshape(rows, HD), QUERY_AXES, axis=0, tiled=True)]
    pallas_call x0 -> x3, Pallas kernels: none -> 21.2 us  [the longest x1 17.2 us: attend(): pl.pallas_call(functools.partial(attend_kernel, rows_at_once), grid=(bloc...]
    all_to_all x0 -> x2, starting transfers between devices: none -> 19.5 us  [the longest x1 11.6 us: body(): q = lax.all_to_all(q, Z, 0, 0, tiled=True)]
    dot_general x34 -> x0, matrix products: 18 us -> none  [the longest x16 10 us: absorb(): jnp.dot(weights.astype(jnp.bfloat16), key_value[1], preferred_element_typ...]
    psum x1 -> x0, blocking collectives: 16.8 us -> none  [body(): return lax.psum(partial_sum, 'grp')]
  transfers between devices with their start and end apart: 21 -> 5, of which waited for: 21 -> 2; matrix products, arithmetic and copies ran while one was open for 0% -> 0% of each run, Pallas kernels for 0% -> 0%
where the time goes in v1:
time: 145 us; the launch traced here: 144 us
  blocking collectives  84.1 us (58%)
  starting transfers between devices  29.6 us (20%)
  Pallas kernels  21.2 us (15%)
  waiting for transfers between devices  7.41 us (5%)
  local copies, waits for them, and re-layouts  1.65 us (1%)
    all_to_all x1, blocking collectives, body(): kv = lax.all_to_all(kv, Z, 0, 0, tiled=True)  33.7 us
    all_gather x1, blocking collectives, body(): lax.all_gather(q.reshape(rows, HD), QUERY_AXES, axis=0, tiled=True)  19.3 us
    all_to_all x1, blocking collectives, body(): velocity = lax.all_to_all(velocity, Z, 0, 0, tiled=True)  17.9 us
    pallas_call x1, Pallas kernels, attend(): pl.pallas_call(functools.partial(attend_kernel, rows_at_once), grid=(bloc...  17.2 us
    all_gather x1, blocking collectives, body(): everywhere = lax.all_gather(velocity, GRP, axis=0)  13.1 us
    all_to_all x1, starting transfers between devices, body(): q = lax.all_to_all(q, Z, 0, 0, tiled=True)  11.6 us
    ppermute x3, starting transfers between devices, body(): lax.ppermute(kv, 'y', [(i, (i + by) % around) for i in range(around)])  10.1 us
    all_to_all x1, starting transfers between devices, body(): shares = lax.all_to_all(shares, QUERY_AXES, 0, 0, tiled=True)  7.83 us
  transfers between devices with their start and end apart: 5, of which 2 were waited for; matrix products, arithmetic and copies ran while one was open for 0% of the time, Pallas kernels for 0%

profile of v1, /device:TPU:1, one launch (start us, length us, event | category | flops | bytes accessed | tf_op | source)
XLA Modules:
  0.0 144.0 jit_solution(3040692701558237612)
XLA Ops:
  0.0 2.1 %pack.1 = (bf16[16,48,128]{2,1,0:T(8,128)(2,1)}, bf16[16,2,48,128]{3,2,1,0:T(8,128)(2,1)}) custom-call(bf16[96,640]{1,0:T(8,128)(2,1)} %qm.1, bf16[96,640]{1,0:T(8,128)(2,1)} %km.1, bf16[96,640]{1,0:T(8,128)(2,1)} %vm.1, bf16[96,384]{1,0:T(8,128)(2,1)} %qg.1, bf16[96,384]{1,0:T(8,128)(2,1)} %kg.1, bf16[96,384]{1,0:T(8,128)(2,1)} %vg.1), custom_call_target="tpu_custom_call" | custom-call | tf_op jit(solution)/shard_map/pack/pallas_call | solution.py:163
  2.1 33.7 %all_to_all.20.refs_0_ = bf16[16,2,48,128]{3,2,1,0:T(8,128)(2,1)S(1)} all-to-all(bf16[16,2,48,128]{3,2,1,0:T(8,128)(2,1)} %get-tuple-element.8), channel_id=1, replica_groups=mesh['y'=4,'zh'=8,'z0'=2,'xl'=2,'xh'=2,'c'=2] {'zh','z0'}, dimensions={0} | all-to-all | bytes 786432 | tf_op jit(solution)/shard_map/to_heads/all_to_all | solution.py:174
  35.8 0.0 copy-start.1
  35.8 0.0 copy-start.2
  35.8 11.6 %all-to-all-start = ((bf16[16,48,128]{2,1,0:T(8,128)(2,1)}), bf16[16,48,128]{2,1,0:T(8,128)(2,1)S(1)}, u32[]{:S(2)}, u32[]{:S(2)}) async-start(bf16[16,48,128]{2,1,0:T(8,128)(2,1)} %get-tuple-element.7), calls=%async_computation | async-start | bytes 393216 | tf_op jit(solution)/shard_map/to_heads/all_to_all | solution.py:173
  47.4 0.0 copy-done.1
  47.5 0.0 copy-done.2
  47.5 4.8 %collective-permute-start.2 = (bf16[16,2,48,128]{3,2,1,0:T(8,128)(2,1)S(1)}, bf16[16,2,48,128]{3,2,1,0:T(8,128)(2,1)S(1)}, u32[]{:S(2)}, u32[]{:S(2)}) collective-permute-start(bf16[16,2,48,128]{3,2,1,0:T(8,128)(2,1)S(1)} %all_to_all.20.refs_0_), channel_id=1, source_target_pairs={{0,256},{128,384},{256,0},{384,128},{1,257},{129,385},{257,1},{385... | collective-permute-start | bytes 1179656 | tf_op jit(solution)/shard_map/gather/ppermute | solution.py:180
  52.3 2.7 %collective-permute-start.1 = (bf16[16,2,48,128]{3,2,1,0:T(8,128)(2,1)S(1)}, bf16[16,2,48,128]{3,2,1,0:T(8,128)(2,1)S(1)}, u32[]{:S(2)}, u32[]{:S(2)}) collective-permute-start(bf16[16,2,48,128]{3,2,1,0:T(8,128)(2,1)S(1)} %all_to_all.20.refs_0_), channel_id=1, source_target_pairs={{0,384},{128,0},{256,128},{384,256},{1,385},{129,1},{257,129},{385... | collective-permute-start | bytes 1179656 | tf_op jit(solution)/shard_map/gather/ppermute | solution.py:180
  55.0 2.6 %collective-permute-start = (bf16[16,2,48,128]{3,2,1,0:T(8,128)(2,1)S(1)}, bf16[16,2,48,128]{3,2,1,0:T(8,128)(2,1)S(1)}, u32[]{:S(2)}, u32[]{:S(2)}) collective-permute-start(bf16[16,2,48,128]{3,2,1,0:T(8,128)(2,1)S(1)} %all_to_all.20.refs_0_), channel_id=1, source_target_pairs={{0,128},{128,256},{256,384},{384,0},{1,129},{129,257},{257,385},{3... | collective-permute-start | bytes 1179656 | tf_op jit(solution)/shard_map/gather/ppermute | solution.py:180
  57.7 2.1 %all-to-all-done = bf16[16,48,128]{2,1,0:T(8,128)(2,1)S(1)} async-done(((bf16[16,48,128]{2,1,0:T(8,128)(2,1)}), bf16[16,48,128]{2,1,0:T(8,128)(2,1)S(1)}, u32[]{:S(2)}, u32[]{:S(2)}) %all-to-all-start) | async-done | bytes 196640 | tf_op jit(solution)/shard_map/to_heads/all_to_all | solution.py:173
  59.8 19.3 %all_gather.9.q_ref = bf16[3072,128]{1,0:T(8,128)(2,1)S(1)} all-gather(bf16[768,128]{1,0:T(8,128)(2,1)S(1)} %bitcast.20), channel_id=1, replica_groups=mesh['y'=4,'zh'=8,'z0'=2,'xl'=2,'xh'=2,'c'=2] {'z0','xl'}, dimensions={0}, use_global_device_ids=true | all-gather | bytes 983040 | tf_op jit(solution)/shard_map/gather/all_gather | solution.py:177
  79.2 0.0 collective-permute-done.2.refs_3_
  79.2 0.0 collective-permute-done.1.refs_2_
  79.2 0.0 collective-permute-done.refs_1_
  79.2 17.2 %attend.1 = bf16[4,80,768]{2,1,0:T(8,128)(2,1)} custom-call(bf16[3072,128]{1,0:T(8,128)(2,1)S(1)} %all_gather.9.q_ref, bf16[16,2,48,128]{3,2,1,0:T(8,128)(2,1)S(1)} %all_to_all.20.refs_0_, bf16[16,2,48,128]{3,2,1,0:T(8,128)(2,1)S(1)} %collective-permute-done.refs_1_, bf16[16,2,48,128]{3,2,1,0:T(8,128)(2,1)S(1)} %collective-permute-done.1.refs_2_, ...), custom_call_target="tpu_custom_call" | custom-call | flops 4831838208 | bytes 3145728 | tf_op jit(solution)/shard_map/attend/pallas_call | solution.py:116
  96.3 7.8 %all-to-all-start.2 = ((bf16[4,80,768]{2,1,0:T(8,128)(2,1)}), bf16[4,80,768]{2,1,0:T(8,128)(2,1)S(1)}, u32[]{:S(2)}, u32[]{:S(2)}) async-start(bf16[4,80,768]{2,1,0:T(8,128)(2,1)} %attend.1), calls=%async_computation.2 | async-start | bytes 983040 | tf_op jit(solution)/shard_map/combine/all_to_all | solution.py:186
  104.2 5.3 %all-to-all-done.2.in_ref = bf16[4,80,768]{2,1,0:T(8,128)(2,1)S(1)} async-done(((bf16[4,80,768]{2,1,0:T(8,128)(2,1)}), bf16[4,80,768]{2,1,0:T(8,128)(2,1)S(1)}, u32[]{:S(2)}, u32[]{:S(2)}) %all-to-all-start.2) | async-done | bytes 491552 | tf_op jit(solution)/shard_map/combine/all_to_all | solution.py:186
  109.5 0.0 copy-start
  109.5 0.8 copy-done
  110.2 2.0 %combine.1 = bf16[16,24,128]{2,1,0:T(8,128)(2,1)} custom-call(f32[1]{0:T(128)} %bitcast.gain_ref, bf16[4,80,768]{2,1,0:T(8,128)(2,1)} %copy-done), custom_call_target="tpu_custom_call" | custom-call | tf_op jit(solution)/shard_map/combine/pallas_call | solution.py:187
  112.2 17.9 %all_to_all.21 = bf16[16,24,128]{2,1,0:T(8,128)(2,1)S(1)} all-to-all(bf16[16,24,128]{2,1,0:T(8,128)(2,1)} %combine.1), channel_id=1, replica_groups=mesh['y'=4,'zh'=8,'z0'=2,'xl'=2,'xh'=2,'c'=2] {'zh','z0'}, dimensions={0} | all-to-all | bytes 196608 | tf_op jit(solution)/shard_map/to_tokens/all_to_all | solution.py:194
  130.1 13.1 %all-gather = f32[192,128]{1,0:T(8,128)S(1)} all-gather(f32[48,128]{1,0:T(8,128)S(1)} %convert_reduce_fusion), channel_id=2, replica_groups=mesh['y'=4,'zh'=8,'z0'=2,'xl'=2,'xh'=2,'c'=2] {'xh','c'}, dimensions={0}, use_global_device_ids=true | all-gather | bytes 122880 | tf_op jit(solution)/shard_map/to_tokens/all_gather | solution.py:198
  143.2 0.1 reshape.21
  143.3 0.7 copy.15
  (7 shorter events, 0.1 us)
Async XLA Ops:
  35.8 11.6 %copy-start.1 = (bf16[640,64]{0,1:T(8,128)(2,1)S(1)}, bf16[640,64]{0,1:T(8,128)(2,1)}, u32[]{:S(2)}) copy-start(bf16[640,64]{0,1:T(8,128)(2,1)} %param.14) | copy-start | bytes 245764
  35.8 11.6 %copy-start.2 = (bf16[384,64]{0,1:T(8,128)(2,1)S(1)}, bf16[384,64]{0,1:T(8,128)(2,1)}, u32[]{:S(2)}) copy-start(bf16[384,64]{0,1:T(8,128)(2,1)} %param.15) | copy-start | bytes 147460
  35.8 24.0 %all-to-all-start = ((bf16[16,48,128]{2,1,0:T(8,128)(2,1)}), bf16[16,48,128]{2,1,0:T(8,128)(2,1)S(1)}, u32[]{:S(2)}, u32[]{:S(2)}) async-start(bf16[16,48,128]{2,1,0:T(8,128)(2,1)} %get-tuple-element.7), calls=%async_computation | async-start | bytes 393216 | tf_op jit(solution)/shard_map/to_heads/all_to_all | solution.py:173
  47.5 31.6 %collective-permute-start.2 = (bf16[16,2,48,128]{3,2,1,0:T(8,128)(2,1)S(1)}, bf16[16,2,48,128]{3,2,1,0:T(8,128)(2,1)S(1)}, u32[]{:S(2)}, u32[]{:S(2)}) collective-permute-start(bf16[16,2,48,128]{3,2,1,0:T(8,128)(2,1)S(1)} %all_to_all.20.refs_0_), channel_id=1, source_target_pairs={{0,256},{128,384},{256,0},{384,128},{1,257},{129,385},{257,1},{385... | collective-permute-start | bytes 1179656 | tf_op jit(solution)/shard_map/gather/ppermute | solution.py:180
  52.3 26.8 %collective-permute-start.1 = (bf16[16,2,48,128]{3,2,1,0:T(8,128)(2,1)S(1)}, bf16[16,2,48,128]{3,2,1,0:T(8,128)(2,1)S(1)}, u32[]{:S(2)}, u32[]{:S(2)}) collective-permute-start(bf16[16,2,48,128]{3,2,1,0:T(8,128)(2,1)S(1)} %all_to_all.20.refs_0_), channel_id=1, source_target_pairs={{0,384},{128,0},{256,128},{384,256},{1,385},{129,1},{257,129},{385... | collective-permute-start | bytes 1179656 | tf_op jit(solution)/shard_map/gather/ppermute | solution.py:180
  55.0 24.1 %collective-permute-start = (bf16[16,2,48,128]{3,2,1,0:T(8,128)(2,1)S(1)}, bf16[16,2,48,128]{3,2,1,0:T(8,128)(2,1)S(1)}, u32[]{:S(2)}, u32[]{:S(2)}) collective-permute-start(bf16[16,2,48,128]{3,2,1,0:T(8,128)(2,1)S(1)} %all_to_all.20.refs_0_), channel_id=1, source_target_pairs={{0,128},{128,256},{256,384},{384,0},{1,129},{129,257},{257,385},{3... | collective-permute-start | bytes 1179656 | tf_op jit(solution)/shard_map/gather/ppermute | solution.py:180
  96.3 13.1 %all-to-all-start.2 = ((bf16[4,80,768]{2,1,0:T(8,128)(2,1)}), bf16[4,80,768]{2,1,0:T(8,128)(2,1)S(1)}, u32[]{:S(2)}, u32[]{:S(2)}) async-start(bf16[4,80,768]{2,1,0:T(8,128)(2,1)} %attend.1), calls=%async_computation.2 | async-start | bytes 983040 | tf_op jit(solution)/shard_map/combine/all_to_all | solution.py:186
  109.5 0.8 copy-start

commit v2 on v1

v2 whole, which is shorter than its diff:
```python
import functools
import math

import jax
import jax.numpy as jnp
from jax import lax
from jax.experimental import pallas as pl
from jax.experimental.pallas import tpu as pltpu
from jax.sharding import Mesh
from jax.sharding import PartitionSpec as P

HD = 128
CH = 64
guidance = 2.5
SCALE = math.log2(math.e) / math.sqrt(HD)
F32 = jnp.float32
BF16 = jnp.bfloat16
VMEM = pl.BlockSpec(memory_space=pltpu.VMEM)
SMEM = pl.BlockSpec(memory_space=pltpu.SMEM)
SMALL = pltpu.CompilerParams(vmem_limit_bytes=12 << 20)
MESSAGE_ROWS = CH + 16

SEQ = ("y", "zh", "z0", "xl")
GRP = ("xh", "c")
QUERY_AXES = ("z0", "xl")


def dot_t(a, b):
    return lax.dot_general(a, b, (((1,), (1,)), ((), ())), preferred_element_type=F32)


def pack_kernel(main_heads, guide_heads, qm, km, vm, qg, kg, vg, out_ref):
    for h in range(main_heads + guide_heads):
        at = (h if h < main_heads else h - main_heads) * HD
        for t, ref in enumerate((qm, km, vm) if h < main_heads else (qg, kg, vg)):
            out_ref[h, t] = ref[:, at : at + HD]


def split_two(x):
    high = x.astype(BF16).astype(F32)
    return high, x - high


def attend_kernel(member, q_refs, kv_refs, map_ref, before_ref, out_ref, sums_ref):
    keys = kv_refs[0].shape[0] * kv_refs[0].shape[2]
    rows = out_ref.shape[2]
    last = out_ref.dtype == BF16
    ones = jnp.ones((keys, HD), BF16)
    lane = lax.broadcasted_iota(jnp.int32, (rows, HD), 1)
    picks = lax.broadcasted_iota(jnp.int32, (16, HD), 0) == lax.broadcasted_iota(
        jnp.int32, (16, HD), 1
    )
    picks = picks.astype(F32).astype(BF16)

    def block(piece):
        return piece[:, 0].reshape(keys, HD), piece[:, 1].reshape(keys, HD)

    def weighted(queries, shift):
        total = None
        for piece in kv_refs:
            k, v = block(piece)
            scores = dot_t(queries, k) * SCALE
            if shift is not None:
                scores = scores - shift
            weights = jnp.exp2(scores).astype(BF16)
            part = jnp.dot(
                weights, jnp.concatenate([v, ones], axis=1), preferred_element_type=F32
            )
            total = part if total is None else total + part
        return total

    def highest(queries):
        top = None
        for piece in kv_refs:
            k, _ = block(piece)
            here = jnp.max(dot_t(queries, k), axis=1, keepdims=True)
            top = here if top is None else jnp.maximum(top, here)
        return jnp.ceil(top * SCALE)

    def emit(i, total, shift):
        velocity = dot_t(map_ref[...], total[:, :HD].astype(BF16))
        high, low = split_two(total[:, HD:])
        rest = jnp.where(lane == 0, high, jnp.where(lane == 1, low, 0.0))
        if shift is not None:
            high, low = split_two(shift)
            rest = jnp.where(lane == 2, high, jnp.where(lane == 3, low, rest))
        stats = dot_t(picks, rest.astype(BF16))
        summed = stats[0:1] + stats[1:2]
        top = stats[2:3] + stats[3:4]
        if before_ref is not None:
            top_before = before_ref[i, CH + 1 : CH + 2, :]
            both = jnp.maximum(top, top_before)
            scale, scale_before = jnp.exp2(top - both), jnp.exp2(top_before - both)
            velocity = velocity * scale + before_ref[i, :CH, :] * scale_before
            summed = summed * scale + before_ref[i, CH : CH + 1, :] * scale_before
            top = both
        to = member ^ i if last else i
        out_ref[to, :CH, :] = velocity.astype(out_ref.dtype)
        if last:
            tail = split_two(summed) + split_two(top)
        else:
            tail = (summed, top)
        filler = jnp.zeros((out_ref.shape[1] - CH - len(tail), rows), F32)
        out_ref[to, CH:, :] = jnp.concatenate(tail + (filler,), axis=0).astype(out_ref.dtype)

    for i, q_ref in enumerate(q_refs):
        queries = q_ref[...]
        total = weighted(queries, None)
        emit(i, total, None)
        sums_ref[...] = total[:, HD:]
        least = jnp.min(sums_ref[...])
        most = jnp.max(sums_ref[...])

        @pl.when(jnp.logical_not((least > 1e-20) & (most < 1e25)))
        def _():
            shift = highest(queries)
            emit(i, weighted(queries, shift), shift)


def attend(member, queries, key_values, map_t, before, last):
    rows = queries[0].shape[0]
    blocks = len(queries)
    keys = key_values[0].shape[0] * key_values[0].shape[2] * len(key_values)
    operands = [*queries, *key_values, map_t] + ([] if before is None else [before])

    def kernel(member_ref, *refs):
        q_refs, refs = refs[:blocks], refs[blocks:]
        kv_refs, refs = refs[: len(key_values)], refs[len(key_values) :]
        map_ref, refs = refs[0], refs[1:]
        before_ref = None
        if before is not None:
            before_ref, refs = refs[0], refs[1:]
        attend_kernel(member_ref[0], q_refs, kv_refs, map_ref, before_ref, *refs)

    out = (blocks, MESSAGE_ROWS, rows) if last else (blocks, CH + 8, rows)
    return pl.pallas_call(
        kernel,
        in_specs=[SMEM] + [VMEM] * len(operands),
        out_specs=VMEM,
        out_shape=jax.ShapeDtypeStruct(out, BF16 if last else F32),
        scratch_shapes=[pltpu.VMEM((rows, HD), F32)],
        compiler_params=pltpu.CompilerParams(vmem_limit_bytes=40 << 20),
        cost_estimate=pl.CostEstimate(
            flops=8 * blocks * rows * keys * HD,
            bytes_accessed=3 << 20,
            transcendentals=blocks * rows * keys,
        ),
    )(member, *operands)


def combine_kernel(gain_ref, in_ref, out_ref):
    parts = in_ref.shape[0]
    half = out_ref.shape[1]
    stats = [in_ref[p, CH:, :].astype(F32) for p in range(parts)]
    shifts = [s[2:3] + s[3:4] for s in stats]
    top = functools.reduce(jnp.maximum, shifts)
    scales = [jnp.exp2(shift - top) for shift in shifts]
    summed = sum((s[0:1] + s[1:2]) * scale for s, scale in zip(stats, scales))
    velocity = sum(in_ref[p, :CH, :].astype(F32) * scale for p, scale in enumerate(scales))
    velocity = (velocity * (gain_ref[0] / summed)).T
    velocity = velocity.reshape(out_ref.shape[0], 2, half, CH)
    out_ref[...] = jnp.concatenate([velocity[:, 0], velocity[:, 1]], axis=2).astype(BF16)


def body(
    query_main, key_main, value_main, query_guide, key_guide, value_guide, map_main, map_guide
):
    tokens_here = query_main.shape[0]
    main_heads = query_main.shape[1] // HD
    guide_heads = query_guide.shape[1] // HD
    heads = main_heads + guide_heads
    head = lax.axis_index("zh")

    maps = jnp.concatenate([map_main, map_guide], axis=0).reshape(-1, HD, CH)
    map_t = lax.dynamic_index_in_dim(maps, head, 0, keepdims=False).T
    gain = jnp.where(head < main_heads, guidance, 1.0 - guidance).astype(F32).reshape(1)

    with jax.named_scope("pack"):
        packed = pl.pallas_call(
            functools.partial(pack_kernel, main_heads, guide_heads),
            in_specs=[VMEM] * 6,
            out_specs=VMEM,
            out_shape=jax.ShapeDtypeStruct((heads, 3, tokens_here, HD), BF16),
            compiler_params=SMALL,
        )(query_main, key_main, value_main, query_guide, key_guide, value_guide)
    with jax.named_scope("to_heads"):
        arrived = lax.all_to_all(packed, "zh", 0, 0, tiled=True)
    rows = heads * tokens_here
    with jax.named_scope("gather"):
        q = arrived[:, 0].reshape(rows, HD)
        kv = arrived[:, 1:]
        queries = [q] + [
            lax.ppermute(q, QUERY_AXES, [(i, i ^ by) for i in range(4)]) for by in (1, 2, 3)
        ]
        around = lax.axis_size("y")
        key_values = [kv] + [
            lax.ppermute(kv, "y", [(i, (i + by) % around) for i in range(around)])
            for by in (1, around - 1, 2)
        ]
    with jax.named_scope("attend"):
        member = lax.axis_index(QUERY_AXES).reshape(1)
        shares = attend(member, queries, key_values[:1], map_t, None, False)
        shares = attend(member, queries, key_values[1:3], map_t, shares, False)
        shares = attend(member, queries, key_values[3:], map_t, shares, True)
    with jax.named_scope("combine"):
        shares = lax.all_to_all(shares, QUERY_AXES, 0, 0, tiled=True)
        velocity = pl.pallas_call(
            combine_kernel,
            in_specs=[SMEM, VMEM],
            out_specs=VMEM,
            out_shape=jax.ShapeDtypeStruct((heads, tokens_here // 2, 2 * CH), BF16),
            compiler_params=SMALL,
        )(gain, shares)
    with jax.named_scope("to_tokens"):
        velocity = lax.all_to_all(velocity, "zh", 0, 0, tiled=True)
        velocity = jnp.sum(velocity.astype(F32), axis=0)
        everywhere = lax.all_gather(velocity, GRP, axis=0)
        velocity = jnp.sum(everywhere, axis=0)
    return velocity.reshape(tokens_here // 2, 2, CH).transpose(1, 0, 2).reshape(tokens_here, CH)


def solution(mesh):
    fine = Mesh(mesh.devices.reshape(4, 8, 2, 2, 2, 2), SEQ + GRP)
    placed = (P(SEQ, GRP),) * 6 + (P(GRP, None),) * 2
    return jax.shard_map(
        body, mesh=fine, in_specs=placed, out_specs=P(SEQ, None), check_vma=False
    )
```

time: 145 us -> 147 us (1.014)
  local copies, waits for them, and re-layouts: 1.65 us -> 6.27 us
  starting transfers between devices: 29.6 us -> 25.7 us
  waiting for transfers between devices: 7.41 us -> 9.66 us
    all_gather x1 -> x0, blocking collectives: 19.3 us -> none  [body(): lax.all_gather(q.reshape(rows, HD), QUERY_AXES, axis=0, tiled=True)]
    all_to_all x2, blocking collectives: 51.6 us -> 63.4 us  [the longest x1 44.4 us: body(): arrived = lax.all_to_all(packed, 'zh', 0, 0, tiled=True)]
    all_to_all x1 -> x0, starting transfers between devices: 11.6 us -> none  [body(): q = lax.all_to_all(q, Z, 0, 0, tiled=True)]
    ppermute x0 -> x3, starting transfers between devices: none -> 9.73 us  [body(): lax.ppermute(q, QUERY_AXES, [(i, i ^ by) for i in range(4)])]
    all_gather x1, blocking collectives: 13.1 us -> 21 us  [body(): everywhere = lax.all_gather(velocity, GRP, axis=0)]
    unnamed x8 -> x18, local copies, waits for them, and re-layouts: 0.81 us -> 5.39 us
    ppermute x3, waiting for transfers between devices: 0.01 us -> 4.35 us  [body(): lax.ppermute(kv, 'y', [(i, (i + by) % around) for i in range(around)])]
    all_to_all x1 -> x0, waiting for transfers between devices: 2.1 us -> none  [body(): q = lax.all_to_all(q, Z, 0, 0, tiled=True)]
  transfers between devices with their start and end apart: 5 -> 7, of which waited for: 2 -> 2; matrix products, arithmetic and copies ran while one was open for 0% -> 0% of each run, Pallas kernels for 0% -> 10%
where the time goes in v2:
time: 147 us
  blocking collectives  84.4 us (57%)
  starting transfers between devices  25.7 us (17%)
  Pallas kernels  20.4 us (14%)
  waiting for transfers between devices  9.66 us (7%)
  local copies, waits for them, and re-layouts  6.27 us (4%)
    all_to_all x1, blocking collectives, body(): arrived = lax.all_to_all(packed, 'zh', 0, 0, tiled=True)  44.4 us
    all_gather x1, blocking collectives, body(): everywhere = lax.all_gather(velocity, GRP, axis=0)  21 us
    pallas_call x3, Pallas kernels, attend(): pl.pallas_call(kernel, in_specs=[SMEM] + [VMEM] * len(operands), out_spec...  20 us
    all_to_all x1, blocking collectives, body(): velocity = lax.all_to_all(velocity, 'zh', 0, 0, tiled=True)  19 us
    ppermute x3, starting transfers between devices, body(): lax.ppermute(kv, 'y', [(i, (i + by) % around) for i in range(around)])  10.1 us
    ppermute x3, starting transfers between devices, body(): lax.ppermute(q, QUERY_AXES, [(i, i ^ by) for i in range(4)])  9.73 us
    all_to_all x1, starting transfers between devices, body(): shares = lax.all_to_all(shares, QUERY_AXES, 0, 0, tiled=True)  5.9 us
    unnamed x18, local copies, waits for them, and re-layouts  5.39 us
  transfers between devices with their start and end apart: 7, of which 2 were waited for; matrix products, arithmetic and copies ran while one was open for 0% of the time, Pallas kernels for 10%

profile of v2, /device:TPU:1, one launch (start us, length us, event | category | flops | bytes accessed | tf_op | source)
XLA Modules:
  0.0 146.7 jit_solution(15403207180372713613)
XLA Ops:
  0.0 0.0 copy-start
  0.0 0.9 copy-done
  0.9 0.0 copy-start.1
  0.9 0.9 copy-done.1
  1.8 0.0 copy-start.2
  1.8 0.9 copy-done.2
  2.7 0.0 copy-start.3
  2.7 0.9 copy-done.3
  3.6 0.0 copy-start.4
  3.6 0.9 copy-done.4
  4.5 0.0 copy-start.5
  4.5 0.9 copy-done.5
  5.4 0.1 pack.1
  5.5 44.4 %all_to_all.15 = bf16[8,3,96,128]{3,2,1,0:T(8,128)(2,1)S(1)} all-to-all(bf16[8,3,96,128]{3,2,1,0:T(8,128)(2,1)S(1)} %pack.1), channel_id=1, replica_groups=mesh['y'=4,'zh'=8,'z0'=2,'xl'=2,'xh'=2,'c'=2] {'zh'}, dimensions={0} | all-to-all | bytes 1179648 | tf_op jit(solution)/shard_map/to_heads/all_to_all | solution.py:187
  49.9 0.0 copy-start.6
  49.9 0.0 copy-start.7
  49.9 5.6 %collective-permute-start.2 = (bf16[768,128]{1,0:T(8,128)(2,1)S(1)}, bf16[768,128]{1,0:T(8,128)(2,1)S(1)}, u32[]{:S(2)}, u32[]{:S(2)}) collective-permute-start(bf16[768,128]{1,0:T(8,128)(2,1)S(1)} %bitcast.16), channel_id=1, source_target_pairs={{0,12},{4,8},{8,4},{12,0},{1,13},{5,9},{9,5},{13,1},{2,14},{6,10},... | collective-permute-start | bytes 589832 | tf_op jit(solution)/shard_map/gather/ppermute | solution.py:193
  55.5 1.9 %collective-permute-start.1 = (bf16[768,128]{1,0:T(8,128)(2,1)S(1)}, bf16[768,128]{1,0:T(8,128)(2,1)S(1)}, u32[]{:S(2)}, u32[]{:S(2)}) collective-permute-start(bf16[768,128]{1,0:T(8,128)(2,1)S(1)} %bitcast.17), channel_id=1, source_target_pairs={{0,8},{4,12},{8,0},{12,4},{1,9},{5,13},{9,1},{13,5},{2,10},{6,14},... | collective-permute-start | bytes 589832 | tf_op jit(solution)/shard_map/gather/ppermute | solution.py:193
  57.4 2.2 %collective-permute-start = (bf16[768,128]{1,0:T(8,128)(2,1)S(1)}, bf16[768,128]{1,0:T(8,128)(2,1)S(1)}, u32[]{:S(2)}, u32[]{:S(2)}) collective-permute-start(bf16[768,128]{1,0:T(8,128)(2,1)S(1)} %bitcast.18), channel_id=1, source_target_pairs={{0,4},{4,0},{8,12},{12,8},{1,5},{5,1},{9,13},{13,9},{2,6},{6,2},{1... | collective-permute-start | bytes 589832 | tf_op jit(solution)/shard_map/gather/ppermute | solution.py:193
  59.7 4.6 %collective-permute-start.5 = (bf16[8,2,96,128]{3,2,1,0:T(8,128)(2,1)S(1)}, bf16[8,2,96,128]{3,2,1,0:T(8,128)(2,1)S(1)}, u32[]{:S(2)}, u32[]{:S(2)}) collective-permute-start(bf16[8,2,96,128]{3,2,1,0:T(8,128)(2,1)S(1)} %slice.9.refs_4_), channel_id=1, source_target_pairs={{0,384},{128,0},{256,128},{384,256},{1,385},{129,1},{257,129},{385... | collective-permute-start | bytes 1179656 | tf_op jit(solution)/shard_map/gather/ppermute | solution.py:197
  64.3 1.9 %collective-permute-start.4 = (bf16[8,2,96,128]{3,2,1,0:T(8,128)(2,1)S(1)}, bf16[8,2,96,128]{3,2,1,0:T(8,128)(2,1)S(1)}, u32[]{:S(2)}, u32[]{:S(2)}) collective-permute-start(bf16[8,2,96,128]{3,2,1,0:T(8,128)(2,1)S(1)} %slice.9.refs_4_), channel_id=1, source_target_pairs={{0,128},{128,256},{256,384},{384,0},{1,129},{129,257},{257,385},{3... | collective-permute-start | bytes 1179656 | tf_op jit(solution)/shard_map/gather/ppermute | solution.py:197
  66.3 0.0 copy-done.6
  66.3 0.0 copy-done.7
  66.4 0.0 collective-permute-done.2.refs_3_
  66.4 3.5 %collective-permute-start.3 = (bf16[8,2,96,128]{3,2,1,0:T(8,128)(2,1)S(1)}, bf16[8,2,96,128]{3,2,1,0:T(8,128)(2,1)S(1)}, u32[]{:S(2)}, u32[]{:S(2)}) collective-permute-start(bf16[8,2,96,128]{3,2,1,0:T(8,128)(2,1)S(1)} %slice.9.refs_4_), channel_id=1, source_target_pairs={{0,256},{128,384},{256,0},{384,128},{1,257},{129,385},{257,1},{385... | collective-permute-start | bytes 1179656 | tf_op jit(solution)/shard_map/gather/ppermute | solution.py:197
  70.0 0.0 collective-permute-done.1.refs_2_
  70.0 0.0 collective-permute-done.refs_1_
  70.0 4.5 %attend.3.refs_7_ = f32[4,72,768]{2,1,0:T(8,128)S(1)} custom-call(s32[1]{0:T(128)} %bitcast.1.member_ref, bf16[768,128]{1,0:T(8,128)(2,1)S(1)} %bitcast.19, bf16[768,128]{1,0:T(8,128)(2,1)S(1)} %collective-permute-done.refs_1_, bf16[768,128]{1,0:T(8,128)(2,1)S(1)} %collective-permute-done.1.refs_2_, bf16[768,128]{1,0:T(8,128)(2,1)S(1)} %collective-permute-done.2.refs_3_, ...), custom_call_target="tpu_custom_call" | custom-call | flops 2415919104 | bytes 3145728 | tf_op jit(solution)/shard_map/attend/pallas_call | solution.py:136
  74.5 0.0 collective-permute-done.5.refs_5_
  74.5 4.3 %collective-permute-done.4.refs_4_ = bf16[8,2,96,128]{3,2,1,0:T(8,128)(2,1)S(1)} collective-permute-done((bf16[8,2,96,128]{3,2,1,0:T(8,128)(2,1)S(1)}, bf16[8,2,96,128]{3,2,1,0:T(8,128)(2,1)S(1)}, u32[]{:S(2)}, u32[]{:S(2)}) %collective-permute-start.4) | collective-permute-done | bytes 393248 | tf_op jit(solution)/shard_map/gather/ppermute | solution.py:197
  78.9 9.9 %attend.4.refs_6_ = f32[4,72,768]{2,1,0:T(8,128)S(1)} custom-call(s32[1]{0:T(128)} %bitcast.1.member_ref, bf16[768,128]{1,0:T(8,128)(2,1)S(1)} %bitcast.20, bf16[768,128]{1,0:T(8,128)(2,1)S(1)} %collective-permute-done.refs_1_, bf16[768,128]{1,0:T(8,128)(2,1)S(1)} %collective-permute-done.1.refs_2_, bf16[768,128]{1,0:T(8,128)(2,1)S(1)} %collective-permute-done.2.refs_3_, ...), custom_call_target="tpu_custom_call" | custom-call | flops 4831838208 | bytes 3145728 | tf_op jit(solution)/shard_map/attend/pallas_call | solution.py:136
  88.8 0.0 collective-permute-done.3.refs_4_
  88.8 5.5 %attend.5 = bf16[4,80,768]{2,1,0:T(8,128)(2,1)} custom-call(s32[1]{0:T(128)} %bitcast.1.member_ref, bf16[768,128]{1,0:T(8,128)(2,1)S(1)} %bitcast.21, bf16[768,128]{1,0:T(8,128)(2,1)S(1)} %collective-permute-done.refs_1_, bf16[768,128]{1,0:T(8,128)(2,1)S(1)} %collective-permute-done.1.refs_2_, bf16[768,128]{1,0:T(8,128)(2,1)S(1)} %collective-permute-done.2.refs_3_, ...), custom_call_target="tpu_custom_call" | custom-call | flops 2415919104 | bytes 3145728 | tf_op jit(solution)/shard_map/attend/pallas_call | solution.py:136
  94.4 5.9 %all-to-all-start.1 = ((bf16[4,80,768]{2,1,0:T(8,128)(2,1)}), bf16[4,80,768]{2,1,0:T(8,128)(2,1)S(1)}, u32[]{:S(2)}, u32[]{:S(2)}) async-start(bf16[4,80,768]{2,1,0:T(8,128)(2,1)} %attend.5), calls=%async_computation.1 | async-start | bytes 983040 | tf_op jit(solution)/shard_map/combine/all_to_all | solution.py:206
  100.3 5.3 %all-to-all-done.1.in_ref = bf16[4,80,768]{2,1,0:T(8,128)(2,1)S(1)} async-done(((bf16[4,80,768]{2,1,0:T(8,128)(2,1)}), bf16[4,80,768]{2,1,0:T(8,128)(2,1)S(1)}, u32[]{:S(2)}, u32[]{:S(2)}) %all-to-all-start.1) | async-done | bytes 491552 | tf_op jit(solution)/shard_map/combine/all_to_all | solution.py:206
  105.6 0.3 combine.1
  105.9 19.0 %all_to_all.16 = bf16[8,48,128]{2,1,0:T(8,128)(2,1)S(1)} all-to-all(bf16[8,48,128]{2,1,0:T(8,128)(2,1)S(1)} %combine.1), channel_id=1, replica_groups=mesh['y'=4,'zh'=8,'z0'=2,'xl'=2,'xh'=2,'c'=2] {'zh'}, dimensions={0} | all-to-all | bytes 196608 | tf_op jit(solution)/shard_map/to_tokens/all_to_all | solution.py:215
  124.9 21.0 %all-gather = f32[192,128]{1,0:T(8,128)S(1)} all-gather(f32[48,128]{1,0:T(8,128)S(1)} %convert_reduce_fusion), channel_id=2, replica_groups=mesh['y'=4,'zh'=8,'z0'=2,'xl'=2,'xh'=2,'c'=2] {'xh','c'}, dimensions={0}, use_global_device_ids=true | all-gather | bytes 122880 | tf_op jit(solution)/shard_map/to_tokens/all_gather | solution.py:217
  145.9 0.1 reshape.18
  146.0 0.7 copy.15
  (9 shorter events, 0.2 us)
Async XLA Ops:
  0.0 0.9 copy-start
  0.9 0.9 copy-start.1
  1.8 0.9 copy-start.2
  2.7 0.9 copy-start.3
  3.6 0.9 copy-start.4
  4.5 0.9 copy-start.5
  49.9 16.4 %copy-start.6 = (bf16[640,64]{0,1:T(8,128)(2,1)S(1)}, bf16[640,64]{0,1:T(8,128)(2,1)}, u32[]{:S(2)}) copy-start(bf16[640,64]{0,1:T(8,128)(2,1)} %param.14) | copy-start | bytes 245764
  49.9 16.4 %copy-start.7 = (bf16[384,64]{0,1:T(8,128)(2,1)S(1)}, bf16[384,64]{0,1:T(8,128)(2,1)}, u32[]{:S(2)}) copy-start(bf16[384,64]{0,1:T(8,128)(2,1)} %param.15) | copy-start | bytes 147460
  49.9 16.5 %collective-permute-start.2 = (bf16[768,128]{1,0:T(8,128)(2,1)S(1)}, bf16[768,128]{1,0:T(8,128)(2,1)S(1)}, u32[]{:S(2)}, u32[]{:S(2)}) collective-permute-start(bf16[768,128]{1,0:T(8,128)(2,1)S(1)} %bitcast.16), channel_id=1, source_target_pairs={{0,12},{4,8},{8,4},{12,0},{1,13},{5,9},{9,5},{13,1},{2,14},{6,10},... | collective-permute-start | bytes 589832 | tf_op jit(solution)/shard_map/gather/ppermute | solution.py:193
  55.5 14.5 %collective-permute-start.1 = (bf16[768,128]{1,0:T(8,128)(2,1)S(1)}, bf16[768,128]{1,0:T(8,128)(2,1)S(1)}, u32[]{:S(2)}, u32[]{:S(2)}) collective-permute-start(bf16[768,128]{1,0:T(8,128)(2,1)S(1)} %bitcast.17), channel_id=1, source_target_pairs={{0,8},{4,12},{8,0},{12,4},{1,9},{5,13},{9,1},{13,5},{2,10},{6,14},... | collective-permute-start | bytes 589832 | tf_op jit(solution)/shard_map/gather/ppermute | solution.py:193
  57.4 12.5 %collective-permute-start = (bf16[768,128]{1,0:T(8,128)(2,1)S(1)}, bf16[768,128]{1,0:T(8,128)(2,1)S(1)}, u32[]{:S(2)}, u32[]{:S(2)}) collective-permute-start(bf16[768,128]{1,0:T(8,128)(2,1)S(1)} %bitcast.18), channel_id=1, source_target_pairs={{0,4},{4,0},{8,12},{12,8},{1,5},{5,1},{9,13},{13,9},{2,6},{6,2},{1... | collective-permute-start | bytes 589832 | tf_op jit(solution)/shard_map/gather/ppermute | solution.py:193
  59.7 14.9 %collective-permute-start.5 = (bf16[8,2,96,128]{3,2,1,0:T(8,128)(2,1)S(1)}, bf16[8,2,96,128]{3,2,1,0:T(8,128)(2,1)S(1)}, u32[]{:S(2)}, u32[]{:S(2)}) collective-permute-start(bf16[8,2,96,128]{3,2,1,0:T(8,128)(2,1)S(1)} %slice.9.refs_4_), channel_id=1, source_target_pairs={{0,384},{128,0},{256,128},{384,256},{1,385},{129,1},{257,129},{385... | collective-permute-start | bytes 1179656 | tf_op jit(solution)/shard_map/gather/ppermute | solution.py:197
  64.3 14.6 %collective-permute-start.4 = (bf16[8,2,96,128]{3,2,1,0:T(8,128)(2,1)S(1)}, bf16[8,2,96,128]{3,2,1,0:T(8,128)(2,1)S(1)}, u32[]{:S(2)}, u32[]{:S(2)}) collective-permute-start(bf16[8,2,96,128]{3,2,1,0:T(8,128)(2,1)S(1)} %slice.9.refs_4_), channel_id=1, source_target_pairs={{0,128},{128,256},{256,384},{384,0},{1,129},{129,257},{257,385},{3... | collective-permute-start | bytes 1179656 | tf_op jit(solution)/shard_map/gather/ppermute | solution.py:197
  66.4 22.4 %collective-permute-start.3 = (bf16[8,2,96,128]{3,2,1,0:T(8,128)(2,1)S(1)}, bf16[8,2,96,128]{3,2,1,0:T(8,128)(2,1)S(1)}, u32[]{:S(2)}, u32[]{:S(2)}) collective-permute-start(bf16[8,2,96,128]{3,2,1,0:T(8,128)(2,1)S(1)} %slice.9.refs_4_), channel_id=1, source_target_pairs={{0,256},{128,384},{256,0},{384,128},{1,257},{129,385},{257,1},{385... | collective-permute-start | bytes 1179656 | tf_op jit(solution)/shard_map/gather/ppermute | solution.py:197
  94.4 11.2 %all-to-all-start.1 = ((bf16[4,80,768]{2,1,0:T(8,128)(2,1)}), bf16[4,80,768]{2,1,0:T(8,128)(2,1)S(1)}, u32[]{:S(2)}, u32[]{:S(2)}) async-start(bf16[4,80,768]{2,1,0:T(8,128)(2,1)} %attend.5), calls=%async_computation.1 | async-start | bytes 983040 | tf_op jit(solution)/shard_map/combine/all_to_all | solution.py:206

commit v3 on v1

v3 whole, which is shorter than its diff:
```python
import functools
import math

import jax
import jax.numpy as jnp
from jax import lax
from jax.experimental import pallas as pl
from jax.experimental.pallas import tpu as pltpu
from jax.sharding import Mesh
from jax.sharding import PartitionSpec as P

HD = 128
CH = 64
guidance = 2.5
SCALE = math.log2(math.e) / math.sqrt(HD)
F32 = jnp.float32
BF16 = jnp.bfloat16
VMEM = pl.BlockSpec(memory_space=pltpu.VMEM)
SMEM = pl.BlockSpec(memory_space=pltpu.SMEM)
SMALL = pltpu.CompilerParams(vmem_limit_bytes=12 << 20)
MESSAGE_ROWS = CH + 16

SEQ = ("y", "zh", "z0", "xl")
GRP = ("xh", "c")
Z = ("zh", "z0")
PLANE_SETS = ([0, 2, 4, 6, 9, 11, 13, 15], [1, 3, 5, 7, 8, 10, 12, 14])
QUERY_AXES = ("y", "z0")
QUERY_STEPS = (1, 6, 7)
KEY_AXES = ("y", "xl")
KEY_STEPS = (1, 2, 3)


def exchange(x):
    return lax.all_to_all(x, Z, 0, 0, tiled=True, axis_index_groups=PLANE_SETS)


def from_partners(x, axes, steps):
    size = lax.axis_size(axes)
    return [lax.ppermute(x, axes, [(i, i ^ step) for i in range(size)]) for step in steps]


def dot_t(a, b):
    return lax.dot_general(a, b, (((1,), (1,)), ((), ())), preferred_element_type=F32)


def pack_kernel(main_heads, guide_heads, qm, km, vm, qg, kg, vg, q_out, kv_out):
    for h in range(main_heads + guide_heads):
        at = (h if h < main_heads else h - main_heads) * HD
        q, k, v = (qm, km, vm) if h < main_heads else (qg, kg, vg)
        q_out[h] = q[:, at : at + HD]
        kv_out[h, 0] = k[:, at : at + HD]
        kv_out[h, 1] = v[:, at : at + HD]


def split_two(x):
    high = x.astype(BF16).astype(F32)
    return high, x - high


def attend_kernel(q_ref, *refs):
    *kv_refs, map_ref, out_ref, sums_ref = refs
    rows = out_ref.shape[1]
    keys = kv_refs[0].shape[0] * kv_refs[0].shape[2]

    def all_pieces(which):
        return jnp.concatenate([ref[:, which].reshape(keys, HD) for ref in kv_refs], axis=0)

    def weighted(queries, shift):
        scores = dot_t(queries, all_pieces(0)) * SCALE
        if shift is not None:
            scores = scores - shift
        values = all_pieces(1)
        values = jnp.concatenate([values, jnp.ones_like(values)], axis=1)
        weights = jnp.exp2(scores).astype(BF16)
        return jnp.dot(weights, values, preferred_element_type=F32)

    def emit(at, total, shift):
        count = total.shape[0]
        lane = lax.broadcasted_iota(jnp.int32, (count, HD), 1)
        picks = lax.broadcasted_iota(jnp.int32, (16, HD), 0) == lax.broadcasted_iota(
            jnp.int32, (16, HD), 1
        )
        out_ref[:CH, at] = dot_t(map_ref[...], total[:, :HD].astype(BF16)).astype(BF16)
        high, low = split_two(total[:, HD:])
        rest = jnp.where(lane == 0, high, jnp.where(lane == 1, low, 0.0))
        if shift is not None:
            high, low = split_two(shift)
            rest = jnp.where(lane == 2, high, jnp.where(lane == 3, low, rest))
        rest = dot_t(picks.astype(F32).astype(BF16), rest.astype(BF16))
        out_ref[CH:, at] = rest.astype(BF16)

    total = weighted(q_ref[...], None)
    emit(slice(None), total, None)
    sums_ref[...] = total[:, HD:]
    least = jnp.min(sums_ref[...])
    most = jnp.max(sums_ref[...])

    @pl.when(jnp.logical_not((least > 1e-20) & (most < 1e25)))
    def _():
        @pl.loop(0, rows // HD)
        def _(i):
            at = pl.ds(pl.multiple_of(i * HD, HD), HD)
            queries = q_ref[at, :]
            top = jnp.max(dot_t(queries, all_pieces(0)), axis=1, keepdims=True)
            shift = jnp.ceil(top * SCALE)
            emit(at, weighted(queries, shift), shift)


def attend(queries, key_values, map_t):
    rows = queries.shape[0]
    keys = key_values[0].shape[0] * key_values[0].shape[2] * len(key_values)
    return pl.pallas_call(
        attend_kernel,
        in_specs=[VMEM] * (2 + len(key_values)),
        out_specs=VMEM,
        out_shape=jax.ShapeDtypeStruct((MESSAGE_ROWS, rows), BF16),
        scratch_shapes=[pltpu.VMEM((rows, HD), F32)],
        compiler_params=pltpu.CompilerParams(vmem_limit_bytes=40 << 20),
        cost_estimate=pl.CostEstimate(
            flops=8 * rows * keys * HD, bytes_accessed=2 << 20, transcendentals=rows * keys
        ),
    )(queries, *key_values, map_t)


def combine_kernel(gain_ref, *refs):
    *in_refs, out_ref = refs
    half = out_ref.shape[1]
    stats = [ref[CH:, :].astype(F32) for ref in in_refs]
    shifts = [s[2:3] + s[3:4] for s in stats]
    top = functools.reduce(jnp.maximum, shifts)
    scales = [jnp.exp2(shift - top) for shift in shifts]
    summed = sum((s[0:1] + s[1:2]) * scale for s, scale in zip(stats, scales))
    velocity = sum(ref[:CH, :].astype(F32) * scale for ref, scale in zip(in_refs, scales))
    velocity = (velocity * (gain_ref[0] / summed)).T
    velocity = velocity.reshape(out_ref.shape[0], 2, half, CH)
    out_ref[...] = jnp.concatenate([velocity[:, 0], velocity[:, 1]], axis=2).astype(BF16)


def body(
    query_main, key_main, value_main, query_guide, key_guide, value_guide, map_main, map_guide
):
    tokens_here = query_main.shape[0]
    main_heads = query_main.shape[1] // HD
    guide_heads = query_guide.shape[1] // HD
    heads = main_heads + guide_heads
    head = lax.axis_index("zh")

    maps = jnp.concatenate([map_main, map_guide], axis=0).reshape(-1, HD, CH)
    map_t = lax.dynamic_index_in_dim(maps, head, 0, keepdims=False).T
    gain = jnp.where(head < main_heads, guidance, 1.0 - guidance).astype(F32).reshape(1)

    with jax.named_scope("pack"):
        q, kv = pl.pallas_call(
            functools.partial(pack_kernel, main_heads, guide_heads),
            in_specs=[VMEM] * 6,
            out_specs=[VMEM] * 2,
            out_shape=[
                jax.ShapeDtypeStruct((heads, tokens_here, HD), BF16),
                jax.ShapeDtypeStruct((heads, 2, tokens_here, HD), BF16),
            ],
        )(query_main, key_main, value_main, query_guide, key_guide, value_guide)
    with jax.named_scope("to_heads"):
        kv = exchange(kv)
        q = exchange(q).reshape(heads * tokens_here, HD)
    with jax.named_scope("gather"):
        key_values = [kv] + from_partners(kv, KEY_AXES, KEY_STEPS)
        queries = from_partners(q, QUERY_AXES, QUERY_STEPS)
    with jax.named_scope("attend"):
        shares = [
            from_partners(attend(piece, key_values, map_t), QUERY_AXES, (step,))[0]
            for piece, step in zip(queries, QUERY_STEPS)
        ]
        shares.append(attend(q, key_values, map_t))
    with jax.named_scope("combine"):
        velocity = pl.pallas_call(
            combine_kernel,
            in_specs=[SMEM] + [VMEM] * len(shares),
            out_specs=VMEM,
            out_shape=jax.ShapeDtypeStruct((heads, tokens_here // 2, 2 * CH), BF16),
            compiler_params=SMALL,
        )(gain, *shares)
    with jax.named_scope("to_tokens"):
        velocity = jnp.sum(exchange(velocity).astype(F32), axis=0)
        everywhere = lax.all_gather(velocity, GRP, axis=0)
        velocity = jnp.sum(everywhere, axis=0)
    return velocity.reshape(tokens_here // 2, 2, CH).transpose(1, 0, 2).reshape(tokens_here, CH)


def solution(mesh):
    fine = Mesh(mesh.devices.reshape(4, 8, 2, 2, 2, 2), SEQ + GRP)
    placed = (P(SEQ, GRP),) * 6 + (P(GRP, None),) * 2
    return jax.shard_map(
        body, mesh=fine, in_specs=placed, out_specs=P(SEQ, None), check_vma=False
    )
```

time: 145 us -> 136 us (0.938)
  starting transfers between devices: 29.6 us -> 44.5 us
  blocking collectives: 84.1 us -> 69.5 us
  Pallas kernels: 21.2 us -> 14.4 us
    ppermute x3 -> x9, starting transfers between devices: 10.1 us -> 38.1 us  [from_partners(): lax.ppermute(x, axes, [(i, i ^ step) for i in range(size)])]
    all_gather x1 -> x0, blocking collectives: 19.3 us -> none  [body(): lax.all_gather(q.reshape(rows, HD), QUERY_AXES, axis=0, tiled=True)]
    all_to_all x2 -> x1, starting transfers between devices: 19.5 us -> 6.41 us  [exchange(): return lax.all_to_all(x, Z, 0, 0, tiled=True, axis_index_groups=PLANE_SETS)]
    pallas_call x3 -> x6, Pallas kernels: 21.2 us -> 14.4 us  [the longest x4 12 us: attend(): pl.pallas_call(attend_kernel, in_specs=[VMEM] * (2 + len(key_values)), ou...]
    all_to_all x2, blocking collectives: 51.6 us -> 57.1 us  [exchange(): return lax.all_to_all(x, Z, 0, 0, tiled=True, axis_index_groups=PLANE_SETS)]
    all_to_all x2 -> x1, waiting for transfers between devices: 7.4 us -> 3.41 us  [exchange(): return lax.all_to_all(x, Z, 0, 0, tiled=True, axis_index_groups=PLANE_SETS)]
    ppermute x3 -> x9, waiting for transfers between devices: 0.01 us -> 2.84 us  [from_partners(): lax.ppermute(x, axes, [(i, i ^ step) for i in range(size)])]
  transfers between devices with their start and end apart: 5 -> 10, of which waited for: 2 -> 2; matrix products, arithmetic and copies ran while one was open for 0% -> 0% of each run, Pallas kernels for 0% -> 9%
where the time goes in v3:
time: 136 us
  blocking collectives  69.5 us (51%)
  starting transfers between devices  44.5 us (33%)
  Pallas kernels  14.4 us (11%)
  waiting for transfers between devices  6.25 us (5%)
    all_to_all x2, blocking collectives, exchange(): return lax.all_to_all(x, Z, 0, 0, tiled=True, axis_index_groups=PLANE_SETS)  57.1 us
    ppermute x9, starting transfers between devices, from_partners(): lax.ppermute(x, axes, [(i, i ^ step) for i in range(size)])  38.1 us
    all_gather x1, blocking collectives, body(): everywhere = lax.all_gather(velocity, GRP, axis=0)  12.4 us
    pallas_call x4, Pallas kernels, attend(): pl.pallas_call(attend_kernel, in_specs=[VMEM] * (2 + len(key_values)), ou...  12 us
    all_to_all x1, starting transfers between devices, exchange(): return lax.all_to_all(x, Z, 0, 0, tiled=True, axis_index_groups=PLANE_SETS)  6.41 us
    all_to_all x1, waiting for transfers between devices, exchange(): return lax.all_to_all(x, Z, 0, 0, tiled=True, axis_index_groups=PLANE_SETS)  3.41 us
    ppermute x9, waiting for transfers between devices, from_partners(): lax.ppermute(x, axes, [(i, i ^ step) for i in range(size)])  2.84 us
  transfers between devices with their start and end apart: 10, of which 2 were waited for; matrix products, arithmetic and copies ran while one was open for 0% of the time, Pallas kernels for 9%

profile of v3, /device:TPU:1, one launch (start us, length us, event | category | flops | bytes accessed | tf_op | source)
XLA Modules:
  0.0 135.8 jit_solution(5642058878280759607)
XLA Ops:
  0.0 2.1 %pack.1 = (bf16[8,96,128]{2,1,0:T(8,128)(2,1)}, bf16[8,2,96,128]{3,2,1,0:T(8,128)(2,1)}) custom-call(bf16[96,640]{1,0:T(8,128)(2,1)} %qm.1, bf16[96,640]{1,0:T(8,128)(2,1)} %km.1, bf16[96,640]{1,0:T(8,128)(2,1)} %vm.1, bf16[96,384]{1,0:T(8,128)(2,1)} %qg.1, bf16[96,384]{1,0:T(8,128)(2,1)} %kg.1, bf16[96,384]{1,0:T(8,128)(2,1)} %vg.1), custom_call_target="tpu_custom_call" | custom-call | tf_op jit(solution)/shard_map/pack/pallas_call | solution.py:153
  2.1 36.0 %all_to_all.15.refs_0_ = bf16[8,2,96,128]{3,2,1,0:T(8,128)(2,1)S(1)} all-to-all(bf16[8,2,96,128]{3,2,1,0:T(8,128)(2,1)} %get-tuple-element.8), channel_id=1, replica_groups={{0,16,32,48,72,88,104,120},{8,24,40,56,64,80,96,112},{1,17,33,49,73,89,..., dimensions={0} | all-to-all | bytes 786432 | tf_op jit(solution)/shard_map/to_heads/all_to_all | solution.py:34
  38.1 0.0 copy-start
  38.1 0.0 copy-start.1
  38.1 6.4 %all-to-all-start = ((bf16[8,96,128]{2,1,0:T(8,128)(2,1)}), bf16[8,96,128]{2,1,0:T(8,128)(2,1)S(1)}, u32[]{:S(2)}, u32[]{:S(2)}) async-start(bf16[8,96,128]{2,1,0:T(8,128)(2,1)} %get-tuple-element.7), calls=%async_computation | async-start | bytes 393216 | tf_op jit(solution)/shard_map/to_heads/all_to_all | solution.py:34
  44.5 3.1 %collective-permute-start.1 = (bf16[8,2,96,128]{3,2,1,0:T(8,128)(2,1)S(1)}, bf16[8,2,96,128]{3,2,1,0:T(8,128)(2,1)S(1)}, u32[]{:S(2)}, u32[]{:S(2)}) collective-permute-start(bf16[8,2,96,128]{3,2,1,0:T(8,128)(2,1)S(1)} %all_to_all.15.refs_0_), channel_id=1, source_target_pairs={{0,4},{4,0},{128,132},{132,128},{256,260},{260,256},{384,388},{388... | collective-permute-start | bytes 1179656 | tf_op jit(solution)/shard_map/gather/ppermute | solution.py:39
  47.6 3.2 %collective-permute-start.2 = (bf16[8,2,96,128]{3,2,1,0:T(8,128)(2,1)S(1)}, bf16[8,2,96,128]{3,2,1,0:T(8,128)(2,1)S(1)}, u32[]{:S(2)}, u32[]{:S(2)}) collective-permute-start(bf16[8,2,96,128]{3,2,1,0:T(8,128)(2,1)S(1)} %all_to_all.15.refs_0_), channel_id=1, source_target_pairs={{0,128},{4,132},{128,0},{132,4},{256,384},{260,388},{384,256},{388... | collective-permute-start | bytes 1179656 | tf_op jit(solution)/shard_map/gather/ppermute | solution.py:39
  50.8 2.0 %collective-permute-start.3 = (bf16[8,2,96,128]{3,2,1,0:T(8,128)(2,1)S(1)}, bf16[8,2,96,128]{3,2,1,0:T(8,128)(2,1)S(1)}, u32[]{:S(2)}, u32[]{:S(2)}) collective-permute-start(bf16[8,2,96,128]{3,2,1,0:T(8,128)(2,1)S(1)} %all_to_all.15.refs_0_), channel_id=1, source_target_pairs={{0,132},{4,128},{128,4},{132,0},{256,388},{260,384},{384,260},{388... | collective-permute-start | bytes 1179656 | tf_op jit(solution)/shard_map/gather/ppermute | solution.py:39
  52.9 3.4 %all-to-all-done = bf16[8,96,128]{2,1,0:T(8,128)(2,1)S(1)} async-done(((bf16[8,96,128]{2,1,0:T(8,128)(2,1)}), bf16[8,96,128]{2,1,0:T(8,128)(2,1)S(1)}, u32[]{:S(2)}, u32[]{:S(2)}) %all-to-all-start) | async-done | bytes 196640 | tf_op jit(solution)/shard_map/to_heads/all_to_all | solution.py:34
  56.3 5.5 %collective-permute-start = (bf16[768,128]{1,0:T(8,128)(2,1)S(1)}, bf16[768,128]{1,0:T(8,128)(2,1)S(1)}, u32[]{:S(2)}, u32[]{:S(2)}) collective-permute-start(bf16[768,128]{1,0:T(8,128)(2,1)S(1)} %bitcast.15), channel_id=1, source_target_pairs={{0,8},{8,0},{128,136},{136,128},{256,264},{264,256},{384,392},{392... | collective-permute-start | bytes 589832 | tf_op jit(solution)/shard_map/gather/ppermute | solution.py:39
  61.8 0.0 copy-done
  61.8 0.0 copy-done.1
  61.9 4.6 %collective-permute-start.5 = (bf16[768,128]{1,0:T(8,128)(2,1)S(1)}, bf16[768,128]{1,0:T(8,128)(2,1)S(1)}, u32[]{:S(2)}, u32[]{:S(2)}) collective-permute-start(bf16[768,128]{1,0:T(8,128)(2,1)S(1)} %bitcast.16), channel_id=1, source_target_pairs={{0,384},{8,392},{128,256},{136,264},{256,128},{264,136},{384,0},{3... | collective-permute-start | bytes 589832 | tf_op jit(solution)/shard_map/gather/ppermute | solution.py:39
  66.6 0.0 collective-permute-done.q_ref
  66.6 4.3 %collective-permute-start.7 = (bf16[768,128]{1,0:T(8,128)(2,1)S(1)}, bf16[768,128]{1,0:T(8,128)(2,1)S(1)}, u32[]{:S(2)}, u32[]{:S(2)}) collective-permute-start(bf16[768,128]{1,0:T(8,128)(2,1)S(1)} %bitcast.17), channel_id=1, source_target_pairs={{0,392},{8,384},{128,264},{136,256},{256,136},{264,128},{384,8},{3... | collective-permute-start | bytes 589832 | tf_op jit(solution)/shard_map/gather/ppermute | solution.py:39
  71.0 0.0 collective-permute-done.1.refs_1_
  71.0 0.0 collective-permute-done.2.refs_2_
  71.0 0.0 collective-permute-done.3.refs_3_
  71.0 3.0 %attend.4 = bf16[80,768]{1,0:T(8,128)(2,1)S(1)} custom-call(bf16[768,128]{1,0:T(8,128)(2,1)S(1)} %collective-permute-done.q_ref, bf16[8,2,96,128]{3,2,1,0:T(8,128)(2,1)S(1)} %all_to_all.15.refs_0_, bf16[8,2,96,128]{3,2,1,0:T(8,128)(2,1)S(1)} %collective-permute-done.1.refs_1_, bf16[8,2,96,128]{3,2,1,0:T(8,128)(2,1)S(1)} %collective-permute-done.2.refs_2_, ...), custom_call_target="tpu_custom_call" | custom-call | flops 2415919104 | bytes 2097152 | tf_op jit(solution)/shard_map/attend/pallas_call | solution.py:112
  74.0 1.9 %collective-permute-start.4 = (bf16[80,768]{1,0:T(8,128)(2,1)S(1)}, bf16[80,768]{1,0:T(8,128)(2,1)S(1)}, u32[]{:S(2)}, u32[]{:S(2)}) collective-permute-start(bf16[80,768]{1,0:T(8,128)(2,1)S(1)} %attend.4), channel_id=1, source_target_pairs={{0,8},{8,0},{128,136},{136,128},{256,264},{264,256},{384,392},{392... | collective-permute-start | bytes 368648 | tf_op jit(solution)/shard_map/attend/ppermute | solution.py:39
  75.9 0.0 collective-permute-done.5.q_ref
  75.9 3.0 %attend.5 = bf16[80,768]{1,0:T(8,128)(2,1)S(1)} custom-call(bf16[768,128]{1,0:T(8,128)(2,1)S(1)} %collective-permute-done.5.q_ref, bf16[8,2,96,128]{3,2,1,0:T(8,128)(2,1)S(1)} %all_to_all.15.refs_0_, bf16[8,2,96,128]{3,2,1,0:T(8,128)(2,1)S(1)} %collective-permute-done.1.refs_1_, bf16[8,2,96,128]{3,2,1,0:T(8,128)(2,1)S(1)} %collective-permute-done.2.refs_2_, ...), custom_call_target="tpu_custom_call" | custom-call | flops 2415919104 | bytes 2097152 | tf_op jit(solution)/shard_map/attend/pallas_call | solution.py:112
  78.9 11.4 %collective-permute-start.6 = (bf16[80,768]{1,0:T(8,128)(2,1)S(1)}, bf16[80,768]{1,0:T(8,128)(2,1)S(1)}, u32[]{:S(2)}, u32[]{:S(2)}) collective-permute-start(bf16[80,768]{1,0:T(8,128)(2,1)S(1)} %attend.5), channel_id=1, source_target_pairs={{0,384},{8,392},{128,256},{136,264},{256,128},{264,136},{384,0},{3... | collective-permute-start | bytes 368648 | tf_op jit(solution)/shard_map/attend/ppermute | solution.py:39
  90.3 0.0 collective-permute-done.7.q_ref
  90.3 3.1 %attend.6 = bf16[80,768]{1,0:T(8,128)(2,1)S(1)} custom-call(bf16[768,128]{1,0:T(8,128)(2,1)S(1)} %collective-permute-done.7.q_ref, bf16[8,2,96,128]{3,2,1,0:T(8,128)(2,1)S(1)} %all_to_all.15.refs_0_, bf16[8,2,96,128]{3,2,1,0:T(8,128)(2,1)S(1)} %collective-permute-done.1.refs_1_, bf16[8,2,96,128]{3,2,1,0:T(8,128)(2,1)S(1)} %collective-permute-done.2.refs_2_, ...), custom_call_target="tpu_custom_call" | custom-call | flops 2415919104 | bytes 2097152 | tf_op jit(solution)/shard_map/attend/pallas_call | solution.py:112
  93.4 1.9 %collective-permute-start.8 = (bf16[80,768]{1,0:T(8,128)(2,1)S(1)}, bf16[80,768]{1,0:T(8,128)(2,1)S(1)}, u32[]{:S(2)}, u32[]{:S(2)}) collective-permute-start(bf16[80,768]{1,0:T(8,128)(2,1)S(1)} %attend.6), channel_id=1, source_target_pairs={{0,392},{8,384},{128,264},{136,256},{256,136},{264,128},{384,8},{3... | collective-permute-start | bytes 368648 | tf_op jit(solution)/shard_map/attend/ppermute | solution.py:39
  95.3 3.0 %attend.7.refs_3_ = bf16[80,768]{1,0:T(8,128)(2,1)S(1)} custom-call(bf16[768,128]{1,0:T(8,128)(2,1)S(1)} %bitcast.18, bf16[8,2,96,128]{3,2,1,0:T(8,128)(2,1)S(1)} %all_to_all.15.refs_0_, bf16[8,2,96,128]{3,2,1,0:T(8,128)(2,1)S(1)} %collective-permute-done.1.refs_1_, bf16[8,2,96,128]{3,2,1,0:T(8,128)(2,1)S(1)} %collective-permute-done.2.refs_2_, ...), custom_call_target="tpu_custom_call" | custom-call | flops 2415919104 | bytes 2097152 | tf_op jit(solution)/shard_map/attend/pallas_call | solution.py:112
  98.3 0.0 collective-permute-done.4.refs_0_
  98.3 0.0 collective-permute-done.6.refs_1_
  98.3 2.8 %collective-permute-done.8.refs_2_ = bf16[80,768]{1,0:T(8,128)(2,1)S(1)} collective-permute-done((bf16[80,768]{1,0:T(8,128)(2,1)S(1)}, bf16[80,768]{1,0:T(8,128)(2,1)S(1)}, u32[]{:S(2)}, u32[]{:S(2)}) %collective-permute-start.8) | collective-permute-done | bytes 122912 | tf_op jit(solution)/shard_map/attend/ppermute | solution.py:39
  101.1 0.3 combine.1
  101.4 21.1 %all_to_all.16 = bf16[8,48,128]{2,1,0:T(8,128)(2,1)S(1)} all-to-all(bf16[8,48,128]{2,1,0:T(8,128)(2,1)S(1)} %combine.1), channel_id=1, replica_groups={{0,16,32,48,72,88,104,120},{8,24,40,56,64,80,96,112},{1,17,33,49,73,89,..., dimensions={0} | all-to-all | bytes 196608 | tf_op jit(solution)/shard_map/to_tokens/all_to_all | solution.py:34
  122.6 12.4 %all-gather = f32[192,128]{1,0:T(8,128)S(1)} all-gather(f32[48,128]{1,0:T(8,128)S(1)} %convert_reduce_fusion), channel_id=2, replica_groups=mesh['y'=4,'zh'=8,'z0'=2,'xl'=2,'xh'=2,'c'=2] {'xh','c'}, dimensions={0}, use_global_device_ids=true | all-gather | bytes 122880 | tf_op jit(solution)/shard_map/to_tokens/all_gather | solution.py:184
  135.0 0.1 reshape.18
  135.1 0.7 copy.15
  (7 shorter events, 0.1 us)
Async XLA Ops:
  38.1 23.7 %copy-start = (bf16[640,64]{0,1:T(8,128)(2,1)S(1)}, bf16[640,64]{0,1:T(8,128)(2,1)}, u32[]{:S(2)}) copy-start(bf16[640,64]{0,1:T(8,128)(2,1)} %param.14) | copy-start | bytes 245764
  38.1 23.8 %copy-start.1 = (bf16[384,64]{0,1:T(8,128)(2,1)S(1)}, bf16[384,64]{0,1:T(8,128)(2,1)}, u32[]{:S(2)}) copy-start(bf16[384,64]{0,1:T(8,128)(2,1)} %param.15) | copy-start | bytes 147460
  38.1 18.2 %all-to-all-start = ((bf16[8,96,128]{2,1,0:T(8,128)(2,1)}), bf16[8,96,128]{2,1,0:T(8,128)(2,1)S(1)}, u32[]{:S(2)}, u32[]{:S(2)}) async-start(bf16[8,96,128]{2,1,0:T(8,128)(2,1)} %get-tuple-element.7), calls=%async_computation | async-start | bytes 393216 | tf_op jit(solution)/shard_map/to_heads/all_to_all | solution.py:34
  44.5 26.5 %collective-permute-start.1 = (bf16[8,2,96,128]{3,2,1,0:T(8,128)(2,1)S(1)}, bf16[8,2,96,128]{3,2,1,0:T(8,128)(2,1)S(1)}, u32[]{:S(2)}, u32[]{:S(2)}) collective-permute-start(bf16[8,2,96,128]{3,2,1,0:T(8,128)(2,1)S(1)} %all_to_all.15.refs_0_), channel_id=1, source_target_pairs={{0,4},{4,0},{128,132},{132,128},{256,260},{260,256},{384,388},{388... | collective-permute-start | bytes 1179656 | tf_op jit(solution)/shard_map/gather/ppermute | solution.py:39
  47.6 23.4 %collective-permute-start.2 = (bf16[8,2,96,128]{3,2,1,0:T(8,128)(2,1)S(1)}, bf16[8,2,96,128]{3,2,1,0:T(8,128)(2,1)S(1)}, u32[]{:S(2)}, u32[]{:S(2)}) collective-permute-start(bf16[8,2,96,128]{3,2,1,0:T(8,128)(2,1)S(1)} %all_to_all.15.refs_0_), channel_id=1, source_target_pairs={{0,128},{4,132},{128,0},{132,4},{256,384},{260,388},{384,256},{388... | collective-permute-start | bytes 1179656 | tf_op jit(solution)/shard_map/gather/ppermute | solution.py:39
  50.8 20.2 %collective-permute-start.3 = (bf16[8,2,96,128]{3,2,1,0:T(8,128)(2,1)S(1)}, bf16[8,2,96,128]{3,2,1,0:T(8,128)(2,1)S(1)}, u32[]{:S(2)}, u32[]{:S(2)}) collective-permute-start(bf16[8,2,96,128]{3,2,1,0:T(8,128)(2,1)S(1)} %all_to_all.15.refs_0_), channel_id=1, source_target_pairs={{0,132},{4,128},{128,4},{132,0},{256,388},{260,384},{384,260},{388... | collective-permute-start | bytes 1179656 | tf_op jit(solution)/shard_map/gather/ppermute | solution.py:39
  56.3 10.3 %collective-permute-start = (bf16[768,128]{1,0:T(8,128)(2,1)S(1)}, bf16[768,128]{1,0:T(8,128)(2,1)S(1)}, u32[]{:S(2)}, u32[]{:S(2)}) collective-permute-start(bf16[768,128]{1,0:T(8,128)(2,1)S(1)} %bitcast.15), channel_id=1, source_target_pairs={{0,8},{8,0},{128,136},{136,128},{256,264},{264,256},{384,392},{392... | collective-permute-start | bytes 589832 | tf_op jit(solution)/shard_map/gather/ppermute | solution.py:39
  61.9 13.9 %collective-permute-start.5 = (bf16[768,128]{1,0:T(8,128)(2,1)S(1)}, bf16[768,128]{1,0:T(8,128)(2,1)S(1)}, u32[]{:S(2)}, u32[]{:S(2)}) collective-permute-start(bf16[768,128]{1,0:T(8,128)(2,1)S(1)} %bitcast.16), channel_id=1, source_target_pairs={{0,384},{8,392},{128,256},{136,264},{256,128},{264,136},{384,0},{3... | collective-permute-start | bytes 589832 | tf_op jit(solution)/shard_map/gather/ppermute | solution.py:39
  66.6 23.7 %collective-permute-start.7 = (bf16[768,128]{1,0:T(8,128)(2,1)S(1)}, bf16[768,128]{1,0:T(8,128)(2,1)S(1)}, u32[]{:S(2)}, u32[]{:S(2)}) collective-permute-start(bf16[768,128]{1,0:T(8,128)(2,1)S(1)} %bitcast.17), channel_id=1, source_target_pairs={{0,392},{8,384},{128,264},{136,256},{256,136},{264,128},{384,8},{3... | collective-permute-start | bytes 589832 | tf_op jit(solution)/shard_map/gather/ppermute | solution.py:39
  74.0 24.3 %collective-permute-start.4 = (bf16[80,768]{1,0:T(8,128)(2,1)S(1)}, bf16[80,768]{1,0:T(8,128)(2,1)S(1)}, u32[]{:S(2)}, u32[]{:S(2)}) collective-permute-start(bf16[80,768]{1,0:T(8,128)(2,1)S(1)} %attend.4), channel_id=1, source_target_pairs={{0,8},{8,0},{128,136},{136,128},{256,264},{264,256},{384,392},{392... | collective-permute-start | bytes 368648 | tf_op jit(solution)/shard_map/attend/ppermute | solution.py:39
  78.9 19.4 %collective-permute-start.6 = (bf16[80,768]{1,0:T(8,128)(2,1)S(1)}, bf16[80,768]{1,0:T(8,128)(2,1)S(1)}, u32[]{:S(2)}, u32[]{:S(2)}) collective-permute-start(bf16[80,768]{1,0:T(8,128)(2,1)S(1)} %attend.5), channel_id=1, source_target_pairs={{0,384},{8,392},{128,256},{136,264},{256,128},{264,136},{384,0},{3... | collective-permute-start | bytes 368648 | tf_op jit(solution)/shard_map/attend/ppermute | solution.py:39
  93.4 7.7 %collective-permute-start.8 = (bf16[80,768]{1,0:T(8,128)(2,1)S(1)}, bf16[80,768]{1,0:T(8,128)(2,1)S(1)}, u32[]{:S(2)}, u32[]{:S(2)}) collective-permute-start(bf16[80,768]{1,0:T(8,128)(2,1)S(1)} %attend.6), channel_id=1, source_target_pairs={{0,392},{8,384},{128,264},{136,256},{256,136},{264,128},{384,8},{3... | collective-permute-start | bytes 368648 | tf_op jit(solution)/shard_map/attend/ppermute | solution.py:39

commit v4 on v3

--- a/solution.py
+++ b/solution.py
@@ -27,11 +27,14 @@
 QUERY_AXES = ("y", "z0")
 QUERY_STEPS = (1, 6, 7)
 KEY_AXES = ("y", "xl")
-KEY_STEPS = (1, 2, 3)
+KEY_SETS = ([0, 1, 2, 3], [4, 5, 6, 7])
+SIDES = 2
+PLANE_AXES = Z + ("xh",)
+SIDE_SETS = [[SIDES * z + x for z in planes for x in range(SIDES)] for planes in PLANE_SETS]
 
 
-def exchange(x):
-    return lax.all_to_all(x, Z, 0, 0, tiled=True, axis_index_groups=PLANE_SETS)
+def exchange(x, axes, sets):
+    return lax.all_to_all(x, axes, 0, 0, tiled=True, axis_index_groups=sets)
 
 
 def from_partners(x, axes, steps):
@@ -43,13 +46,11 @@
     return lax.dot_general(a, b, (((1,), (1,)), ((), ())), preferred_element_type=F32)
 
 
-def pack_kernel(main_heads, guide_heads, qm, km, vm, qg, kg, vg, q_out, kv_out):
+def pack_kernel(main_heads, guide_heads, qm, km, vm, qg, kg, vg, out_ref):
     for h in range(main_heads + guide_heads):
         at = (h if h < main_heads else h - main_heads) * HD
-        q, k, v = (qm, km, vm) if h < main_heads else (qg, kg, vg)
-        q_out[h] = q[:, at : at + HD]
-        kv_out[h, 0] = k[:, at : at + HD]
-        kv_out[h, 1] = v[:, at : at + HD]
+        for t, ref in enumerate((qm, km, vm) if h < main_heads else (qg, kg, vg)):
+            out_ref[h, t] = ref[:, at : at + HD]
 
 
 def split_two(x):
@@ -57,13 +58,11 @@
     return high, x - high
 
 
-def attend_kernel(q_ref, *refs):
-    *kv_refs, map_ref, out_ref, sums_ref = refs
+def attend_kernel(q_ref, kv_ref, map_ref, out_ref, sums_ref):
     rows = out_ref.shape[1]
-    keys = kv_refs[0].shape[0] * kv_refs[0].shape[2]
 
     def all_pieces(which):
-        return jnp.concatenate([ref[:, which].reshape(keys, HD) for ref in kv_refs], axis=0)
+        return kv_ref[:, which].reshape(-1, HD)
 
     def weighted(queries, shift):
         scores = dot_t(queries, all_pieces(0)) * SCALE
@@ -108,10 +107,10 @@
 
 def attend(queries, key_values, map_t):
     rows = queries.shape[0]
-    keys = key_values[0].shape[0] * key_values[0].shape[2] * len(key_values)
+    keys = key_values.shape[0] * key_values.shape[2]
     return pl.pallas_call(
         attend_kernel,
-        in_specs=[VMEM] * (2 + len(key_values)),
+        in_specs=[VMEM] * 3,
         out_specs=VMEM,
         out_shape=jax.ShapeDtypeStruct((MESSAGE_ROWS, rows), BF16),
         scratch_shapes=[pltpu.VMEM((rows, HD), F32)],
@@ -119,12 +118,12 @@
         cost_estimate=pl.CostEstimate(
             flops=8 * rows * keys * HD, bytes_accessed=2 << 20, transcendentals=rows * keys
         ),
-    )(queries, *key_values, map_t)
+    )(queries, key_values, map_t)
 
 
 def combine_kernel(gain_ref, *refs):
     *in_refs, out_ref = refs
-    half = out_ref.shape[1]
+    half = out_ref.shape[2]
     stats = [ref[CH:, :].astype(F32) for ref in in_refs]
     shifts = [s[2:3] + s[3:4] for s in stats]
     top = functools.reduce(jnp.maximum, shifts)
@@ -133,7 +132,9 @@
     velocity = sum(ref[:CH, :].astype(F32) * scale for ref, scale in zip(in_refs, scales))
     velocity = (velocity * (gain_ref[0] / summed)).T
     velocity = velocity.reshape(out_ref.shape[0], 2, half, CH)
-    out_ref[...] = jnp.concatenate([velocity[:, 0], velocity[:, 1]], axis=2).astype(BF16)
+    velocity = jnp.concatenate([velocity[:, 0], velocity[:, 1]], axis=2).astype(BF16)
+    for side in range(out_ref.shape[1]):
+        out_ref[:, side] = velocity
 
 
 def body(
@@ -150,20 +151,19 @@
     gain = jnp.where(head < main_heads, guidance, 1.0 - guidance).astype(F32).reshape(1)
 
     with jax.named_scope("pack"):
-        q, kv = pl.pallas_call(
+        packed = pl.pallas_call(
             functools.partial(pack_kernel, main_heads, guide_heads),
             in_specs=[VMEM] * 6,
-            out_specs=[VMEM] * 2,
-            out_shape=[
-                jax.ShapeDtypeStruct((heads, tokens_here, HD), BF16),
-                jax.ShapeDtypeStruct((heads, 2, tokens_here, HD), BF16),
-            ],
+            out_specs=VMEM,
+            out_shape=jax.ShapeDtypeStruct((heads, 3, tokens_here, HD), BF16),
         )(query_main, key_main, value_main, query_guide, key_guide, value_guide)
     with jax.named_scope("to_heads"):
-        kv = exchange(kv)
-        q = exchange(q).reshape(heads * tokens_here, HD)
+        arrived = exchange(packed, Z, PLANE_SETS)
     with jax.named_scope("gather"):
-        key_values = [kv] + from_partners(kv, KEY_AXES, KEY_STEPS)
+        kv = arrived[:, 1:]
+        copies = jnp.broadcast_to(kv[None], (len(KEY_SETS[0]),) + kv.shape)
+        key_values = exchange(copies.reshape((-1,) + kv.shape[1:]), KEY_AXES, KEY_SETS)
+        q = arrived[:, 0].reshape(heads * tokens_here, HD)
         queries = from_partners(q, QUERY_AXES, QUERY_STEPS)
     with jax.named_scope("attend"):
         shares = [
@@ -176,13 +176,14 @@
             combine_kernel,
             in_specs=[SMEM] + [VMEM] * len(shares),
             out_specs=VMEM,
-            out_shape=jax.ShapeDtypeStruct((heads, tokens_here // 2, 2 * CH), BF16),
+            out_shape=jax.ShapeDtypeStruct((heads, SIDES, tokens_here // 2, 2 * CH), BF16),
             compiler_params=SMALL,
         )(gain, *shares)
     with jax.named_scope("to_tokens"):
-        velocity = jnp.sum(exchange(velocity).astype(F32), axis=0)
-        everywhere = lax.all_gather(velocity, GRP, axis=0)
-        velocity = jnp.sum(everywhere, axis=0)
+        velocity = velocity.reshape((heads * SIDES,) + velocity.shape[2:])
+        velocity = exchange(velocity, PLANE_AXES, SIDE_SETS)
+        velocity = jnp.sum(velocity.astype(F32), axis=0)
+        velocity = jnp.sum(lax.all_gather(velocity, "c", axis=0), axis=0)
     return velocity.reshape(tokens_here // 2, 2, CH).transpose(1, 0, 2).reshape(tokens_here, CH)
 
 

time: 136 us -> 136 us (level)
  starting transfers between devices: 44.5 us -> 28.9 us
  blocking collectives: 69.5 us -> 78.3 us
  waiting for transfers between devices: 6.25 us -> 11.2 us
  local copies, waits for them, and re-layouts: 0.87 us -> 2.43 us
    all_to_all x2, blocking collectives: 57.1 us -> 73.4 us  [exchange(): return lax.all_to_all(x, axes, 0, 0, tiled=True, axis_index_groups=sets)]
    ppermute x9 -> x6, starting transfers between devices: 38.1 us -> 25.2 us  [from_partners(): lax.ppermute(x, axes, [(i, i ^ step) for i in range(size)])]
    all_gather x1, blocking collectives: 12.4 us -> 4.96 us  [body(): velocity = jnp.sum(lax.all_gather(velocity, 'c', axis=0), axis=0)]
    all_to_all x1, waiting for transfers between devices: 3.41 us -> 8.39 us  [exchange(): return lax.all_to_all(x, axes, 0, 0, tiled=True, axis_index_groups=sets)]
    all_to_all x1, starting transfers between devices: 6.41 us -> 3.69 us  [exchange(): return lax.all_to_all(x, axes, 0, 0, tiled=True, axis_index_groups=sets)]
    broadcast_in_dim x0 -> x1, local copies, waits for them, and re-layouts: none -> 1.52 us  [body(): copies = jnp.broadcast_to(kv[None], (len(KEY_SETS[0]),) + kv.shape)]
    ppermute x9 -> x6, waiting for transfers between devices: 2.84 us -> 2.84 us  [from_partners(): lax.ppermute(x, axes, [(i, i ^ step) for i in range(size)])]
  transfers between devices with their start and end apart: 10 -> 7, of which waited for: 2 -> 2; matrix products, arithmetic and copies ran while one was open for 0% -> 0% of each run, Pallas kernels for 9% -> 9%
where the time goes in v4:
time: 136 us
  blocking collectives  78.3 us (58%)
  starting transfers between devices  28.9 us (21%)
  Pallas kernels  14.4 us (11%)
  waiting for transfers between devices  11.2 us (8%)
  local copies, waits for them, and re-layouts  2.43 us (2%)
    all_to_all x2, blocking collectives, exchange(): return lax.all_to_all(x, axes, 0, 0, tiled=True, axis_index_groups=sets)  73.4 us
    ppermute x6, starting transfers between devices, from_partners(): lax.ppermute(x, axes, [(i, i ^ step) for i in range(size)])  25.2 us
    pallas_call x4, Pallas kernels, attend(): pl.pallas_call(attend_kernel, in_specs=[VMEM] * 3, out_specs=VMEM, out_sh...  12 us
    all_to_all x1, waiting for transfers between devices, exchange(): return lax.all_to_all(x, axes, 0, 0, tiled=True, axis_index_groups=sets)  8.39 us
    all_gather x1, blocking collectives, body(): velocity = jnp.sum(lax.all_gather(velocity, 'c', axis=0), axis=0)  4.96 us
    all_to_all x1, starting transfers between devices, exchange(): return lax.all_to_all(x, axes, 0, 0, tiled=True, axis_index_groups=sets)  3.69 us
    ppermute x6, waiting for transfers between devices, from_partners(): lax.ppermute(x, axes, [(i, i ^ step) for i in range(size)])  2.84 us
  transfers between devices with their start and end apart: 7, of which 2 were waited for; matrix products, arithmetic and copies ran while one was open for 0% of the time, Pallas kernels for 9%

profile of v4, /device:TPU:1, one launch (start us, length us, event | category | flops | bytes accessed | tf_op | source)
XLA Modules:
  0.0 135.5 jit_solution(1790986145192343554)
XLA Ops:
  0.0 2.1 %pack.1 = bf16[8,3,96,128]{3,2,1,0:T(8,128)(2,1)} custom-call(bf16[96,640]{1,0:T(8,128)(2,1)} %qm.1, bf16[96,640]{1,0:T(8,128)(2,1)} %km.1, bf16[96,640]{1,0:T(8,128)(2,1)} %vm.1, bf16[96,384]{1,0:T(8,128)(2,1)} %qg.1, bf16[96,384]{1,0:T(8,128)(2,1)} %kg.1, bf16[96,384]{1,0:T(8,128)(2,1)} %vg.1), custom_call_target="tpu_custom_call" | custom-call | tf_op jit(solution)/shard_map/pack/pallas_call | solution.py:154
  2.1 47.6 %all_to_all.15 = bf16[8,3,96,128]{3,2,1,0:T(8,128)(2,1)S(1)} all-to-all(bf16[8,3,96,128]{3,2,1,0:T(8,128)(2,1)} %pack.1), channel_id=1, replica_groups={{0,16,32,48,72,88,104,120},{8,24,40,56,64,80,96,112},{1,17,33,49,73,89,..., dimensions={0} | all-to-all | bytes 1179648 | tf_op jit(solution)/shard_map/to_heads/all_to_all | solution.py:37
  49.7 1.5 %broadcast_in_dim.2 = bf16[4,8,2,96,128]{4,3,2,1,0:T(8,128)(2,1)} broadcast(bf16[8,2,96,128]{3,2,1,0:T(8,128)(2,1)S(1)} %slice.9), dimensions={1,2,3,4} | broadcast | bytes 1966080 | tf_op jit(solution)/shard_map/gather/broadcast_in_dim | solution.py:164
  51.2 0.0 copy-start
  51.2 0.0 copy-start.1
  51.2 3.7 %all-to-all-start.1 = ((bf16[32,2,96,128]{3,2,1,0:T(8,128)(2,1)}), bf16[32,2,96,128]{3,2,1,0:T(8,128)(2,1)S(1)}, u32[]{:S(2)}, u32[]{:S(2)}) async-start(bf16[32,2,96,128]{3,2,1,0:T(8,128)(2,1)} %bitcast.2), calls=%async_computation.1 | async-start | bytes 3145728 | tf_op jit(solution)/shard_map/gather/all_to_all | solution.py:37
  54.9 2.3 %collective-permute-start = (bf16[768,128]{1,0:T(8,128)(2,1)S(1)}, bf16[768,128]{1,0:T(8,128)(2,1)S(1)}, u32[]{:S(2)}, u32[]{:S(2)}) collective-permute-start(bf16[768,128]{1,0:T(8,128)(2,1)S(1)} %bitcast.18), channel_id=1, source_target_pairs={{0,8},{8,0},{128,136},{136,128},{256,264},{264,256},{384,392},{392... | collective-permute-start | bytes 589832 | tf_op jit(solution)/shard_map/gather/ppermute | solution.py:42
  57.2 0.0 copy-done
  57.2 0.0 copy-done.1
  57.3 5.1 %collective-permute-start.2 = (bf16[768,128]{1,0:T(8,128)(2,1)S(1)}, bf16[768,128]{1,0:T(8,128)(2,1)S(1)}, u32[]{:S(2)}, u32[]{:S(2)}) collective-permute-start(bf16[768,128]{1,0:T(8,128)(2,1)S(1)} %bitcast.19), channel_id=1, source_target_pairs={{0,384},{8,392},{128,256},{136,264},{256,128},{264,136},{384,0},{3... | collective-permute-start | bytes 589832 | tf_op jit(solution)/shard_map/gather/ppermute | solution.py:42
  62.4 2.7 %collective-permute-start.4 = (bf16[768,128]{1,0:T(8,128)(2,1)S(1)}, bf16[768,128]{1,0:T(8,128)(2,1)S(1)}, u32[]{:S(2)}, u32[]{:S(2)}) collective-permute-start(bf16[768,128]{1,0:T(8,128)(2,1)S(1)} %bitcast.20), channel_id=1, source_target_pairs={{0,392},{8,384},{128,264},{136,256},{256,136},{264,128},{384,8},{3... | collective-permute-start | bytes 589832 | tf_op jit(solution)/shard_map/gather/ppermute | solution.py:42
  65.2 0.0 collective-permute-done.q_ref
  65.2 8.4 %all-to-all-done.1.kv_ref = bf16[32,2,96,128]{3,2,1,0:T(8,128)(2,1)S(1)} async-done(((bf16[32,2,96,128]{3,2,1,0:T(8,128)(2,1)}), bf16[32,2,96,128]{3,2,1,0:T(8,128)(2,1)S(1)}, u32[]{:S(2)}, u32[]{:S(2)}) %all-to-all-start.1) | async-done | bytes 1572896 | tf_op jit(solution)/shard_map/gather/all_to_all | solution.py:37
  73.6 3.0 %attend.4 = bf16[80,768]{1,0:T(8,128)(2,1)S(1)} custom-call(bf16[768,128]{1,0:T(8,128)(2,1)S(1)} %collective-permute-done.q_ref, bf16[32,2,96,128]{3,2,1,0:T(8,128)(2,1)S(1)} %all-to-all-done.1.kv_ref, bf16[64,128]{1,0:T(8,128)(2,1)S(1)} %bitcast.22), custom_call_target="tpu_custom_call" | custom-call | flops 2415919104 | bytes 2097152 | tf_op jit(solution)/shard_map/attend/pallas_call | solution.py:111
  76.5 2.3 %collective-permute-start.1 = (bf16[80,768]{1,0:T(8,128)(2,1)S(1)}, bf16[80,768]{1,0:T(8,128)(2,1)S(1)}, u32[]{:S(2)}, u32[]{:S(2)}) collective-permute-start(bf16[80,768]{1,0:T(8,128)(2,1)S(1)} %attend.4), channel_id=1, source_target_pairs={{0,8},{8,0},{128,136},{136,128},{256,264},{264,256},{384,392},{392... | collective-permute-start | bytes 368648 | tf_op jit(solution)/shard_map/attend/ppermute | solution.py:42
  78.8 0.0 collective-permute-done.2.q_ref
  78.8 3.0 %attend.5 = bf16[80,768]{1,0:T(8,128)(2,1)S(1)} custom-call(bf16[768,128]{1,0:T(8,128)(2,1)S(1)} %collective-permute-done.2.q_ref, bf16[32,2,96,128]{3,2,1,0:T(8,128)(2,1)S(1)} %all-to-all-done.1.kv_ref, bf16[64,128]{1,0:T(8,128)(2,1)S(1)} %bitcast.23), custom_call_target="tpu_custom_call" | custom-call | flops 2415919104 | bytes 2097152 | tf_op jit(solution)/shard_map/attend/pallas_call | solution.py:111
  81.8 11.0 %collective-permute-start.3 = (bf16[80,768]{1,0:T(8,128)(2,1)S(1)}, bf16[80,768]{1,0:T(8,128)(2,1)S(1)}, u32[]{:S(2)}, u32[]{:S(2)}) collective-permute-start(bf16[80,768]{1,0:T(8,128)(2,1)S(1)} %attend.5), channel_id=1, source_target_pairs={{0,384},{8,392},{128,256},{136,264},{256,128},{264,136},{384,0},{3... | collective-permute-start | bytes 368648 | tf_op jit(solution)/shard_map/attend/ppermute | solution.py:42
  92.7 0.0 collective-permute-done.4.q_ref
  92.8 3.1 %attend.6 = bf16[80,768]{1,0:T(8,128)(2,1)S(1)} custom-call(bf16[768,128]{1,0:T(8,128)(2,1)S(1)} %collective-permute-done.4.q_ref, bf16[32,2,96,128]{3,2,1,0:T(8,128)(2,1)S(1)} %all-to-all-done.1.kv_ref, bf16[64,128]{1,0:T(8,128)(2,1)S(1)} %bitcast.24), custom_call_target="tpu_custom_call" | custom-call | flops 2415919104 | bytes 2097152 | tf_op jit(solution)/shard_map/attend/pallas_call | solution.py:111
  95.8 1.9 %collective-permute-start.5 = (bf16[80,768]{1,0:T(8,128)(2,1)S(1)}, bf16[80,768]{1,0:T(8,128)(2,1)S(1)}, u32[]{:S(2)}, u32[]{:S(2)}) collective-permute-start(bf16[80,768]{1,0:T(8,128)(2,1)S(1)} %attend.6), channel_id=1, source_target_pairs={{0,392},{8,384},{128,264},{136,256},{256,136},{264,128},{384,8},{3... | collective-permute-start | bytes 368648 | tf_op jit(solution)/shard_map/attend/ppermute | solution.py:42
  97.8 3.0 %attend.7.refs_3_ = bf16[80,768]{1,0:T(8,128)(2,1)S(1)} custom-call(bf16[768,128]{1,0:T(8,128)(2,1)S(1)} %bitcast.21, bf16[32,2,96,128]{3,2,1,0:T(8,128)(2,1)S(1)} %all-to-all-done.1.kv_ref, bf16[64,128]{1,0:T(8,128)(2,1)S(1)} %bitcast.25), custom_call_target="tpu_custom_call" | custom-call | flops 2415919104 | bytes 2097152 | tf_op jit(solution)/shard_map/attend/pallas_call | solution.py:111
  100.7 0.0 collective-permute-done.1.refs_0_
  100.8 0.0 collective-permute-done.3.refs_1_
  100.8 2.8 %collective-permute-done.5.refs_2_ = bf16[80,768]{1,0:T(8,128)(2,1)S(1)} collective-permute-done((bf16[80,768]{1,0:T(8,128)(2,1)S(1)}, bf16[80,768]{1,0:T(8,128)(2,1)S(1)}, u32[]{:S(2)}, u32[]{:S(2)}) %collective-permute-start.5) | collective-permute-done | bytes 122912 | tf_op jit(solution)/shard_map/attend/ppermute | solution.py:42
  103.6 0.3 combine.1
  103.9 25.8 %all_to_all.16 = bf16[16,48,128]{2,1,0:T(8,128)(2,1)S(1)} all-to-all(bf16[16,48,128]{2,1,0:T(8,128)(2,1)S(1)} %bitcast.17), channel_id=1, replica_groups={{0,2,16,18,32,34,48,50,72,74,88,90,104,106,120,122},{8,10,24,26,40,42,5..., dimensions={0} | all-to-all | bytes 393216 | tf_op jit(solution)/shard_map/to_tokens/all_to_all | solution.py:37
  129.7 5.0 %all-gather = f32[96,128]{1,0:T(8,128)S(1)} all-gather(f32[48,128]{1,0:T(8,128)S(1)} %convert_reduce_fusion), channel_id=2, replica_groups=mesh['y'=4,'zh'=8,'z0'=2,'xl'=2,'xh'=2,'c'=2] {'c'}, dimensions={0}, use_global_device_ids=true | all-gather | bytes 73728 | tf_op jit(solution)/shard_map/to_tokens/all_gather | solution.py:186
  134.7 0.1 reshape.23
  134.8 0.7 copy.15
  (9 shorter events, 0.2 us)
Async XLA Ops:
  51.2 6.0 %copy-start = (bf16[640,64]{0,1:T(8,128)(2,1)S(1)}, bf16[640,64]{0,1:T(8,128)(2,1)}, u32[]{:S(2)}) copy-start(bf16[640,64]{0,1:T(8,128)(2,1)} %param.14) | copy-start | bytes 245764
  51.2 6.0 %copy-start.1 = (bf16[384,64]{0,1:T(8,128)(2,1)S(1)}, bf16[384,64]{0,1:T(8,128)(2,1)}, u32[]{:S(2)}) copy-start(bf16[384,64]{0,1:T(8,128)(2,1)} %param.15) | copy-start | bytes 147460
  51.2 22.4 %all-to-all-start.1 = ((bf16[32,2,96,128]{3,2,1,0:T(8,128)(2,1)}), bf16[32,2,96,128]{3,2,1,0:T(8,128)(2,1)S(1)}, u32[]{:S(2)}, u32[]{:S(2)}) async-start(bf16[32,2,96,128]{3,2,1,0:T(8,128)(2,1)} %bitcast.2), calls=%async_computation.1 | async-start | bytes 3145728 | tf_op jit(solution)/shard_map/gather/all_to_all | solution.py:37
  54.9 10.2 %collective-permute-start = (bf16[768,128]{1,0:T(8,128)(2,1)S(1)}, bf16[768,128]{1,0:T(8,128)(2,1)S(1)}, u32[]{:S(2)}, u32[]{:S(2)}) collective-permute-start(bf16[768,128]{1,0:T(8,128)(2,1)S(1)} %bitcast.18), channel_id=1, source_target_pairs={{0,8},{8,0},{128,136},{136,128},{256,264},{264,256},{384,392},{392... | collective-permute-start | bytes 589832 | tf_op jit(solution)/shard_map/gather/ppermute | solution.py:42
  57.3 21.5 %collective-permute-start.2 = (bf16[768,128]{1,0:T(8,128)(2,1)S(1)}, bf16[768,128]{1,0:T(8,128)(2,1)S(1)}, u32[]{:S(2)}, u32[]{:S(2)}) collective-permute-start(bf16[768,128]{1,0:T(8,128)(2,1)S(1)} %bitcast.19), channel_id=1, source_target_pairs={{0,384},{8,392},{128,256},{136,264},{256,128},{264,136},{384,0},{3... | collective-permute-start | bytes 589832 | tf_op jit(solution)/shard_map/gather/ppermute | solution.py:42
  62.4 30.3 %collective-permute-start.4 = (bf16[768,128]{1,0:T(8,128)(2,1)S(1)}, bf16[768,128]{1,0:T(8,128)(2,1)S(1)}, u32[]{:S(2)}, u32[]{:S(2)}) collective-permute-start(bf16[768,128]{1,0:T(8,128)(2,1)S(1)} %bitcast.20), channel_id=1, source_target_pairs={{0,392},{8,384},{128,264},{136,256},{256,136},{264,128},{384,8},{3... | collective-permute-start | bytes 589832 | tf_op jit(solution)/shard_map/gather/ppermute | solution.py:42
  76.5 24.2 %collective-permute-start.1 = (bf16[80,768]{1,0:T(8,128)(2,1)S(1)}, bf16[80,768]{1,0:T(8,128)(2,1)S(1)}, u32[]{:S(2)}, u32[]{:S(2)}) collective-permute-start(bf16[80,768]{1,0:T(8,128)(2,1)S(1)} %attend.4), channel_id=1, source_target_pairs={{0,8},{8,0},{128,136},{136,128},{256,264},{264,256},{384,392},{392... | collective-permute-start | bytes 368648 | tf_op jit(solution)/shard_map/attend/ppermute | solution.py:42
  81.8 19.0 %collective-permute-start.3 = (bf16[80,768]{1,0:T(8,128)(2,1)S(1)}, bf16[80,768]{1,0:T(8,128)(2,1)S(1)}, u32[]{:S(2)}, u32[]{:S(2)}) collective-permute-start(bf16[80,768]{1,0:T(8,128)(2,1)S(1)} %attend.5), channel_id=1, source_target_pairs={{0,384},{8,392},{128,256},{136,264},{256,128},{264,136},{384,0},{3... | collective-permute-start | bytes 368648 | tf_op jit(solution)/shard_map/attend/ppermute | solution.py:42
  95.8 7.7 %collective-permute-start.5 = (bf16[80,768]{1,0:T(8,128)(2,1)S(1)}, bf16[80,768]{1,0:T(8,128)(2,1)S(1)}, u32[]{:S(2)}, u32[]{:S(2)}) collective-permute-start(bf16[80,768]{1,0:T(8,128)(2,1)S(1)} %attend.6), channel_id=1, source_target_pairs={{0,392},{8,384},{128,264},{136,256},{256,136},{264,128},{384,8},{3... | collective-permute-start | bytes 368648 | tf_op jit(solution)/shard_map/attend/ppermute | solution.py:42

commit v5 on v4

--- a/solution.py
+++ b/solution.py
@@ -24,6 +24,9 @@
 GRP = ("xh", "c")
 Z = ("zh", "z0")
 PLANE_SETS = ([0, 2, 4, 6, 9, 11, 13, 15], [1, 3, 5, 7, 8, 10, 12, 14])
+FIRST = (0, 1, 6, 7)
+SECOND = (4, 5, 2, 3)
+QUERY_ORDER = SECOND + FIRST
 QUERY_AXES = ("y", "z0")
 QUERY_STEPS = (1, 6, 7)
 KEY_AXES = ("y", "xl")
@@ -37,6 +40,11 @@
     return lax.all_to_all(x, axes, 0, 0, tiled=True, axis_index_groups=sets)
 
 
+def from_place(x, step):
+    pairs = [(planes[i], planes[i ^ step]) for planes in PLANE_SETS for i in range(len(planes))]
+    return lax.ppermute(x, Z, pairs)
+
+
 def from_partners(x, axes, steps):
     size = lax.axis_size(axes)
     return [lax.ppermute(x, axes, [(i, i ^ step) for i in range(size)]) for step in steps]
@@ -46,11 +54,44 @@
     return lax.dot_general(a, b, (((1,), (1,)), ((), ())), preferred_element_type=F32)
 
 
-def pack_kernel(main_heads, guide_heads, qm, km, vm, qg, kg, vg, out_ref):
-    for h in range(main_heads + guide_heads):
-        at = (h if h < main_heads else h - main_heads) * HD
-        for t, ref in enumerate((qm, km, vm) if h < main_heads else (qg, kg, vg)):
-            out_ref[h, t] = ref[:, at : at + HD]
+def pack_kernel(main_heads, guide_heads, place_ref, qm, km, vm, qg, kg, vg, *out_refs):
+    heads = main_heads + guide_heads
+    for place in range(heads):
+
+        @pl.when(place_ref[0] == place)
+        def _():
+            for j, out_ref in enumerate(out_refs):
+                h = place ^ j
+                at = (h if h < main_heads else h - main_heads) * HD
+                for t, ref in enumerate((qm, km, vm) if h < main_heads else (qg, kg, vg)):
+                    out_ref[t] = ref[:, at : at + HD]
+
+
+def join_kernel(pieces, with_queries, *refs):
+    in_refs, (copies_ref, *rest) = refs[:pieces], refs[pieces:]
+    for copy in range(copies_ref.shape[0]):
+        for i in range(copies_ref.shape[1]):
+            copies_ref[copy, i] = in_refs[i][1:]
+    if with_queries:
+        (q_ref,) = rest
+        step = in_refs[0].shape[1]
+        for i, j in enumerate(QUERY_ORDER):
+            q_ref[j * step : (j + 1) * step, :] = in_refs[i][0]
+
+
+def join(pieces, keys_of, with_queries):
+    _, tokens, _ = pieces[0].shape
+    shapes = [jax.ShapeDtypeStruct((len(KEY_SETS[0]), keys_of, 2, tokens, HD), BF16)]
+    if with_queries:
+        shapes.append(jax.ShapeDtypeStruct((len(pieces) * tokens, HD), BF16))
+    copies, *rest = pl.pallas_call(
+        functools.partial(join_kernel, len(pieces), with_queries),
+        in_specs=[VMEM] * len(pieces),
+        out_specs=[VMEM] * len(shapes),
+        out_shape=shapes,
+        compiler_params=SMALL,
+    )(*pieces)
+    return copies.reshape((-1,) + copies.shape[2:]), *rest
 
 
 def split_two(x):
@@ -58,11 +99,12 @@
     return high, x - high
 
 
-def attend_kernel(q_ref, kv_ref, map_ref, out_ref, sums_ref):
+def attend_kernel(q_ref, *refs):
+    *kv_refs, map_ref, out_ref, sums_ref = refs
     rows = out_ref.shape[1]
 
     def all_pieces(which):
-        return kv_ref[:, which].reshape(-1, HD)
+        return jnp.concatenate([ref[:, which].reshape(-1, HD) for ref in kv_refs], axis=0)
 
     def weighted(queries, shift):
         scores = dot_t(queries, all_pieces(0)) * SCALE
@@ -107,10 +149,10 @@
 
 def attend(queries, key_values, map_t):
     rows = queries.shape[0]
-    keys = key_values.shape[0] * key_values.shape[2]
+    keys = key_values[0].shape[0] * key_values[0].shape[2] * len(key_values)
     return pl.pallas_call(
         attend_kernel,
-        in_specs=[VMEM] * 3,
+        in_specs=[VMEM] * (2 + len(key_values)),
         out_specs=VMEM,
         out_shape=jax.ShapeDtypeStruct((MESSAGE_ROWS, rows), BF16),
         scratch_shapes=[pltpu.VMEM((rows, HD), F32)],
@@ -118,10 +160,10 @@
         cost_estimate=pl.CostEstimate(
             flops=8 * rows * keys * HD, bytes_accessed=2 << 20, transcendentals=rows * keys
         ),
-    )(queries, key_values, map_t)
-
-
-def combine_kernel(gain_ref, *refs):
+    )(queries, *key_values, map_t)
+
+
+def combine_kernel(place_ref, gain_ref, *refs):
     *in_refs, out_ref = refs
     half = out_ref.shape[2]
     stats = [ref[CH:, :].astype(F32) for ref in in_refs]
@@ -133,8 +175,9 @@
     velocity = (velocity * (gain_ref[0] / summed)).T
     velocity = velocity.reshape(out_ref.shape[0], 2, half, CH)
     velocity = jnp.concatenate([velocity[:, 0], velocity[:, 1]], axis=2).astype(BF16)
-    for side in range(out_ref.shape[1]):
-        out_ref[:, side] = velocity
+    for j in range(out_ref.shape[0]):
+        for side in range(out_ref.shape[1]):
+            out_ref[place_ref[0] ^ j, side] = velocity[j]
 
 
 def body(
@@ -150,20 +193,23 @@
     map_t = lax.dynamic_index_in_dim(maps, head, 0, keepdims=False).T
     gain = jnp.where(head < main_heads, guidance, 1.0 - guidance).astype(F32).reshape(1)
 
+    place = head.astype(jnp.int32).reshape(1)
     with jax.named_scope("pack"):
         packed = pl.pallas_call(
             functools.partial(pack_kernel, main_heads, guide_heads),
-            in_specs=[VMEM] * 6,
-            out_specs=VMEM,
-            out_shape=jax.ShapeDtypeStruct((heads, 3, tokens_here, HD), BF16),
-        )(query_main, key_main, value_main, query_guide, key_guide, value_guide)
+            in_specs=[SMEM] + [VMEM] * 6,
+            out_specs=[VMEM] * heads,
+            out_shape=[jax.ShapeDtypeStruct((3, tokens_here, HD), BF16)] * heads,
+        )(place, query_main, key_main, value_main, query_guide, key_guide, value_guide)
     with jax.named_scope("to_heads"):
-        arrived = exchange(packed, Z, PLANE_SETS)
+        first = [from_place(packed[j], j) if j else packed[j] for j in FIRST]
+        second = [from_place(packed[j], j) for j in SECOND]
     with jax.named_scope("gather"):
-        kv = arrived[:, 1:]
-        copies = jnp.broadcast_to(kv[None], (len(KEY_SETS[0]),) + kv.shape)
-        key_values = exchange(copies.reshape((-1,) + kv.shape[1:]), KEY_AXES, KEY_SETS)
-        q = arrived[:, 0].reshape(heads * tokens_here, HD)
+        (copies,) = join(first, len(FIRST), False)
+        key_values = [exchange(copies, KEY_AXES, KEY_SETS)]
+        key_values[0], second = lax.optimization_barrier((key_values[0], second))
+        copies, q = join(second + first, len(SECOND), True)
+        key_values.append(exchange(copies, KEY_AXES, KEY_SETS))
         queries = from_partners(q, QUERY_AXES, QUERY_STEPS)
     with jax.named_scope("attend"):
         shares = [
@@ -174,11 +220,11 @@
     with jax.named_scope("combine"):
         velocity = pl.pallas_call(
             combine_kernel,
-            in_specs=[SMEM] + [VMEM] * len(shares),
+            in_specs=[SMEM] * 2 + [VMEM] * len(shares),
             out_specs=VMEM,
             out_shape=jax.ShapeDtypeStruct((heads, SIDES, tokens_here // 2, 2 * CH), BF16),
             compiler_params=SMALL,
-        )(gain, *shares)
+        )(place, gain, *shares)
     with jax.named_scope("to_tokens"):
         velocity = velocity.reshape((heads * SIDES,) + velocity.shape[2:])
         velocity = exchange(velocity, PLANE_AXES, SIDE_SETS)

time: 136 us -> 150 us (1.10)
  starting transfers between devices: 28.9 us -> 74.7 us
  blocking collectives: 78.3 us -> 32.8 us
  waiting for transfers between devices: 11.2 us -> 22.9 us
  Pallas kernels: 14.4 us -> 16.3 us
    all_to_all x2 -> x1, blocking collectives: 73.4 us -> 23.4 us  [exchange(): return lax.all_to_all(x, axes, 0, 0, tiled=True, axis_index_groups=sets)]
    ppermute x0 -> x7, starting transfers between devices: none -> 41 us  [from_place(): return lax.ppermute(x, Z, pairs)]
    ppermute x0 -> x7, waiting for transfers between devices: none -> 22.2 us  [from_place(): return lax.ppermute(x, Z, pairs)]
    all_to_all x1 -> x2, waiting for transfers between devices: 8.39 us -> 0.01 us  [exchange(): return lax.all_to_all(x, axes, 0, 0, tiled=True, axis_index_groups=sets)]
    all_gather x1, blocking collectives: 4.96 us -> 9.35 us  [body(): velocity = jnp.sum(lax.all_gather(velocity, 'c', axis=0), axis=0)]
    all_to_all x1 -> x2, starting transfers between devices: 3.69 us -> 7.44 us  [exchange(): return lax.all_to_all(x, axes, 0, 0, tiled=True, axis_index_groups=sets)]
    ppermute x6, waiting for transfers between devices: 2.84 us -> 0.72 us  [from_partners(): lax.ppermute(x, axes, [(i, i ^ step) for i in range(size)])]
    pallas_call x5 -> x7, Pallas kernels: 12.3 us -> 14.2 us  [the longest x4 11.9 us: attend(): pl.pallas_call(attend_kernel, in_specs=[VMEM] * (2 + len(key_values)), ou...]
  transfers between devices with their start and end apart: 7 -> 15, of which waited for: 2 -> 4; matrix products, arithmetic and copies ran while one was open for 0% -> 0% of each run, Pallas kernels for 9% -> 8%
where the time goes in v5:
time: 150 us; the launch traced here: 149 us
  starting transfers between devices  74.7 us (50%)
  blocking collectives  32.8 us (22%)
  waiting for transfers between devices  22.9 us (15%)
  Pallas kernels  16.3 us (11%)
  local copies, waits for them, and re-layouts  1.78 us (1%)
    ppermute x7, starting transfers between devices, from_place(): return lax.ppermute(x, Z, pairs)  41 us
    ppermute x6, starting transfers between devices, from_partners(): lax.ppermute(x, axes, [(i, i ^ step) for i in range(size)])  26.2 us
    all_to_all x1, blocking collectives, exchange(): return lax.all_to_all(x, axes, 0, 0, tiled=True, axis_index_groups=sets)  23.4 us
    ppermute x7, waiting for transfers between devices, from_place(): return lax.ppermute(x, Z, pairs)  22.2 us
    pallas_call x4, Pallas kernels, attend(): pl.pallas_call(attend_kernel, in_specs=[VMEM] * (2 + len(key_values)), ou...  11.9 us
    all_gather x1, blocking collectives, body(): velocity = jnp.sum(lax.all_gather(velocity, 'c', axis=0), axis=0)  9.35 us
    all_to_all x2, starting transfers between devices, exchange(): return lax.all_to_all(x, axes, 0, 0, tiled=True, axis_index_groups=sets)  7.44 us
  transfers between devices with their start and end apart: 15, of which 4 were waited for; matrix products, arithmetic and copies ran while one was open for 0% of the time, Pallas kernels for 8%

profile of v5, /device:TPU:1, one launch (start us, length us, event | category | flops | bytes accessed | tf_op | source)
XLA Modules:
  0.0 148.8 jit_solution(660320684812565329)
XLA Ops:
  0.0 2.2 %pack.1 = (bf16[3,96,128]{2,1,0:T(8,128)(2,1)}, bf16[3,96,128]{2,1,0:T(8,128)(2,1)}, bf16[3,96,128]{2,1,0:T(8,128)(2,1)}, bf16[3,96,128]{2,1,0:T(8,128)(2,1)}, b...) custom-call(s32[1]{0:T(128)} %bitcast.place_ref, ...), custom_call_target="tpu_custom_call" | custom-call | tf_op jit(solution)/shard_map/pack/pallas_call | solution.py:198
  2.2 5.7 %collective-permute-start = (bf16[3,96,128]{2,1,0:T(8,128)(2,1)}, bf16[3,96,128]{2,1,0:T(8,128)(2,1)S(1)}, u32[]{:S(2)}, u32[]{:S(2)}) collective-permute-start(bf16[3,96,128]{2,1,0:T(8,128)(2,1)} %get-tuple-element.21), channel_id=1, source_target_pairs={{0,16},{16,0},{32,48},{48,32},{72,88},{88,72},{104,120},{120,104},... | collective-permute-start | bytes 221192 | tf_op jit(solution)/shard_map/to_heads/ppermute | solution.py:45
  7.9 10.2 %collective-permute-start.1 = (bf16[3,96,128]{2,1,0:T(8,128)(2,1)}, bf16[3,96,128]{2,1,0:T(8,128)(2,1)S(1)}, u32[]{:S(2)}, u32[]{:S(2)}) collective-permute-start(bf16[3,96,128]{2,1,0:T(8,128)(2,1)} %get-tuple-element.22), channel_id=1, source_target_pairs={{0,104},{16,120},{32,72},{48,88},{72,32},{88,48},{104,0},{120,16},... | collective-permute-start | bytes 221192 | tf_op jit(solution)/shard_map/to_heads/ppermute | solution.py:45
  18.0 1.9 %collective-permute-start.2 = (bf16[3,96,128]{2,1,0:T(8,128)(2,1)}, bf16[3,96,128]{2,1,0:T(8,128)(2,1)S(1)}, u32[]{:S(2)}, u32[]{:S(2)}) collective-permute-start(bf16[3,96,128]{2,1,0:T(8,128)(2,1)} %get-tuple-element.23), channel_id=1, source_target_pairs={{0,120},{16,104},{32,88},{48,72},{72,48},{88,32},{104,16},{120,0},... | collective-permute-start | bytes 221192 | tf_op jit(solution)/shard_map/to_heads/ppermute | solution.py:45
  20.0 0.0 collective-permute-done.refs_1_.refs_5_
  20.0 3.4 %collective-permute-done.1.refs_2_.refs_6_ = bf16[3,96,128]{2,1,0:T(8,128)(2,1)S(1)} collective-permute-done((bf16[3,96,128]{2,1,0:T(8,128)(2,1)}, bf16[3,96,128]{2,1,0:T(8,128)(2,1)S(1)}, u32[]{:S(2)}, u32[]{:S(2)}) %collective-permute-start.1) | collective-permute-done | bytes 73760 | tf_op jit(solution)/shard_map/to_heads/ppermute | solution.py:45
  23.4 7.4 %collective-permute-done.2.refs_3_.refs_7_ = bf16[3,96,128]{2,1,0:T(8,128)(2,1)S(1)} collective-permute-done((bf16[3,96,128]{2,1,0:T(8,128)(2,1)}, bf16[3,96,128]{2,1,0:T(8,128)(2,1)S(1)}, u32[]{:S(2)}, u32[]{:S(2)}) %collective-permute-start.2) | collective-permute-done | bytes 73760 | tf_op jit(solution)/shard_map/to_heads/ppermute | solution.py:45
  30.8 0.0 copy-start
  30.8 0.9 copy-done
  31.7 1.0 gather.2
  32.7 0.0 copy-start.7
  32.7 0.0 copy-start.6
  32.7 0.0 copy-start.5
  32.7 0.0 copy-start.4
  32.7 0.0 copy-start.1
  32.7 3.6 %all-to-all-start = ((bf16[16,2,96,128]{3,2,1,0:T(8,128)(2,1)}), bf16[16,2,96,128]{3,2,1,0:T(8,128)(2,1)S(1)}, u32[]{:S(2)}, u32[]{:S(2)}) async-start(bf16[16,2,96,128]{3,2,1,0:T(8,128)(2,1)} %bitcast.2), calls=%async_computation | async-start | bytes 1572864 | tf_op jit(solution)/shard_map/gather/all_to_all | solution.py:40
  36.4 0.0 copy-done.7
  36.4 7.3 %collective-permute-start.3 = (bf16[3,96,128]{2,1,0:T(8,128)(2,1)S(1)}, bf16[3,96,128]{2,1,0:T(8,128)(2,1)S(1)}, u32[]{:S(2)}, u32[]{:S(2)}) collective-permute-start(bf16[3,96,128]{2,1,0:T(8,128)(2,1)S(1)} %copy-done.7), channel_id=1, source_target_pairs={{0,72},{16,88},{32,104},{48,120},{72,0},{88,16},{104,32},{120,48},... | collective-permute-start | bytes 221192 | tf_op jit(solution)/shard_map/to_heads/ppermute | solution.py:45
  43.6 0.0 copy-done.6
  43.7 2.4 %collective-permute-start.4 = (bf16[3,96,128]{2,1,0:T(8,128)(2,1)S(1)}, bf16[3,96,128]{2,1,0:T(8,128)(2,1)S(1)}, u32[]{:S(2)}, u32[]{:S(2)}) collective-permute-start(bf16[3,96,128]{2,1,0:T(8,128)(2,1)S(1)} %copy-done.6), channel_id=1, source_target_pairs={{0,88},{16,72},{32,120},{48,104},{72,16},{88,0},{104,48},{120,32},... | collective-permute-start | bytes 221192 | tf_op jit(solution)/shard_map/to_heads/ppermute | solution.py:45
  46.1 0.0 copy-done.5
  46.1 4.9 %collective-permute-start.5 = (bf16[3,96,128]{2,1,0:T(8,128)(2,1)S(1)}, bf16[3,96,128]{2,1,0:T(8,128)(2,1)S(1)}, u32[]{:S(2)}, u32[]{:S(2)}) collective-permute-start(bf16[3,96,128]{2,1,0:T(8,128)(2,1)S(1)} %copy-done.5), channel_id=1, source_target_pairs={{0,32},{16,48},{32,0},{48,16},{72,104},{88,120},{104,72},{120,88},... | collective-permute-start | bytes 221192 | tf_op jit(solution)/shard_map/to_heads/ppermute | solution.py:45
  51.1 0.0 copy-done.4
  51.1 8.5 %collective-permute-start.6 = (bf16[3,96,128]{2,1,0:T(8,128)(2,1)S(1)}, bf16[3,96,128]{2,1,0:T(8,128)(2,1)S(1)}, u32[]{:S(2)}, u32[]{:S(2)}) collective-permute-start(bf16[3,96,128]{2,1,0:T(8,128)(2,1)S(1)} %copy-done.4), channel_id=1, source_target_pairs={{0,48},{16,32},{32,16},{48,0},{72,120},{88,104},{104,88},{120,72},... | collective-permute-start | bytes 221192 | tf_op jit(solution)/shard_map/to_heads/ppermute | solution.py:45
  59.6 0.0 collective-permute-done.3.refs_0_
  59.6 0.0 collective-permute-done.4.refs_1_
  59.6 11.3 %collective-permute-done.5.refs_2_ = bf16[3,96,128]{2,1,0:T(8,128)(2,1)S(1)} collective-permute-done((bf16[3,96,128]{2,1,0:T(8,128)(2,1)S(1)}, bf16[3,96,128]{2,1,0:T(8,128)(2,1)S(1)}, u32[]{:S(2)}, u32[]{:S(2)}) %collective-permute-start.5) | collective-permute-done | bytes 73760 | tf_op jit(solution)/shard_map/to_heads/ppermute | solution.py:45
  71.0 0.0 collective-permute-done.6.refs_3_
  71.0 0.0 all-to-all-done.refs_0_
  71.0 0.0 copy-done.1
  71.0 1.0 gather.3
  72.0 0.0 copy-start.2
  72.0 0.0 copy-start.3
  72.0 3.8 %all-to-all-start.1 = ((bf16[16,2,96,128]{3,2,1,0:T(8,128)(2,1)}), bf16[16,2,96,128]{3,2,1,0:T(8,128)(2,1)S(1)}, u32[]{:S(2)}, u32[]{:S(2)}) async-start(bf16[16,2,96,128]{3,2,1,0:T(8,128)(2,1)} %bitcast.3), calls=%async_computation.1 | async-start | bytes 1572864 | tf_op jit(solution)/shard_map/gather/all_to_all | solution.py:40
  75.8 1.9 %collective-permute-start.11 = (bf16[768,128]{1,0:T(8,128)(2,1)S(1)}, bf16[768,128]{1,0:T(8,128)(2,1)S(1)}, u32[]{:S(2)}, u32[]{:S(2)}) collective-permute-start(bf16[768,128]{1,0:T(8,128)(2,1)S(1)} %get-tuple-element.32.q_ref), channel_id=1, source_target_pairs={{0,392},{8,384},{128,264},{136,256},{256,136},{264,128},{384,8},{3... | collective-permute-start | bytes 589832 | tf_op jit(solution)/shard_map/gather/ppermute | solution.py:50
  77.7 0.0 copy-done.2
  77.7 0.0 copy-done.3
  77.8 5.1 %collective-permute-start.9 = (bf16[768,128]{1,0:T(8,128)(2,1)S(1)}, bf16[768,128]{1,0:T(8,128)(2,1)S(1)}, u32[]{:S(2)}, u32[]{:S(2)}) collective-permute-start(bf16[768,128]{1,0:T(8,128)(2,1)S(1)} %get-tuple-element.32.q_ref), channel_id=1, source_target_pairs={{0,384},{8,392},{128,256},{136,264},{256,128},{264,136},{384,0},{3... | collective-permute-start | bytes 589832 | tf_op jit(solution)/shard_map/gather/ppermute | solution.py:50
  82.9 3.1 %collective-permute-start.7 = (bf16[768,128]{1,0:T(8,128)(2,1)S(1)}, bf16[768,128]{1,0:T(8,128)(2,1)S(1)}, u32[]{:S(2)}, u32[]{:S(2)}) collective-permute-start(bf16[768,128]{1,0:T(8,128)(2,1)S(1)} %get-tuple-element.32.q_ref), channel_id=1, source_target_pairs={{0,8},{8,0},{128,136},{136,128},{256,264},{264,256},{384,392},{392... | collective-permute-start | bytes 589832 | tf_op jit(solution)/shard_map/gather/ppermute | solution.py:50
  86.0 0.0 collective-permute-done.11.q_ref
  86.1 0.0 all-to-all-done.1.refs_1_
  86.1 3.0 %attend.6 = bf16[80,768]{1,0:T(8,128)(2,1)S(1)} custom-call(bf16[768,128]{1,0:T(8,128)(2,1)S(1)} %collective-permute-done.11.q_ref, bf16[16,2,96,128]{3,2,1,0:T(8,128)(2,1)S(1)} %all-to-all-done.refs_0_, bf16[16,2,96,128]{3,2,1,0:T(8,128)(2,1)S(1)} %all-to-all-done.1.refs_1_, bf16[64,128]{1,0:T(8,128)(2,1)S(1)} %bitcast.19), custom_call_target="tpu_custom_call" | custom-call | flops 2415919104 | bytes 2097152 | tf_op jit(solution)/shard_map/attend/pallas_call | solution.py:153
  89.0 4.3 %collective-permute-start.12 = (bf16[80,768]{1,0:T(8,128)(2,1)S(1)}, bf16[80,768]{1,0:T(8,128)(2,1)S(1)}, u32[]{:S(2)}, u32[]{:S(2)}) collective-permute-start(bf16[80,768]{1,0:T(8,128)(2,1)S(1)} %attend.6), channel_id=1, source_target_pairs={{0,392},{8,384},{128,264},{136,256},{256,136},{264,128},{384,8},{3... | collective-permute-start | bytes 368648 | tf_op jit(solution)/shard_map/attend/ppermute | solution.py:50
  93.3 0.0 collective-permute-done.9.q_ref
  93.4 3.0 %attend.5 = bf16[80,768]{1,0:T(8,128)(2,1)S(1)} custom-call(bf16[768,128]{1,0:T(8,128)(2,1)S(1)} %collective-permute-done.9.q_ref, bf16[16,2,96,128]{3,2,1,0:T(8,128)(2,1)S(1)} %all-to-all-done.refs_0_, bf16[16,2,96,128]{3,2,1,0:T(8,128)(2,1)S(1)} %all-to-all-done.1.refs_1_, bf16[64,128]{1,0:T(8,128)(2,1)S(1)} %bitcast.20), custom_call_target="tpu_custom_call" | custom-call | flops 2415919104 | bytes 2097152 | tf_op jit(solution)/shard_map/attend/pallas_call | solution.py:153
  96.3 9.9 %collective-permute-start.10 = (bf16[80,768]{1,0:T(8,128)(2,1)S(1)}, bf16[80,768]{1,0:T(8,128)(2,1)S(1)}, u32[]{:S(2)}, u32[]{:S(2)}) collective-permute-start(bf16[80,768]{1,0:T(8,128)(2,1)S(1)} %attend.5), channel_id=1, source_target_pairs={{0,384},{8,392},{128,256},{136,264},{256,128},{264,136},{384,0},{3... | collective-permute-start | bytes 368648 | tf_op jit(solution)/shard_map/attend/ppermute | solution.py:50
  106.2 0.0 collective-permute-done.7.q_ref
  106.3 3.0 %attend.4 = bf16[80,768]{1,0:T(8,128)(2,1)S(1)} custom-call(bf16[768,128]{1,0:T(8,128)(2,1)S(1)} %collective-permute-done.7.q_ref, bf16[16,2,96,128]{3,2,1,0:T(8,128)(2,1)S(1)} %all-to-all-done.refs_0_, bf16[16,2,96,128]{3,2,1,0:T(8,128)(2,1)S(1)} %all-to-all-done.1.refs_1_, bf16[64,128]{1,0:T(8,128)(2,1)S(1)} %bitcast.21), custom_call_target="tpu_custom_call" | custom-call | flops 2415919104 | bytes 2097152 | tf_op jit(solution)/shard_map/attend/pallas_call | solution.py:153
  109.2 1.9 %collective-permute-start.8 = (bf16[80,768]{1,0:T(8,128)(2,1)S(1)}, bf16[80,768]{1,0:T(8,128)(2,1)S(1)}, u32[]{:S(2)}, u32[]{:S(2)}) collective-permute-start(bf16[80,768]{1,0:T(8,128)(2,1)S(1)} %attend.4), channel_id=1, source_target_pairs={{0,8},{8,0},{128,136},{136,128},{256,264},{264,256},{384,392},{392... | collective-permute-start | bytes 368648 | tf_op jit(solution)/shard_map/attend/ppermute | solution.py:50
  111.2 3.0 %attend.7.refs_3_ = bf16[80,768]{1,0:T(8,128)(2,1)S(1)} custom-call(bf16[768,128]{1,0:T(8,128)(2,1)S(1)} %get-tuple-element.32.q_ref, bf16[16,2,96,128]{3,2,1,0:T(8,128)(2,1)S(1)} %all-to-all-done.refs_0_, bf16[16,2,96,128]{3,2,1,0:T(8,128)(2,1)S(1)} %all-to-all-done.1.refs_1_, bf16[64,128]{1,0:T(8,128)(2,1)S(1)} %bitcast.22), custom_call_target="tpu_custom_call" | custom-call | flops 2415919104 | bytes 2097152 | tf_op jit(solution)/shard_map/attend/pallas_call | solution.py:153
  114.1 0.0 collective-permute-done.12.refs_2_
  114.1 0.0 collective-permute-done.10.refs_1_
  114.1 0.7 collective-permute-done.8.refs_0_
  114.9 0.3 combine.1
  115.2 23.4 %all_to_all.15 = bf16[16,48,128]{2,1,0:T(8,128)(2,1)S(1)} all-to-all(bf16[16,48,128]{2,1,0:T(8,128)(2,1)S(1)} %bitcast.18), channel_id=1, replica_groups={{0,2,16,18,32,34,48,50,72,74,88,90,104,106,120,122},{8,10,24,26,40,42,5..., dimensions={0} | all-to-all | bytes 393216 | tf_op jit(solution)/shard_map/to_tokens/all_to_all | solution.py:40
  138.6 9.3 %all-gather = f32[96,128]{1,0:T(8,128)S(1)} all-gather(f32[48,128]{1,0:T(8,128)S(1)} %convert_reduce_fusion), channel_id=2, replica_groups=mesh['y'=4,'zh'=8,'z0'=2,'xl'=2,'xh'=2,'c'=2] {'c'}, dimensions={0}, use_global_device_ids=true | all-gather | bytes 73728 | tf_op jit(solution)/shard_map/to_tokens/all_gather | solution.py:232
  148.0 0.1 reshape.30
  148.1 0.7 copy.15
  (7 shorter events, 0.1 us)
Async XLA Ops:
  2.2 17.8 %collective-permute-start = (bf16[3,96,128]{2,1,0:T(8,128)(2,1)}, bf16[3,96,128]{2,1,0:T(8,128)(2,1)S(1)}, u32[]{:S(2)}, u32[]{:S(2)}) collective-permute-start(bf16[3,96,128]{2,1,0:T(8,128)(2,1)} %get-tuple-element.21), channel_id=1, source_target_pairs={{0,16},{16,0},{32,48},{48,32},{72,88},{88,72},{104,120},{120,104},... | collective-permute-start | bytes 221192 | tf_op jit(solution)/shard_map/to_heads/ppermute | solution.py:45
  7.9 15.5 %collective-permute-start.1 = (bf16[3,96,128]{2,1,0:T(8,128)(2,1)}, bf16[3,96,128]{2,1,0:T(8,128)(2,1)S(1)}, u32[]{:S(2)}, u32[]{:S(2)}) collective-permute-start(bf16[3,96,128]{2,1,0:T(8,128)(2,1)} %get-tuple-element.22), channel_id=1, source_target_pairs={{0,104},{16,120},{32,72},{48,88},{72,32},{88,48},{104,0},{120,16},... | collective-permute-start | bytes 221192 | tf_op jit(solution)/shard_map/to_heads/ppermute | solution.py:45
  18.0 12.8 %collective-permute-start.2 = (bf16[3,96,128]{2,1,0:T(8,128)(2,1)}, bf16[3,96,128]{2,1,0:T(8,128)(2,1)S(1)}, u32[]{:S(2)}, u32[]{:S(2)}) collective-permute-start(bf16[3,96,128]{2,1,0:T(8,128)(2,1)} %get-tuple-element.23), channel_id=1, source_target_pairs={{0,120},{16,104},{32,88},{48,72},{72,48},{88,32},{104,16},{120,0},... | collective-permute-start | bytes 221192 | tf_op jit(solution)/shard_map/to_heads/ppermute | solution.py:45
  30.8 0.9 copy-start
  32.7 3.7 %copy-start.7 = (bf16[3,96,128]{2,1,0:T(8,128)(2,1)S(1)}, bf16[3,96,128]{2,1,0:T(8,128)(2,1)}, u32[]{:S(2)}) copy-start(bf16[3,96,128]{2,1,0:T(8,128)(2,1)} %get-tuple-element.24) | copy-start | bytes 221188
  32.7 10.9 %copy-start.6 = (bf16[3,96,128]{2,1,0:T(8,128)(2,1)S(1)}, bf16[3,96,128]{2,1,0:T(8,128)(2,1)}, u32[]{:S(2)}) copy-start(bf16[3,96,128]{2,1,0:T(8,128)(2,1)} %get-tuple-element.25) | copy-start | bytes 221188
  32.7 13.4 %copy-start.5 = (bf16[3,96,128]{2,1,0:T(8,128)(2,1)S(1)}, bf16[3,96,128]{2,1,0:T(8,128)(2,1)}, u32[]{:S(2)}) copy-start(bf16[3,96,128]{2,1,0:T(8,128)(2,1)} %get-tuple-element.26) | copy-start | bytes 221188
  32.7 18.4 %copy-start.4 = (bf16[3,96,128]{2,1,0:T(8,128)(2,1)S(1)}, bf16[3,96,128]{2,1,0:T(8,128)(2,1)}, u32[]{:S(2)}) copy-start(bf16[3,96,128]{2,1,0:T(8,128)(2,1)} %get-tuple-element.27) | copy-start | bytes 221188
  32.7 38.3 %copy-start.1 = (bf16[3,96,128]{2,1,0:T(8,128)(2,1)S(1)}, bf16[3,96,128]{2,1,0:T(8,128)(2,1)}, u32[]{:S(2)}) copy-start(bf16[3,96,128]{2,1,0:T(8,128)(2,1)} %get-tuple-element.20.refs_0_.refs_4_) | copy-start | bytes 221188
  32.7 38.2 %all-to-all-start = ((bf16[16,2,96,128]{3,2,1,0:T(8,128)(2,1)}), bf16[16,2,96,128]{3,2,1,0:T(8,128)(2,1)S(1)}, u32[]{:S(2)}, u32[]{:S(2)}) async-start(bf16[16,2,96,128]{3,2,1,0:T(8,128)(2,1)} %bitcast.2), calls=%async_computation | async-start | bytes 1572864 | tf_op jit(solution)/shard_map/gather/all_to_all | solution.py:40
  36.4 23.3 %collective-permute-start.3 = (bf16[3,96,128]{2,1,0:T(8,128)(2,1)S(1)}, bf16[3,96,128]{2,1,0:T(8,128)(2,1)S(1)}, u32[]{:S(2)}, u32[]{:S(2)}) collective-permute-start(bf16[3,96,128]{2,1,0:T(8,128)(2,1)S(1)} %copy-done.7), channel_id=1, source_target_pairs={{0,72},{16,88},{32,104},{48,120},{72,0},{88,16},{104,32},{120,48},... | collective-permute-start | bytes 221192 | tf_op jit(solution)/shard_map/to_heads/ppermute | solution.py:45
  43.7 16.0 %collective-permute-start.4 = (bf16[3,96,128]{2,1,0:T(8,128)(2,1)S(1)}, bf16[3,96,128]{2,1,0:T(8,128)(2,1)S(1)}, u32[]{:S(2)}, u32[]{:S(2)}) collective-permute-start(bf16[3,96,128]{2,1,0:T(8,128)(2,1)S(1)} %copy-done.6), channel_id=1, source_target_pairs={{0,88},{16,72},{32,120},{48,104},{72,16},{88,0},{104,48},{120,32},... | collective-permute-start | bytes 221192 | tf_op jit(solution)/shard_map/to_heads/ppermute | solution.py:45
  46.1 24.8 %collective-permute-start.5 = (bf16[3,96,128]{2,1,0:T(8,128)(2,1)S(1)}, bf16[3,96,128]{2,1,0:T(8,128)(2,1)S(1)}, u32[]{:S(2)}, u32[]{:S(2)}) collective-permute-start(bf16[3,96,128]{2,1,0:T(8,128)(2,1)S(1)} %copy-done.5), channel_id=1, source_target_pairs={{0,32},{16,48},{32,0},{48,16},{72,104},{88,120},{104,72},{120,88},... | collective-permute-start | bytes 221192 | tf_op jit(solution)/shard_map/to_heads/ppermute | solution.py:45
  51.1 19.9 %collective-permute-start.6 = (bf16[3,96,128]{2,1,0:T(8,128)(2,1)S(1)}, bf16[3,96,128]{2,1,0:T(8,128)(2,1)S(1)}, u32[]{:S(2)}, u32[]{:S(2)}) collective-permute-start(bf16[3,96,128]{2,1,0:T(8,128)(2,1)S(1)} %copy-done.4), channel_id=1, source_target_pairs={{0,48},{16,32},{32,16},{48,0},{72,120},{88,104},{104,88},{120,72},... | collective-permute-start | bytes 221192 | tf_op jit(solution)/shard_map/to_heads/ppermute | solution.py:45
  72.0 5.7 %copy-start.2 = (bf16[640,64]{0,1:T(8,128)(2,1)S(1)}, bf16[640,64]{0,1:T(8,128)(2,1)}, u32[]{:S(2)}) copy-start(bf16[640,64]{0,1:T(8,128)(2,1)} %param.14) | copy-start | bytes 245764
  72.0 5.7 %copy-start.3 = (bf16[384,64]{0,1:T(8,128)(2,1)S(1)}, bf16[384,64]{0,1:T(8,128)(2,1)}, u32[]{:S(2)}) copy-start(bf16[384,64]{0,1:T(8,128)(2,1)} %param.15) | copy-start | bytes 147460
  72.0 14.1 %all-to-all-start.1 = ((bf16[16,2,96,128]{3,2,1,0:T(8,128)(2,1)}), bf16[16,2,96,128]{3,2,1,0:T(8,128)(2,1)S(1)}, u32[]{:S(2)}, u32[]{:S(2)}) async-start(bf16[16,2,96,128]{3,2,1,0:T(8,128)(2,1)} %bitcast.3), calls=%async_computation.1 | async-start | bytes 1572864 | tf_op jit(solution)/shard_map/gather/all_to_all | solution.py:40
  75.8 10.3 %collective-permute-start.11 = (bf16[768,128]{1,0:T(8,128)(2,1)S(1)}, bf16[768,128]{1,0:T(8,128)(2,1)S(1)}, u32[]{:S(2)}, u32[]{:S(2)}) collective-permute-start(bf16[768,128]{1,0:T(8,128)(2,1)S(1)} %get-tuple-element.32.q_ref), channel_id=1, source_target_pairs={{0,392},{8,384},{128,264},{136,256},{256,136},{264,128},{384,8},{3... | collective-permute-start | bytes 589832 | tf_op jit(solution)/shard_map/gather/ppermute | solution.py:50
  77.8 15.5 %collective-permute-start.9 = (bf16[768,128]{1,0:T(8,128)(2,1)S(1)}, bf16[768,128]{1,0:T(8,128)(2,1)S(1)}, u32[]{:S(2)}, u32[]{:S(2)}) collective-permute-start(bf16[768,128]{1,0:T(8,128)(2,1)S(1)} %get-tuple-element.32.q_ref), channel_id=1, source_target_pairs={{0,384},{8,392},{128,256},{136,264},{256,128},{264,136},{384,0},{3... | collective-permute-start | bytes 589832 | tf_op jit(solution)/shard_map/gather/ppermute | solution.py:50
  82.9 23.3 %collective-permute-start.7 = (bf16[768,128]{1,0:T(8,128)(2,1)S(1)}, bf16[768,128]{1,0:T(8,128)(2,1)S(1)}, u32[]{:S(2)}, u32[]{:S(2)}) collective-permute-start(bf16[768,128]{1,0:T(8,128)(2,1)S(1)} %get-tuple-element.32.q_ref), channel_id=1, source_target_pairs={{0,8},{8,0},{128,136},{136,128},{256,264},{264,256},{384,392},{392... | collective-permute-start | bytes 589832 | tf_op jit(solution)/shard_map/gather/ppermute | solution.py:50
  89.0 25.1 %collective-permute-start.12 = (bf16[80,768]{1,0:T(8,128)(2,1)S(1)}, bf16[80,768]{1,0:T(8,128)(2,1)S(1)}, u32[]{:S(2)}, u32[]{:S(2)}) collective-permute-start(bf16[80,768]{1,0:T(8,128)(2,1)S(1)} %attend.6), channel_id=1, source_target_pairs={{0,392},{8,384},{128,264},{136,256},{256,136},{264,128},{384,8},{3... | collective-permute-start | bytes 368648 | tf_op jit(solution)/shard_map/attend/ppermute | solution.py:50
  96.3 17.8 %collective-permute-start.10 = (bf16[80,768]{1,0:T(8,128)(2,1)S(1)}, bf16[80,768]{1,0:T(8,128)(2,1)S(1)}, u32[]{:S(2)}, u32[]{:S(2)}) collective-permute-start(bf16[80,768]{1,0:T(8,128)(2,1)S(1)} %attend.5), channel_id=1, source_target_pairs={{0,384},{8,392},{128,256},{136,264},{256,128},{264,136},{384,0},{3... | collective-permute-start | bytes 368648 | tf_op jit(solution)/shard_map/attend/ppermute | solution.py:50
  109.2 5.6 %collective-permute-start.8 = (bf16[80,768]{1,0:T(8,128)(2,1)S(1)}, bf16[80,768]{1,0:T(8,128)(2,1)S(1)}, u32[]{:S(2)}, u32[]{:S(2)}) collective-permute-start(bf16[80,768]{1,0:T(8,128)(2,1)S(1)} %attend.4), channel_id=1, source_target_pairs={{0,8},{8,0},{128,136},{136,128},{256,264},{264,256},{384,392},{392... | collective-permute-start | bytes 368648 | tf_op jit(solution)/shard_map/attend/ppermute | solution.py:50

commit v6 on v4

--- a/solution.py
+++ b/solution.py
@@ -26,6 +26,7 @@
 PLANE_SETS = ([0, 2, 4, 6, 9, 11, 13, 15], [1, 3, 5, 7, 8, 10, 12, 14])
 QUERY_AXES = ("y", "z0")
 QUERY_STEPS = (1, 6, 7)
+QUERY_SETS = ([0, 1, 6, 7], [2, 3, 4, 5])
 KEY_AXES = ("y", "xl")
 KEY_SETS = ([0, 1, 2, 3], [4, 5, 6, 7])
 SIDES = 2
@@ -53,13 +54,22 @@
             out_ref[h, t] = ref[:, at : at + HD]
 
 
+def copy_kernel(in_ref, q_ref, copies_ref):
+    heads, _, tokens, _ = in_ref.shape
+    for h in range(heads):
+        q_ref[h * tokens : (h + 1) * tokens, :] = in_ref[h, 0]
+        for copy in range(copies_ref.shape[0]):
+            copies_ref[copy, h] = in_ref[h, 1:]
+
+
 def split_two(x):
     high = x.astype(BF16).astype(F32)
     return high, x - high
 
 
-def attend_kernel(q_ref, kv_ref, map_ref, out_ref, sums_ref):
-    rows = out_ref.shape[1]
+def attend_kernel(place_ref, *refs):
+    *q_refs, kv_ref, map_ref, out_ref, sums_ref = refs
+    rows = out_ref.shape[2]
 
     def all_pieces(which):
         return kv_ref[:, which].reshape(-1, HD)
@@ -73,56 +83,63 @@
         weights = jnp.exp2(scores).astype(BF16)
         return jnp.dot(weights, values, preferred_element_type=F32)
 
-    def emit(at, total, shift):
+    def emit(k, at, total, shift):
+        to = place_ref[0] ^ k
         count = total.shape[0]
         lane = lax.broadcasted_iota(jnp.int32, (count, HD), 1)
         picks = lax.broadcasted_iota(jnp.int32, (16, HD), 0) == lax.broadcasted_iota(
             jnp.int32, (16, HD), 1
         )
-        out_ref[:CH, at] = dot_t(map_ref[...], total[:, :HD].astype(BF16)).astype(BF16)
+        out_ref[to, :CH, at] = dot_t(map_ref[...], total[:, :HD].astype(BF16)).astype(BF16)
         high, low = split_two(total[:, HD:])
         rest = jnp.where(lane == 0, high, jnp.where(lane == 1, low, 0.0))
         if shift is not None:
             high, low = split_two(shift)
             rest = jnp.where(lane == 2, high, jnp.where(lane == 3, low, rest))
         rest = dot_t(picks.astype(F32).astype(BF16), rest.astype(BF16))
-        out_ref[CH:, at] = rest.astype(BF16)
-
-    total = weighted(q_ref[...], None)
-    emit(slice(None), total, None)
-    sums_ref[...] = total[:, HD:]
-    least = jnp.min(sums_ref[...])
-    most = jnp.max(sums_ref[...])
-
-    @pl.when(jnp.logical_not((least > 1e-20) & (most < 1e25)))
-    def _():
-        @pl.loop(0, rows // HD)
-        def _(i):
-            at = pl.ds(pl.multiple_of(i * HD, HD), HD)
-            queries = q_ref[at, :]
-            top = jnp.max(dot_t(queries, all_pieces(0)), axis=1, keepdims=True)
-            shift = jnp.ceil(top * SCALE)
-            emit(at, weighted(queries, shift), shift)
-
-
-def attend(queries, key_values, map_t):
-    rows = queries.shape[0]
+        out_ref[to, CH:, at] = rest.astype(BF16)
+
+    for k, q_ref in enumerate(q_refs):
+        total = weighted(q_ref[...], None)
+        emit(k, slice(None), total, None)
+        sums_ref[k] = total[:, HD:]
+
+    for k, q_ref in enumerate(q_refs):
+        least = jnp.min(sums_ref[k])
+        most = jnp.max(sums_ref[k])
+
+        @pl.when(jnp.logical_not((least > 1e-20) & (most < 1e25)))
+        def _():
+            @pl.loop(0, rows // HD)
+            def _(i):
+                at = pl.ds(pl.multiple_of(i * HD, HD), HD)
+                queries = q_ref[at, :]
+                top = jnp.max(dot_t(queries, all_pieces(0)), axis=1, keepdims=True)
+                shift = jnp.ceil(top * SCALE)
+                emit(k, at, weighted(queries, shift), shift)
+
+
+def attend(place, queries, key_values, map_t):
+    rows = queries[0].shape[0]
     keys = key_values.shape[0] * key_values.shape[2]
+    blocks = len(queries)
     return pl.pallas_call(
         attend_kernel,
-        in_specs=[VMEM] * 3,
+        in_specs=[SMEM] + [VMEM] * (2 + blocks),
         out_specs=VMEM,
-        out_shape=jax.ShapeDtypeStruct((MESSAGE_ROWS, rows), BF16),
-        scratch_shapes=[pltpu.VMEM((rows, HD), F32)],
-        compiler_params=pltpu.CompilerParams(vmem_limit_bytes=40 << 20),
+        out_shape=jax.ShapeDtypeStruct((blocks, MESSAGE_ROWS, rows), BF16),
+        scratch_shapes=[pltpu.VMEM((blocks, rows, HD), F32)],
+        compiler_params=pltpu.CompilerParams(vmem_limit_bytes=48 << 20),
         cost_estimate=pl.CostEstimate(
-            flops=8 * rows * keys * HD, bytes_accessed=2 << 20, transcendentals=rows * keys
+            flops=8 * blocks * rows * keys * HD,
+            bytes_accessed=2 << 20,
+            transcendentals=blocks * rows * keys,
         ),
-    )(queries, key_values, map_t)
-
-
-def combine_kernel(gain_ref, *refs):
-    *in_refs, out_ref = refs
+    )(place, *queries, key_values, map_t)
+
+
+def combine_kernel(gain_ref, in_ref, out_ref):
+    in_refs = [in_ref.at[k] for k in range(in_ref.shape[0])]
     half = out_ref.shape[2]
     stats = [ref[CH:, :].astype(F32) for ref in in_refs]
     shifts = [s[2:3] + s[3:4] for s in stats]
@@ -160,25 +177,31 @@
     with jax.named_scope("to_heads"):
         arrived = exchange(packed, Z, PLANE_SETS)
     with jax.named_scope("gather"):
-        kv = arrived[:, 1:]
-        copies = jnp.broadcast_to(kv[None], (len(KEY_SETS[0]),) + kv.shape)
-        key_values = exchange(copies.reshape((-1,) + kv.shape[1:]), KEY_AXES, KEY_SETS)
-        q = arrived[:, 0].reshape(heads * tokens_here, HD)
-        queries = from_partners(q, QUERY_AXES, QUERY_STEPS)
+        copies = (len(KEY_SETS[0]), heads, 2, tokens_here, HD)
+        q, copies = pl.pallas_call(
+            copy_kernel,
+            in_specs=[VMEM],
+            out_specs=[VMEM] * 2,
+            out_shape=[
+                jax.ShapeDtypeStruct((heads * tokens_here, HD), BF16),
+                jax.ShapeDtypeStruct(copies, BF16),
+            ],
+            compiler_params=SMALL,
+        )(arrived)
+        key_values = exchange(copies.reshape((-1,) + copies.shape[2:]), KEY_AXES, KEY_SETS)
+        queries = [q] + from_partners(q, QUERY_AXES, QUERY_STEPS)
     with jax.named_scope("attend"):
-        shares = [
-            from_partners(attend(piece, key_values, map_t), QUERY_AXES, (step,))[0]
-            for piece, step in zip(queries, QUERY_STEPS)
-        ]
-        shares.append(attend(q, key_values, map_t))
+        place = (lax.axis_index("y") >> 1) * 2 + lax.axis_index("z0")
+        shares = attend(place.astype(jnp.int32).reshape(1), queries, key_values, map_t)
     with jax.named_scope("combine"):
+        shares = exchange(shares, QUERY_AXES, QUERY_SETS)
         velocity = pl.pallas_call(
             combine_kernel,
-            in_specs=[SMEM] + [VMEM] * len(shares),
+            in_specs=[SMEM, VMEM],
             out_specs=VMEM,
             out_shape=jax.ShapeDtypeStruct((heads, SIDES, tokens_here // 2, 2 * CH), BF16),
             compiler_params=SMALL,
-        )(gain, *shares)
+        )(gain, shares)
     with jax.named_scope("to_tokens"):
         velocity = velocity.reshape((heads * SIDES,) + velocity.shape[2:])
         velocity = exchange(velocity, PLANE_AXES, SIDE_SETS)

time: 136 us -> 143 us (1.051)
  Pallas kernels: 14.4 us -> 25.3 us
  starting transfers between devices: 28.9 us -> 24.1 us
  waiting for transfers between devices: 11.2 us -> 14.9 us
  local copies, waits for them, and re-layouts: 2.43 us -> 0.87 us
    ppermute x6 -> x3, starting transfers between devices: 25.2 us -> 10.1 us  [from_partners(): lax.ppermute(x, axes, [(i, i ^ step) for i in range(size)])]
    pallas_call x5 -> x3, Pallas kernels: 12.3 us -> 23.2 us  [the longest x1 21.5 us: attend(): pl.pallas_call(attend_kernel, in_specs=[SMEM] + [VMEM] * (2 + blocks), ou...]
    all_to_all x1 -> x2, starting transfers between devices: 3.69 us -> 14 us  [exchange(): return lax.all_to_all(x, axes, 0, 0, tiled=True, axis_index_groups=sets)]
    all_to_all x2, blocking collectives: 73.4 us -> 70.9 us  [exchange(): return lax.all_to_all(x, axes, 0, 0, tiled=True, axis_index_groups=sets)]
    ppermute x6 -> x3, waiting for transfers between devices: 2.84 us -> 4.91 us  [from_partners(): lax.ppermute(x, axes, [(i, i ^ step) for i in range(size)])]
    all_gather x1, blocking collectives: 4.96 us -> 6.66 us  [body(): velocity = jnp.sum(lax.all_gather(velocity, 'c', axis=0), axis=0)]
    all_to_all x1 -> x2, waiting for transfers between devices: 8.39 us -> 9.98 us  [exchange(): return lax.all_to_all(x, axes, 0, 0, tiled=True, axis_index_groups=sets)]
    broadcast_in_dim x1 -> x0, local copies, waits for them, and re-layouts: 1.52 us -> none  [body(): copies = jnp.broadcast_to(kv[None], (len(KEY_SETS[0]),) + kv.shape)]
  transfers between devices with their start and end apart: 7 -> 5, of which waited for: 2 -> 4; matrix products, arithmetic and copies ran while one was open for 0% -> 0% of each run, Pallas kernels for 9% -> 0%
where the time goes in v6:
time: 143 us
  blocking collectives  77.6 us (54%)
  Pallas kernels  25.3 us (18%)
  starting transfers between devices  24.1 us (17%)
  waiting for transfers between devices  14.9 us (10%)
    all_to_all x2, blocking collectives, exchange(): return lax.all_to_all(x, axes, 0, 0, tiled=True, axis_index_groups=sets)  70.9 us
    pallas_call x1, Pallas kernels, attend(): pl.pallas_call(attend_kernel, in_specs=[SMEM] + [VMEM] * (2 + blocks), ou...  21.5 us
    all_to_all x2, starting transfers between devices, exchange(): return lax.all_to_all(x, axes, 0, 0, tiled=True, axis_index_groups=sets)  14 us
    ppermute x3, starting transfers between devices, from_partners(): lax.ppermute(x, axes, [(i, i ^ step) for i in range(size)])  10.1 us
    all_to_all x2, waiting for transfers between devices, exchange(): return lax.all_to_all(x, axes, 0, 0, tiled=True, axis_index_groups=sets)  9.98 us
    all_gather x1, blocking collectives, body(): velocity = jnp.sum(lax.all_gather(velocity, 'c', axis=0), axis=0)  6.66 us
    ppermute x3, waiting for transfers between devices, from_partners(): lax.ppermute(x, axes, [(i, i ^ step) for i in range(size)])  4.91 us
  transfers between devices with their start and end apart: 5, of which 4 were waited for; matrix products, arithmetic and copies ran while one was open for 0% of the time, Pallas kernels for 0%

profile of v6, /device:TPU:1, one launch (start us, length us, event | category | flops | bytes accessed | tf_op | source)
XLA Modules:
  0.0 142.9 jit_solution(11086109967573932003)
XLA Ops:
  0.0 2.1 %pack.1 = bf16[8,3,96,128]{3,2,1,0:T(8,128)(2,1)} custom-call(bf16[96,640]{1,0:T(8,128)(2,1)} %qm.1, bf16[96,640]{1,0:T(8,128)(2,1)} %km.1, bf16[96,640]{1,0:T(8,128)(2,1)} %vm.1, bf16[96,384]{1,0:T(8,128)(2,1)} %qg.1, bf16[96,384]{1,0:T(8,128)(2,1)} %kg.1, bf16[96,384]{1,0:T(8,128)(2,1)} %vg.1), custom_call_target="tpu_custom_call" | custom-call | tf_op jit(solution)/shard_map/pack/pallas_call | solution.py:171
  2.1 47.6 %all_to_all.20.in_ref = bf16[8,3,96,128]{3,2,1,0:T(8,128)(2,1)S(1)} all-to-all(bf16[8,3,96,128]{3,2,1,0:T(8,128)(2,1)} %pack.1), channel_id=1, replica_groups={{0,16,32,48,72,88,104,120},{8,24,40,56,64,80,96,112},{1,17,33,49,73,89,..., dimensions={0} | all-to-all | bytes 1179648 | tf_op jit(solution)/shard_map/to_heads/all_to_all | solution.py:38
  49.6 1.4 gather.1
  51.0 0.0 copy-start
  51.0 0.0 copy-start.1
  51.0 3.7 %all-to-all-start.1 = ((bf16[32,2,96,128]{3,2,1,0:T(8,128)(2,1)}), bf16[32,2,96,128]{3,2,1,0:T(8,128)(2,1)S(1)}, u32[]{:S(2)}, u32[]{:S(2)}) async-start(bf16[32,2,96,128]{3,2,1,0:T(8,128)(2,1)} %bitcast.2), calls=%async_computation.1 | async-start | bytes 3145728 | tf_op jit(solution)/shard_map/gather/all_to_all | solution.py:38
  54.7 5.1 %collective-permute-start.2 = (bf16[768,128]{1,0:T(8,128)(2,1)S(1)}, bf16[768,128]{1,0:T(8,128)(2,1)S(1)}, u32[]{:S(2)}, u32[]{:S(2)}) collective-permute-start(bf16[768,128]{1,0:T(8,128)(2,1)S(1)} %get-tuple-element.7.refs_0_), channel_id=1, source_target_pairs={{0,392},{8,384},{128,264},{136,256},{256,136},{264,128},{384,8},{3... | collective-permute-start | bytes 589832 | tf_op jit(solution)/shard_map/gather/ppermute | solution.py:43
  59.9 1.9 %collective-permute-start.1 = (bf16[768,128]{1,0:T(8,128)(2,1)S(1)}, bf16[768,128]{1,0:T(8,128)(2,1)S(1)}, u32[]{:S(2)}, u32[]{:S(2)}) collective-permute-start(bf16[768,128]{1,0:T(8,128)(2,1)S(1)} %get-tuple-element.7.refs_0_), channel_id=1, source_target_pairs={{0,384},{8,392},{128,256},{136,264},{256,128},{264,136},{384,0},{3... | collective-permute-start | bytes 589832 | tf_op jit(solution)/shard_map/gather/ppermute | solution.py:43
  61.8 3.0 %collective-permute-start = (bf16[768,128]{1,0:T(8,128)(2,1)S(1)}, bf16[768,128]{1,0:T(8,128)(2,1)S(1)}, u32[]{:S(2)}, u32[]{:S(2)}) collective-permute-start(bf16[768,128]{1,0:T(8,128)(2,1)S(1)} %get-tuple-element.7.refs_0_), channel_id=1, source_target_pairs={{0,8},{8,0},{128,136},{136,128},{256,264},{264,256},{384,392},{392... | collective-permute-start | bytes 589832 | tf_op jit(solution)/shard_map/gather/ppermute | solution.py:43
  64.8 0.0 copy-done
  64.8 0.0 copy-done.1
  65.0 0.0 collective-permute-done.2.refs_3_
  65.0 3.9 %collective-permute-done.1.refs_2_ = bf16[768,128]{1,0:T(8,128)(2,1)S(1)} collective-permute-done((bf16[768,128]{1,0:T(8,128)(2,1)S(1)}, bf16[768,128]{1,0:T(8,128)(2,1)S(1)}, u32[]{:S(2)}, u32[]{:S(2)}) %collective-permute-start.1) | collective-permute-done | bytes 196640 | tf_op jit(solution)/shard_map/gather/ppermute | solution.py:43
  68.9 1.0 collective-permute-done.refs_1_
  69.9 3.5 %all-to-all-done.1.refs_4_ = bf16[32,2,96,128]{3,2,1,0:T(8,128)(2,1)S(1)} async-done(((bf16[32,2,96,128]{3,2,1,0:T(8,128)(2,1)}), bf16[32,2,96,128]{3,2,1,0:T(8,128)(2,1)S(1)}, u32[]{:S(2)}, u32[]{:S(2)}) %all-to-all-start.1) | async-done | bytes 1572896 | tf_op jit(solution)/shard_map/gather/all_to_all | solution.py:38
  73.4 21.5 %attend.1 = bf16[4,80,768]{2,1,0:T(8,128)(2,1)} custom-call(s32[1]{0:T(128)} %bitcast.1.place_ref, bf16[768,128]{1,0:T(8,128)(2,1)S(1)} %get-tuple-element.7.refs_0_, bf16[768,128]{1,0:T(8,128)(2,1)S(1)} %collective-permute-done.refs_1_, bf16[768,128]{1,0:T(8,128)(2,1)S(1)} %collective-permute-done.1.refs_2_, ...), custom_call_target="tpu_custom_call" | custom-call | flops 9663676416 | bytes 2097152 | tf_op jit(solution)/shard_map/attend/pallas_call | solution.py:126
  94.9 10.3 %all-to-all-start.2 = ((bf16[4,80,768]{2,1,0:T(8,128)(2,1)}), bf16[4,80,768]{2,1,0:T(8,128)(2,1)S(1)}, u32[]{:S(2)}, u32[]{:S(2)}) async-start(bf16[4,80,768]{2,1,0:T(8,128)(2,1)} %attend.1), calls=%async_computation.2 | async-start | bytes 983040 | tf_op jit(solution)/shard_map/combine/all_to_all | solution.py:38
  105.2 6.5 %all-to-all-done.2.in_ref = bf16[4,80,768]{2,1,0:T(8,128)(2,1)S(1)} async-done(((bf16[4,80,768]{2,1,0:T(8,128)(2,1)}), bf16[4,80,768]{2,1,0:T(8,128)(2,1)S(1)}, u32[]{:S(2)}, u32[]{:S(2)}) %all-to-all-start.2) | async-done | bytes 491552 | tf_op jit(solution)/shard_map/combine/all_to_all | solution.py:38
  111.7 0.3 combine.1
  112.0 23.4 %all_to_all.21 = bf16[16,48,128]{2,1,0:T(8,128)(2,1)S(1)} all-to-all(bf16[16,48,128]{2,1,0:T(8,128)(2,1)S(1)} %bitcast.17), channel_id=1, replica_groups={{0,2,16,18,32,34,48,50,72,74,88,90,104,106,120,122},{8,10,24,26,40,42,5..., dimensions={0} | all-to-all | bytes 393216 | tf_op jit(solution)/shard_map/to_tokens/all_to_all | solution.py:38
  135.4 6.7 %all-gather = f32[96,128]{1,0:T(8,128)S(1)} all-gather(f32[48,128]{1,0:T(8,128)S(1)} %convert_reduce_fusion), channel_id=2, replica_groups=mesh['y'=4,'zh'=8,'z0'=2,'xl'=2,'xh'=2,'c'=2] {'c'}, dimensions={0}, use_global_device_ids=true | all-gather | bytes 73728 | tf_op jit(solution)/shard_map/to_tokens/all_gather | solution.py:209
  142.1 0.1 reshape.26
  142.2 0.7 copy.15
  (7 shorter events, 0.1 us)
Async XLA Ops:
  51.0 13.8 %copy-start = (bf16[640,64]{0,1:T(8,128)(2,1)S(1)}, bf16[640,64]{0,1:T(8,128)(2,1)}, u32[]{:S(2)}) copy-start(bf16[640,64]{0,1:T(8,128)(2,1)} %param.14) | copy-start | bytes 245764
  51.0 13.8 %copy-start.1 = (bf16[384,64]{0,1:T(8,128)(2,1)S(1)}, bf16[384,64]{0,1:T(8,128)(2,1)}, u32[]{:S(2)}) copy-start(bf16[384,64]{0,1:T(8,128)(2,1)} %param.15) | copy-start | bytes 147460
  51.0 22.4 %all-to-all-start.1 = ((bf16[32,2,96,128]{3,2,1,0:T(8,128)(2,1)}), bf16[32,2,96,128]{3,2,1,0:T(8,128)(2,1)S(1)}, u32[]{:S(2)}, u32[]{:S(2)}) async-start(bf16[32,2,96,128]{3,2,1,0:T(8,128)(2,1)} %bitcast.2), calls=%async_computation.1 | async-start | bytes 3145728 | tf_op jit(solution)/shard_map/gather/all_to_all | solution.py:38
  54.7 10.2 %collective-permute-start.2 = (bf16[768,128]{1,0:T(8,128)(2,1)S(1)}, bf16[768,128]{1,0:T(8,128)(2,1)S(1)}, u32[]{:S(2)}, u32[]{:S(2)}) collective-permute-start(bf16[768,128]{1,0:T(8,128)(2,1)S(1)} %get-tuple-element.7.refs_0_), channel_id=1, source_target_pairs={{0,392},{8,384},{128,264},{136,256},{256,136},{264,128},{384,8},{3... | collective-permute-start | bytes 589832 | tf_op jit(solution)/shard_map/gather/ppermute | solution.py:43
  59.9 9.0 %collective-permute-start.1 = (bf16[768,128]{1,0:T(8,128)(2,1)S(1)}, bf16[768,128]{1,0:T(8,128)(2,1)S(1)}, u32[]{:S(2)}, u32[]{:S(2)}) collective-permute-start(bf16[768,128]{1,0:T(8,128)(2,1)S(1)} %get-tuple-element.7.refs_0_), channel_id=1, source_target_pairs={{0,384},{8,392},{128,256},{136,264},{256,128},{264,136},{384,0},{3... | collective-permute-start | bytes 589832 | tf_op jit(solution)/shard_map/gather/ppermute | solution.py:43
  61.8 8.1 %collective-permute-start = (bf16[768,128]{1,0:T(8,128)(2,1)S(1)}, bf16[768,128]{1,0:T(8,128)(2,1)S(1)}, u32[]{:S(2)}, u32[]{:S(2)}) collective-permute-start(bf16[768,128]{1,0:T(8,128)(2,1)S(1)} %get-tuple-element.7.refs_0_), channel_id=1, source_target_pairs={{0,8},{8,0},{128,136},{136,128},{256,264},{264,256},{384,392},{392... | collective-permute-start | bytes 589832 | tf_op jit(solution)/shard_map/gather/ppermute | solution.py:43
  94.9 16.8 %all-to-all-start.2 = ((bf16[4,80,768]{2,1,0:T(8,128)(2,1)}), bf16[4,80,768]{2,1,0:T(8,128)(2,1)S(1)}, u32[]{:S(2)}, u32[]{:S(2)}) async-start(bf16[4,80,768]{2,1,0:T(8,128)(2,1)} %attend.1), calls=%async_computation.2 | async-start | bytes 983040 | tf_op jit(solution)/shard_map/combine/all_to_all | solution.py:38

commit v7 on v6

--- a/solution.py
+++ b/solution.py
@@ -25,8 +25,7 @@
 Z = ("zh", "z0")
 PLANE_SETS = ([0, 2, 4, 6, 9, 11, 13, 15], [1, 3, 5, 7, 8, 10, 12, 14])
 QUERY_AXES = ("y", "z0")
-QUERY_STEPS = (1, 6, 7)
-QUERY_SETS = ([0, 1, 6, 7], [2, 3, 4, 5])
+Z0_STEP, Y_STEP = 1, 6
 KEY_AXES = ("y", "xl")
 KEY_SETS = ([0, 1, 2, 3], [4, 5, 6, 7])
 SIDES = 2
@@ -38,9 +37,9 @@
     return lax.all_to_all(x, axes, 0, 0, tiled=True, axis_index_groups=sets)
 
 
-def from_partners(x, axes, steps):
-    size = lax.axis_size(axes)
-    return [lax.ppermute(x, axes, [(i, i ^ step) for i in range(size)]) for step in steps]
+def from_partner(x, step):
+    size = lax.axis_size(QUERY_AXES)
+    return lax.ppermute(x, QUERY_AXES, [(i, i ^ step) for i in range(size)])
 
 
 def dot_t(a, b):
@@ -67,9 +66,11 @@
     return high, x - high
 
 
-def attend_kernel(place_ref, *refs):
-    *q_refs, kv_ref, map_ref, out_ref, sums_ref = refs
+def attend_kernel(*refs):
+    *q_refs, kv_ref, map_ref, out_ref, staged_ref, sums_ref = refs
     rows = out_ref.shape[2]
+    for k, q_ref in enumerate(q_refs):
+        staged_ref[k] = q_ref[...]
 
     def all_pieces(which):
         return kv_ref[:, which].reshape(-1, HD)
@@ -84,69 +85,79 @@
         return jnp.dot(weights, values, preferred_element_type=F32)
 
     def emit(k, at, total, shift):
-        to = place_ref[0] ^ k
         count = total.shape[0]
         lane = lax.broadcasted_iota(jnp.int32, (count, HD), 1)
         picks = lax.broadcasted_iota(jnp.int32, (16, HD), 0) == lax.broadcasted_iota(
             jnp.int32, (16, HD), 1
         )
-        out_ref[to, :CH, at] = dot_t(map_ref[...], total[:, :HD].astype(BF16)).astype(BF16)
+        out_ref[k, :CH, at] = dot_t(map_ref[...], total[:, :HD].astype(BF16)).astype(BF16)
         high, low = split_two(total[:, HD:])
         rest = jnp.where(lane == 0, high, jnp.where(lane == 1, low, 0.0))
         if shift is not None:
             high, low = split_two(shift)
             rest = jnp.where(lane == 2, high, jnp.where(lane == 3, low, rest))
         rest = dot_t(picks.astype(F32).astype(BF16), rest.astype(BF16))
-        out_ref[to, CH:, at] = rest.astype(BF16)
-
-    for k, q_ref in enumerate(q_refs):
-        total = weighted(q_ref[...], None)
+        out_ref[k, CH:, at] = rest.astype(BF16)
+
+    @pl.loop(0, len(q_refs))
+    def _(k):
+        total = weighted(staged_ref[k], None)
         emit(k, slice(None), total, None)
-        sums_ref[k] = total[:, HD:]
-
-    for k, q_ref in enumerate(q_refs):
-        least = jnp.min(sums_ref[k])
-        most = jnp.max(sums_ref[k])
+        sums_ref[...] = total[:, HD:]
+        least = jnp.min(sums_ref[...])
+        most = jnp.max(sums_ref[...])
 
         @pl.when(jnp.logical_not((least > 1e-20) & (most < 1e25)))
         def _():
             @pl.loop(0, rows // HD)
             def _(i):
                 at = pl.ds(pl.multiple_of(i * HD, HD), HD)
-                queries = q_ref[at, :]
+                queries = staged_ref[k, at, :]
                 top = jnp.max(dot_t(queries, all_pieces(0)), axis=1, keepdims=True)
                 shift = jnp.ceil(top * SCALE)
                 emit(k, at, weighted(queries, shift), shift)
 
 
-def attend(place, queries, key_values, map_t):
+def attend(queries, key_values, map_t):
     rows = queries[0].shape[0]
     keys = key_values.shape[0] * key_values.shape[2]
     blocks = len(queries)
     return pl.pallas_call(
         attend_kernel,
-        in_specs=[SMEM] + [VMEM] * (2 + blocks),
+        in_specs=[VMEM] * (2 + blocks),
         out_specs=VMEM,
         out_shape=jax.ShapeDtypeStruct((blocks, MESSAGE_ROWS, rows), BF16),
-        scratch_shapes=[pltpu.VMEM((blocks, rows, HD), F32)],
-        compiler_params=pltpu.CompilerParams(vmem_limit_bytes=48 << 20),
+        scratch_shapes=[pltpu.VMEM((blocks, rows, HD), BF16), pltpu.VMEM((rows, HD), F32)],
+        compiler_params=pltpu.CompilerParams(vmem_limit_bytes=40 << 20),
         cost_estimate=pl.CostEstimate(
             flops=8 * blocks * rows * keys * HD,
             bytes_accessed=2 << 20,
             transcendentals=blocks * rows * keys,
         ),
-    )(place, *queries, key_values, map_t)
-
-
-def combine_kernel(gain_ref, in_ref, out_ref):
-    in_refs = [in_ref.at[k] for k in range(in_ref.shape[0])]
-    half = out_ref.shape[2]
-    stats = [ref[CH:, :].astype(F32) for ref in in_refs]
+    )(*queries, key_values, map_t)
+
+
+def added(shares):
+    stats = [share[CH:, :].astype(F32) for share in shares]
     shifts = [s[2:3] + s[3:4] for s in stats]
     top = functools.reduce(jnp.maximum, shifts)
     scales = [jnp.exp2(shift - top) for shift in shifts]
     summed = sum((s[0:1] + s[1:2]) * scale for s, scale in zip(stats, scales))
-    velocity = sum(ref[:CH, :].astype(F32) * scale for ref, scale in zip(in_refs, scales))
+    velocity = sum(share[:CH, :].astype(F32) * scale for share, scale in zip(shares, scales))
+    return velocity, summed, top
+
+
+def add_kernel(here_ref, there_ref, out_ref):
+    velocity, summed, top = added([here_ref[1], there_ref[1]])
+    out_ref[:CH, :] = velocity.astype(BF16)
+    tail = split_two(summed) + split_two(top)
+    filler = jnp.zeros((out_ref.shape[0] - CH - len(tail), out_ref.shape[1]), F32)
+    out_ref[CH:, :] = jnp.concatenate(tail + (filler,), axis=0).astype(BF16)
+
+
+def combine_kernel(gain_ref, here_ref, there_ref, beside_ref, out_ref):
+    half = out_ref.shape[2]
+    velocity, summed, _ = added([here_ref[0], there_ref[0], beside_ref[...]])
     velocity = (velocity * (gain_ref[0] / summed)).T
     velocity = velocity.reshape(out_ref.shape[0], 2, half, CH)
     velocity = jnp.concatenate([velocity[:, 0], velocity[:, 1]], axis=2).astype(BF16)
@@ -189,19 +200,26 @@
             compiler_params=SMALL,
         )(arrived)
         key_values = exchange(copies.reshape((-1,) + copies.shape[2:]), KEY_AXES, KEY_SETS)
-        queries = [q] + from_partners(q, QUERY_AXES, QUERY_STEPS)
+        beside = from_partner(q, Z0_STEP)
+        across = [from_partner(q, Y_STEP), from_partner(q, Y_STEP ^ Z0_STEP)]
     with jax.named_scope("attend"):
-        place = (lax.axis_index("y") >> 1) * 2 + lax.axis_index("z0")
-        shares = attend(place.astype(jnp.int32).reshape(1), queries, key_values, map_t)
+        there = from_partner(attend(across, key_values, map_t), Y_STEP)
+        here = attend([q, beside], key_values, map_t)
     with jax.named_scope("combine"):
-        shares = exchange(shares, QUERY_AXES, QUERY_SETS)
+        share = pl.pallas_call(
+            add_kernel,
+            in_specs=[VMEM] * 2,
+            out_specs=VMEM,
+            out_shape=jax.ShapeDtypeStruct(here.shape[1:], BF16),
+            compiler_params=SMALL,
+        )(here, there)
         velocity = pl.pallas_call(
             combine_kernel,
-            in_specs=[SMEM, VMEM],
+            in_specs=[SMEM] + [VMEM] * 3,
             out_specs=VMEM,
             out_shape=jax.ShapeDtypeStruct((heads, SIDES, tokens_here // 2, 2 * CH), BF16),
             compiler_params=SMALL,
-        )(gain, shares)
+        )(gain, here, there, from_partner(share, Z0_STEP))
     with jax.named_scope("to_tokens"):
         velocity = velocity.reshape((heads * SIDES,) + velocity.shape[2:])
         velocity = exchange(velocity, PLANE_AXES, SIDE_SETS)

time: 143 us -> 132 us (0.923)
  Pallas kernels: 25.3 us -> 15.7 us
  waiting for transfers between devices: 14.9 us -> 12.1 us
  starting transfers between devices: 24.1 us -> 26.6 us
    ppermute x3 -> x5, starting transfers between devices: 10.1 us -> 22.9 us  [from_partner(): return lax.ppermute(x, QUERY_AXES, [(i, i ^ step) for i in range(size)])]
    all_to_all x2 -> x1, starting transfers between devices: 14 us -> 3.69 us  [exchange(): return lax.all_to_all(x, axes, 0, 0, tiled=True, axis_index_groups=sets)]
    pallas_call x2 -> x4, Pallas kernels: 21.8 us -> 12.3 us  [the longest x2 11.9 us: attend(): pl.pallas_call(attend_kernel, in_specs=[VMEM] * (2 + blocks), out_specs=V...]
    all_to_all x2 -> x1, waiting for transfers between devices: 9.98 us -> 4.49 us  [exchange(): return lax.all_to_all(x, axes, 0, 0, tiled=True, axis_index_groups=sets)]
    ppermute x3 -> x5, waiting for transfers between devices: 4.91 us -> 7.63 us  [from_partner(): return lax.ppermute(x, QUERY_AXES, [(i, i ^ step) for i in range(size)])]
    all_gather x1, blocking collectives: 6.66 us -> 5.14 us  [body(): velocity = jnp.sum(lax.all_gather(velocity, 'c', axis=0), axis=0)]
  transfers between devices with their start and end apart: 5 -> 6, of which waited for: 4 -> 3; matrix products, arithmetic and copies ran while one was open for 0% -> 0% of each run, Pallas kernels for 0% -> 9%
where the time goes in v7:
time: 132 us
  blocking collectives  76.2 us (58%)
  starting transfers between devices  26.6 us (20%)
  Pallas kernels  15.7 us (12%)
  waiting for transfers between devices  12.1 us (9%)
    all_to_all x2, blocking collectives, exchange(): return lax.all_to_all(x, axes, 0, 0, tiled=True, axis_index_groups=sets)  71.1 us
    ppermute x5, starting transfers between devices, from_partner(): return lax.ppermute(x, QUERY_AXES, [(i, i ^ step) for i in range(size)])  22.9 us
    pallas_call x2, Pallas kernels, attend(): pl.pallas_call(attend_kernel, in_specs=[VMEM] * (2 + blocks), out_specs=V...  11.9 us
    ppermute x5, waiting for transfers between devices, from_partner(): return lax.ppermute(x, QUERY_AXES, [(i, i ^ step) for i in range(size)])  7.63 us
    all_gather x1, blocking collectives, body(): velocity = jnp.sum(lax.all_gather(velocity, 'c', axis=0), axis=0)  5.14 us
    all_to_all x1, waiting for transfers between devices, exchange(): return lax.all_to_all(x, axes, 0, 0, tiled=True, axis_index_groups=sets)  4.49 us
    all_to_all x1, starting transfers between devices, exchange(): return lax.all_to_all(x, axes, 0, 0, tiled=True, axis_index_groups=sets)  3.69 us
  transfers between devices with their start and end apart: 6, of which 3 were waited for; matrix products, arithmetic and copies ran while one was open for 0% of the time, Pallas kernels for 9%

profile of v7, /device:TPU:1, one launch (start us, length us, event | category | flops | bytes accessed | tf_op | source)
XLA Modules:
  0.0 131.8 jit_solution(5641760426161054907)
XLA Ops:
  0.0 2.1 %pack.1 = bf16[8,3,96,128]{3,2,1,0:T(8,128)(2,1)} custom-call(bf16[96,640]{1,0:T(8,128)(2,1)} %qm.1, bf16[96,640]{1,0:T(8,128)(2,1)} %km.1, bf16[96,640]{1,0:T(8,128)(2,1)} %vm.1, bf16[96,384]{1,0:T(8,128)(2,1)} %qg.1, bf16[96,384]{1,0:T(8,128)(2,1)} %kg.1, bf16[96,384]{1,0:T(8,128)(2,1)} %vg.1), custom_call_target="tpu_custom_call" | custom-call | tf_op jit(solution)/shard_map/pack/pallas_call | solution.py:182
  2.1 47.6 %all_to_all.15.in_ref = bf16[8,3,96,128]{3,2,1,0:T(8,128)(2,1)S(1)} all-to-all(bf16[8,3,96,128]{3,2,1,0:T(8,128)(2,1)} %pack.1), channel_id=1, replica_groups={{0,16,32,48,72,88,104,120},{8,24,40,56,64,80,96,112},{1,17,33,49,73,89,..., dimensions={0} | all-to-all | bytes 1179648 | tf_op jit(solution)/shard_map/to_heads/all_to_all | solution.py:37
  49.6 1.4 %gather.1 = (bf16[768,128]{1,0:T(8,128)(2,1)S(1)}, bf16[4,8,2,96,128]{4,3,2,1,0:T(8,128)(2,1)}) custom-call(bf16[8,3,96,128]{3,2,1,0:T(8,128)(2,1)S(1)} %all_to_all.15.in_ref), custom_call_target="tpu_custom_call" | custom-call | tf_op jit(solution)/shard_map/gather/pallas_call | solution.py:192
  51.0 0.0 copy-start
  51.0 0.0 copy-start.1
  51.0 3.7 %all-to-all-start.1 = ((bf16[32,2,96,128]{3,2,1,0:T(8,128)(2,1)}), bf16[32,2,96,128]{3,2,1,0:T(8,128)(2,1)S(1)}, u32[]{:S(2)}, u32[]{:S(2)}) async-start(bf16[32,2,96,128]{3,2,1,0:T(8,128)(2,1)} %bitcast.1), calls=%async_computation.1 | async-start | bytes 3145728 | tf_op jit(solution)/shard_map/gather/all_to_all | solution.py:37
  54.7 5.1 %collective-permute-start.2 = (bf16[768,128]{1,0:T(8,128)(2,1)S(1)}, bf16[768,128]{1,0:T(8,128)(2,1)S(1)}, u32[]{:S(2)}, u32[]{:S(2)}) collective-permute-start(bf16[768,128]{1,0:T(8,128)(2,1)S(1)} %get-tuple-element.7.refs_0_), channel_id=1, source_target_pairs={{0,392},{8,384},{128,264},{136,256},{256,136},{264,128},{384,8},{3... | collective-permute-start | bytes 589832 | tf_op jit(solution)/shard_map/gather/ppermute | solution.py:42
  59.9 1.9 %collective-permute-start.1 = (bf16[768,128]{1,0:T(8,128)(2,1)S(1)}, bf16[768,128]{1,0:T(8,128)(2,1)S(1)}, u32[]{:S(2)}, u32[]{:S(2)}) collective-permute-start(bf16[768,128]{1,0:T(8,128)(2,1)S(1)} %get-tuple-element.7.refs_0_), channel_id=1, source_target_pairs={{0,384},{8,392},{128,256},{136,264},{256,128},{264,136},{384,0},{3... | collective-permute-start | bytes 589832 | tf_op jit(solution)/shard_map/gather/ppermute | solution.py:42
  61.8 0.0 copy-done
  61.8 0.0 copy-done.1
  61.9 3.0 %collective-permute-start = (bf16[768,128]{1,0:T(8,128)(2,1)S(1)}, bf16[768,128]{1,0:T(8,128)(2,1)S(1)}, u32[]{:S(2)}, u32[]{:S(2)}) collective-permute-start(bf16[768,128]{1,0:T(8,128)(2,1)S(1)} %get-tuple-element.7.refs_0_), channel_id=1, source_target_pairs={{0,8},{8,0},{128,136},{136,128},{256,264},{264,256},{384,392},{392... | collective-permute-start | bytes 589832 | tf_op jit(solution)/shard_map/gather/ppermute | solution.py:42
  64.9 0.0 collective-permute-done.2.refs_1_
  65.0 3.9 %collective-permute-done.1.refs_0_ = bf16[768,128]{1,0:T(8,128)(2,1)S(1)} collective-permute-done((bf16[768,128]{1,0:T(8,128)(2,1)S(1)}, bf16[768,128]{1,0:T(8,128)(2,1)S(1)}, u32[]{:S(2)}, u32[]{:S(2)}) %collective-permute-start.1) | collective-permute-done | bytes 196640 | tf_op jit(solution)/shard_map/gather/ppermute | solution.py:42
  68.9 4.5 %all-to-all-done.1.refs_2_ = bf16[32,2,96,128]{3,2,1,0:T(8,128)(2,1)S(1)} async-done(((bf16[32,2,96,128]{3,2,1,0:T(8,128)(2,1)}), bf16[32,2,96,128]{3,2,1,0:T(8,128)(2,1)S(1)}, u32[]{:S(2)}, u32[]{:S(2)}) %all-to-all-start.1) | async-done | bytes 1572896 | tf_op jit(solution)/shard_map/gather/all_to_all | solution.py:37
  73.4 6.0 %attend.3 = bf16[2,80,768]{2,1,0:T(8,128)(2,1)S(1)} custom-call(bf16[768,128]{1,0:T(8,128)(2,1)S(1)} %collective-permute-done.1.refs_0_, bf16[768,128]{1,0:T(8,128)(2,1)S(1)} %collective-permute-done.2.refs_1_, bf16[32,2,96,128]{3,2,1,0:T(8,128)(2,1)S(1)} %all-to-all-done.1.refs_2_, bf16[64,128]{1,0:T(8,128)(2,1)S(1)} %bitcast.17), custom_call_target="tpu_custom_call" | custom-call | flops 4831838208 | bytes 2097152 | tf_op jit(solution)/shard_map/attend/pallas_call | solution.py:125
  79.4 11.0 %collective-permute-start.3 = (bf16[2,80,768]{2,1,0:T(8,128)(2,1)S(1)}, bf16[2,80,768]{2,1,0:T(8,128)(2,1)S(1)}, u32[]{:S(2)}, u32[]{:S(2)}) collective-permute-start(bf16[2,80,768]{2,1,0:T(8,128)(2,1)S(1)} %attend.3), channel_id=1, source_target_pairs={{0,384},{8,392},{128,256},{136,264},{256,128},{264,136},{384,0},{3... | collective-permute-start | bytes 737288 | tf_op jit(solution)/shard_map/attend/ppermute | solution.py:42
  90.3 0.0 collective-permute-done.refs_1_
  90.3 6.0 %attend.2.here_ref = bf16[2,80,768]{2,1,0:T(8,128)(2,1)S(1)} custom-call(bf16[768,128]{1,0:T(8,128)(2,1)S(1)} %get-tuple-element.7.refs_0_, bf16[768,128]{1,0:T(8,128)(2,1)S(1)} %collective-permute-done.refs_1_, bf16[32,2,96,128]{3,2,1,0:T(8,128)(2,1)S(1)} %all-to-all-done.1.refs_2_, bf16[64,128]{1,0:T(8,128)(2,1)S(1)} %bitcast.18), custom_call_target="tpu_custom_call" | custom-call | flops 4831838208 | bytes 2097152 | tf_op jit(solution)/shard_map/attend/pallas_call | solution.py:125
  96.3 0.0 collective-permute-done.3.there_ref
  96.3 0.1 combine.2
  96.4 1.9 %collective-permute-start.4 = (bf16[80,768]{1,0:T(8,128)(2,1)S(1)}, bf16[80,768]{1,0:T(8,128)(2,1)S(1)}, u32[]{:S(2)}, u32[]{:S(2)}) collective-permute-start(bf16[80,768]{1,0:T(8,128)(2,1)S(1)} %combine.2), channel_id=1, source_target_pairs={{0,8},{8,0},{128,136},{136,128},{256,264},{264,256},{384,392},{392... | collective-permute-start | bytes 368648 | tf_op jit(solution)/shard_map/combine/ppermute | solution.py:42
  98.3 3.7 %collective-permute-done.4.beside_ref = bf16[80,768]{1,0:T(8,128)(2,1)S(1)} collective-permute-done((bf16[80,768]{1,0:T(8,128)(2,1)S(1)}, bf16[80,768]{1,0:T(8,128)(2,1)S(1)}, u32[]{:S(2)}, u32[]{:S(2)}) %collective-permute-start.4) | collective-permute-done | bytes 122912 | tf_op jit(solution)/shard_map/combine/ppermute | solution.py:42
  102.0 0.3 combine.3
  102.3 23.5 %all_to_all.16 = bf16[16,48,128]{2,1,0:T(8,128)(2,1)S(1)} all-to-all(bf16[16,48,128]{2,1,0:T(8,128)(2,1)S(1)} %bitcast.16), channel_id=1, replica_groups={{0,2,16,18,32,34,48,50,72,74,88,90,104,106,120,122},{8,10,24,26,40,42,5..., dimensions={0} | all-to-all | bytes 393216 | tf_op jit(solution)/shard_map/to_tokens/all_to_all | solution.py:37
  125.8 5.1 %all-gather = f32[96,128]{1,0:T(8,128)S(1)} all-gather(f32[48,128]{1,0:T(8,128)S(1)} %convert_reduce_fusion), channel_id=2, replica_groups=mesh['y'=4,'zh'=8,'z0'=2,'xl'=2,'xh'=2,'c'=2] {'c'}, dimensions={0}, use_global_device_ids=true | all-gather | bytes 73728 | tf_op jit(solution)/shard_map/to_tokens/all_gather | solution.py:227
  131.0 0.1 reshape.22
  131.1 0.7 copy.15
  (7 shorter events, 0.1 us)
Async XLA Ops:
  51.0 10.8 %copy-start = (bf16[640,64]{0,1:T(8,128)(2,1)S(1)}, bf16[640,64]{0,1:T(8,128)(2,1)}, u32[]{:S(2)}) copy-start(bf16[640,64]{0,1:T(8,128)(2,1)} %param.14) | copy-start | bytes 245764
  51.0 10.8 %copy-start.1 = (bf16[384,64]{0,1:T(8,128)(2,1)S(1)}, bf16[384,64]{0,1:T(8,128)(2,1)}, u32[]{:S(2)}) copy-start(bf16[384,64]{0,1:T(8,128)(2,1)} %param.15) | copy-start | bytes 147460
  51.0 22.4 %all-to-all-start.1 = ((bf16[32,2,96,128]{3,2,1,0:T(8,128)(2,1)}), bf16[32,2,96,128]{3,2,1,0:T(8,128)(2,1)S(1)}, u32[]{:S(2)}, u32[]{:S(2)}) async-start(bf16[32,2,96,128]{3,2,1,0:T(8,128)(2,1)} %bitcast.1), calls=%async_computation.1 | async-start | bytes 3145728 | tf_op jit(solution)/shard_map/gather/all_to_all | solution.py:37
  54.7 10.2 %collective-permute-start.2 = (bf16[768,128]{1,0:T(8,128)(2,1)S(1)}, bf16[768,128]{1,0:T(8,128)(2,1)S(1)}, u32[]{:S(2)}, u32[]{:S(2)}) collective-permute-start(bf16[768,128]{1,0:T(8,128)(2,1)S(1)} %get-tuple-element.7.refs_0_), channel_id=1, source_target_pairs={{0,392},{8,384},{128,264},{136,256},{256,136},{264,128},{384,8},{3... | collective-permute-start | bytes 589832 | tf_op jit(solution)/shard_map/gather/ppermute | solution.py:42
  59.9 9.0 %collective-permute-start.1 = (bf16[768,128]{1,0:T(8,128)(2,1)S(1)}, bf16[768,128]{1,0:T(8,128)(2,1)S(1)}, u32[]{:S(2)}, u32[]{:S(2)}) collective-permute-start(bf16[768,128]{1,0:T(8,128)(2,1)S(1)} %get-tuple-element.7.refs_0_), channel_id=1, source_target_pairs={{0,384},{8,392},{128,256},{136,264},{256,128},{264,136},{384,0},{3... | collective-permute-start | bytes 589832 | tf_op jit(solution)/shard_map/gather/ppermute | solution.py:42
  61.9 28.4 %collective-permute-start = (bf16[768,128]{1,0:T(8,128)(2,1)S(1)}, bf16[768,128]{1,0:T(8,128)(2,1)S(1)}, u32[]{:S(2)}, u32[]{:S(2)}) collective-permute-start(bf16[768,128]{1,0:T(8,128)(2,1)S(1)} %get-tuple-element.7.refs_0_), channel_id=1, source_target_pairs={{0,8},{8,0},{128,136},{136,128},{256,264},{264,256},{384,392},{392... | collective-permute-start | bytes 589832 | tf_op jit(solution)/shard_map/gather/ppermute | solution.py:42
  79.4 16.9 %collective-permute-start.3 = (bf16[2,80,768]{2,1,0:T(8,128)(2,1)S(1)}, bf16[2,80,768]{2,1,0:T(8,128)(2,1)S(1)}, u32[]{:S(2)}, u32[]{:S(2)}) collective-permute-start(bf16[2,80,768]{2,1,0:T(8,128)(2,1)S(1)} %attend.3), channel_id=1, source_target_pairs={{0,384},{8,392},{128,256},{136,264},{256,128},{264,136},{384,0},{3... | collective-permute-start | bytes 737288 | tf_op jit(solution)/shard_map/attend/ppermute | solution.py:42
  96.4 5.6 %collective-permute-start.4 = (bf16[80,768]{1,0:T(8,128)(2,1)S(1)}, bf16[80,768]{1,0:T(8,128)(2,1)S(1)}, u32[]{:S(2)}, u32[]{:S(2)}) collective-permute-start(bf16[80,768]{1,0:T(8,128)(2,1)S(1)} %combine.2), channel_id=1, source_target_pairs={{0,8},{8,0},{128,136},{136,128},{256,264},{264,256},{384,392},{392... | collective-permute-start | bytes 368648 | tf_op jit(solution)/shard_map/combine/ppermute | solution.py:42

commit v8 on v7

--- a/solution.py
+++ b/solution.py
@@ -27,7 +27,7 @@
 QUERY_AXES = ("y", "z0")
 Z0_STEP, Y_STEP = 1, 6
 KEY_AXES = ("y", "xl")
-KEY_SETS = ([0, 1, 2, 3], [4, 5, 6, 7])
+NEAR_STEPS, FAR_STEP = (1, 2), 3
 SIDES = 2
 PLANE_AXES = Z + ("xh",)
 SIDE_SETS = [[SIDES * z + x for z in planes for x in range(SIDES)] for planes in PLANE_SETS]
@@ -37,9 +37,8 @@
     return lax.all_to_all(x, axes, 0, 0, tiled=True, axis_index_groups=sets)
 
 
-def from_partner(x, step):
-    size = lax.axis_size(QUERY_AXES)
-    return lax.ppermute(x, QUERY_AXES, [(i, i ^ step) for i in range(size)])
+def from_partner(x, step, axes=QUERY_AXES):
+    return lax.ppermute(x, axes, [(i, i ^ step) for i in range(lax.axis_size(axes))])
 
 
 def dot_t(a, b):
@@ -53,12 +52,11 @@
             out_ref[h, t] = ref[:, at : at + HD]
 
 
-def copy_kernel(in_ref, q_ref, copies_ref):
+def copy_kernel(in_ref, q_ref, kv_ref):
     heads, _, tokens, _ = in_ref.shape
     for h in range(heads):
         q_ref[h * tokens : (h + 1) * tokens, :] = in_ref[h, 0]
-        for copy in range(copies_ref.shape[0]):
-            copies_ref[copy, h] = in_ref[h, 1:]
+        kv_ref[h] = in_ref[h, 1:]
 
 
 def split_two(x):
@@ -66,14 +64,22 @@
     return high, x - high
 
 
-def attend_kernel(*refs):
-    *q_refs, kv_ref, map_ref, out_ref, staged_ref, sums_ref = refs
+def message(velocity, summed, top, rows, dtype):
+    tail = split_two(summed) + split_two(top) if dtype == BF16 else (summed, top)
+    filler = jnp.zeros((rows - CH - len(tail), velocity.shape[1]), F32)
+    return jnp.concatenate((velocity,) + tail + (filler,), axis=0).astype(dtype)
+
+
+def attend_kernel(count, pieces, first_before, *refs):
+    q_refs, kv_refs, map_ref, refs = refs[:count], refs[count:pieces], refs[pieces], refs[pieces + 1 :]
+    before_ref, refs = (None, refs) if first_before is None else (refs[0], refs[1:])
+    out_ref, staged_ref, sums_ref = refs
     rows = out_ref.shape[2]
     for k, q_ref in enumerate(q_refs):
         staged_ref[k] = q_ref[...]
 
     def all_pieces(which):
-        return kv_ref[:, which].reshape(-1, HD)
+        return jnp.concatenate([ref[:, which].reshape(-1, HD) for ref in kv_refs], axis=0)
 
     def weighted(queries, shift):
         scores = dot_t(queries, all_pieces(0)) * SCALE
@@ -90,14 +96,20 @@
         picks = lax.broadcasted_iota(jnp.int32, (16, HD), 0) == lax.broadcasted_iota(
             jnp.int32, (16, HD), 1
         )
-        out_ref[k, :CH, at] = dot_t(map_ref[...], total[:, :HD].astype(BF16)).astype(BF16)
+        velocity = dot_t(map_ref[...], total[:, :HD].astype(BF16))
         high, low = split_two(total[:, HD:])
         rest = jnp.where(lane == 0, high, jnp.where(lane == 1, low, 0.0))
         if shift is not None:
             high, low = split_two(shift)
             rest = jnp.where(lane == 2, high, jnp.where(lane == 3, low, rest))
         rest = dot_t(picks.astype(F32).astype(BF16), rest.astype(BF16))
-        out_ref[k, CH:, at] = rest.astype(BF16)
+        summed, top = rest[0:1] + rest[1:2], rest[2:3] + rest[3:4]
+        if before_ref is not None:
+            before = before_ref[first_before + k, :, at]
+            velocity, summed, top = joined(
+                [velocity, before[:CH]], [summed, before[CH : CH + 1]], [top, before[CH + 1 : CH + 2]]
+            )
+        out_ref[k, :, at] = message(velocity, summed, top, out_ref.shape[1], out_ref.dtype)
 
     @pl.loop(0, len(q_refs))
     def _(k):
@@ -118,15 +130,18 @@
                 emit(k, at, weighted(queries, shift), shift)
 
 
-def attend(queries, key_values, map_t):
+def attend(queries, key_values, map_t, before=None, first_before=None):
     rows = queries[0].shape[0]
-    keys = key_values.shape[0] * key_values.shape[2]
+    keys = key_values[0].shape[0] * key_values[0].shape[2] * len(key_values)
     blocks = len(queries)
+    pieces = blocks + len(key_values)
+    operands = [*queries, *key_values, map_t] + ([] if before is None else [before])
+    out = (blocks, CH + 8, rows) if before is None else (blocks, MESSAGE_ROWS, rows)
     return pl.pallas_call(
-        attend_kernel,
-        in_specs=[VMEM] * (2 + blocks),
+        functools.partial(attend_kernel, blocks, pieces, first_before),
+        in_specs=[VMEM] * len(operands),
         out_specs=VMEM,
-        out_shape=jax.ShapeDtypeStruct((blocks, MESSAGE_ROWS, rows), BF16),
+        out_shape=jax.ShapeDtypeStruct(out, F32 if before is None else BF16),
         scratch_shapes=[pltpu.VMEM((blocks, rows, HD), BF16), pltpu.VMEM((rows, HD), F32)],
         compiler_params=pltpu.CompilerParams(vmem_limit_bytes=40 << 20),
         cost_estimate=pl.CostEstimate(
@@ -134,25 +149,29 @@
             bytes_accessed=2 << 20,
             transcendentals=blocks * rows * keys,
         ),
-    )(*queries, key_values, map_t)
+    )(*operands)
+
+
+def joined(velocities, sums, shifts):
+    top = functools.reduce(jnp.maximum, shifts)
+    scales = [jnp.exp2(shift - top) for shift in shifts]
+    summed = sum(s * scale for s, scale in zip(sums, scales))
+    velocity = sum(v * scale for v, scale in zip(velocities, scales))
+    return velocity, summed, top
 
 
 def added(shares):
     stats = [share[CH:, :].astype(F32) for share in shares]
-    shifts = [s[2:3] + s[3:4] for s in stats]
-    top = functools.reduce(jnp.maximum, shifts)
-    scales = [jnp.exp2(shift - top) for shift in shifts]
-    summed = sum((s[0:1] + s[1:2]) * scale for s, scale in zip(stats, scales))
-    velocity = sum(share[:CH, :].astype(F32) * scale for share, scale in zip(shares, scales))
-    return velocity, summed, top
+    return joined(
+        [share[:CH, :].astype(F32) for share in shares],
+        [s[0:1] + s[1:2] for s in stats],
+        [s[2:3] + s[3:4] for s in stats],
+    )
 
 
 def add_kernel(here_ref, there_ref, out_ref):
-    velocity, summed, top = added([here_ref[1], there_ref[1]])
-    out_ref[:CH, :] = velocity.astype(BF16)
-    tail = split_two(summed) + split_two(top)
-    filler = jnp.zeros((out_ref.shape[0] - CH - len(tail), out_ref.shape[1]), F32)
-    out_ref[CH:, :] = jnp.concatenate(tail + (filler,), axis=0).astype(BF16)
+    share = added([here_ref[1], there_ref[1]])
+    out_ref[...] = message(*share, out_ref.shape[0], BF16)
 
 
 def combine_kernel(gain_ref, here_ref, there_ref, beside_ref, out_ref):
@@ -188,23 +207,24 @@
     with jax.named_scope("to_heads"):
         arrived = exchange(packed, Z, PLANE_SETS)
     with jax.named_scope("gather"):
-        copies = (len(KEY_SETS[0]), heads, 2, tokens_here, HD)
-        q, copies = pl.pallas_call(
+        q, kv = pl.pallas_call(
             copy_kernel,
             in_specs=[VMEM],
             out_specs=[VMEM] * 2,
             out_shape=[
                 jax.ShapeDtypeStruct((heads * tokens_here, HD), BF16),
-                jax.ShapeDtypeStruct(copies, BF16),
+                jax.ShapeDtypeStruct((heads, 2, tokens_here, HD), BF16),
             ],
             compiler_params=SMALL,
         )(arrived)
-        key_values = exchange(copies.reshape((-1,) + copies.shape[2:]), KEY_AXES, KEY_SETS)
+        near = [kv] + [from_partner(kv, step, KEY_AXES) for step in NEAR_STEPS]
+        far = [from_partner(kv, FAR_STEP, KEY_AXES)]
         beside = from_partner(q, Z0_STEP)
         across = [from_partner(q, Y_STEP), from_partner(q, Y_STEP ^ Z0_STEP)]
     with jax.named_scope("attend"):
-        there = from_partner(attend(across, key_values, map_t), Y_STEP)
-        here = attend([q, beside], key_values, map_t)
+        before = attend(across + [q, beside], near, map_t)
+        there = from_partner(attend(across, far, map_t, before, 0), Y_STEP)
+        here = attend([q, beside], far, map_t, before, len(across))
     with jax.named_scope("combine"):
         share = pl.pallas_call(
             add_kernel,

time: 132 us -> 134 us (1.015)
  waiting for transfers between devices: 12.1 us -> 7.21 us
  blocking collectives: 76.2 us -> 79.3 us
  starting transfers between devices: 26.6 us -> 29.4 us
    ppermute x5 -> x8, starting transfers between devices: 22.9 us -> 29.4 us  [from_partner(): lax.ppermute(x, axes, [(i, i ^ step) for i in range(lax.axis_size(axes))])]
    all_to_all x1 -> x0, waiting for transfers between devices: 4.49 us -> none  [exchange(): return lax.all_to_all(x, axes, 0, 0, tiled=True, axis_index_groups=sets)]
    all_gather x1, blocking collectives: 5.14 us -> 9.26 us  [body(): velocity = jnp.sum(lax.all_gather(velocity, 'c', axis=0), axis=0)]
    all_to_all x1 -> x0, starting transfers between devices: 3.69 us -> none  [exchange(): return lax.all_to_all(x, axes, 0, 0, tiled=True, axis_index_groups=sets)]
    pallas_call x2 -> x3, Pallas kernels: 11.9 us -> 14.2 us  [attend(): pl.pallas_call(functools.partial(attend_kernel, blocks, pieces, first_bef...]
    pallas_call x1, Pallas kernels: 1.38 us -> 0.04 us  [body(): pl.pallas_call(copy_kernel, in_specs=[VMEM], out_specs=[VMEM] * 2, out_sh...]
    ppermute x5 -> x8, waiting for transfers between devices: 7.63 us -> 7.21 us  [from_partner(): lax.ppermute(x, axes, [(i, i ^ step) for i in range(lax.axis_size(axes))])]
  transfers between devices with their start and end apart: 6 -> 8, of which waited for: 3 -> 4; matrix products, arithmetic and copies ran while one was open for 0% -> 0% of each run, Pallas kernels for 9% -> 9%
where the time goes in v8:
time: 134 us
  blocking collectives  79.3 us (59%)
  starting transfers between devices  29.4 us (22%)
  Pallas kernels  16.7 us (12%)
  waiting for transfers between devices  7.21 us (5%)
    all_to_all x2, blocking collectives, exchange(): return lax.all_to_all(x, axes, 0, 0, tiled=True, axis_index_groups=sets)  70 us
    ppermute x8, starting transfers between devices, from_partner(): lax.ppermute(x, axes, [(i, i ^ step) for i in range(lax.axis_size(axes))])  29.4 us
    pallas_call x3, Pallas kernels, attend(): pl.pallas_call(functools.partial(attend_kernel, blocks, pieces, first_bef...  14.2 us
    all_gather x1, blocking collectives, body(): velocity = jnp.sum(lax.all_gather(velocity, 'c', axis=0), axis=0)  9.26 us
    ppermute x8, waiting for transfers between devices, from_partner(): lax.ppermute(x, axes, [(i, i ^ step) for i in range(lax.axis_size(axes))])  7.21 us
  transfers between devices with their start and end apart: 8, of which 4 were waited for; matrix products, arithmetic and copies ran while one was open for 0% of the time, Pallas kernels for 9%

profile of v8, /device:TPU:1, one launch (start us, length us, event | category | flops | bytes accessed | tf_op | source)
XLA Modules:
  0.0 133.6 jit_solution(18190069847532731482)
XLA Ops:
  0.0 2.1 %pack.1 = bf16[8,3,96,128]{3,2,1,0:T(8,128)(2,1)} custom-call(bf16[96,640]{1,0:T(8,128)(2,1)} %qm.1, bf16[96,640]{1,0:T(8,128)(2,1)} %km.1, bf16[96,640]{1,0:T(8,128)(2,1)} %vm.1, bf16[96,384]{1,0:T(8,128)(2,1)} %qg.1, bf16[96,384]{1,0:T(8,128)(2,1)} %kg.1, bf16[96,384]{1,0:T(8,128)(2,1)} %vg.1), custom_call_target="tpu_custom_call" | custom-call | tf_op jit(solution)/shard_map/pack/pallas_call | solution.py:201
  2.1 47.6 %all_to_all.10.in_ref = bf16[8,3,96,128]{3,2,1,0:T(8,128)(2,1)S(1)} all-to-all(bf16[8,3,96,128]{3,2,1,0:T(8,128)(2,1)} %pack.1), channel_id=1, replica_groups={{0,16,32,48,72,88,104,120},{8,24,40,56,64,80,96,112},{1,17,33,49,73,89,..., dimensions={0} | all-to-all | bytes 1179648 | tf_op jit(solution)/shard_map/to_heads/all_to_all | solution.py:37
  49.6 0.0 copy-start
  49.6 0.0 copy-start.1
  49.7 3.3 %collective-permute-start.5 = (bf16[8,2,96,128]{3,2,1,0:T(8,128)(2,1)S(1)}, bf16[8,2,96,128]{3,2,1,0:T(8,128)(2,1)S(1)}, u32[]{:S(2)}, u32[]{:S(2)}) collective-permute-start(bf16[8,2,96,128]{3,2,1,0:T(8,128)(2,1)S(1)} %get-tuple-element.8.refs_4_), channel_id=1, source_target_pairs={{0,128},{4,132},{128,0},{132,4},{256,384},{260,388},{384,256},{388... | collective-permute-start | bytes 1179656 | tf_op jit(solution)/shard_map/gather/ppermute | solution.py:41
  53.0 3.1 %collective-permute-start.4 = (bf16[8,2,96,128]{3,2,1,0:T(8,128)(2,1)S(1)}, bf16[8,2,96,128]{3,2,1,0:T(8,128)(2,1)S(1)}, u32[]{:S(2)}, u32[]{:S(2)}) collective-permute-start(bf16[8,2,96,128]{3,2,1,0:T(8,128)(2,1)S(1)} %get-tuple-element.8.refs_4_), channel_id=1, source_target_pairs={{0,4},{4,0},{128,132},{132,128},{256,260},{260,256},{384,388},{388... | collective-permute-start | bytes 1179656 | tf_op jit(solution)/shard_map/gather/ppermute | solution.py:41
  56.2 3.9 %collective-permute-start.3 = (bf16[768,128]{1,0:T(8,128)(2,1)S(1)}, bf16[768,128]{1,0:T(8,128)(2,1)S(1)}, u32[]{:S(2)}, u32[]{:S(2)}) collective-permute-start(bf16[768,128]{1,0:T(8,128)(2,1)S(1)} %get-tuple-element.7.refs_2_.refs_0_), channel_id=1, source_target_pairs={{0,392},{8,384},{128,264},{136,256},{256,136},{264,128},{384,8},{3... | collective-permute-start | bytes 589832 | tf_op jit(solution)/shard_map/gather/ppermute | solution.py:41
  60.0 2.7 %collective-permute-start.2 = (bf16[768,128]{1,0:T(8,128)(2,1)S(1)}, bf16[768,128]{1,0:T(8,128)(2,1)S(1)}, u32[]{:S(2)}, u32[]{:S(2)}) collective-permute-start(bf16[768,128]{1,0:T(8,128)(2,1)S(1)} %get-tuple-element.7.refs_2_.refs_0_), channel_id=1, source_target_pairs={{0,384},{8,392},{128,256},{136,264},{256,128},{264,136},{384,0},{3... | collective-permute-start | bytes 589832 | tf_op jit(solution)/shard_map/gather/ppermute | solution.py:41
  62.7 3.0 %collective-permute-start = (bf16[768,128]{1,0:T(8,128)(2,1)S(1)}, bf16[768,128]{1,0:T(8,128)(2,1)S(1)}, u32[]{:S(2)}, u32[]{:S(2)}) collective-permute-start(bf16[768,128]{1,0:T(8,128)(2,1)S(1)} %get-tuple-element.7.refs_2_.refs_0_), channel_id=1, source_target_pairs={{0,8},{8,0},{128,136},{136,128},{256,264},{264,256},{384,392},{392... | collective-permute-start | bytes 589832 | tf_op jit(solution)/shard_map/gather/ppermute | solution.py:41
  65.8 0.0 copy-done
  65.8 0.0 copy-done.1
  65.9 0.0 collective-permute-done.3.refs_1_
  65.9 1.9 %collective-permute-start.1 = (bf16[8,2,96,128]{3,2,1,0:T(8,128)(2,1)S(1)}, bf16[8,2,96,128]{3,2,1,0:T(8,128)(2,1)S(1)}, u32[]{:S(2)}, u32[]{:S(2)}) collective-permute-start(bf16[8,2,96,128]{3,2,1,0:T(8,128)(2,1)S(1)} %get-tuple-element.8.refs_4_), channel_id=1, source_target_pairs={{0,132},{4,128},{128,4},{132,0},{256,388},{260,384},{384,260},{388... | collective-permute-start | bytes 1179656 | tf_op jit(solution)/shard_map/gather/ppermute | solution.py:41
  67.8 1.9 %collective-permute-done.2.refs_0_ = bf16[768,128]{1,0:T(8,128)(2,1)S(1)} collective-permute-done((bf16[768,128]{1,0:T(8,128)(2,1)S(1)}, bf16[768,128]{1,0:T(8,128)(2,1)S(1)}, u32[]{:S(2)}, u32[]{:S(2)}) %collective-permute-start.2) | collective-permute-done | bytes 196640 | tf_op jit(solution)/shard_map/gather/ppermute | solution.py:41
  69.8 0.3 collective-permute-done.refs_3_.refs_1_
  70.1 0.0 collective-permute-done.5.refs_6_
  70.1 0.0 collective-permute-done.4.refs_5_
  70.1 9.5 %attend.3.refs_4_ = f32[4,72,768]{2,1,0:T(8,128)S(1)} custom-call(bf16[768,128]{1,0:T(8,128)(2,1)S(1)} %collective-permute-done.2.refs_0_, bf16[768,128]{1,0:T(8,128)(2,1)S(1)} %collective-permute-done.3.refs_1_, bf16[768,128]{1,0:T(8,128)(2,1)S(1)} %get-tuple-element.7.refs_2_.refs_0_, bf16[768,128]{1,0:T(8,128)(2,1)S(1)} %collective-permute-done.refs_3_.refs_1_, ...), custom_call_target="tpu_custom_call" | custom-call | flops 7247757312 | bytes 2097152 | tf_op jit(solution)/shard_map/attend/pallas_call | solution.py:140
  79.6 0.0 collective-permute-done.1.refs_2_
  79.6 2.4 %attend.5 = bf16[2,80,768]{2,1,0:T(8,128)(2,1)S(1)} custom-call(bf16[768,128]{1,0:T(8,128)(2,1)S(1)} %collective-permute-done.2.refs_0_, bf16[768,128]{1,0:T(8,128)(2,1)S(1)} %collective-permute-done.3.refs_1_, bf16[8,2,96,128]{3,2,1,0:T(8,128)(2,1)S(1)} %collective-permute-done.1.refs_2_, bf16[64,128]{1,0:T(8,128)(2,1)S(1)} %bitcast.17, ...), custom_call_target="tpu_custom_call" | custom-call | flops 1207959552 | bytes 2097152 | tf_op jit(solution)/shard_map/attend/pallas_call | solution.py:140
  82.0 9.5 %collective-permute-start.6 = (bf16[2,80,768]{2,1,0:T(8,128)(2,1)S(1)}, bf16[2,80,768]{2,1,0:T(8,128)(2,1)S(1)}, u32[]{:S(2)}, u32[]{:S(2)}) collective-permute-start(bf16[2,80,768]{2,1,0:T(8,128)(2,1)S(1)} %attend.5), channel_id=1, source_target_pairs={{0,384},{8,392},{128,256},{136,264},{256,128},{264,136},{384,0},{3... | collective-permute-start | bytes 737288 | tf_op jit(solution)/shard_map/attend/ppermute | solution.py:41
  91.5 2.4 %attend.4.here_ref = bf16[2,80,768]{2,1,0:T(8,128)(2,1)S(1)} custom-call(bf16[768,128]{1,0:T(8,128)(2,1)S(1)} %get-tuple-element.7.refs_2_.refs_0_, bf16[768,128]{1,0:T(8,128)(2,1)S(1)} %collective-permute-done.refs_3_.refs_1_, bf16[8,2,96,128]{3,2,1,0:T(8,128)(2,1)S(1)} %collective-permute-done.1.refs_2_, bf16[64,128]{1,0:T(8,128)(2,1)S(1)} %bitcast.18, ...), custom_call_target="tpu_custom_call" | custom-call | flops 1207959552 | bytes 2097152 | tf_op jit(solution)/shard_map/attend/pallas_call | solution.py:140
  93.8 1.2 collective-permute-done.6.there_ref
  95.0 0.1 combine.2
  95.1 1.9 %collective-permute-start.7 = (bf16[80,768]{1,0:T(8,128)(2,1)S(1)}, bf16[80,768]{1,0:T(8,128)(2,1)S(1)}, u32[]{:S(2)}, u32[]{:S(2)}) collective-permute-start(bf16[80,768]{1,0:T(8,128)(2,1)S(1)} %combine.2), channel_id=1, source_target_pairs={{0,8},{8,0},{128,136},{136,128},{256,264},{264,256},{384,392},{392... | collective-permute-start | bytes 368648 | tf_op jit(solution)/shard_map/combine/ppermute | solution.py:41
  97.1 3.7 %collective-permute-done.7.beside_ref = bf16[80,768]{1,0:T(8,128)(2,1)S(1)} collective-permute-done((bf16[80,768]{1,0:T(8,128)(2,1)S(1)}, bf16[80,768]{1,0:T(8,128)(2,1)S(1)}, u32[]{:S(2)}, u32[]{:S(2)}) %collective-permute-start.7) | collective-permute-done | bytes 122912 | tf_op jit(solution)/shard_map/combine/ppermute | solution.py:41
  100.8 0.3 combine.3
  101.1 22.4 %all_to_all.11 = bf16[16,48,128]{2,1,0:T(8,128)(2,1)S(1)} all-to-all(bf16[16,48,128]{2,1,0:T(8,128)(2,1)S(1)} %bitcast.15), channel_id=1, replica_groups={{0,2,16,18,32,34,48,50,72,74,88,90,104,106,120,122},{8,10,24,26,40,42,5..., dimensions={0} | all-to-all | bytes 393216 | tf_op jit(solution)/shard_map/to_tokens/all_to_all | solution.py:37
  123.5 9.3 %all-gather = f32[96,128]{1,0:T(8,128)S(1)} all-gather(f32[48,128]{1,0:T(8,128)S(1)} %convert_reduce_fusion), channel_id=2, replica_groups=mesh['y'=4,'zh'=8,'z0'=2,'xl'=2,'xh'=2,'c'=2] {'c'}, dimensions={0}, use_global_device_ids=true | all-gather | bytes 73728 | tf_op jit(solution)/shard_map/to_tokens/all_gather | solution.py:247
  132.8 0.1 reshape.18
  132.9 0.7 copy.15
  (8 shorter events, 0.2 us)
Async XLA Ops:
  49.6 16.1 %copy-start = (bf16[640,64]{0,1:T(8,128)(2,1)S(1)}, bf16[640,64]{0,1:T(8,128)(2,1)}, u32[]{:S(2)}) copy-start(bf16[640,64]{0,1:T(8,128)(2,1)} %param.14) | copy-start | bytes 245764
  49.6 16.1 %copy-start.1 = (bf16[384,64]{0,1:T(8,128)(2,1)S(1)}, bf16[384,64]{0,1:T(8,128)(2,1)}, u32[]{:S(2)}) copy-start(bf16[384,64]{0,1:T(8,128)(2,1)} %param.15) | copy-start | bytes 147460
  49.7 20.4 %collective-permute-start.5 = (bf16[8,2,96,128]{3,2,1,0:T(8,128)(2,1)S(1)}, bf16[8,2,96,128]{3,2,1,0:T(8,128)(2,1)S(1)}, u32[]{:S(2)}, u32[]{:S(2)}) collective-permute-start(bf16[8,2,96,128]{3,2,1,0:T(8,128)(2,1)S(1)} %get-tuple-element.8.refs_4_), channel_id=1, source_target_pairs={{0,128},{4,132},{128,0},{132,4},{256,384},{260,388},{384,256},{388... | collective-permute-start | bytes 1179656 | tf_op jit(solution)/shard_map/gather/ppermute | solution.py:41
  53.0 17.1 %collective-permute-start.4 = (bf16[8,2,96,128]{3,2,1,0:T(8,128)(2,1)S(1)}, bf16[8,2,96,128]{3,2,1,0:T(8,128)(2,1)S(1)}, u32[]{:S(2)}, u32[]{:S(2)}) collective-permute-start(bf16[8,2,96,128]{3,2,1,0:T(8,128)(2,1)S(1)} %get-tuple-element.8.refs_4_), channel_id=1, source_target_pairs={{0,4},{4,0},{128,132},{132,128},{256,260},{260,256},{384,388},{388... | collective-permute-start | bytes 1179656 | tf_op jit(solution)/shard_map/gather/ppermute | solution.py:41
  56.2 9.7 %collective-permute-start.3 = (bf16[768,128]{1,0:T(8,128)(2,1)S(1)}, bf16[768,128]{1,0:T(8,128)(2,1)S(1)}, u32[]{:S(2)}, u32[]{:S(2)}) collective-permute-start(bf16[768,128]{1,0:T(8,128)(2,1)S(1)} %get-tuple-element.7.refs_2_.refs_0_), channel_id=1, source_target_pairs={{0,392},{8,384},{128,264},{136,256},{256,136},{264,128},{384,8},{3... | collective-permute-start | bytes 589832 | tf_op jit(solution)/shard_map/gather/ppermute | solution.py:41
  60.0 9.7 %collective-permute-start.2 = (bf16[768,128]{1,0:T(8,128)(2,1)S(1)}, bf16[768,128]{1,0:T(8,128)(2,1)S(1)}, u32[]{:S(2)}, u32[]{:S(2)}) collective-permute-start(bf16[768,128]{1,0:T(8,128)(2,1)S(1)} %get-tuple-element.7.refs_2_.refs_0_), channel_id=1, source_target_pairs={{0,384},{8,392},{128,256},{136,264},{256,128},{264,136},{384,0},{3... | collective-permute-start | bytes 589832 | tf_op jit(solution)/shard_map/gather/ppermute | solution.py:41
  62.7 7.4 %collective-permute-start = (bf16[768,128]{1,0:T(8,128)(2,1)S(1)}, bf16[768,128]{1,0:T(8,128)(2,1)S(1)}, u32[]{:S(2)}, u32[]{:S(2)}) collective-permute-start(bf16[768,128]{1,0:T(8,128)(2,1)S(1)} %get-tuple-element.7.refs_2_.refs_0_), channel_id=1, source_target_pairs={{0,8},{8,0},{128,136},{136,128},{256,264},{264,256},{384,392},{392... | collective-permute-start | bytes 589832 | tf_op jit(solution)/shard_map/gather/ppermute | solution.py:41
  65.9 13.7 %collective-permute-start.1 = (bf16[8,2,96,128]{3,2,1,0:T(8,128)(2,1)S(1)}, bf16[8,2,96,128]{3,2,1,0:T(8,128)(2,1)S(1)}, u32[]{:S(2)}, u32[]{:S(2)}) collective-permute-start(bf16[8,2,96,128]{3,2,1,0:T(8,128)(2,1)S(1)} %get-tuple-element.8.refs_4_), channel_id=1, source_target_pairs={{0,132},{4,128},{128,4},{132,0},{256,388},{260,384},{384,260},{388... | collective-permute-start | bytes 1179656 | tf_op jit(solution)/shard_map/gather/ppermute | solution.py:41
  82.0 13.1 %collective-permute-start.6 = (bf16[2,80,768]{2,1,0:T(8,128)(2,1)S(1)}, bf16[2,80,768]{2,1,0:T(8,128)(2,1)S(1)}, u32[]{:S(2)}, u32[]{:S(2)}) collective-permute-start(bf16[2,80,768]{2,1,0:T(8,128)(2,1)S(1)} %attend.5), channel_id=1, source_target_pairs={{0,384},{8,392},{128,256},{136,264},{256,128},{264,136},{384,0},{3... | collective-permute-start | bytes 737288 | tf_op jit(solution)/shard_map/attend/ppermute | solution.py:41
  95.1 5.7 %collective-permute-start.7 = (bf16[80,768]{1,0:T(8,128)(2,1)S(1)}, bf16[80,768]{1,0:T(8,128)(2,1)S(1)}, u32[]{:S(2)}, u32[]{:S(2)}) collective-permute-start(bf16[80,768]{1,0:T(8,128)(2,1)S(1)} %combine.2), channel_id=1, source_target_pairs={{0,8},{8,0},{128,136},{136,128},{256,264},{264,256},{384,392},{392... | collective-permute-start | bytes 368648 | tf_op jit(solution)/shard_map/combine/ppermute | solution.py:41

commit v9 on v7

--- a/solution.py
+++ b/solution.py
@@ -24,10 +24,10 @@
 GRP = ("xh", "c")
 Z = ("zh", "z0")
 PLANE_SETS = ([0, 2, 4, 6, 9, 11, 13, 15], [1, 3, 5, 7, 8, 10, 12, 14])
-QUERY_AXES = ("y", "z0")
-Z0_STEP, Y_STEP = 1, 6
-KEY_AXES = ("y", "xl")
-KEY_SETS = ([0, 1, 2, 3], [4, 5, 6, 7])
+QUERY_AXES = ("y", "xl")
+X_STEP, Y_STEP = 1, 2
+KEY_AXES = ("y", "z0")
+KEY_SETS = ([0, 1, 6, 7], [2, 3, 4, 5])
 SIDES = 2
 PLANE_AXES = Z + ("xh",)
 SIDE_SETS = [[SIDES * z + x for z in planes for x in range(SIDES)] for planes in PLANE_SETS]
@@ -200,8 +200,8 @@
             compiler_params=SMALL,
         )(arrived)
         key_values = exchange(copies.reshape((-1,) + copies.shape[2:]), KEY_AXES, KEY_SETS)
-        beside = from_partner(q, Z0_STEP)
-        across = [from_partner(q, Y_STEP), from_partner(q, Y_STEP ^ Z0_STEP)]
+        beside = from_partner(q, X_STEP)
+        across = [from_partner(q, Y_STEP), from_partner(q, Y_STEP ^ X_STEP)]
     with jax.named_scope("attend"):
         there = from_partner(attend(across, key_values, map_t), Y_STEP)
         here = attend([q, beside], key_values, map_t)
@@ -219,7 +219,7 @@
             out_specs=VMEM,
             out_shape=jax.ShapeDtypeStruct((heads, SIDES, tokens_here // 2, 2 * CH), BF16),
             compiler_params=SMALL,
-        )(gain, here, there, from_partner(share, Z0_STEP))
+        )(gain, here, there, from_partner(share, X_STEP))
     with jax.named_scope("to_tokens"):
         velocity = velocity.reshape((heads * SIDES,) + velocity.shape[2:])
         velocity = exchange(velocity, PLANE_AXES, SIDE_SETS)

time: 132 us -> 130 us (0.985)
  blocking collectives: 76.2 us -> 73.7 us
  starting transfers between devices: 26.6 us -> 25.1 us
  waiting for transfers between devices: 12.1 us -> 13.6 us
    all_to_all x1, waiting for transfers between devices: 4.49 us -> 6.82 us  [exchange(): return lax.all_to_all(x, axes, 0, 0, tiled=True, axis_index_groups=sets)]
    ppermute x5, starting transfers between devices: 22.9 us -> 20.9 us  [from_partner(): return lax.ppermute(x, QUERY_AXES, [(i, i ^ step) for i in range(size)])]
    all_to_all x2, blocking collectives: 71.1 us -> 69.4 us  [exchange(): return lax.all_to_all(x, axes, 0, 0, tiled=True, axis_index_groups=sets)]
where the time goes in v9:
time: 130 us; the launch traced here: 129 us
  blocking collectives  73.7 us (57%)
  starting transfers between devices  25.1 us (19%)
  Pallas kernels  15.7 us (12%)
  waiting for transfers between devices  13.6 us (10%)
    all_to_all x2, blocking collectives, exchange(): return lax.all_to_all(x, axes, 0, 0, tiled=True, axis_index_groups=sets)  69.4 us
    ppermute x5, starting transfers between devices, from_partner(): return lax.ppermute(x, QUERY_AXES, [(i, i ^ step) for i in range(size)])  20.9 us
    pallas_call x2, Pallas kernels, attend(): pl.pallas_call(attend_kernel, in_specs=[VMEM] * (2 + blocks), out_specs=V...  12 us
    all_to_all x1, waiting for transfers between devices, exchange(): return lax.all_to_all(x, axes, 0, 0, tiled=True, axis_index_groups=sets)  6.82 us
    ppermute x5, waiting for transfers between devices, from_partner(): return lax.ppermute(x, QUERY_AXES, [(i, i ^ step) for i in range(size)])  6.82 us
    all_gather x1, blocking collectives, body(): velocity = jnp.sum(lax.all_gather(velocity, 'c', axis=0), axis=0)  4.38 us
    all_to_all x1, starting transfers between devices, exchange(): return lax.all_to_all(x, axes, 0, 0, tiled=True, axis_index_groups=sets)  4.21 us
  transfers between devices with their start and end apart: 6, of which 3 were waited for; matrix products, arithmetic and copies ran while one was open for 0% of the time, Pallas kernels for 9%

profile of v9, /device:TPU:1, one launch (start us, length us, event | category | flops | bytes accessed | tf_op | source)
XLA Modules:
  0.0 129.3 jit_solution(18249714856796896544)
XLA Ops:
  0.0 2.1 %pack.1 = bf16[8,3,96,128]{3,2,1,0:T(8,128)(2,1)} custom-call(bf16[96,640]{1,0:T(8,128)(2,1)} %qm.1, bf16[96,640]{1,0:T(8,128)(2,1)} %km.1, bf16[96,640]{1,0:T(8,128)(2,1)} %vm.1, bf16[96,384]{1,0:T(8,128)(2,1)} %qg.1, bf16[96,384]{1,0:T(8,128)(2,1)} %kg.1, bf16[96,384]{1,0:T(8,128)(2,1)} %vg.1), custom_call_target="tpu_custom_call" | custom-call | tf_op jit(solution)/shard_map/pack/pallas_call | solution.py:182
  2.1 47.6 %all_to_all.15.in_ref = bf16[8,3,96,128]{3,2,1,0:T(8,128)(2,1)S(1)} all-to-all(bf16[8,3,96,128]{3,2,1,0:T(8,128)(2,1)} %pack.1), channel_id=1, replica_groups={{0,16,32,48,72,88,104,120},{8,24,40,56,64,80,96,112},{1,17,33,49,73,89,..., dimensions={0} | all-to-all | bytes 1179648 | tf_op jit(solution)/shard_map/to_heads/all_to_all | solution.py:37
  49.6 1.4 %gather.1 = (bf16[768,128]{1,0:T(8,128)(2,1)S(1)}, bf16[4,8,2,96,128]{4,3,2,1,0:T(8,128)(2,1)}) custom-call(bf16[8,3,96,128]{3,2,1,0:T(8,128)(2,1)S(1)} %all_to_all.15.in_ref), custom_call_target="tpu_custom_call" | custom-call | tf_op jit(solution)/shard_map/gather/pallas_call | solution.py:192
  51.0 0.0 copy-start
  51.0 0.0 copy-start.1
  51.0 4.2 %all-to-all-start.1 = ((bf16[32,2,96,128]{3,2,1,0:T(8,128)(2,1)}), bf16[32,2,96,128]{3,2,1,0:T(8,128)(2,1)S(1)}, u32[]{:S(2)}, u32[]{:S(2)}) async-start(bf16[32,2,96,128]{3,2,1,0:T(8,128)(2,1)} %bitcast.1), calls=%async_computation.1 | async-start | bytes 3145728 | tf_op jit(solution)/shard_map/gather/all_to_all | solution.py:37
  55.2 3.6 %collective-permute-start.2 = (bf16[768,128]{1,0:T(8,128)(2,1)S(1)}, bf16[768,128]{1,0:T(8,128)(2,1)S(1)}, u32[]{:S(2)}, u32[]{:S(2)}) collective-permute-start(bf16[768,128]{1,0:T(8,128)(2,1)S(1)} %get-tuple-element.7.refs_0_), channel_id=1, source_target_pairs={{0,132},{4,128},{128,4},{132,0},{256,388},{260,384},{384,260},{388... | collective-permute-start | bytes 589832 | tf_op jit(solution)/shard_map/gather/ppermute | solution.py:42
  58.9 2.6 %collective-permute-start.1 = (bf16[768,128]{1,0:T(8,128)(2,1)S(1)}, bf16[768,128]{1,0:T(8,128)(2,1)S(1)}, u32[]{:S(2)}, u32[]{:S(2)}) collective-permute-start(bf16[768,128]{1,0:T(8,128)(2,1)S(1)} %get-tuple-element.7.refs_0_), channel_id=1, source_target_pairs={{0,128},{4,132},{128,0},{132,4},{256,384},{260,388},{384,256},{388... | collective-permute-start | bytes 589832 | tf_op jit(solution)/shard_map/gather/ppermute | solution.py:42
  61.4 0.0 copy-done
  61.5 0.0 copy-done.1
  61.6 2.2 %collective-permute-start = (bf16[768,128]{1,0:T(8,128)(2,1)S(1)}, bf16[768,128]{1,0:T(8,128)(2,1)S(1)}, u32[]{:S(2)}, u32[]{:S(2)}) collective-permute-start(bf16[768,128]{1,0:T(8,128)(2,1)S(1)} %get-tuple-element.7.refs_0_), channel_id=1, source_target_pairs={{0,4},{4,0},{128,132},{132,128},{256,260},{260,256},{384,388},{388... | collective-permute-start | bytes 589832 | tf_op jit(solution)/shard_map/gather/ppermute | solution.py:42
  63.8 0.0 collective-permute-done.2.refs_1_
  63.8 4.6 %collective-permute-done.1.refs_0_ = bf16[768,128]{1,0:T(8,128)(2,1)S(1)} collective-permute-done((bf16[768,128]{1,0:T(8,128)(2,1)S(1)}, bf16[768,128]{1,0:T(8,128)(2,1)S(1)}, u32[]{:S(2)}, u32[]{:S(2)}) %collective-permute-start.1) | collective-permute-done | bytes 196640 | tf_op jit(solution)/shard_map/gather/ppermute | solution.py:42
  68.3 6.8 %all-to-all-done.1.refs_2_ = bf16[32,2,96,128]{3,2,1,0:T(8,128)(2,1)S(1)} async-done(((bf16[32,2,96,128]{3,2,1,0:T(8,128)(2,1)}), bf16[32,2,96,128]{3,2,1,0:T(8,128)(2,1)S(1)}, u32[]{:S(2)}, u32[]{:S(2)}) %all-to-all-start.1) | async-done | bytes 1572896 | tf_op jit(solution)/shard_map/gather/all_to_all | solution.py:37
  75.1 6.0 %attend.3 = bf16[2,80,768]{2,1,0:T(8,128)(2,1)S(1)} custom-call(bf16[768,128]{1,0:T(8,128)(2,1)S(1)} %collective-permute-done.1.refs_0_, bf16[768,128]{1,0:T(8,128)(2,1)S(1)} %collective-permute-done.2.refs_1_, bf16[32,2,96,128]{3,2,1,0:T(8,128)(2,1)S(1)} %all-to-all-done.1.refs_2_, bf16[64,128]{1,0:T(8,128)(2,1)S(1)} %bitcast.17), custom_call_target="tpu_custom_call" | custom-call | flops 4831838208 | bytes 2097152 | tf_op jit(solution)/shard_map/attend/pallas_call | solution.py:125
  81.1 1.9 %collective-permute-start.3 = (bf16[2,80,768]{2,1,0:T(8,128)(2,1)S(1)}, bf16[2,80,768]{2,1,0:T(8,128)(2,1)S(1)}, u32[]{:S(2)}, u32[]{:S(2)}) collective-permute-start(bf16[2,80,768]{2,1,0:T(8,128)(2,1)S(1)} %attend.3), channel_id=1, source_target_pairs={{0,128},{4,132},{128,0},{132,4},{256,384},{260,388},{384,256},{388... | collective-permute-start | bytes 737288 | tf_op jit(solution)/shard_map/attend/ppermute | solution.py:42
  83.0 0.0 collective-permute-done.refs_1_
  83.1 6.0 %attend.2.here_ref = bf16[2,80,768]{2,1,0:T(8,128)(2,1)S(1)} custom-call(bf16[768,128]{1,0:T(8,128)(2,1)S(1)} %get-tuple-element.7.refs_0_, bf16[768,128]{1,0:T(8,128)(2,1)S(1)} %collective-permute-done.refs_1_, bf16[32,2,96,128]{3,2,1,0:T(8,128)(2,1)S(1)} %all-to-all-done.1.refs_2_, bf16[64,128]{1,0:T(8,128)(2,1)S(1)} %bitcast.18), custom_call_target="tpu_custom_call" | custom-call | flops 4831838208 | bytes 2097152 | tf_op jit(solution)/shard_map/attend/pallas_call | solution.py:125
  89.0 0.0 collective-permute-done.3.there_ref
  89.0 0.1 combine.2
  89.1 10.7 %collective-permute-start.4 = (bf16[80,768]{1,0:T(8,128)(2,1)S(1)}, bf16[80,768]{1,0:T(8,128)(2,1)S(1)}, u32[]{:S(2)}, u32[]{:S(2)}) collective-permute-start(bf16[80,768]{1,0:T(8,128)(2,1)S(1)} %combine.2), channel_id=1, source_target_pairs={{0,4},{4,0},{128,132},{132,128},{256,260},{260,256},{384,388},{388... | collective-permute-start | bytes 368648 | tf_op jit(solution)/shard_map/combine/ppermute | solution.py:42
  99.8 2.2 %collective-permute-done.4.beside_ref = bf16[80,768]{1,0:T(8,128)(2,1)S(1)} collective-permute-done((bf16[80,768]{1,0:T(8,128)(2,1)S(1)}, bf16[80,768]{1,0:T(8,128)(2,1)S(1)}, u32[]{:S(2)}, u32[]{:S(2)}) %collective-permute-start.4) | collective-permute-done | bytes 122912 | tf_op jit(solution)/shard_map/combine/ppermute | solution.py:42
  102.0 0.3 combine.3
  102.3 21.8 %all_to_all.16 = bf16[16,48,128]{2,1,0:T(8,128)(2,1)S(1)} all-to-all(bf16[16,48,128]{2,1,0:T(8,128)(2,1)S(1)} %bitcast.16), channel_id=1, replica_groups={{0,2,16,18,32,34,48,50,72,74,88,90,104,106,120,122},{8,10,24,26,40,42,5..., dimensions={0} | all-to-all | bytes 393216 | tf_op jit(solution)/shard_map/to_tokens/all_to_all | solution.py:37
  124.1 4.4 %all-gather = f32[96,128]{1,0:T(8,128)S(1)} all-gather(f32[48,128]{1,0:T(8,128)S(1)} %convert_reduce_fusion), channel_id=2, replica_groups=mesh['y'=4,'zh'=8,'z0'=2,'xl'=2,'xh'=2,'c'=2] {'c'}, dimensions={0}, use_global_device_ids=true | all-gather | bytes 73728 | tf_op jit(solution)/shard_map/to_tokens/all_gather | solution.py:227
  128.5 0.1 reshape.22
  128.6 0.7 copy.15
  (7 shorter events, 0.1 us)
Async XLA Ops:
  51.0 10.4 %copy-start = (bf16[640,64]{0,1:T(8,128)(2,1)S(1)}, bf16[640,64]{0,1:T(8,128)(2,1)}, u32[]{:S(2)}) copy-start(bf16[640,64]{0,1:T(8,128)(2,1)} %param.14) | copy-start | bytes 245764
  51.0 10.4 %copy-start.1 = (bf16[384,64]{0,1:T(8,128)(2,1)S(1)}, bf16[384,64]{0,1:T(8,128)(2,1)}, u32[]{:S(2)}) copy-start(bf16[384,64]{0,1:T(8,128)(2,1)} %param.15) | copy-start | bytes 147460
  51.0 24.1 %all-to-all-start.1 = ((bf16[32,2,96,128]{3,2,1,0:T(8,128)(2,1)}), bf16[32,2,96,128]{3,2,1,0:T(8,128)(2,1)S(1)}, u32[]{:S(2)}, u32[]{:S(2)}) async-start(bf16[32,2,96,128]{3,2,1,0:T(8,128)(2,1)} %bitcast.1), calls=%async_computation.1 | async-start | bytes 3145728 | tf_op jit(solution)/shard_map/gather/all_to_all | solution.py:37
  55.2 8.5 %collective-permute-start.2 = (bf16[768,128]{1,0:T(8,128)(2,1)S(1)}, bf16[768,128]{1,0:T(8,128)(2,1)S(1)}, u32[]{:S(2)}, u32[]{:S(2)}) collective-permute-start(bf16[768,128]{1,0:T(8,128)(2,1)S(1)} %get-tuple-element.7.refs_0_), channel_id=1, source_target_pairs={{0,132},{4,128},{128,4},{132,0},{256,388},{260,384},{384,260},{388... | collective-permute-start | bytes 589832 | tf_op jit(solution)/shard_map/gather/ppermute | solution.py:42
  58.9 9.5 %collective-permute-start.1 = (bf16[768,128]{1,0:T(8,128)(2,1)S(1)}, bf16[768,128]{1,0:T(8,128)(2,1)S(1)}, u32[]{:S(2)}, u32[]{:S(2)}) collective-permute-start(bf16[768,128]{1,0:T(8,128)(2,1)S(1)} %get-tuple-element.7.refs_0_), channel_id=1, source_target_pairs={{0,128},{4,132},{128,0},{132,4},{256,384},{260,388},{384,256},{388... | collective-permute-start | bytes 589832 | tf_op jit(solution)/shard_map/gather/ppermute | solution.py:42
  61.6 21.5 %collective-permute-start = (bf16[768,128]{1,0:T(8,128)(2,1)S(1)}, bf16[768,128]{1,0:T(8,128)(2,1)S(1)}, u32[]{:S(2)}, u32[]{:S(2)}) collective-permute-start(bf16[768,128]{1,0:T(8,128)(2,1)S(1)} %get-tuple-element.7.refs_0_), channel_id=1, source_target_pairs={{0,4},{4,0},{128,132},{132,128},{256,260},{260,256},{384,388},{388... | collective-permute-start | bytes 589832 | tf_op jit(solution)/shard_map/gather/ppermute | solution.py:42
  81.1 7.9 %collective-permute-start.3 = (bf16[2,80,768]{2,1,0:T(8,128)(2,1)S(1)}, bf16[2,80,768]{2,1,0:T(8,128)(2,1)S(1)}, u32[]{:S(2)}, u32[]{:S(2)}) collective-permute-start(bf16[2,80,768]{2,1,0:T(8,128)(2,1)S(1)} %attend.3), channel_id=1, source_target_pairs={{0,128},{4,132},{128,0},{132,4},{256,384},{260,388},{384,256},{388... | collective-permute-start | bytes 737288 | tf_op jit(solution)/shard_map/attend/ppermute | solution.py:42
  89.1 12.9 %collective-permute-start.4 = (bf16[80,768]{1,0:T(8,128)(2,1)S(1)}, bf16[80,768]{1,0:T(8,128)(2,1)S(1)}, u32[]{:S(2)}, u32[]{:S(2)}) collective-permute-start(bf16[80,768]{1,0:T(8,128)(2,1)S(1)} %combine.2), channel_id=1, source_target_pairs={{0,4},{4,0},{128,132},{132,128},{256,260},{260,256},{384,388},{388... | collective-permute-start | bytes 368648 | tf_op jit(solution)/shard_map/combine/ppermute | solution.py:42

commit v10 on v8

--- a/solution.py
+++ b/solution.py
@@ -27,7 +27,7 @@
 QUERY_AXES = ("y", "z0")
 Z0_STEP, Y_STEP = 1, 6
 KEY_AXES = ("y", "xl")
-NEAR_STEPS, FAR_STEP = (1, 2), 3
+KEY_SETS = ([0, 1, 2, 3], [4, 5, 6, 7])
 SIDES = 2
 PLANE_AXES = Z + ("xh",)
 SIDE_SETS = [[SIDES * z + x for z in planes for x in range(SIDES)] for planes in PLANE_SETS]
@@ -37,8 +37,9 @@
     return lax.all_to_all(x, axes, 0, 0, tiled=True, axis_index_groups=sets)
 
 
-def from_partner(x, step, axes=QUERY_AXES):
-    return lax.ppermute(x, axes, [(i, i ^ step) for i in range(lax.axis_size(axes))])
+def from_partner(x, step):
+    size = lax.axis_size(QUERY_AXES)
+    return lax.ppermute(x, QUERY_AXES, [(i, i ^ step) for i in range(size)])
 
 
 def dot_t(a, b):
@@ -52,11 +53,12 @@
             out_ref[h, t] = ref[:, at : at + HD]
 
 
-def copy_kernel(in_ref, q_ref, kv_ref):
+def copy_kernel(in_ref, q_ref, copies_ref):
     heads, _, tokens, _ = in_ref.shape
     for h in range(heads):
         q_ref[h * tokens : (h + 1) * tokens, :] = in_ref[h, 0]
-        kv_ref[h] = in_ref[h, 1:]
+        for copy in range(copies_ref.shape[0]):
+            copies_ref[copy, h] = in_ref[h, 1:]
 
 
 def split_two(x):
@@ -70,16 +72,25 @@
     return jnp.concatenate((velocity,) + tail + (filler,), axis=0).astype(dtype)
 
 
-def attend_kernel(count, pieces, first_before, *refs):
-    q_refs, kv_refs, map_ref, refs = refs[:count], refs[count:pieces], refs[pieces], refs[pieces + 1 :]
-    before_ref, refs = (None, refs) if first_before is None else (refs[0], refs[1:])
-    out_ref, staged_ref, sums_ref = refs
+def attend_kernel(count, first_before, *refs):
+    q_refs, refs = refs[:count], refs[count:]
+    if first_before is None:
+        arrived_ref, map_ref, out_ref, staged_ref, sums_ref = refs
+        before_ref = None
+    else:
+        own_ref, kv_ref, map_ref, before_ref, out_ref, staged_ref, sums_ref = refs
     rows = out_ref.shape[2]
     for k, q_ref in enumerate(q_refs):
         staged_ref[k] = q_ref[...]
 
     def all_pieces(which):
-        return jnp.concatenate([ref[:, which].reshape(-1, HD) for ref in kv_refs], axis=0)
+        if first_before is None:
+            return arrived_ref[:, 1 + which].reshape(-1, HD)
+        blocks = len(KEY_SETS[0])
+        size = kv_ref.shape[0] // blocks
+        starts = [(own_ref[0] ^ i) * size for i in range(1, blocks)]
+        pieces = [kv_ref[pl.ds(start, size), which].reshape(-1, HD) for start in starts]
+        return jnp.concatenate(pieces, axis=0)
 
     def weighted(queries, shift):
         scores = dot_t(queries, all_pieces(0)) * SCALE
@@ -130,18 +141,21 @@
                 emit(k, at, weighted(queries, shift), shift)
 
 
-def attend(queries, key_values, map_t, before=None, first_before=None):
+def attend(queries, keys_in, map_t, first_before=None):
     rows = queries[0].shape[0]
-    keys = key_values[0].shape[0] * key_values[0].shape[2] * len(key_values)
     blocks = len(queries)
-    pieces = blocks + len(key_values)
-    operands = [*queries, *key_values, map_t] + ([] if before is None else [before])
-    out = (blocks, CH + 8, rows) if before is None else (blocks, MESSAGE_ROWS, rows)
+    last = first_before is not None
+    keys = rows * (len(KEY_SETS[0]) - 1 if last else 1)
+    operands = [*queries, *keys_in[:2], map_t, *keys_in[2:]]
+    specs = [VMEM] * len(operands)
+    if last:
+        specs[blocks] = SMEM
+    out = (blocks, MESSAGE_ROWS, rows) if last else (blocks, CH + 8, rows)
     return pl.pallas_call(
-        functools.partial(attend_kernel, blocks, pieces, first_before),
-        in_specs=[VMEM] * len(operands),
+        functools.partial(attend_kernel, blocks, first_before),
+        in_specs=specs,
         out_specs=VMEM,
-        out_shape=jax.ShapeDtypeStruct(out, F32 if before is None else BF16),
+        out_shape=jax.ShapeDtypeStruct(out, BF16 if last else F32),
         scratch_shapes=[pltpu.VMEM((blocks, rows, HD), BF16), pltpu.VMEM((rows, HD), F32)],
         compiler_params=pltpu.CompilerParams(vmem_limit_bytes=40 << 20),
         cost_estimate=pl.CostEstimate(
@@ -207,24 +221,26 @@
     with jax.named_scope("to_heads"):
         arrived = exchange(packed, Z, PLANE_SETS)
     with jax.named_scope("gather"):
-        q, kv = pl.pallas_call(
+        copies = (len(KEY_SETS[0]), heads, 2, tokens_here, HD)
+        q, copies = pl.pallas_call(
             copy_kernel,
             in_specs=[VMEM],
             out_specs=[VMEM] * 2,
             out_shape=[
                 jax.ShapeDtypeStruct((heads * tokens_here, HD), BF16),
-                jax.ShapeDtypeStruct((heads, 2, tokens_here, HD), BF16),
+                jax.ShapeDtypeStruct(copies, BF16),
             ],
             compiler_params=SMALL,
         )(arrived)
-        near = [kv] + [from_partner(kv, step, KEY_AXES) for step in NEAR_STEPS]
-        far = [from_partner(kv, FAR_STEP, KEY_AXES)]
+        key_values = exchange(copies.reshape((-1,) + copies.shape[2:]), KEY_AXES, KEY_SETS)
         beside = from_partner(q, Z0_STEP)
         across = [from_partner(q, Y_STEP), from_partner(q, Y_STEP ^ Z0_STEP)]
     with jax.named_scope("attend"):
-        before = attend(across + [q, beside], near, map_t)
-        there = from_partner(attend(across, far, map_t, before, 0), Y_STEP)
-        here = attend([q, beside], far, map_t, before, len(across))
+        before = attend(across + [q, beside], [arrived], map_t)
+        own = lax.axis_index(KEY_AXES).astype(jnp.int32) & 3
+        others = [own.reshape(1), key_values, before]
+        there = from_partner(attend(across, others, map_t, 0), Y_STEP)
+        here = attend([q, beside], others, map_t, len(across))
     with jax.named_scope("combine"):
         share = pl.pallas_call(
             add_kernel,

time: 134 us -> 134 us (level)
  starting transfers between devices: 29.4 us -> 25.3 us
  local copies, waits for them, and re-layouts: 0.87 us -> 4.09 us
  waiting for transfers between devices: 7.21 us -> 8.6 us
    ppermute x8 -> x5, starting transfers between devices: 29.4 us -> 21.6 us  [from_partner(): return lax.ppermute(x, QUERY_AXES, [(i, i ^ step) for i in range(size)])]
    all_to_all x0 -> x1, starting transfers between devices: none -> 3.69 us  [exchange(): return lax.all_to_all(x, axes, 0, 0, tiled=True, axis_index_groups=sets)]
    unnamed x6 -> x12, local copies, waits for them, and re-layouts: 0.03 us -> 3.25 us
    ppermute x8 -> x5, waiting for transfers between devices: 7.21 us -> 8.6 us  [from_partner(): return lax.ppermute(x, QUERY_AXES, [(i, i ^ step) for i in range(size)])]
  transfers between devices with their start and end apart: 8 -> 6, of which waited for: 4 -> 3; matrix products, arithmetic and copies ran while one was open for 0% -> 0% of each run, Pallas kernels for 9% -> 7%
where the time goes in v10:
time: 134 us
  blocking collectives  78.8 us (59%)
  starting transfers between devices  25.3 us (19%)
  Pallas kernels  16.8 us (13%)
  waiting for transfers between devices  8.6 us (6%)
  local copies, waits for them, and re-layouts  4.09 us (3%)
    all_to_all x2, blocking collectives, exchange(): return lax.all_to_all(x, axes, 0, 0, tiled=True, axis_index_groups=sets)  70.5 us
    ppermute x5, starting transfers between devices, from_partner(): return lax.ppermute(x, QUERY_AXES, [(i, i ^ step) for i in range(size)])  21.6 us
    pallas_call x3, Pallas kernels, attend(): pl.pallas_call(functools.partial(attend_kernel, blocks, first_before), in...  14.2 us
    ppermute x5, waiting for transfers between devices, from_partner(): return lax.ppermute(x, QUERY_AXES, [(i, i ^ step) for i in range(size)])  8.6 us
    all_gather x1, blocking collectives, body(): velocity = jnp.sum(lax.all_gather(velocity, 'c', axis=0), axis=0)  8.35 us
    all_to_all x1, starting transfers between devices, exchange(): return lax.all_to_all(x, axes, 0, 0, tiled=True, axis_index_groups=sets)  3.69 us
    unnamed x12, local copies, waits for them, and re-layouts  3.25 us
  transfers between devices with their start and end apart: 6, of which 3 were waited for; matrix products, arithmetic and copies ran while one was open for 0% of the time, Pallas kernels for 7%

profile of v10, /device:TPU:1, one launch (start us, length us, event | category | flops | bytes accessed | tf_op | source)
XLA Modules:
  0.0 133.9 jit_solution(9003606070348120654)
XLA Ops:
  0.0 2.0 %pack.1 = bf16[8,3,96,128]{3,2,1,0:T(8,128)(2,1)} custom-call(bf16[96,640]{1,0:T(8,128)(2,1)} %qm.1, bf16[96,640]{1,0:T(8,128)(2,1)} %km.1, bf16[96,640]{1,0:T(8,128)(2,1)} %vm.1, bf16[96,384]{1,0:T(8,128)(2,1)} %qg.1, bf16[96,384]{1,0:T(8,128)(2,1)} %kg.1, bf16[96,384]{1,0:T(8,128)(2,1)} %vg.1), custom_call_target="tpu_custom_call" | custom-call | tf_op jit(solution)/shard_map/pack/pallas_call | solution.py:215
  2.0 47.6 %all_to_all.15.in_ref.refs_4_ = bf16[8,3,96,128]{3,2,1,0:T(8,128)(2,1)S(1)} all-to-all(bf16[8,3,96,128]{3,2,1,0:T(8,128)(2,1)} %pack.1), channel_id=1, replica_groups={{0,16,32,48,72,88,104,120},{8,24,40,56,64,80,96,112},{1,17,33,49,73,89,..., dimensions={0} | all-to-all | bytes 1179648 | tf_op jit(solution)/shard_map/to_heads/all_to_all | solution.py:37
  49.6 0.2 gather.1
  49.8 0.0 copy-start
  49.8 1.1 copy-done
  51.0 0.0 copy-start.3
  51.0 0.0 copy-start.4
  51.0 3.7 %all-to-all-start.1 = ((bf16[32,2,96,128]{3,2,1,0:T(8,128)(2,1)}), bf16[32,2,96,128]{3,2,1,0:T(8,128)(2,1)S(1)}, u32[]{:S(2)}, u32[]{:S(2)}) async-start(bf16[32,2,96,128]{3,2,1,0:T(8,128)(2,1)} %bitcast.17), calls=%async_computation.1 | async-start | bytes 3145728 | tf_op jit(solution)/shard_map/gather/all_to_all | solution.py:37
  54.7 5.1 %collective-permute-start.2 = (bf16[768,128]{1,0:T(8,128)(2,1)S(1)}, bf16[768,128]{1,0:T(8,128)(2,1)S(1)}, u32[]{:S(2)}, u32[]{:S(2)}) collective-permute-start(bf16[768,128]{1,0:T(8,128)(2,1)S(1)} %get-tuple-element.7.refs_2_.refs_0_), channel_id=1, source_target_pairs={{0,392},{8,384},{128,264},{136,256},{256,136},{264,128},{384,8},{3... | collective-permute-start | bytes 589832 | tf_op jit(solution)/shard_map/gather/ppermute | solution.py:42
  59.8 1.9 %collective-permute-start.1 = (bf16[768,128]{1,0:T(8,128)(2,1)S(1)}, bf16[768,128]{1,0:T(8,128)(2,1)S(1)}, u32[]{:S(2)}, u32[]{:S(2)}) collective-permute-start(bf16[768,128]{1,0:T(8,128)(2,1)S(1)} %get-tuple-element.7.refs_2_.refs_0_), channel_id=1, source_target_pairs={{0,384},{8,392},{128,256},{136,264},{256,128},{264,136},{384,0},{3... | collective-permute-start | bytes 589832 | tf_op jit(solution)/shard_map/gather/ppermute | solution.py:42
  61.8 3.0 %collective-permute-start = (bf16[768,128]{1,0:T(8,128)(2,1)S(1)}, bf16[768,128]{1,0:T(8,128)(2,1)S(1)}, u32[]{:S(2)}, u32[]{:S(2)}) collective-permute-start(bf16[768,128]{1,0:T(8,128)(2,1)S(1)} %get-tuple-element.7.refs_2_.refs_0_), channel_id=1, source_target_pairs={{0,8},{8,0},{128,136},{136,128},{256,264},{264,256},{384,392},{392... | collective-permute-start | bytes 589832 | tf_op jit(solution)/shard_map/gather/ppermute | solution.py:42
  64.8 0.0 copy-done.3
  64.8 0.0 copy-done.4
  64.9 0.0 collective-permute-done.2.refs_1_
  64.9 3.9 %collective-permute-done.1.refs_0_ = bf16[768,128]{1,0:T(8,128)(2,1)S(1)} collective-permute-done((bf16[768,128]{1,0:T(8,128)(2,1)S(1)}, bf16[768,128]{1,0:T(8,128)(2,1)S(1)}, u32[]{:S(2)}, u32[]{:S(2)}) %collective-permute-start.1) | collective-permute-done | bytes 196640 | tf_op jit(solution)/shard_map/gather/ppermute | solution.py:42
  68.9 1.0 collective-permute-done.refs_3_.refs_1_
  69.8 4.6 %attend.3.refs_5_ = f32[4,72,768]{2,1,0:T(8,128)S(1)} custom-call(bf16[768,128]{1,0:T(8,128)(2,1)S(1)} %collective-permute-done.1.refs_0_, bf16[768,128]{1,0:T(8,128)(2,1)S(1)} %collective-permute-done.2.refs_1_, bf16[768,128]{1,0:T(8,128)(2,1)S(1)} %get-tuple-element.7.refs_2_.refs_0_, bf16[768,128]{1,0:T(8,128)(2,1)S(1)} %collective-permute-done.refs_3_.refs_1_, ...), custom_call_target="tpu_custom_call" | custom-call | flops 2415919104 | bytes 2097152 | tf_op jit(solution)/shard_map/attend/pallas_call | solution.py:154
  74.4 0.0 copy-start.1
  74.4 0.9 copy-done.1
  75.3 0.0 all-to-all-done.1.refs_3_
  75.4 0.0 copy-start.2
  75.4 1.2 copy-done.2
  76.5 4.8 %attend.5 = bf16[2,80,768]{2,1,0:T(8,128)(2,1)S(1)} custom-call(bf16[768,128]{1,0:T(8,128)(2,1)S(1)} %collective-permute-done.1.refs_0_, bf16[768,128]{1,0:T(8,128)(2,1)S(1)} %collective-permute-done.2.refs_1_, s32[1]{0:T(128)} %bitcast.1.refs_2_, bf16[32,2,96,128]{3,2,1,0:T(8,128)(2,1)S(1)} %all-to-all-done.1.refs_3_, bf16[64,128]{1,0:T(8,128)(2,1)S(1)} %bitcast.20, ...), custom_call_target="tpu_custom_call" | custom-call | flops 3623878656 | bytes 2097152 | tf_op jit(solution)/shard_map/attend/pallas_call | solution.py:154
  81.3 9.6 %collective-permute-start.3 = (bf16[2,80,768]{2,1,0:T(8,128)(2,1)S(1)}, bf16[2,80,768]{2,1,0:T(8,128)(2,1)S(1)}, u32[]{:S(2)}, u32[]{:S(2)}) collective-permute-start(bf16[2,80,768]{2,1,0:T(8,128)(2,1)S(1)} %attend.5), channel_id=1, source_target_pairs={{0,384},{8,392},{128,256},{136,264},{256,128},{264,136},{384,0},{3... | collective-permute-start | bytes 737288 | tf_op jit(solution)/shard_map/attend/ppermute | solution.py:42
  91.0 4.8 %attend.4.here_ref = bf16[2,80,768]{2,1,0:T(8,128)(2,1)S(1)} custom-call(bf16[768,128]{1,0:T(8,128)(2,1)S(1)} %get-tuple-element.7.refs_2_.refs_0_, bf16[768,128]{1,0:T(8,128)(2,1)S(1)} %collective-permute-done.refs_3_.refs_1_, s32[1]{0:T(128)} %bitcast.1.refs_2_, bf16[32,2,96,128]{3,2,1,0:T(8,128)(2,1)S(1)} %all-to-all-done.1.refs_3_, ...), custom_call_target="tpu_custom_call" | custom-call | flops 3623878656 | bytes 2097152 | tf_op jit(solution)/shard_map/attend/pallas_call | solution.py:154
  95.8 0.0 collective-permute-done.3.there_ref
  95.8 0.1 combine.2
  95.9 1.9 %collective-permute-start.4 = (bf16[80,768]{1,0:T(8,128)(2,1)S(1)}, bf16[80,768]{1,0:T(8,128)(2,1)S(1)}, u32[]{:S(2)}, u32[]{:S(2)}) collective-permute-start(bf16[80,768]{1,0:T(8,128)(2,1)S(1)} %combine.2), channel_id=1, source_target_pairs={{0,8},{8,0},{128,136},{136,128},{256,264},{264,256},{384,392},{392... | collective-permute-start | bytes 368648 | tf_op jit(solution)/shard_map/combine/ppermute | solution.py:42
  97.9 3.7 %collective-permute-done.4.beside_ref = bf16[80,768]{1,0:T(8,128)(2,1)S(1)} collective-permute-done((bf16[80,768]{1,0:T(8,128)(2,1)S(1)}, bf16[80,768]{1,0:T(8,128)(2,1)S(1)}, u32[]{:S(2)}, u32[]{:S(2)}) %collective-permute-start.4) | collective-permute-done | bytes 122912 | tf_op jit(solution)/shard_map/combine/ppermute | solution.py:42
  101.5 0.3 combine.3
  101.8 22.9 %all_to_all.16 = bf16[16,48,128]{2,1,0:T(8,128)(2,1)S(1)} all-to-all(bf16[16,48,128]{2,1,0:T(8,128)(2,1)S(1)} %bitcast.18), channel_id=1, replica_groups={{0,2,16,18,32,34,48,50,72,74,88,90,104,106,120,122},{8,10,24,26,40,42,5..., dimensions={0} | all-to-all | bytes 393216 | tf_op jit(solution)/shard_map/to_tokens/all_to_all | solution.py:37
  124.8 8.3 %all-gather = f32[96,128]{1,0:T(8,128)S(1)} all-gather(f32[48,128]{1,0:T(8,128)S(1)} %convert_reduce_fusion), channel_id=2, replica_groups=mesh['y'=4,'zh'=8,'z0'=2,'xl'=2,'xh'=2,'c'=2] {'c'}, dimensions={0}, use_global_device_ids=true | all-gather | bytes 73728 | tf_op jit(solution)/shard_map/to_tokens/all_gather | solution.py:263
  133.1 0.1 reshape.26
  133.2 0.7 copy.15
  (7 shorter events, 0.1 us)
Async XLA Ops:
  49.8 1.1 copy-start
  51.0 13.8 %copy-start.3 = (bf16[640,64]{0,1:T(8,128)(2,1)S(1)}, bf16[640,64]{0,1:T(8,128)(2,1)}, u32[]{:S(2)}) copy-start(bf16[640,64]{0,1:T(8,128)(2,1)} %param.14) | copy-start | bytes 245764
  51.0 13.8 %copy-start.4 = (bf16[384,64]{0,1:T(8,128)(2,1)S(1)}, bf16[384,64]{0,1:T(8,128)(2,1)}, u32[]{:S(2)}) copy-start(bf16[384,64]{0,1:T(8,128)(2,1)} %param.15) | copy-start | bytes 147460
  51.0 24.4 %all-to-all-start.1 = ((bf16[32,2,96,128]{3,2,1,0:T(8,128)(2,1)}), bf16[32,2,96,128]{3,2,1,0:T(8,128)(2,1)S(1)}, u32[]{:S(2)}, u32[]{:S(2)}) async-start(bf16[32,2,96,128]{3,2,1,0:T(8,128)(2,1)} %bitcast.17), calls=%async_computation.1 | async-start | bytes 3145728 | tf_op jit(solution)/shard_map/gather/all_to_all | solution.py:37
  54.7 10.2 %collective-permute-start.2 = (bf16[768,128]{1,0:T(8,128)(2,1)S(1)}, bf16[768,128]{1,0:T(8,128)(2,1)S(1)}, u32[]{:S(2)}, u32[]{:S(2)}) collective-permute-start(bf16[768,128]{1,0:T(8,128)(2,1)S(1)} %get-tuple-element.7.refs_2_.refs_0_), channel_id=1, source_target_pairs={{0,392},{8,384},{128,264},{136,256},{256,136},{264,128},{384,8},{3... | collective-permute-start | bytes 589832 | tf_op jit(solution)/shard_map/gather/ppermute | solution.py:42
  59.8 9.0 %collective-permute-start.1 = (bf16[768,128]{1,0:T(8,128)(2,1)S(1)}, bf16[768,128]{1,0:T(8,128)(2,1)S(1)}, u32[]{:S(2)}, u32[]{:S(2)}) collective-permute-start(bf16[768,128]{1,0:T(8,128)(2,1)S(1)} %get-tuple-element.7.refs_2_.refs_0_), channel_id=1, source_target_pairs={{0,384},{8,392},{128,256},{136,264},{256,128},{264,136},{384,0},{3... | collective-permute-start | bytes 589832 | tf_op jit(solution)/shard_map/gather/ppermute | solution.py:42
  61.8 8.1 %collective-permute-start = (bf16[768,128]{1,0:T(8,128)(2,1)S(1)}, bf16[768,128]{1,0:T(8,128)(2,1)S(1)}, u32[]{:S(2)}, u32[]{:S(2)}) collective-permute-start(bf16[768,128]{1,0:T(8,128)(2,1)S(1)} %get-tuple-element.7.refs_2_.refs_0_), channel_id=1, source_target_pairs={{0,8},{8,0},{128,136},{136,128},{256,264},{264,256},{384,392},{392... | collective-permute-start | bytes 589832 | tf_op jit(solution)/shard_map/gather/ppermute | solution.py:42
  74.4 0.9 copy-start.1
  75.4 1.2 copy-start.2
  81.3 14.5 %collective-permute-start.3 = (bf16[2,80,768]{2,1,0:T(8,128)(2,1)S(1)}, bf16[2,80,768]{2,1,0:T(8,128)(2,1)S(1)}, u32[]{:S(2)}, u32[]{:S(2)}) collective-permute-start(bf16[2,80,768]{2,1,0:T(8,128)(2,1)S(1)} %attend.5), channel_id=1, source_target_pairs={{0,384},{8,392},{128,256},{136,264},{256,128},{264,136},{384,0},{3... | collective-permute-start | bytes 737288 | tf_op jit(solution)/shard_map/attend/ppermute | solution.py:42
  95.9 5.6 %collective-permute-start.4 = (bf16[80,768]{1,0:T(8,128)(2,1)S(1)}, bf16[80,768]{1,0:T(8,128)(2,1)S(1)}, u32[]{:S(2)}, u32[]{:S(2)}) collective-permute-start(bf16[80,768]{1,0:T(8,128)(2,1)S(1)} %combine.2), channel_id=1, source_target_pairs={{0,8},{8,0},{128,136},{136,128},{256,264},{264,256},{384,392},{392... | collective-permute-start | bytes 368648 | tf_op jit(solution)/shard_map/combine/ppermute | solution.py:42

commit v11 on v7

--- a/solution.py
+++ b/solution.py
@@ -27,7 +27,7 @@
 QUERY_AXES = ("y", "z0")
 Z0_STEP, Y_STEP = 1, 6
 KEY_AXES = ("y", "xl")
-KEY_SETS = ([0, 1, 2, 3], [4, 5, 6, 7])
+KEY_STEPS = (1, 2, 3)
 SIDES = 2
 PLANE_AXES = Z + ("xh",)
 SIDE_SETS = [[SIDES * z + x for z in planes for x in range(SIDES)] for planes in PLANE_SETS]
@@ -37,9 +37,8 @@
     return lax.all_to_all(x, axes, 0, 0, tiled=True, axis_index_groups=sets)
 
 
-def from_partner(x, step):
-    size = lax.axis_size(QUERY_AXES)
-    return lax.ppermute(x, QUERY_AXES, [(i, i ^ step) for i in range(size)])
+def from_partner(x, step, axes=QUERY_AXES):
+    return lax.ppermute(x, axes, [(i, i ^ step) for i in range(lax.axis_size(axes))])
 
 
 def dot_t(a, b):
@@ -53,12 +52,11 @@
             out_ref[h, t] = ref[:, at : at + HD]
 
 
-def copy_kernel(in_ref, q_ref, copies_ref):
+def copy_kernel(in_ref, q_ref, kv_ref):
     heads, _, tokens, _ = in_ref.shape
     for h in range(heads):
         q_ref[h * tokens : (h + 1) * tokens, :] = in_ref[h, 0]
-        for copy in range(copies_ref.shape[0]):
-            copies_ref[copy, h] = in_ref[h, 1:]
+        kv_ref[h] = in_ref[h, 1:]
 
 
 def split_two(x):
@@ -66,14 +64,15 @@
     return high, x - high
 
 
-def attend_kernel(*refs):
-    *q_refs, kv_ref, map_ref, out_ref, staged_ref, sums_ref = refs
+def attend_kernel(count, *refs):
+    q_refs, refs = refs[:count], refs[count:]
+    *kv_refs, map_ref, out_ref, staged_ref, sums_ref = refs
     rows = out_ref.shape[2]
     for k, q_ref in enumerate(q_refs):
         staged_ref[k] = q_ref[...]
 
     def all_pieces(which):
-        return kv_ref[:, which].reshape(-1, HD)
+        return jnp.concatenate([ref[:, which].reshape(-1, HD) for ref in kv_refs], axis=0)
 
     def weighted(queries, shift):
         scores = dot_t(queries, all_pieces(0)) * SCALE
@@ -120,11 +119,11 @@
 
 def attend(queries, key_values, map_t):
     rows = queries[0].shape[0]
-    keys = key_values.shape[0] * key_values.shape[2]
+    keys = key_values[0].shape[0] * key_values[0].shape[2] * len(key_values)
     blocks = len(queries)
     return pl.pallas_call(
-        attend_kernel,
-        in_specs=[VMEM] * (2 + blocks),
+        functools.partial(attend_kernel, blocks),
+        in_specs=[VMEM] * (1 + blocks + len(key_values)),
         out_specs=VMEM,
         out_shape=jax.ShapeDtypeStruct((blocks, MESSAGE_ROWS, rows), BF16),
         scratch_shapes=[pltpu.VMEM((blocks, rows, HD), BF16), pltpu.VMEM((rows, HD), F32)],
@@ -134,7 +133,7 @@
             bytes_accessed=2 << 20,
             transcendentals=blocks * rows * keys,
         ),
-    )(*queries, key_values, map_t)
+    )(*queries, *key_values, map_t)
 
 
 def added(shares):
@@ -188,18 +187,17 @@
     with jax.named_scope("to_heads"):
         arrived = exchange(packed, Z, PLANE_SETS)
     with jax.named_scope("gather"):
-        copies = (len(KEY_SETS[0]), heads, 2, tokens_here, HD)
-        q, copies = pl.pallas_call(
+        q, kv = pl.pallas_call(
             copy_kernel,
             in_specs=[VMEM],
             out_specs=[VMEM] * 2,
             out_shape=[
                 jax.ShapeDtypeStruct((heads * tokens_here, HD), BF16),
-                jax.ShapeDtypeStruct(copies, BF16),
+                jax.ShapeDtypeStruct((heads, 2, tokens_here, HD), BF16),
             ],
             compiler_params=SMALL,
         )(arrived)
-        key_values = exchange(copies.reshape((-1,) + copies.shape[2:]), KEY_AXES, KEY_SETS)
+        key_values = [kv] + [from_partner(kv, step, KEY_AXES) for step in KEY_STEPS]
         beside = from_partner(q, Z0_STEP)
         across = [from_partner(q, Y_STEP), from_partner(q, Y_STEP ^ Z0_STEP)]
     with jax.named_scope("attend"):

time: 132 us -> 135 us (1.023)
  blocking collectives: 76.2 us -> 82 us
  waiting for transfers between devices: 12.1 us -> 7.94 us
  starting transfers between devices: 26.6 us -> 29.3 us
    ppermute x5 -> x8, starting transfers between devices: 22.9 us -> 29.3 us  [from_partner(): lax.ppermute(x, axes, [(i, i ^ step) for i in range(lax.axis_size(axes))])]
    all_gather x1, blocking collectives: 5.14 us -> 10.2 us  [body(): velocity = jnp.sum(lax.all_gather(velocity, 'c', axis=0), axis=0)]
    all_to_all x1 -> x0, waiting for transfers between devices: 4.49 us -> none  [exchange(): return lax.all_to_all(x, axes, 0, 0, tiled=True, axis_index_groups=sets)]
    all_to_all x1 -> x0, starting transfers between devices: 3.69 us -> none  [exchange(): return lax.all_to_all(x, axes, 0, 0, tiled=True, axis_index_groups=sets)]
    ppermute x5 -> x8, waiting for transfers between devices: 7.63 us -> 7.94 us  [from_partner(): lax.ppermute(x, axes, [(i, i ^ step) for i in range(lax.axis_size(axes))])]
  transfers between devices with their start and end apart: 6 -> 8, of which waited for: 3 -> 3; matrix products, arithmetic and copies ran while one was open for 0% -> 0% of each run, Pallas kernels for 9% -> 9%
where the time goes in v11:
time: 135 us
  blocking collectives  82 us (61%)
  starting transfers between devices  29.3 us (22%)
  Pallas kernels  14.4 us (11%)
  waiting for transfers between devices  7.94 us (6%)
    all_to_all x2, blocking collectives, exchange(): return lax.all_to_all(x, axes, 0, 0, tiled=True, axis_index_groups=sets)  71.8 us
    ppermute x8, starting transfers between devices, from_partner(): lax.ppermute(x, axes, [(i, i ^ step) for i in range(lax.axis_size(axes))])  29.3 us
    pallas_call x2, Pallas kernels, attend(): pl.pallas_call(functools.partial(attend_kernel, blocks), in_specs=[VMEM]...  12 us
    all_gather x1, blocking collectives, body(): velocity = jnp.sum(lax.all_gather(velocity, 'c', axis=0), axis=0)  10.2 us
    ppermute x8, waiting for transfers between devices, from_partner(): lax.ppermute(x, axes, [(i, i ^ step) for i in range(lax.axis_size(axes))])  7.94 us
  transfers between devices with their start and end apart: 8, of which 3 were waited for; matrix products, arithmetic and copies ran while one was open for 0% of the time, Pallas kernels for 9%

profile of v11, /device:TPU:1, one launch (start us, length us, event | category | flops | bytes accessed | tf_op | source)
XLA Modules:
  0.0 134.8 jit_solution(2842428381528374032)
XLA Ops:
  0.0 2.1 %pack.1 = bf16[8,3,96,128]{3,2,1,0:T(8,128)(2,1)} custom-call(bf16[96,640]{1,0:T(8,128)(2,1)} %qm.1, bf16[96,640]{1,0:T(8,128)(2,1)} %km.1, bf16[96,640]{1,0:T(8,128)(2,1)} %vm.1, bf16[96,384]{1,0:T(8,128)(2,1)} %qg.1, bf16[96,384]{1,0:T(8,128)(2,1)} %kg.1, bf16[96,384]{1,0:T(8,128)(2,1)} %vg.1), custom_call_target="tpu_custom_call" | custom-call | tf_op jit(solution)/shard_map/pack/pallas_call | solution.py:181
  2.1 47.6 %all_to_all.10.in_ref = bf16[8,3,96,128]{3,2,1,0:T(8,128)(2,1)S(1)} all-to-all(bf16[8,3,96,128]{3,2,1,0:T(8,128)(2,1)} %pack.1), channel_id=1, replica_groups={{0,16,32,48,72,88,104,120},{8,24,40,56,64,80,96,112},{1,17,33,49,73,89,..., dimensions={0} | all-to-all | bytes 1179648 | tf_op jit(solution)/shard_map/to_heads/all_to_all | solution.py:37
  49.6 0.0 copy-start
  49.6 0.0 copy-start.1
  49.7 3.3 %collective-permute-start.1 = (bf16[8,2,96,128]{3,2,1,0:T(8,128)(2,1)S(1)}, bf16[8,2,96,128]{3,2,1,0:T(8,128)(2,1)S(1)}, u32[]{:S(2)}, u32[]{:S(2)}) collective-permute-start(bf16[8,2,96,128]{3,2,1,0:T(8,128)(2,1)S(1)} %get-tuple-element.8.refs_2_), channel_id=1, source_target_pairs={{0,4},{4,0},{128,132},{132,128},{256,260},{260,256},{384,388},{388... | collective-permute-start | bytes 1179656 | tf_op jit(solution)/shard_map/gather/ppermute | solution.py:41
  52.9 3.2 %collective-permute-start.2 = (bf16[8,2,96,128]{3,2,1,0:T(8,128)(2,1)S(1)}, bf16[8,2,96,128]{3,2,1,0:T(8,128)(2,1)S(1)}, u32[]{:S(2)}, u32[]{:S(2)}) collective-permute-start(bf16[8,2,96,128]{3,2,1,0:T(8,128)(2,1)S(1)} %get-tuple-element.8.refs_2_), channel_id=1, source_target_pairs={{0,128},{4,132},{128,0},{132,4},{256,384},{260,388},{384,256},{388... | collective-permute-start | bytes 1179656 | tf_op jit(solution)/shard_map/gather/ppermute | solution.py:41
  56.2 2.0 %collective-permute-start.3 = (bf16[8,2,96,128]{3,2,1,0:T(8,128)(2,1)S(1)}, bf16[8,2,96,128]{3,2,1,0:T(8,128)(2,1)S(1)}, u32[]{:S(2)}, u32[]{:S(2)}) collective-permute-start(bf16[8,2,96,128]{3,2,1,0:T(8,128)(2,1)S(1)} %get-tuple-element.8.refs_2_), channel_id=1, source_target_pairs={{0,132},{4,128},{128,4},{132,0},{256,388},{260,384},{384,260},{388... | collective-permute-start | bytes 1179656 | tf_op jit(solution)/shard_map/gather/ppermute | solution.py:41
  58.2 4.6 %collective-permute-start.4 = (bf16[768,128]{1,0:T(8,128)(2,1)S(1)}, bf16[768,128]{1,0:T(8,128)(2,1)S(1)}, u32[]{:S(2)}, u32[]{:S(2)}) collective-permute-start(bf16[768,128]{1,0:T(8,128)(2,1)S(1)} %get-tuple-element.7.refs_0_), channel_id=1, source_target_pairs={{0,384},{8,392},{128,256},{136,264},{256,128},{264,136},{384,0},{3... | collective-permute-start | bytes 589832 | tf_op jit(solution)/shard_map/gather/ppermute | solution.py:41
  62.9 2.0 %collective-permute-start.5 = (bf16[768,128]{1,0:T(8,128)(2,1)S(1)}, bf16[768,128]{1,0:T(8,128)(2,1)S(1)}, u32[]{:S(2)}, u32[]{:S(2)}) collective-permute-start(bf16[768,128]{1,0:T(8,128)(2,1)S(1)} %get-tuple-element.7.refs_0_), channel_id=1, source_target_pairs={{0,392},{8,384},{128,264},{136,256},{256,136},{264,128},{384,8},{3... | collective-permute-start | bytes 589832 | tf_op jit(solution)/shard_map/gather/ppermute | solution.py:41
  64.9 0.0 copy-done
  64.9 0.0 copy-done.1
  65.0 1.0 collective-permute-done.4.refs_0_
  66.0 2.3 %collective-permute-start = (bf16[768,128]{1,0:T(8,128)(2,1)S(1)}, bf16[768,128]{1,0:T(8,128)(2,1)S(1)}, u32[]{:S(2)}, u32[]{:S(2)}) collective-permute-start(bf16[768,128]{1,0:T(8,128)(2,1)S(1)} %get-tuple-element.7.refs_0_), channel_id=1, source_target_pairs={{0,8},{8,0},{128,136},{136,128},{256,264},{264,256},{384,392},{392... | collective-permute-start | bytes 589832 | tf_op jit(solution)/shard_map/gather/ppermute | solution.py:41
  68.3 3.2 %collective-permute-done.5.refs_1_ = bf16[768,128]{1,0:T(8,128)(2,1)S(1)} collective-permute-done((bf16[768,128]{1,0:T(8,128)(2,1)S(1)}, bf16[768,128]{1,0:T(8,128)(2,1)S(1)}, u32[]{:S(2)}, u32[]{:S(2)}) %collective-permute-start.5) | collective-permute-done | bytes 196640 | tf_op jit(solution)/shard_map/gather/ppermute | solution.py:41
  71.5 0.0 collective-permute-done.1.refs_3_
  71.5 0.0 collective-permute-done.2.refs_4_
  71.5 0.0 collective-permute-done.3.refs_5_
  71.5 6.0 %attend.3 = bf16[2,80,768]{2,1,0:T(8,128)(2,1)S(1)} custom-call(bf16[768,128]{1,0:T(8,128)(2,1)S(1)} %collective-permute-done.4.refs_0_, bf16[768,128]{1,0:T(8,128)(2,1)S(1)} %collective-permute-done.5.refs_1_, bf16[8,2,96,128]{3,2,1,0:T(8,128)(2,1)S(1)} %get-tuple-element.8.refs_2_, bf16[8,2,96,128]{3,2,1,0:T(8,128)(2,1)S(1)} %collective-permute-done.1.refs_3_, ...), custom_call_target="tpu_custom_call" | custom-call | flops 4831838208 | bytes 2097152 | tf_op jit(solution)/shard_map/attend/pallas_call | solution.py:124
  77.5 10.0 %collective-permute-start.6 = (bf16[2,80,768]{2,1,0:T(8,128)(2,1)S(1)}, bf16[2,80,768]{2,1,0:T(8,128)(2,1)S(1)}, u32[]{:S(2)}, u32[]{:S(2)}) collective-permute-start(bf16[2,80,768]{2,1,0:T(8,128)(2,1)S(1)} %attend.3), channel_id=1, source_target_pairs={{0,384},{8,392},{128,256},{136,264},{256,128},{264,136},{384,0},{3... | collective-permute-start | bytes 737288 | tf_op jit(solution)/shard_map/attend/ppermute | solution.py:41
  87.5 0.0 collective-permute-done.refs_1_
  87.5 6.0 %attend.2.here_ref = bf16[2,80,768]{2,1,0:T(8,128)(2,1)S(1)} custom-call(bf16[768,128]{1,0:T(8,128)(2,1)S(1)} %get-tuple-element.7.refs_0_, bf16[768,128]{1,0:T(8,128)(2,1)S(1)} %collective-permute-done.refs_1_, bf16[8,2,96,128]{3,2,1,0:T(8,128)(2,1)S(1)} %get-tuple-element.8.refs_2_, bf16[8,2,96,128]{3,2,1,0:T(8,128)(2,1)S(1)} %collective-permute-done.1.refs_3_, ...), custom_call_target="tpu_custom_call" | custom-call | flops 4831838208 | bytes 2097152 | tf_op jit(solution)/shard_map/attend/pallas_call | solution.py:124
  93.5 0.0 collective-permute-done.6.there_ref
  93.5 0.1 combine.2
  93.6 1.9 %collective-permute-start.7 = (bf16[80,768]{1,0:T(8,128)(2,1)S(1)}, bf16[80,768]{1,0:T(8,128)(2,1)S(1)}, u32[]{:S(2)}, u32[]{:S(2)}) collective-permute-start(bf16[80,768]{1,0:T(8,128)(2,1)S(1)} %combine.2), channel_id=1, source_target_pairs={{0,8},{8,0},{128,136},{136,128},{256,264},{264,256},{384,392},{392... | collective-permute-start | bytes 368648 | tf_op jit(solution)/shard_map/combine/ppermute | solution.py:41
  95.5 3.7 %collective-permute-done.7.beside_ref = bf16[80,768]{1,0:T(8,128)(2,1)S(1)} collective-permute-done((bf16[80,768]{1,0:T(8,128)(2,1)S(1)}, bf16[80,768]{1,0:T(8,128)(2,1)S(1)}, u32[]{:S(2)}, u32[]{:S(2)}) %collective-permute-start.7) | collective-permute-done | bytes 122912 | tf_op jit(solution)/shard_map/combine/ppermute | solution.py:41
  99.2 0.3 combine.3
  99.5 24.2 %all_to_all.11 = bf16[16,48,128]{2,1,0:T(8,128)(2,1)S(1)} all-to-all(bf16[16,48,128]{2,1,0:T(8,128)(2,1)S(1)} %bitcast.15), channel_id=1, replica_groups={{0,2,16,18,32,34,48,50,72,74,88,90,104,106,120,122},{8,10,24,26,40,42,5..., dimensions={0} | all-to-all | bytes 393216 | tf_op jit(solution)/shard_map/to_tokens/all_to_all | solution.py:37
  123.8 10.2 %all-gather = f32[96,128]{1,0:T(8,128)S(1)} all-gather(f32[48,128]{1,0:T(8,128)S(1)} %convert_reduce_fusion), channel_id=2, replica_groups=mesh['y'=4,'zh'=8,'z0'=2,'xl'=2,'xh'=2,'c'=2] {'c'}, dimensions={0}, use_global_device_ids=true | all-gather | bytes 73728 | tf_op jit(solution)/shard_map/to_tokens/all_gather | solution.py:225
  134.0 0.1 reshape.18
  134.1 0.7 copy.15
  (8 shorter events, 0.2 us)
Async XLA Ops:
  49.6 15.2 %copy-start = (bf16[640,64]{0,1:T(8,128)(2,1)S(1)}, bf16[640,64]{0,1:T(8,128)(2,1)}, u32[]{:S(2)}) copy-start(bf16[640,64]{0,1:T(8,128)(2,1)} %param.14) | copy-start | bytes 245764
  49.6 15.2 %copy-start.1 = (bf16[384,64]{0,1:T(8,128)(2,1)S(1)}, bf16[384,64]{0,1:T(8,128)(2,1)}, u32[]{:S(2)}) copy-start(bf16[384,64]{0,1:T(8,128)(2,1)} %param.15) | copy-start | bytes 147460
  49.7 21.8 %collective-permute-start.1 = (bf16[8,2,96,128]{3,2,1,0:T(8,128)(2,1)S(1)}, bf16[8,2,96,128]{3,2,1,0:T(8,128)(2,1)S(1)}, u32[]{:S(2)}, u32[]{:S(2)}) collective-permute-start(bf16[8,2,96,128]{3,2,1,0:T(8,128)(2,1)S(1)} %get-tuple-element.8.refs_2_), channel_id=1, source_target_pairs={{0,4},{4,0},{128,132},{132,128},{256,260},{260,256},{384,388},{388... | collective-permute-start | bytes 1179656 | tf_op jit(solution)/shard_map/gather/ppermute | solution.py:41
  52.9 18.6 %collective-permute-start.2 = (bf16[8,2,96,128]{3,2,1,0:T(8,128)(2,1)S(1)}, bf16[8,2,96,128]{3,2,1,0:T(8,128)(2,1)S(1)}, u32[]{:S(2)}, u32[]{:S(2)}) collective-permute-start(bf16[8,2,96,128]{3,2,1,0:T(8,128)(2,1)S(1)} %get-tuple-element.8.refs_2_), channel_id=1, source_target_pairs={{0,128},{4,132},{128,0},{132,4},{256,384},{260,388},{384,256},{388... | collective-permute-start | bytes 1179656 | tf_op jit(solution)/shard_map/gather/ppermute | solution.py:41
  56.2 15.4 %collective-permute-start.3 = (bf16[8,2,96,128]{3,2,1,0:T(8,128)(2,1)S(1)}, bf16[8,2,96,128]{3,2,1,0:T(8,128)(2,1)S(1)}, u32[]{:S(2)}, u32[]{:S(2)}) collective-permute-start(bf16[8,2,96,128]{3,2,1,0:T(8,128)(2,1)S(1)} %get-tuple-element.8.refs_2_), channel_id=1, source_target_pairs={{0,132},{4,128},{128,4},{132,0},{256,388},{260,384},{384,260},{388... | collective-permute-start | bytes 1179656 | tf_op jit(solution)/shard_map/gather/ppermute | solution.py:41
  58.2 7.8 %collective-permute-start.4 = (bf16[768,128]{1,0:T(8,128)(2,1)S(1)}, bf16[768,128]{1,0:T(8,128)(2,1)S(1)}, u32[]{:S(2)}, u32[]{:S(2)}) collective-permute-start(bf16[768,128]{1,0:T(8,128)(2,1)S(1)} %get-tuple-element.7.refs_0_), channel_id=1, source_target_pairs={{0,384},{8,392},{128,256},{136,264},{256,128},{264,136},{384,0},{3... | collective-permute-start | bytes 589832 | tf_op jit(solution)/shard_map/gather/ppermute | solution.py:41
  62.9 8.6 %collective-permute-start.5 = (bf16[768,128]{1,0:T(8,128)(2,1)S(1)}, bf16[768,128]{1,0:T(8,128)(2,1)S(1)}, u32[]{:S(2)}, u32[]{:S(2)}) collective-permute-start(bf16[768,128]{1,0:T(8,128)(2,1)S(1)} %get-tuple-element.7.refs_0_), channel_id=1, source_target_pairs={{0,392},{8,384},{128,264},{136,256},{256,136},{264,128},{384,8},{3... | collective-permute-start | bytes 589832 | tf_op jit(solution)/shard_map/gather/ppermute | solution.py:41
  66.0 21.5 %collective-permute-start = (bf16[768,128]{1,0:T(8,128)(2,1)S(1)}, bf16[768,128]{1,0:T(8,128)(2,1)S(1)}, u32[]{:S(2)}, u32[]{:S(2)}) collective-permute-start(bf16[768,128]{1,0:T(8,128)(2,1)S(1)} %get-tuple-element.7.refs_0_), channel_id=1, source_target_pairs={{0,8},{8,0},{128,136},{136,128},{256,264},{264,256},{384,392},{392... | collective-permute-start | bytes 589832 | tf_op jit(solution)/shard_map/gather/ppermute | solution.py:41
  77.5 16.0 %collective-permute-start.6 = (bf16[2,80,768]{2,1,0:T(8,128)(2,1)S(1)}, bf16[2,80,768]{2,1,0:T(8,128)(2,1)S(1)}, u32[]{:S(2)}, u32[]{:S(2)}) collective-permute-start(bf16[2,80,768]{2,1,0:T(8,128)(2,1)S(1)} %attend.3), channel_id=1, source_target_pairs={{0,384},{8,392},{128,256},{136,264},{256,128},{264,136},{384,0},{3... | collective-permute-start | bytes 737288 | tf_op jit(solution)/shard_map/attend/ppermute | solution.py:41
  93.6 5.6 %collective-permute-start.7 = (bf16[80,768]{1,0:T(8,128)(2,1)S(1)}, bf16[80,768]{1,0:T(8,128)(2,1)S(1)}, u32[]{:S(2)}, u32[]{:S(2)}) collective-permute-start(bf16[80,768]{1,0:T(8,128)(2,1)S(1)} %combine.2), channel_id=1, source_target_pairs={{0,8},{8,0},{128,136},{136,128},{256,264},{264,256},{384,392},{392... | collective-permute-start | bytes 368648 | tf_op jit(solution)/shard_map/combine/ppermute | solution.py:41

commit v12 on v7

--- a/solution.py
+++ b/solution.py
@@ -148,16 +148,16 @@
 
 
 def add_kernel(here_ref, there_ref, out_ref):
-    velocity, summed, top = added([here_ref[1], there_ref[1]])
-    out_ref[:CH, :] = velocity.astype(BF16)
+    velocity, summed, top = added([here_ref[0], there_ref[0]])
+    out_ref[0, :CH, :] = velocity.astype(BF16)
     tail = split_two(summed) + split_two(top)
-    filler = jnp.zeros((out_ref.shape[0] - CH - len(tail), out_ref.shape[1]), F32)
-    out_ref[CH:, :] = jnp.concatenate(tail + (filler,), axis=0).astype(BF16)
+    filler = jnp.zeros((out_ref.shape[1] - CH - len(tail), out_ref.shape[2]), F32)
+    out_ref[0, CH:, :] = jnp.concatenate(tail + (filler,), axis=0).astype(BF16)
 
 
 def combine_kernel(gain_ref, here_ref, there_ref, beside_ref, out_ref):
     half = out_ref.shape[2]
-    velocity, summed, _ = added([here_ref[0], there_ref[0], beside_ref[...]])
+    velocity, summed, _ = added([here_ref[0], there_ref[0], beside_ref[0]])
     velocity = (velocity * (gain_ref[0] / summed)).T
     velocity = velocity.reshape(out_ref.shape[0], 2, half, CH)
     velocity = jnp.concatenate([velocity[:, 0], velocity[:, 1]], axis=2).astype(BF16)
@@ -203,23 +203,28 @@
         beside = from_partner(q, Z0_STEP)
         across = [from_partner(q, Y_STEP), from_partner(q, Y_STEP ^ Z0_STEP)]
     with jax.named_scope("attend"):
-        there = from_partner(attend(across, key_values, map_t), Y_STEP)
-        here = attend([q, beside], key_values, map_t)
-    with jax.named_scope("combine"):
+        first, second = across[1], across[0]
+        first_share = attend([first], key_values, map_t)
+        second, first_share = lax.optimization_barrier((second, first_share))
+        there_beside = from_partner(first_share, Y_STEP)
+        there = from_partner(attend([second], key_values, map_t), Y_STEP)
         share = pl.pallas_call(
             add_kernel,
             in_specs=[VMEM] * 2,
             out_specs=VMEM,
-            out_shape=jax.ShapeDtypeStruct(here.shape[1:], BF16),
+            out_shape=jax.ShapeDtypeStruct(there.shape, BF16),
             compiler_params=SMALL,
-        )(here, there)
+        )(attend([beside], key_values, map_t), there_beside)
+        here_beside = from_partner(share, Z0_STEP)
+        here = attend([q], key_values, map_t)
+    with jax.named_scope("combine"):
         velocity = pl.pallas_call(
             combine_kernel,
             in_specs=[SMEM] + [VMEM] * 3,
             out_specs=VMEM,
             out_shape=jax.ShapeDtypeStruct((heads, SIDES, tokens_here // 2, 2 * CH), BF16),
             compiler_params=SMALL,
-        )(gain, here, there, from_partner(share, Z0_STEP))
+        )(gain, here, there, here_beside)
     with jax.named_scope("to_tokens"):
         velocity = velocity.reshape((heads * SIDES,) + velocity.shape[2:])
         velocity = exchange(velocity, PLANE_AXES, SIDE_SETS)

time: 132 us -> 134 us (1.015)
  starting transfers between devices: 26.6 us -> 28.6 us
    ppermute x5 -> x6, waiting for transfers between devices: 7.63 us -> 2.53 us  [from_partner(): return lax.ppermute(x, QUERY_AXES, [(i, i ^ step) for i in range(size)])]
    all_to_all x1, waiting for transfers between devices: 4.49 us -> 8.42 us  [exchange(): return lax.all_to_all(x, axes, 0, 0, tiled=True, axis_index_groups=sets)]
    all_gather x1, blocking collectives: 5.14 us -> 7.86 us  [body(): velocity = jnp.sum(lax.all_gather(velocity, 'c', axis=0), axis=0)]
    all_to_all x2, blocking collectives: 71.1 us -> 69.1 us  [exchange(): return lax.all_to_all(x, axes, 0, 0, tiled=True, axis_index_groups=sets)]
    ppermute x5 -> x6, starting transfers between devices: 22.9 us -> 24.9 us  [from_partner(): return lax.ppermute(x, QUERY_AXES, [(i, i ^ step) for i in range(size)])]
    pallas_call x2 -> x4, Pallas kernels: 11.9 us -> 12 us  [attend(): pl.pallas_call(attend_kernel, in_specs=[VMEM] * (2 + blocks), out_specs=V...]
  transfers between devices with their start and end apart: 6 -> 7, of which waited for: 3 -> 3; matrix products, arithmetic and copies ran while one was open for 0% -> 0% of each run, Pallas kernels for 9% -> 9%
where the time goes in v12:
time: 134 us; the launch traced here: 133 us
  blocking collectives  76.9 us (57%)
  starting transfers between devices  28.6 us (21%)
  Pallas kernels  15.8 us (12%)
  waiting for transfers between devices  10.9 us (8%)
    all_to_all x2, blocking collectives, exchange(): return lax.all_to_all(x, axes, 0, 0, tiled=True, axis_index_groups=sets)  69.1 us
    ppermute x6, starting transfers between devices, from_partner(): return lax.ppermute(x, QUERY_AXES, [(i, i ^ step) for i in range(size)])  24.9 us
    pallas_call x4, Pallas kernels, attend(): pl.pallas_call(attend_kernel, in_specs=[VMEM] * (2 + blocks), out_specs=V...  12 us
    all_to_all x1, waiting for transfers between devices, exchange(): return lax.all_to_all(x, axes, 0, 0, tiled=True, axis_index_groups=sets)  8.42 us
    all_gather x1, blocking collectives, body(): velocity = jnp.sum(lax.all_gather(velocity, 'c', axis=0), axis=0)  7.86 us
    all_to_all x1, starting transfers between devices, exchange(): return lax.all_to_all(x, axes, 0, 0, tiled=True, axis_index_groups=sets)  3.69 us
  transfers between devices with their start and end apart: 7, of which 3 were waited for; matrix products, arithmetic and copies ran while one was open for 0% of the time, Pallas kernels for 9%

profile of v12, /device:TPU:1, one launch (start us, length us, event | category | flops | bytes accessed | tf_op | source)
XLA Modules:
  0.0 133.3 jit_solution(6066897301414475143)
XLA Ops:
  0.0 2.1 %pack.1 = bf16[8,3,96,128]{3,2,1,0:T(8,128)(2,1)} custom-call(bf16[96,640]{1,0:T(8,128)(2,1)} %qm.1, bf16[96,640]{1,0:T(8,128)(2,1)} %km.1, bf16[96,640]{1,0:T(8,128)(2,1)} %vm.1, bf16[96,384]{1,0:T(8,128)(2,1)} %qg.1, bf16[96,384]{1,0:T(8,128)(2,1)} %kg.1, bf16[96,384]{1,0:T(8,128)(2,1)} %vg.1), custom_call_target="tpu_custom_call" | custom-call | tf_op jit(solution)/shard_map/pack/pallas_call | solution.py:182
  2.1 47.6 %all_to_all.15.in_ref = bf16[8,3,96,128]{3,2,1,0:T(8,128)(2,1)S(1)} all-to-all(bf16[8,3,96,128]{3,2,1,0:T(8,128)(2,1)} %pack.1), channel_id=1, replica_groups={{0,16,32,48,72,88,104,120},{8,24,40,56,64,80,96,112},{1,17,33,49,73,89,..., dimensions={0} | all-to-all | bytes 1179648 | tf_op jit(solution)/shard_map/to_heads/all_to_all | solution.py:37
  49.6 1.4 %gather.1 = (bf16[768,128]{1,0:T(8,128)(2,1)S(1)}, bf16[4,8,2,96,128]{4,3,2,1,0:T(8,128)(2,1)}) custom-call(bf16[8,3,96,128]{3,2,1,0:T(8,128)(2,1)S(1)} %all_to_all.15.in_ref), custom_call_target="tpu_custom_call" | custom-call | tf_op jit(solution)/shard_map/gather/pallas_call | solution.py:192
  51.0 0.0 copy-start
  51.0 0.0 copy-start.1
  51.0 3.7 %all-to-all-start.1 = ((bf16[32,2,96,128]{3,2,1,0:T(8,128)(2,1)}), bf16[32,2,96,128]{3,2,1,0:T(8,128)(2,1)S(1)}, u32[]{:S(2)}, u32[]{:S(2)}) async-start(bf16[32,2,96,128]{3,2,1,0:T(8,128)(2,1)} %bitcast.1), calls=%async_computation.1 | async-start | bytes 3145728 | tf_op jit(solution)/shard_map/gather/all_to_all | solution.py:37
  54.7 5.1 %collective-permute-start.1 = (bf16[768,128]{1,0:T(8,128)(2,1)S(1)}, bf16[768,128]{1,0:T(8,128)(2,1)S(1)}, u32[]{:S(2)}, u32[]{:S(2)}) collective-permute-start(bf16[768,128]{1,0:T(8,128)(2,1)S(1)} %get-tuple-element.9.refs_0_), channel_id=1, source_target_pairs={{0,392},{8,384},{128,264},{136,256},{256,136},{264,128},{384,8},{3... | collective-permute-start | bytes 589832 | tf_op jit(solution)/shard_map/gather/ppermute | solution.py:42
  59.8 0.0 copy-done
  59.9 0.0 copy-done.1
  60.0 1.9 %collective-permute-start = (bf16[768,128]{1,0:T(8,128)(2,1)S(1)}, bf16[768,128]{1,0:T(8,128)(2,1)S(1)}, u32[]{:S(2)}, u32[]{:S(2)}) collective-permute-start(bf16[768,128]{1,0:T(8,128)(2,1)S(1)} %get-tuple-element.9.refs_0_), channel_id=1, source_target_pairs={{0,384},{8,392},{128,256},{136,264},{256,128},{264,136},{384,0},{3... | collective-permute-start | bytes 589832 | tf_op jit(solution)/shard_map/gather/ppermute | solution.py:42
  61.9 3.0 %collective-permute-start.3 = (bf16[768,128]{1,0:T(8,128)(2,1)S(1)}, bf16[768,128]{1,0:T(8,128)(2,1)S(1)}, u32[]{:S(2)}, u32[]{:S(2)}) collective-permute-start(bf16[768,128]{1,0:T(8,128)(2,1)S(1)} %get-tuple-element.9.refs_0_), channel_id=1, source_target_pairs={{0,8},{8,0},{128,136},{136,128},{256,264},{264,256},{384,392},{392... | collective-permute-start | bytes 589832 | tf_op jit(solution)/shard_map/gather/ppermute | solution.py:42
  64.9 0.0 collective-permute-done.1.refs_0_
  65.0 8.4 %all-to-all-done.1.refs_1_ = bf16[32,2,96,128]{3,2,1,0:T(8,128)(2,1)S(1)} async-done(((bf16[32,2,96,128]{3,2,1,0:T(8,128)(2,1)}), bf16[32,2,96,128]{3,2,1,0:T(8,128)(2,1)S(1)}, u32[]{:S(2)}, u32[]{:S(2)}) %all-to-all-start.1) | async-done | bytes 1572896 | tf_op jit(solution)/shard_map/gather/all_to_all | solution.py:37
  73.4 3.0 %attend.6 = bf16[1,80,768]{2,1,0:T(8,128)(2,1)S(1)} custom-call(bf16[768,128]{1,0:T(8,128)(2,1)S(1)} %collective-permute-done.1.refs_0_, bf16[32,2,96,128]{3,2,1,0:T(8,128)(2,1)S(1)} %all-to-all-done.1.refs_1_, bf16[64,128]{1,0:T(8,128)(2,1)S(1)} %bitcast.17), custom_call_target="tpu_custom_call" | custom-call | flops 2415919104 | bytes 2097152 | tf_op jit(solution)/shard_map/attend/pallas_call | solution.py:125
  76.4 0.0 collective-permute-done.refs_0_
  76.4 3.0 %attend.7 = bf16[1,80,768]{2,1,0:T(8,128)(2,1)S(1)} custom-call(bf16[768,128]{1,0:T(8,128)(2,1)S(1)} %collective-permute-done.refs_0_, bf16[32,2,96,128]{3,2,1,0:T(8,128)(2,1)S(1)} %all-to-all-done.1.refs_1_, bf16[64,128]{1,0:T(8,128)(2,1)S(1)} %bitcast.18), custom_call_target="tpu_custom_call" | custom-call | flops 2415919104 | bytes 2097152 | tf_op jit(solution)/shard_map/attend/pallas_call | solution.py:125
  79.3 11.0 %collective-permute-start.2 = (bf16[1,80,768]{2,1,0:T(8,128)(2,1)S(1)}, bf16[1,80,768]{2,1,0:T(8,128)(2,1)S(1)}, u32[]{:S(2)}, u32[]{:S(2)}) collective-permute-start(bf16[1,80,768]{2,1,0:T(8,128)(2,1)S(1)} %attend.7), channel_id=1, source_target_pairs={{0,384},{8,392},{128,256},{136,264},{256,128},{264,136},{384,0},{3... | collective-permute-start | bytes 368648 | tf_op jit(solution)/shard_map/attend/ppermute | solution.py:42
  90.3 1.9 %collective-permute-start.4 = (bf16[1,80,768]{2,1,0:T(8,128)(2,1)S(1)}, bf16[1,80,768]{2,1,0:T(8,128)(2,1)S(1)}, u32[]{:S(2)}, u32[]{:S(2)}) collective-permute-start(bf16[1,80,768]{2,1,0:T(8,128)(2,1)S(1)} %attend.6), channel_id=1, source_target_pairs={{0,384},{8,392},{128,256},{136,264},{256,128},{264,136},{384,0},{3... | collective-permute-start | bytes 368648 | tf_op jit(solution)/shard_map/attend/ppermute | solution.py:42
  92.2 0.0 collective-permute-done.3.refs_0_
  92.2 3.1 %attend.8.here_ref = bf16[1,80,768]{2,1,0:T(8,128)(2,1)S(1)} custom-call(bf16[768,128]{1,0:T(8,128)(2,1)S(1)} %collective-permute-done.3.refs_0_, bf16[32,2,96,128]{3,2,1,0:T(8,128)(2,1)S(1)} %all-to-all-done.1.refs_1_, bf16[64,128]{1,0:T(8,128)(2,1)S(1)} %bitcast.19), custom_call_target="tpu_custom_call" | custom-call | flops 2415919104 | bytes 2097152 | tf_op jit(solution)/shard_map/attend/pallas_call | solution.py:125
  95.3 1.8 %collective-permute-done.4.there_ref = bf16[1,80,768]{2,1,0:T(8,128)(2,1)S(1)} collective-permute-done((bf16[1,80,768]{2,1,0:T(8,128)(2,1)S(1)}, bf16[1,80,768]{2,1,0:T(8,128)(2,1)S(1)}, u32[]{:S(2)}, u32[]{:S(2)}) %collective-permute-start.4) | collective-permute-done | bytes 122912 | tf_op jit(solution)/shard_map/attend/ppermute | solution.py:42
  97.1 0.1 attend.9
  97.2 1.9 %collective-permute-start.5 = (bf16[1,80,768]{2,1,0:T(8,128)(2,1)S(1)}, bf16[1,80,768]{2,1,0:T(8,128)(2,1)S(1)}, u32[]{:S(2)}, u32[]{:S(2)}) collective-permute-start(bf16[1,80,768]{2,1,0:T(8,128)(2,1)S(1)} %attend.9), channel_id=1, source_target_pairs={{0,8},{8,0},{128,136},{136,128},{256,264},{264,256},{384,392},{392... | collective-permute-start | bytes 368648 | tf_op jit(solution)/shard_map/attend/ppermute | solution.py:42
  99.1 3.0 %attend.5.here_ref = bf16[1,80,768]{2,1,0:T(8,128)(2,1)S(1)} custom-call(bf16[768,128]{1,0:T(8,128)(2,1)S(1)} %get-tuple-element.9.refs_0_, bf16[32,2,96,128]{3,2,1,0:T(8,128)(2,1)S(1)} %all-to-all-done.1.refs_1_, bf16[64,128]{1,0:T(8,128)(2,1)S(1)} %bitcast.20), custom_call_target="tpu_custom_call" | custom-call | flops 2415919104 | bytes 2097152 | tf_op jit(solution)/shard_map/attend/pallas_call | solution.py:125
  102.1 0.0 collective-permute-done.2.there_ref
  102.1 0.7 collective-permute-done.5.beside_ref
  102.8 0.3 combine.1
  103.1 21.5 %all_to_all.16 = bf16[16,48,128]{2,1,0:T(8,128)(2,1)S(1)} all-to-all(bf16[16,48,128]{2,1,0:T(8,128)(2,1)S(1)} %bitcast.16), channel_id=1, replica_groups={{0,2,16,18,32,34,48,50,72,74,88,90,104,106,120,122},{8,10,24,26,40,42,5..., dimensions={0} | all-to-all | bytes 393216 | tf_op jit(solution)/shard_map/to_tokens/all_to_all | solution.py:37
  124.6 7.9 %all-gather = f32[96,128]{1,0:T(8,128)S(1)} all-gather(f32[48,128]{1,0:T(8,128)S(1)} %convert_reduce_fusion), channel_id=2, replica_groups=mesh['y'=4,'zh'=8,'z0'=2,'xl'=2,'xh'=2,'c'=2] {'c'}, dimensions={0}, use_global_device_ids=true | all-gather | bytes 73728 | tf_op jit(solution)/shard_map/to_tokens/all_gather | solution.py:232
  132.5 0.1 reshape.22
  132.6 0.7 copy.15
  (7 shorter events, 0.1 us)
Async XLA Ops:
  51.0 8.8 %copy-start = (bf16[640,64]{0,1:T(8,128)(2,1)S(1)}, bf16[640,64]{0,1:T(8,128)(2,1)}, u32[]{:S(2)}) copy-start(bf16[640,64]{0,1:T(8,128)(2,1)} %param.14) | copy-start | bytes 245764
  51.0 8.9 %copy-start.1 = (bf16[384,64]{0,1:T(8,128)(2,1)S(1)}, bf16[384,64]{0,1:T(8,128)(2,1)}, u32[]{:S(2)}) copy-start(bf16[384,64]{0,1:T(8,128)(2,1)} %param.15) | copy-start | bytes 147460
  51.0 22.4 %all-to-all-start.1 = ((bf16[32,2,96,128]{3,2,1,0:T(8,128)(2,1)}), bf16[32,2,96,128]{3,2,1,0:T(8,128)(2,1)S(1)}, u32[]{:S(2)}, u32[]{:S(2)}) async-start(bf16[32,2,96,128]{3,2,1,0:T(8,128)(2,1)} %bitcast.1), calls=%async_computation.1 | async-start | bytes 3145728 | tf_op jit(solution)/shard_map/gather/all_to_all | solution.py:37
  54.7 10.2 %collective-permute-start.1 = (bf16[768,128]{1,0:T(8,128)(2,1)S(1)}, bf16[768,128]{1,0:T(8,128)(2,1)S(1)}, u32[]{:S(2)}, u32[]{:S(2)}) collective-permute-start(bf16[768,128]{1,0:T(8,128)(2,1)S(1)} %get-tuple-element.9.refs_0_), channel_id=1, source_target_pairs={{0,392},{8,384},{128,264},{136,256},{256,136},{264,128},{384,8},{3... | collective-permute-start | bytes 589832 | tf_op jit(solution)/shard_map/gather/ppermute | solution.py:42
  60.0 16.4 %collective-permute-start = (bf16[768,128]{1,0:T(8,128)(2,1)S(1)}, bf16[768,128]{1,0:T(8,128)(2,1)S(1)}, u32[]{:S(2)}, u32[]{:S(2)}) collective-permute-start(bf16[768,128]{1,0:T(8,128)(2,1)S(1)} %get-tuple-element.9.refs_0_), channel_id=1, source_target_pairs={{0,384},{8,392},{128,256},{136,264},{256,128},{264,136},{384,0},{3... | collective-permute-start | bytes 589832 | tf_op jit(solution)/shard_map/gather/ppermute | solution.py:42
  61.9 30.3 %collective-permute-start.3 = (bf16[768,128]{1,0:T(8,128)(2,1)S(1)}, bf16[768,128]{1,0:T(8,128)(2,1)S(1)}, u32[]{:S(2)}, u32[]{:S(2)}) collective-permute-start(bf16[768,128]{1,0:T(8,128)(2,1)S(1)} %get-tuple-element.9.refs_0_), channel_id=1, source_target_pairs={{0,8},{8,0},{128,136},{136,128},{256,264},{264,256},{384,392},{392... | collective-permute-start | bytes 589832 | tf_op jit(solution)/shard_map/gather/ppermute | solution.py:42
  79.3 22.8 %collective-permute-start.2 = (bf16[1,80,768]{2,1,0:T(8,128)(2,1)S(1)}, bf16[1,80,768]{2,1,0:T(8,128)(2,1)S(1)}, u32[]{:S(2)}, u32[]{:S(2)}) collective-permute-start(bf16[1,80,768]{2,1,0:T(8,128)(2,1)S(1)} %attend.7), channel_id=1, source_target_pairs={{0,384},{8,392},{128,256},{136,264},{256,128},{264,136},{384,0},{3... | collective-permute-start | bytes 368648 | tf_op jit(solution)/shard_map/attend/ppermute | solution.py:42
  90.3 6.8 %collective-permute-start.4 = (bf16[1,80,768]{2,1,0:T(8,128)(2,1)S(1)}, bf16[1,80,768]{2,1,0:T(8,128)(2,1)S(1)}, u32[]{:S(2)}, u32[]{:S(2)}) collective-permute-start(bf16[1,80,768]{2,1,0:T(8,128)(2,1)S(1)} %attend.6), channel_id=1, source_target_pairs={{0,384},{8,392},{128,256},{136,264},{256,128},{264,136},{384,0},{3... | collective-permute-start | bytes 368648 | tf_op jit(solution)/shard_map/attend/ppermute | solution.py:42
  97.2 5.6 %collective-permute-start.5 = (bf16[1,80,768]{2,1,0:T(8,128)(2,1)S(1)}, bf16[1,80,768]{2,1,0:T(8,128)(2,1)S(1)}, u32[]{:S(2)}, u32[]{:S(2)}) collective-permute-start(bf16[1,80,768]{2,1,0:T(8,128)(2,1)S(1)} %attend.9), channel_id=1, source_target_pairs={{0,8},{8,0},{128,136},{136,128},{256,264},{264,256},{384,392},{392... | collective-permute-start | bytes 368648 | tf_op jit(solution)/shard_map/attend/ppermute | solution.py:42

commit v13 on v10

--- a/solution.py
+++ b/solution.py
@@ -24,10 +24,10 @@
 GRP = ("xh", "c")
 Z = ("zh", "z0")
 PLANE_SETS = ([0, 2, 4, 6, 9, 11, 13, 15], [1, 3, 5, 7, 8, 10, 12, 14])
-QUERY_AXES = ("y", "z0")
-Z0_STEP, Y_STEP = 1, 6
-KEY_AXES = ("y", "xl")
-KEY_SETS = ([0, 1, 2, 3], [4, 5, 6, 7])
+QUERY_AXES = ("y", "xl")
+X_STEP, Y_STEP = 1, 2
+KEY_AXES = ("y", "z0")
+KEY_SETS = ([0, 1, 6, 7], [2, 3, 4, 5])
 SIDES = 2
 PLANE_AXES = Z + ("xh",)
 SIDE_SETS = [[SIDES * z + x for z in planes for x in range(SIDES)] for planes in PLANE_SETS]
@@ -157,7 +157,7 @@
         out_specs=VMEM,
         out_shape=jax.ShapeDtypeStruct(out, BF16 if last else F32),
         scratch_shapes=[pltpu.VMEM((blocks, rows, HD), BF16), pltpu.VMEM((rows, HD), F32)],
-        compiler_params=pltpu.CompilerParams(vmem_limit_bytes=40 << 20),
+        compiler_params=pltpu.CompilerParams(vmem_limit_bytes=28 << 20),
         cost_estimate=pl.CostEstimate(
             flops=8 * blocks * rows * keys * HD,
             bytes_accessed=2 << 20,
@@ -233,11 +233,11 @@
             compiler_params=SMALL,
         )(arrived)
         key_values = exchange(copies.reshape((-1,) + copies.shape[2:]), KEY_AXES, KEY_SETS)
-        beside = from_partner(q, Z0_STEP)
-        across = [from_partner(q, Y_STEP), from_partner(q, Y_STEP ^ Z0_STEP)]
+        beside = from_partner(q, X_STEP)
+        across = [from_partner(q, Y_STEP), from_partner(q, Y_STEP ^ X_STEP)]
     with jax.named_scope("attend"):
         before = attend(across + [q, beside], [arrived], map_t)
-        own = lax.axis_index(KEY_AXES).astype(jnp.int32) & 3
+        own = ((lax.axis_index("y") >> 1) * 2 + lax.axis_index("z0")).astype(jnp.int32)
         others = [own.reshape(1), key_values, before]
         there = from_partner(attend(across, others, map_t, 0), Y_STEP)
         here = attend([q, beside], others, map_t, len(across))
@@ -255,7 +255,7 @@
             out_specs=VMEM,
             out_shape=jax.ShapeDtypeStruct((heads, SIDES, tokens_here // 2, 2 * CH), BF16),
             compiler_params=SMALL,
-        )(gain, here, there, from_partner(share, Z0_STEP))
+        )(gain, here, there, from_partner(share, X_STEP))
     with jax.named_scope("to_tokens"):
         velocity = velocity.reshape((heads * SIDES,) + velocity.shape[2:])
         velocity = exchange(velocity, PLANE_AXES, SIDE_SETS)

time: 134 us -> 130 us (0.970)
  blocking collectives: 78.8 us -> 75.9 us
  starting transfers between devices: 25.3 us -> 23.9 us
    all_gather x1, blocking collectives: 8.35 us -> 3.96 us  [body(): velocity = jnp.sum(lax.all_gather(velocity, 'c', axis=0), axis=0)]
    ppermute x5, starting transfers between devices: 21.6 us -> 19.7 us  [from_partner(): return lax.ppermute(x, QUERY_AXES, [(i, i ^ step) for i in range(size)])]
    ppermute x5, waiting for transfers between devices: 8.6 us -> 6.92 us  [from_partner(): return lax.ppermute(x, QUERY_AXES, [(i, i ^ step) for i in range(size)])]
    all_to_all x2, blocking collectives: 70.5 us -> 72 us  [exchange(): return lax.all_to_all(x, axes, 0, 0, tiled=True, axis_index_groups=sets)]
    all_to_all x1, waiting for transfers between devices: 0.01 us -> 1.38 us  [exchange(): return lax.all_to_all(x, axes, 0, 0, tiled=True, axis_index_groups=sets)]
  transfers between devices with their start and end apart: 6 -> 6, of which waited for: 3 -> 4; matrix products, arithmetic and copies ran while one was open for 0% -> 0% of each run, Pallas kernels for 7% -> 7%
where the time goes in v13:
time: 130 us; the launch traced here: 129 us
  blocking collectives  75.9 us (58%)
  starting transfers between devices  23.9 us (18%)
  Pallas kernels  16.8 us (13%)
  waiting for transfers between devices  8.3 us (6%)
  local copies, waits for them, and re-layouts  4.09 us (3%)
    all_to_all x2, blocking collectives, exchange(): return lax.all_to_all(x, axes, 0, 0, tiled=True, axis_index_groups=sets)  72 us
    ppermute x5, starting transfers between devices, from_partner(): return lax.ppermute(x, QUERY_AXES, [(i, i ^ step) for i in range(size)])  19.7 us
    pallas_call x3, Pallas kernels, attend(): pl.pallas_call(functools.partial(attend_kernel, blocks, first_before), in...  14.2 us
    ppermute x5, waiting for transfers between devices, from_partner(): return lax.ppermute(x, QUERY_AXES, [(i, i ^ step) for i in range(size)])  6.92 us
    all_to_all x1, starting transfers between devices, exchange(): return lax.all_to_all(x, axes, 0, 0, tiled=True, axis_index_groups=sets)  4.21 us
    all_gather x1, blocking collectives, body(): velocity = jnp.sum(lax.all_gather(velocity, 'c', axis=0), axis=0)  3.96 us
    unnamed x12, local copies, waits for them, and re-layouts  3.25 us
  transfers between devices with their start and end apart: 6, of which 4 were waited for; matrix products, arithmetic and copies ran while one was open for 0% of the time, Pallas kernels for 7%

profile of v13, /device:TPU:1, one launch (start us, length us, event | category | flops | bytes accessed | tf_op | source)
XLA Modules:
  0.0 129.3 jit_solution(16400141811158227672)
XLA Ops:
  0.0 2.0 %pack.1 = bf16[8,3,96,128]{3,2,1,0:T(8,128)(2,1)} custom-call(bf16[96,640]{1,0:T(8,128)(2,1)} %qm.1, bf16[96,640]{1,0:T(8,128)(2,1)} %km.1, bf16[96,640]{1,0:T(8,128)(2,1)} %vm.1, bf16[96,384]{1,0:T(8,128)(2,1)} %qg.1, bf16[96,384]{1,0:T(8,128)(2,1)} %kg.1, bf16[96,384]{1,0:T(8,128)(2,1)} %vg.1), custom_call_target="tpu_custom_call" | custom-call | tf_op jit(solution)/shard_map/pack/pallas_call | solution.py:215
  2.0 47.6 %all_to_all.15.in_ref.refs_4_ = bf16[8,3,96,128]{3,2,1,0:T(8,128)(2,1)S(1)} all-to-all(bf16[8,3,96,128]{3,2,1,0:T(8,128)(2,1)} %pack.1), channel_id=1, replica_groups={{0,16,32,48,72,88,104,120},{8,24,40,56,64,80,96,112},{1,17,33,49,73,89,..., dimensions={0} | all-to-all | bytes 1179648 | tf_op jit(solution)/shard_map/to_heads/all_to_all | solution.py:37
  49.6 0.2 gather.1
  49.8 0.0 copy-start
  49.8 1.1 copy-done
  51.0 0.0 copy-start.3
  51.0 0.0 copy-start.4
  51.0 4.2 %all-to-all-start.1 = ((bf16[32,2,96,128]{3,2,1,0:T(8,128)(2,1)}), bf16[32,2,96,128]{3,2,1,0:T(8,128)(2,1)S(1)}, u32[]{:S(2)}, u32[]{:S(2)}) async-start(bf16[32,2,96,128]{3,2,1,0:T(8,128)(2,1)} %bitcast.17), calls=%async_computation.1 | async-start | bytes 3145728 | tf_op jit(solution)/shard_map/gather/all_to_all | solution.py:37
  55.2 3.6 %collective-permute-start.2 = (bf16[768,128]{1,0:T(8,128)(2,1)S(1)}, bf16[768,128]{1,0:T(8,128)(2,1)S(1)}, u32[]{:S(2)}, u32[]{:S(2)}) collective-permute-start(bf16[768,128]{1,0:T(8,128)(2,1)S(1)} %get-tuple-element.7.refs_2_.refs_0_), channel_id=1, source_target_pairs={{0,132},{4,128},{128,4},{132,0},{256,388},{260,384},{384,260},{388... | collective-permute-start | bytes 589832 | tf_op jit(solution)/shard_map/gather/ppermute | solution.py:42
  58.8 2.6 %collective-permute-start.1 = (bf16[768,128]{1,0:T(8,128)(2,1)S(1)}, bf16[768,128]{1,0:T(8,128)(2,1)S(1)}, u32[]{:S(2)}, u32[]{:S(2)}) collective-permute-start(bf16[768,128]{1,0:T(8,128)(2,1)S(1)} %get-tuple-element.7.refs_2_.refs_0_), channel_id=1, source_target_pairs={{0,128},{4,132},{128,0},{132,4},{256,384},{260,388},{384,256},{388... | collective-permute-start | bytes 589832 | tf_op jit(solution)/shard_map/gather/ppermute | solution.py:42
  61.4 2.2 %collective-permute-start = (bf16[768,128]{1,0:T(8,128)(2,1)S(1)}, bf16[768,128]{1,0:T(8,128)(2,1)S(1)}, u32[]{:S(2)}, u32[]{:S(2)}) collective-permute-start(bf16[768,128]{1,0:T(8,128)(2,1)S(1)} %get-tuple-element.7.refs_2_.refs_0_), channel_id=1, source_target_pairs={{0,4},{4,0},{128,132},{132,128},{256,260},{260,256},{384,388},{388... | collective-permute-start | bytes 589832 | tf_op jit(solution)/shard_map/gather/ppermute | solution.py:42
  63.6 0.0 copy-done.3
  63.6 0.0 copy-done.4
  63.7 0.0 collective-permute-done.2.refs_1_
  63.7 4.5 %collective-permute-done.1.refs_0_ = bf16[768,128]{1,0:T(8,128)(2,1)S(1)} collective-permute-done((bf16[768,128]{1,0:T(8,128)(2,1)S(1)}, bf16[768,128]{1,0:T(8,128)(2,1)S(1)}, u32[]{:S(2)}, u32[]{:S(2)}) %collective-permute-start.1) | collective-permute-done | bytes 196640 | tf_op jit(solution)/shard_map/gather/ppermute | solution.py:42
  68.2 0.0 collective-permute-done.refs_3_.refs_1_
  68.2 4.6 %attend.3.refs_5_ = f32[4,72,768]{2,1,0:T(8,128)S(1)} custom-call(bf16[768,128]{1,0:T(8,128)(2,1)S(1)} %collective-permute-done.1.refs_0_, bf16[768,128]{1,0:T(8,128)(2,1)S(1)} %collective-permute-done.2.refs_1_, bf16[768,128]{1,0:T(8,128)(2,1)S(1)} %get-tuple-element.7.refs_2_.refs_0_, bf16[768,128]{1,0:T(8,128)(2,1)S(1)} %collective-permute-done.refs_3_.refs_1_, ...), custom_call_target="tpu_custom_call" | custom-call | flops 2415919104 | bytes 2097152 | tf_op jit(solution)/shard_map/attend/pallas_call | solution.py:154
  72.8 0.0 copy-start.1
  72.8 0.9 copy-done.1
  73.7 1.4 %all-to-all-done.1.refs_3_ = bf16[32,2,96,128]{3,2,1,0:T(8,128)(2,1)S(1)} async-done(((bf16[32,2,96,128]{3,2,1,0:T(8,128)(2,1)}), bf16[32,2,96,128]{3,2,1,0:T(8,128)(2,1)S(1)}, u32[]{:S(2)}, u32[]{:S(2)}) %all-to-all-start.1) | async-done | bytes 1572896 | tf_op jit(solution)/shard_map/gather/all_to_all | solution.py:37
  75.1 0.0 copy-start.2
  75.1 1.2 copy-done.2
  76.3 4.8 %attend.5 = bf16[2,80,768]{2,1,0:T(8,128)(2,1)S(1)} custom-call(bf16[768,128]{1,0:T(8,128)(2,1)S(1)} %collective-permute-done.1.refs_0_, bf16[768,128]{1,0:T(8,128)(2,1)S(1)} %collective-permute-done.2.refs_1_, s32[1]{0:T(128)} %bitcast.1.refs_2_, bf16[32,2,96,128]{3,2,1,0:T(8,128)(2,1)S(1)} %all-to-all-done.1.refs_3_, bf16[64,128]{1,0:T(8,128)(2,1)S(1)} %bitcast.20, ...), custom_call_target="tpu_custom_call" | custom-call | flops 3623878656 | bytes 2097152 | tf_op jit(solution)/shard_map/attend/pallas_call | solution.py:154
  81.1 1.9 %collective-permute-start.3 = (bf16[2,80,768]{2,1,0:T(8,128)(2,1)S(1)}, bf16[2,80,768]{2,1,0:T(8,128)(2,1)S(1)}, u32[]{:S(2)}, u32[]{:S(2)}) collective-permute-start(bf16[2,80,768]{2,1,0:T(8,128)(2,1)S(1)} %attend.5), channel_id=1, source_target_pairs={{0,128},{4,132},{128,0},{132,4},{256,384},{260,388},{384,256},{388... | collective-permute-start | bytes 737288 | tf_op jit(solution)/shard_map/attend/ppermute | solution.py:42
  83.0 4.8 %attend.4.here_ref = bf16[2,80,768]{2,1,0:T(8,128)(2,1)S(1)} custom-call(bf16[768,128]{1,0:T(8,128)(2,1)S(1)} %get-tuple-element.7.refs_2_.refs_0_, bf16[768,128]{1,0:T(8,128)(2,1)S(1)} %collective-permute-done.refs_3_.refs_1_, s32[1]{0:T(128)} %bitcast.1.refs_2_, bf16[32,2,96,128]{3,2,1,0:T(8,128)(2,1)S(1)} %all-to-all-done.1.refs_3_, ...), custom_call_target="tpu_custom_call" | custom-call | flops 3623878656 | bytes 2097152 | tf_op jit(solution)/shard_map/attend/pallas_call | solution.py:154
  87.9 0.2 collective-permute-done.3.there_ref
  88.0 0.1 combine.2
  88.1 9.4 %collective-permute-start.4 = (bf16[80,768]{1,0:T(8,128)(2,1)S(1)}, bf16[80,768]{1,0:T(8,128)(2,1)S(1)}, u32[]{:S(2)}, u32[]{:S(2)}) collective-permute-start(bf16[80,768]{1,0:T(8,128)(2,1)S(1)} %combine.2), channel_id=1, source_target_pairs={{0,4},{4,0},{128,132},{132,128},{256,260},{260,256},{384,388},{388... | collective-permute-start | bytes 368648 | tf_op jit(solution)/shard_map/combine/ppermute | solution.py:42
  97.5 2.2 %collective-permute-done.4.beside_ref = bf16[80,768]{1,0:T(8,128)(2,1)S(1)} collective-permute-done((bf16[80,768]{1,0:T(8,128)(2,1)S(1)}, bf16[80,768]{1,0:T(8,128)(2,1)S(1)}, u32[]{:S(2)}, u32[]{:S(2)}) %collective-permute-start.4) | collective-permute-done | bytes 122912 | tf_op jit(solution)/shard_map/combine/ppermute | solution.py:42
  99.8 0.3 combine.3
  100.1 24.4 %all_to_all.16 = bf16[16,48,128]{2,1,0:T(8,128)(2,1)S(1)} all-to-all(bf16[16,48,128]{2,1,0:T(8,128)(2,1)S(1)} %bitcast.18), channel_id=1, replica_groups={{0,2,16,18,32,34,48,50,72,74,88,90,104,106,120,122},{8,10,24,26,40,42,5..., dimensions={0} | all-to-all | bytes 393216 | tf_op jit(solution)/shard_map/to_tokens/all_to_all | solution.py:37
  124.5 4.0 %all-gather = f32[96,128]{1,0:T(8,128)S(1)} all-gather(f32[48,128]{1,0:T(8,128)S(1)} %convert_reduce_fusion), channel_id=2, replica_groups=mesh['y'=4,'zh'=8,'z0'=2,'xl'=2,'xh'=2,'c'=2] {'c'}, dimensions={0}, use_global_device_ids=true | all-gather | bytes 73728 | tf_op jit(solution)/shard_map/to_tokens/all_gather | solution.py:263
  128.4 0.1 reshape.26
  128.6 0.7 copy.15
  (7 shorter events, 0.1 us)
Async XLA Ops:
  49.8 1.1 copy-start
  51.0 12.6 %copy-start.3 = (bf16[640,64]{0,1:T(8,128)(2,1)S(1)}, bf16[640,64]{0,1:T(8,128)(2,1)}, u32[]{:S(2)}) copy-start(bf16[640,64]{0,1:T(8,128)(2,1)} %param.14) | copy-start | bytes 245764
  51.0 12.6 %copy-start.4 = (bf16[384,64]{0,1:T(8,128)(2,1)S(1)}, bf16[384,64]{0,1:T(8,128)(2,1)}, u32[]{:S(2)}) copy-start(bf16[384,64]{0,1:T(8,128)(2,1)} %param.15) | copy-start | bytes 147460
  51.0 24.1 %all-to-all-start.1 = ((bf16[32,2,96,128]{3,2,1,0:T(8,128)(2,1)}), bf16[32,2,96,128]{3,2,1,0:T(8,128)(2,1)S(1)}, u32[]{:S(2)}, u32[]{:S(2)}) async-start(bf16[32,2,96,128]{3,2,1,0:T(8,128)(2,1)} %bitcast.17), calls=%async_computation.1 | async-start | bytes 3145728 | tf_op jit(solution)/shard_map/gather/all_to_all | solution.py:37
  55.2 8.5 %collective-permute-start.2 = (bf16[768,128]{1,0:T(8,128)(2,1)S(1)}, bf16[768,128]{1,0:T(8,128)(2,1)S(1)}, u32[]{:S(2)}, u32[]{:S(2)}) collective-permute-start(bf16[768,128]{1,0:T(8,128)(2,1)S(1)} %get-tuple-element.7.refs_2_.refs_0_), channel_id=1, source_target_pairs={{0,132},{4,128},{128,4},{132,0},{256,388},{260,384},{384,260},{388... | collective-permute-start | bytes 589832 | tf_op jit(solution)/shard_map/gather/ppermute | solution.py:42
  58.8 9.4 %collective-permute-start.1 = (bf16[768,128]{1,0:T(8,128)(2,1)S(1)}, bf16[768,128]{1,0:T(8,128)(2,1)S(1)}, u32[]{:S(2)}, u32[]{:S(2)}) collective-permute-start(bf16[768,128]{1,0:T(8,128)(2,1)S(1)} %get-tuple-element.7.refs_2_.refs_0_), channel_id=1, source_target_pairs={{0,128},{4,132},{128,0},{132,4},{256,384},{260,388},{384,256},{388... | collective-permute-start | bytes 589832 | tf_op jit(solution)/shard_map/gather/ppermute | solution.py:42
  61.4 6.8 %collective-permute-start = (bf16[768,128]{1,0:T(8,128)(2,1)S(1)}, bf16[768,128]{1,0:T(8,128)(2,1)S(1)}, u32[]{:S(2)}, u32[]{:S(2)}) collective-permute-start(bf16[768,128]{1,0:T(8,128)(2,1)S(1)} %get-tuple-element.7.refs_2_.refs_0_), channel_id=1, source_target_pairs={{0,4},{4,0},{128,132},{132,128},{256,260},{260,256},{384,388},{388... | collective-permute-start | bytes 589832 | tf_op jit(solution)/shard_map/gather/ppermute | solution.py:42
  72.8 0.9 copy-start.1
  75.1 1.2 copy-start.2
  81.1 6.9 %collective-permute-start.3 = (bf16[2,80,768]{2,1,0:T(8,128)(2,1)S(1)}, bf16[2,80,768]{2,1,0:T(8,128)(2,1)S(1)}, u32[]{:S(2)}, u32[]{:S(2)}) collective-permute-start(bf16[2,80,768]{2,1,0:T(8,128)(2,1)S(1)} %attend.5), channel_id=1, source_target_pairs={{0,128},{4,132},{128,0},{132,4},{256,384},{260,388},{384,256},{388... | collective-permute-start | bytes 737288 | tf_op jit(solution)/shard_map/attend/ppermute | solution.py:42
  88.1 11.7 %collective-permute-start.4 = (bf16[80,768]{1,0:T(8,128)(2,1)S(1)}, bf16[80,768]{1,0:T(8,128)(2,1)S(1)}, u32[]{:S(2)}, u32[]{:S(2)}) collective-permute-start(bf16[80,768]{1,0:T(8,128)(2,1)S(1)} %combine.2), channel_id=1, source_target_pairs={{0,4},{4,0},{128,132},{132,128},{256,260},{260,256},{384,388},{388... | collective-permute-start | bytes 368648 | tf_op jit(solution)/shard_map/combine/ppermute | solution.py:42

commit v14 on v13

--- a/solution.py
+++ b/solution.py
@@ -236,11 +236,13 @@
         beside = from_partner(q, X_STEP)
         across = [from_partner(q, Y_STEP), from_partner(q, Y_STEP ^ X_STEP)]
     with jax.named_scope("attend"):
-        before = attend(across + [q, beside], [arrived], map_t)
+        ours = [q, beside]
+        before_across = attend(across, [arrived], map_t)
+        before_ours = attend(ours, [arrived], map_t)
         own = ((lax.axis_index("y") >> 1) * 2 + lax.axis_index("z0")).astype(jnp.int32)
-        others = [own.reshape(1), key_values, before]
-        there = from_partner(attend(across, others, map_t, 0), Y_STEP)
-        here = attend([q, beside], others, map_t, len(across))
+        others = [own.reshape(1), key_values]
+        there = from_partner(attend(across, others + [before_across], map_t, 0), Y_STEP)
+        here = attend(ours, others + [before_ours], map_t, 0)
     with jax.named_scope("combine"):
         share = pl.pallas_call(
             add_kernel,

time: 130 us -> 130 us (level)
    ppermute x5, waiting for transfers between devices: 6.92 us -> 8.85 us  [from_partner(): return lax.ppermute(x, QUERY_AXES, [(i, i ^ step) for i in range(size)])]
    pallas_call x3 -> x4, Pallas kernels: 14.2 us -> 14.2 us  [attend(): pl.pallas_call(functools.partial(attend_kernel, blocks, first_before), in...]
  transfers between devices with their start and end apart: 6 -> 6, of which waited for: 4 -> 5; matrix products, arithmetic and copies ran while one was open for 0% -> 0% of each run, Pallas kernels for 7% -> 7%
where the time goes in v14:
time: 130 us
  blocking collectives  76.8 us (59%)
  starting transfers between devices  23.1 us (18%)
  Pallas kernels  16.8 us (13%)
  waiting for transfers between devices  9.19 us (7%)
  local copies, waits for them, and re-layouts  3.79 us (3%)
    all_to_all x2, blocking collectives, exchange(): return lax.all_to_all(x, axes, 0, 0, tiled=True, axis_index_groups=sets)  73 us
    ppermute x5, starting transfers between devices, from_partner(): return lax.ppermute(x, QUERY_AXES, [(i, i ^ step) for i in range(size)])  18.9 us
    pallas_call x4, Pallas kernels, attend(): pl.pallas_call(functools.partial(attend_kernel, blocks, first_before), in...  14.2 us
    ppermute x5, waiting for transfers between devices, from_partner(): return lax.ppermute(x, QUERY_AXES, [(i, i ^ step) for i in range(size)])  8.85 us
    all_to_all x1, starting transfers between devices, exchange(): return lax.all_to_all(x, axes, 0, 0, tiled=True, axis_index_groups=sets)  4.21 us
    all_gather x1, blocking collectives, body(): velocity = jnp.sum(lax.all_gather(velocity, 'c', axis=0), axis=0)  3.78 us
    unnamed x12, local copies, waits for them, and re-layouts  2.95 us
  transfers between devices with their start and end apart: 6, of which 5 were waited for; matrix products, arithmetic and copies ran while one was open for 0% of the time, Pallas kernels for 7%

profile of v14, /device:TPU:1, one launch (start us, length us, event | category | flops | bytes accessed | tf_op | source)
XLA Modules:
  0.0 130.0 jit_solution(12736130144603308052)
XLA Ops:
  0.0 2.0 %pack.1 = bf16[8,3,96,128]{3,2,1,0:T(8,128)(2,1)} custom-call(bf16[96,640]{1,0:T(8,128)(2,1)} %qm.1, bf16[96,640]{1,0:T(8,128)(2,1)} %km.1, bf16[96,640]{1,0:T(8,128)(2,1)} %vm.1, bf16[96,384]{1,0:T(8,128)(2,1)} %qg.1, bf16[96,384]{1,0:T(8,128)(2,1)} %kg.1, bf16[96,384]{1,0:T(8,128)(2,1)} %vg.1), custom_call_target="tpu_custom_call" | custom-call | tf_op jit(solution)/shard_map/pack/pallas_call | solution.py:215
  2.0 47.6 %all_to_all.15.in_ref.refs_2_ = bf16[8,3,96,128]{3,2,1,0:T(8,128)(2,1)S(1)} all-to-all(bf16[8,3,96,128]{3,2,1,0:T(8,128)(2,1)} %pack.1), channel_id=1, replica_groups={{0,16,32,48,72,88,104,120},{8,24,40,56,64,80,96,112},{1,17,33,49,73,89,..., dimensions={0} | all-to-all | bytes 1179648 | tf_op jit(solution)/shard_map/to_heads/all_to_all | solution.py:37
  49.6 0.2 gather.1
  49.8 0.0 copy-start
  49.8 1.1 copy-done
  51.0 0.0 copy-start.3
  51.0 0.0 copy-start.4
  51.0 4.2 %all-to-all-start.1 = ((bf16[32,2,96,128]{3,2,1,0:T(8,128)(2,1)}), bf16[32,2,96,128]{3,2,1,0:T(8,128)(2,1)S(1)}, u32[]{:S(2)}, u32[]{:S(2)}) async-start(bf16[32,2,96,128]{3,2,1,0:T(8,128)(2,1)} %bitcast.17), calls=%async_computation.1 | async-start | bytes 3145728 | tf_op jit(solution)/shard_map/gather/all_to_all | solution.py:37
  55.2 3.1 %collective-permute-start = (bf16[768,128]{1,0:T(8,128)(2,1)S(1)}, bf16[768,128]{1,0:T(8,128)(2,1)S(1)}, u32[]{:S(2)}, u32[]{:S(2)}) collective-permute-start(bf16[768,128]{1,0:T(8,128)(2,1)S(1)} %get-tuple-element.7.refs_0_), channel_id=1, source_target_pairs={{0,4},{4,0},{128,132},{132,128},{256,260},{260,256},{384,388},{388... | collective-permute-start | bytes 589832 | tf_op jit(solution)/shard_map/gather/ppermute | solution.py:42
  58.3 0.0 copy-done.3
  58.3 0.0 copy-done.4
  58.4 2.7 %collective-permute-start.2 = (bf16[768,128]{1,0:T(8,128)(2,1)S(1)}, bf16[768,128]{1,0:T(8,128)(2,1)S(1)}, u32[]{:S(2)}, u32[]{:S(2)}) collective-permute-start(bf16[768,128]{1,0:T(8,128)(2,1)S(1)} %get-tuple-element.7.refs_0_), channel_id=1, source_target_pairs={{0,132},{4,128},{128,4},{132,0},{256,388},{260,384},{384,260},{388... | collective-permute-start | bytes 589832 | tf_op jit(solution)/shard_map/gather/ppermute | solution.py:42
  61.1 2.6 %collective-permute-start.1 = (bf16[768,128]{1,0:T(8,128)(2,1)S(1)}, bf16[768,128]{1,0:T(8,128)(2,1)S(1)}, u32[]{:S(2)}, u32[]{:S(2)}) collective-permute-start(bf16[768,128]{1,0:T(8,128)(2,1)S(1)} %get-tuple-element.7.refs_0_), channel_id=1, source_target_pairs={{0,128},{4,132},{128,0},{132,4},{256,384},{260,388},{384,256},{388... | collective-permute-start | bytes 589832 | tf_op jit(solution)/shard_map/gather/ppermute | solution.py:42
  63.7 0.0 collective-permute-done.refs_1_
  63.7 2.3 %attend.4.refs_5_ = f32[2,72,768]{2,1,0:T(8,128)S(1)} custom-call(bf16[768,128]{1,0:T(8,128)(2,1)S(1)} %get-tuple-element.7.refs_0_, bf16[768,128]{1,0:T(8,128)(2,1)S(1)} %collective-permute-done.refs_1_, bf16[8,3,96,128]{3,2,1,0:T(8,128)(2,1)S(1)} %all_to_all.15.in_ref.refs_2_, bf16[64,128]{1,0:T(8,128)(2,1)S(1)} %bitcast.19), custom_call_target="tpu_custom_call" | custom-call | flops 1207959552 | bytes 2097152 | tf_op jit(solution)/shard_map/attend/pallas_call | solution.py:154
  66.0 1.7 %collective-permute-done.2.refs_1_ = bf16[768,128]{1,0:T(8,128)(2,1)S(1)} collective-permute-done((bf16[768,128]{1,0:T(8,128)(2,1)S(1)}, bf16[768,128]{1,0:T(8,128)(2,1)S(1)}, u32[]{:S(2)}, u32[]{:S(2)}) %collective-permute-start.2) | collective-permute-done | bytes 196640 | tf_op jit(solution)/shard_map/gather/ppermute | solution.py:42
  67.7 4.0 %collective-permute-done.1.refs_0_ = bf16[768,128]{1,0:T(8,128)(2,1)S(1)} collective-permute-done((bf16[768,128]{1,0:T(8,128)(2,1)S(1)}, bf16[768,128]{1,0:T(8,128)(2,1)S(1)}, u32[]{:S(2)}, u32[]{:S(2)}) %collective-permute-start.1) | collective-permute-done | bytes 196640 | tf_op jit(solution)/shard_map/gather/ppermute | solution.py:42
  71.7 2.3 %attend.6.refs_5_ = f32[2,72,768]{2,1,0:T(8,128)S(1)} custom-call(bf16[768,128]{1,0:T(8,128)(2,1)S(1)} %collective-permute-done.1.refs_0_, bf16[768,128]{1,0:T(8,128)(2,1)S(1)} %collective-permute-done.2.refs_1_, bf16[8,3,96,128]{3,2,1,0:T(8,128)(2,1)S(1)} %all_to_all.15.in_ref.refs_2_, bf16[64,128]{1,0:T(8,128)(2,1)S(1)} %bitcast.20), custom_call_target="tpu_custom_call" | custom-call | flops 1207959552 | bytes 2097152 | tf_op jit(solution)/shard_map/attend/pallas_call | solution.py:154
  74.0 0.0 copy-start.1
  74.0 0.8 copy-done.1
  74.8 0.3 all-to-all-done.1.refs_3_
  75.1 0.0 copy-start.2
  75.1 1.0 copy-done.2
  76.1 4.8 %attend.7 = bf16[2,80,768]{2,1,0:T(8,128)(2,1)S(1)} custom-call(bf16[768,128]{1,0:T(8,128)(2,1)S(1)} %collective-permute-done.1.refs_0_, bf16[768,128]{1,0:T(8,128)(2,1)S(1)} %collective-permute-done.2.refs_1_, s32[1]{0:T(128)} %bitcast.1.refs_2_, bf16[32,2,96,128]{3,2,1,0:T(8,128)(2,1)S(1)} %all-to-all-done.1.refs_3_, bf16[64,128]{1,0:T(8,128)(2,1)S(1)} %bitcast.21, ...), custom_call_target="tpu_custom_call" | custom-call | flops 3623878656 | bytes 2097152 | tf_op jit(solution)/shard_map/attend/pallas_call | solution.py:154
  80.9 2.1 %collective-permute-start.3 = (bf16[2,80,768]{2,1,0:T(8,128)(2,1)S(1)}, bf16[2,80,768]{2,1,0:T(8,128)(2,1)S(1)}, u32[]{:S(2)}, u32[]{:S(2)}) collective-permute-start(bf16[2,80,768]{2,1,0:T(8,128)(2,1)S(1)} %attend.7), channel_id=1, source_target_pairs={{0,128},{4,132},{128,0},{132,4},{256,384},{260,388},{384,256},{388... | collective-permute-start | bytes 737288 | tf_op jit(solution)/shard_map/attend/ppermute | solution.py:42
  83.0 4.8 %attend.5.here_ref = bf16[2,80,768]{2,1,0:T(8,128)(2,1)S(1)} custom-call(bf16[768,128]{1,0:T(8,128)(2,1)S(1)} %get-tuple-element.7.refs_0_, bf16[768,128]{1,0:T(8,128)(2,1)S(1)} %collective-permute-done.refs_1_, s32[1]{0:T(128)} %bitcast.1.refs_2_, bf16[32,2,96,128]{3,2,1,0:T(8,128)(2,1)S(1)} %all-to-all-done.1.refs_3_, bf16[64,128]{1,0:T(8,128)(2,1)S(1)} %bitcast.22, ...), custom_call_target="tpu_custom_call" | custom-call | flops 3623878656 | bytes 2097152 | tf_op jit(solution)/shard_map/attend/pallas_call | solution.py:154
  87.8 0.9 collective-permute-done.3.there_ref
  88.8 0.1 combine.2
  88.8 8.5 %collective-permute-start.4 = (bf16[80,768]{1,0:T(8,128)(2,1)S(1)}, bf16[80,768]{1,0:T(8,128)(2,1)S(1)}, u32[]{:S(2)}, u32[]{:S(2)}) collective-permute-start(bf16[80,768]{1,0:T(8,128)(2,1)S(1)} %combine.2), channel_id=1, source_target_pairs={{0,4},{4,0},{128,132},{132,128},{256,260},{260,256},{384,388},{388... | collective-permute-start | bytes 368648 | tf_op jit(solution)/shard_map/combine/ppermute | solution.py:42
  97.4 2.2 %collective-permute-done.4.beside_ref = bf16[80,768]{1,0:T(8,128)(2,1)S(1)} collective-permute-done((bf16[80,768]{1,0:T(8,128)(2,1)S(1)}, bf16[80,768]{1,0:T(8,128)(2,1)S(1)}, u32[]{:S(2)}, u32[]{:S(2)}) %collective-permute-start.4) | collective-permute-done | bytes 122912 | tf_op jit(solution)/shard_map/combine/ppermute | solution.py:42
  99.6 0.3 combine.3
  99.9 25.4 %all_to_all.16 = bf16[16,48,128]{2,1,0:T(8,128)(2,1)S(1)} all-to-all(bf16[16,48,128]{2,1,0:T(8,128)(2,1)S(1)} %bitcast.18), channel_id=1, replica_groups={{0,2,16,18,32,34,48,50,72,74,88,90,104,106,120,122},{8,10,24,26,40,42,5..., dimensions={0} | all-to-all | bytes 393216 | tf_op jit(solution)/shard_map/to_tokens/all_to_all | solution.py:37
  125.4 3.8 %all-gather = f32[96,128]{1,0:T(8,128)S(1)} all-gather(f32[48,128]{1,0:T(8,128)S(1)} %convert_reduce_fusion), channel_id=2, replica_groups=mesh['y'=4,'zh'=8,'z0'=2,'xl'=2,'xh'=2,'c'=2] {'c'}, dimensions={0}, use_global_device_ids=true | all-gather | bytes 73728 | tf_op jit(solution)/shard_map/to_tokens/all_gather | solution.py:265
  129.2 0.1 reshape.26
  129.3 0.7 copy.15
  (7 shorter events, 0.1 us)
Async XLA Ops:
  49.8 1.1 copy-start
  51.0 7.3 %copy-start.3 = (bf16[640,64]{0,1:T(8,128)(2,1)S(1)}, bf16[640,64]{0,1:T(8,128)(2,1)}, u32[]{:S(2)}) copy-start(bf16[640,64]{0,1:T(8,128)(2,1)} %param.14) | copy-start | bytes 245764
  51.0 7.3 %copy-start.4 = (bf16[384,64]{0,1:T(8,128)(2,1)S(1)}, bf16[384,64]{0,1:T(8,128)(2,1)}, u32[]{:S(2)}) copy-start(bf16[384,64]{0,1:T(8,128)(2,1)} %param.15) | copy-start | bytes 147460
  51.0 24.1 %all-to-all-start.1 = ((bf16[32,2,96,128]{3,2,1,0:T(8,128)(2,1)}), bf16[32,2,96,128]{3,2,1,0:T(8,128)(2,1)S(1)}, u32[]{:S(2)}, u32[]{:S(2)}) async-start(bf16[32,2,96,128]{3,2,1,0:T(8,128)(2,1)} %bitcast.17), calls=%async_computation.1 | async-start | bytes 3145728 | tf_op jit(solution)/shard_map/gather/all_to_all | solution.py:37
  55.2 8.5 %collective-permute-start = (bf16[768,128]{1,0:T(8,128)(2,1)S(1)}, bf16[768,128]{1,0:T(8,128)(2,1)S(1)}, u32[]{:S(2)}, u32[]{:S(2)}) collective-permute-start(bf16[768,128]{1,0:T(8,128)(2,1)S(1)} %get-tuple-element.7.refs_0_), channel_id=1, source_target_pairs={{0,4},{4,0},{128,132},{132,128},{256,260},{260,256},{384,388},{388... | collective-permute-start | bytes 589832 | tf_op jit(solution)/shard_map/gather/ppermute | solution.py:42
  58.4 9.3 %collective-permute-start.2 = (bf16[768,128]{1,0:T(8,128)(2,1)S(1)}, bf16[768,128]{1,0:T(8,128)(2,1)S(1)}, u32[]{:S(2)}, u32[]{:S(2)}) collective-permute-start(bf16[768,128]{1,0:T(8,128)(2,1)S(1)} %get-tuple-element.7.refs_0_), channel_id=1, source_target_pairs={{0,132},{4,128},{128,4},{132,0},{256,388},{260,384},{384,260},{388... | collective-permute-start | bytes 589832 | tf_op jit(solution)/shard_map/gather/ppermute | solution.py:42
  61.1 10.6 %collective-permute-start.1 = (bf16[768,128]{1,0:T(8,128)(2,1)S(1)}, bf16[768,128]{1,0:T(8,128)(2,1)S(1)}, u32[]{:S(2)}, u32[]{:S(2)}) collective-permute-start(bf16[768,128]{1,0:T(8,128)(2,1)S(1)} %get-tuple-element.7.refs_0_), channel_id=1, source_target_pairs={{0,128},{4,132},{128,0},{132,4},{256,384},{260,388},{384,256},{388... | collective-permute-start | bytes 589832 | tf_op jit(solution)/shard_map/gather/ppermute | solution.py:42
  74.0 0.8 copy-start.1
  75.1 1.0 copy-start.2
  80.9 7.8 %collective-permute-start.3 = (bf16[2,80,768]{2,1,0:T(8,128)(2,1)S(1)}, bf16[2,80,768]{2,1,0:T(8,128)(2,1)S(1)}, u32[]{:S(2)}, u32[]{:S(2)}) collective-permute-start(bf16[2,80,768]{2,1,0:T(8,128)(2,1)S(1)} %attend.7), channel_id=1, source_target_pairs={{0,128},{4,132},{128,0},{132,4},{256,384},{260,388},{384,256},{388... | collective-permute-start | bytes 737288 | tf_op jit(solution)/shard_map/attend/ppermute | solution.py:42
  88.8 10.8 %collective-permute-start.4 = (bf16[80,768]{1,0:T(8,128)(2,1)S(1)}, bf16[80,768]{1,0:T(8,128)(2,1)S(1)}, u32[]{:S(2)}, u32[]{:S(2)}) collective-permute-start(bf16[80,768]{1,0:T(8,128)(2,1)S(1)} %combine.2), channel_id=1, source_target_pairs={{0,4},{4,0},{128,132},{132,128},{256,260},{260,256},{384,388},{388... | collective-permute-start | bytes 368648 | tf_op jit(solution)/shard_map/combine/ppermute | solution.py:42

commit v15 on v13

--- a/solution.py
+++ b/solution.py
@@ -46,11 +46,17 @@
     return lax.dot_general(a, b, (((1,), (1,)), ((), ())), preferred_element_type=F32)
 
 
-def pack_kernel(main_heads, guide_heads, qm, km, vm, qg, kg, vg, out_ref):
+def pack_kernel(main_heads, guide_heads, qm, km, vm, qg, kg, vg, out_ref, done):
+    copies = []
     for h in range(main_heads + guide_heads):
         at = (h if h < main_heads else h - main_heads) * HD
         for t, ref in enumerate((qm, km, vm) if h < main_heads else (qg, kg, vg)):
-            out_ref[h, t] = ref[:, at : at + HD]
+            source = ref.at[:, at : at + HD]
+            copies.append(pltpu.make_async_copy(source, out_ref.at[h, t], done.at[h, t]))
+    for copy in copies:
+        copy.start()
+    for copy in copies:
+        copy.wait()
 
 
 def copy_kernel(in_ref, q_ref, copies_ref):
@@ -214,9 +220,10 @@
     with jax.named_scope("pack"):
         packed = pl.pallas_call(
             functools.partial(pack_kernel, main_heads, guide_heads),
-            in_specs=[VMEM] * 6,
-            out_specs=VMEM,
+            in_specs=[pl.BlockSpec(memory_space=pl.ANY)] * 6,
+            out_specs=pl.BlockSpec(memory_space=pl.ANY),
             out_shape=jax.ShapeDtypeStruct((heads, 3, tokens_here, HD), BF16),
+            scratch_shapes=[pltpu.SemaphoreType.DMA((heads, 3))],
         )(query_main, key_main, value_main, query_guide, key_guide, value_guide)
     with jax.named_scope("to_heads"):
         arrived = exchange(packed, Z, PLANE_SETS)

time: 130 us -> 147 us (1.13)
  Pallas kernels: 16.8 us -> 34 us
    pallas_call x1, Pallas kernels: 2.04 us -> 19.2 us  [body(): pl.pallas_call(functools.partial(pack_kernel, main_heads, guide_heads), i...]
  transfers between devices with their start and end apart: 6 -> 6, of which waited for: 4 -> 4; matrix products, arithmetic and copies ran while one was open for 0% -> 0% of each run, Pallas kernels for 7% -> 6%
where the time goes in v15:
time: 147 us; the launch traced here: 146 us
  blocking collectives  75.9 us (52%)
  Pallas kernels  34 us (23%)
  starting transfers between devices  23.9 us (16%)
  waiting for transfers between devices  8.3 us (6%)
  local copies, waits for them, and re-layouts  4.09 us (3%)
    all_to_all x2, blocking collectives, exchange(): return lax.all_to_all(x, axes, 0, 0, tiled=True, axis_index_groups=sets)  72 us
    ppermute x5, starting transfers between devices, from_partner(): return lax.ppermute(x, QUERY_AXES, [(i, i ^ step) for i in range(size)])  19.7 us
    pallas_call x1, Pallas kernels, body(): pl.pallas_call(functools.partial(pack_kernel, main_heads, guide_heads), i...  19.2 us
    pallas_call x3, Pallas kernels, attend(): pl.pallas_call(functools.partial(attend_kernel, blocks, first_before), in...  14.2 us
    ppermute x5, waiting for transfers between devices, from_partner(): return lax.ppermute(x, QUERY_AXES, [(i, i ^ step) for i in range(size)])  6.92 us
    all_to_all x1, starting transfers between devices, exchange(): return lax.all_to_all(x, axes, 0, 0, tiled=True, axis_index_groups=sets)  4.21 us
    all_gather x1, blocking collectives, body(): velocity = jnp.sum(lax.all_gather(velocity, 'c', axis=0), axis=0)  3.96 us
    unnamed x12, local copies, waits for them, and re-layouts  3.25 us
  transfers between devices with their start and end apart: 6, of which 4 were waited for; matrix products, arithmetic and copies ran while one was open for 0% of the time, Pallas kernels for 6%

profile of v15, /device:TPU:1, one launch (start us, length us, event | category | flops | bytes accessed | tf_op | source)
XLA Modules:
  0.0 146.4 jit_solution(13215021332626847990)
XLA Ops:
  0.0 19.2 %pack.1 = bf16[8,3,96,128]{3,2,1,0:T(8,128)(2,1)} custom-call(bf16[96,640]{1,0:T(8,128)(2,1)} %qm.1, bf16[96,640]{1,0:T(8,128)(2,1)} %km.1, bf16[96,640]{1,0:T(8,128)(2,1)} %vm.1, bf16[96,384]{1,0:T(8,128)(2,1)} %qg.1, bf16[96,384]{1,0:T(8,128)(2,1)} %kg.1, bf16[96,384]{1,0:T(8,128)(2,1)} %vg.1), custom_call_target="tpu_custom_call" | custom-call | tf_op jit(solution)/shard_map/pack/pallas_call | solution.py:221
  19.2 47.6 %all_to_all.15.in_ref.refs_4_ = bf16[8,3,96,128]{3,2,1,0:T(8,128)(2,1)S(1)} all-to-all(bf16[8,3,96,128]{3,2,1,0:T(8,128)(2,1)} %pack.1), channel_id=1, replica_groups={{0,16,32,48,72,88,104,120},{8,24,40,56,64,80,96,112},{1,17,33,49,73,89,..., dimensions={0} | all-to-all | bytes 1179648 | tf_op jit(solution)/shard_map/to_heads/all_to_all | solution.py:37
  66.8 0.2 gather.1
  67.0 0.0 copy-start
  67.0 1.1 copy-done
  68.1 0.0 copy-start.3
  68.2 0.0 copy-start.4
  68.2 4.2 %all-to-all-start.1 = ((bf16[32,2,96,128]{3,2,1,0:T(8,128)(2,1)}), bf16[32,2,96,128]{3,2,1,0:T(8,128)(2,1)S(1)}, u32[]{:S(2)}, u32[]{:S(2)}) async-start(bf16[32,2,96,128]{3,2,1,0:T(8,128)(2,1)} %bitcast.17), calls=%async_computation.1 | async-start | bytes 3145728 | tf_op jit(solution)/shard_map/gather/all_to_all | solution.py:37
  72.4 3.6 %collective-permute-start.2 = (bf16[768,128]{1,0:T(8,128)(2,1)S(1)}, bf16[768,128]{1,0:T(8,128)(2,1)S(1)}, u32[]{:S(2)}, u32[]{:S(2)}) collective-permute-start(bf16[768,128]{1,0:T(8,128)(2,1)S(1)} %get-tuple-element.7.refs_2_.refs_0_), channel_id=1, source_target_pairs={{0,132},{4,128},{128,4},{132,0},{256,388},{260,384},{384,260},{388... | collective-permute-start | bytes 589832 | tf_op jit(solution)/shard_map/gather/ppermute | solution.py:42
  76.0 2.6 %collective-permute-start.1 = (bf16[768,128]{1,0:T(8,128)(2,1)S(1)}, bf16[768,128]{1,0:T(8,128)(2,1)S(1)}, u32[]{:S(2)}, u32[]{:S(2)}) collective-permute-start(bf16[768,128]{1,0:T(8,128)(2,1)S(1)} %get-tuple-element.7.refs_2_.refs_0_), channel_id=1, source_target_pairs={{0,128},{4,132},{128,0},{132,4},{256,384},{260,388},{384,256},{388... | collective-permute-start | bytes 589832 | tf_op jit(solution)/shard_map/gather/ppermute | solution.py:42
  78.6 2.2 %collective-permute-start = (bf16[768,128]{1,0:T(8,128)(2,1)S(1)}, bf16[768,128]{1,0:T(8,128)(2,1)S(1)}, u32[]{:S(2)}, u32[]{:S(2)}) collective-permute-start(bf16[768,128]{1,0:T(8,128)(2,1)S(1)} %get-tuple-element.7.refs_2_.refs_0_), channel_id=1, source_target_pairs={{0,4},{4,0},{128,132},{132,128},{256,260},{260,256},{384,388},{388... | collective-permute-start | bytes 589832 | tf_op jit(solution)/shard_map/gather/ppermute | solution.py:42
  80.7 0.0 copy-done.3
  80.8 0.0 copy-done.4
  80.9 0.0 collective-permute-done.2.refs_1_
  80.9 4.5 %collective-permute-done.1.refs_0_ = bf16[768,128]{1,0:T(8,128)(2,1)S(1)} collective-permute-done((bf16[768,128]{1,0:T(8,128)(2,1)S(1)}, bf16[768,128]{1,0:T(8,128)(2,1)S(1)}, u32[]{:S(2)}, u32[]{:S(2)}) %collective-permute-start.1) | collective-permute-done | bytes 196640 | tf_op jit(solution)/shard_map/gather/ppermute | solution.py:42
  85.4 0.0 collective-permute-done.refs_3_.refs_1_
  85.4 4.6 %attend.3.refs_5_ = f32[4,72,768]{2,1,0:T(8,128)S(1)} custom-call(bf16[768,128]{1,0:T(8,128)(2,1)S(1)} %collective-permute-done.1.refs_0_, bf16[768,128]{1,0:T(8,128)(2,1)S(1)} %collective-permute-done.2.refs_1_, bf16[768,128]{1,0:T(8,128)(2,1)S(1)} %get-tuple-element.7.refs_2_.refs_0_, bf16[768,128]{1,0:T(8,128)(2,1)S(1)} %collective-permute-done.refs_3_.refs_1_, ...), custom_call_target="tpu_custom_call" | custom-call | flops 2415919104 | bytes 2097152 | tf_op jit(solution)/shard_map/attend/pallas_call | solution.py:160
  90.0 0.0 copy-start.1
  90.0 0.9 copy-done.1
  90.9 1.4 all-to-all-done.1.refs_3_
  92.3 0.0 copy-start.2
  92.3 1.2 copy-done.2
  93.4 4.8 %attend.5 = bf16[2,80,768]{2,1,0:T(8,128)(2,1)S(1)} custom-call(bf16[768,128]{1,0:T(8,128)(2,1)S(1)} %collective-permute-done.1.refs_0_, bf16[768,128]{1,0:T(8,128)(2,1)S(1)} %collective-permute-done.2.refs_1_, s32[1]{0:T(128)} %bitcast.1.refs_2_, bf16[32,2,96,128]{3,2,1,0:T(8,128)(2,1)S(1)} %all-to-all-done.1.refs_3_, bf16[64,128]{1,0:T(8,128)(2,1)S(1)} %bitcast.20, ...), custom_call_target="tpu_custom_call" | custom-call | flops 3623878656 | bytes 2097152 | tf_op jit(solution)/shard_map/attend/pallas_call | solution.py:160
  98.3 1.9 %collective-permute-start.3 = (bf16[2,80,768]{2,1,0:T(8,128)(2,1)S(1)}, bf16[2,80,768]{2,1,0:T(8,128)(2,1)S(1)}, u32[]{:S(2)}, u32[]{:S(2)}) collective-permute-start(bf16[2,80,768]{2,1,0:T(8,128)(2,1)S(1)} %attend.5), channel_id=1, source_target_pairs={{0,128},{4,132},{128,0},{132,4},{256,384},{260,388},{384,256},{388... | collective-permute-start | bytes 737288 | tf_op jit(solution)/shard_map/attend/ppermute | solution.py:42
  100.2 4.8 %attend.4.here_ref = bf16[2,80,768]{2,1,0:T(8,128)(2,1)S(1)} custom-call(bf16[768,128]{1,0:T(8,128)(2,1)S(1)} %get-tuple-element.7.refs_2_.refs_0_, bf16[768,128]{1,0:T(8,128)(2,1)S(1)} %collective-permute-done.refs_3_.refs_1_, s32[1]{0:T(128)} %bitcast.1.refs_2_, bf16[32,2,96,128]{3,2,1,0:T(8,128)(2,1)S(1)} %all-to-all-done.1.refs_3_, ...), custom_call_target="tpu_custom_call" | custom-call | flops 3623878656 | bytes 2097152 | tf_op jit(solution)/shard_map/attend/pallas_call | solution.py:160
  105.0 0.2 collective-permute-done.3.there_ref
  105.2 0.1 combine.2
  105.3 9.4 %collective-permute-start.4 = (bf16[80,768]{1,0:T(8,128)(2,1)S(1)}, bf16[80,768]{1,0:T(8,128)(2,1)S(1)}, u32[]{:S(2)}, u32[]{:S(2)}) collective-permute-start(bf16[80,768]{1,0:T(8,128)(2,1)S(1)} %combine.2), channel_id=1, source_target_pairs={{0,4},{4,0},{128,132},{132,128},{256,260},{260,256},{384,388},{388... | collective-permute-start | bytes 368648 | tf_op jit(solution)/shard_map/combine/ppermute | solution.py:42
  114.7 2.2 %collective-permute-done.4.beside_ref = bf16[80,768]{1,0:T(8,128)(2,1)S(1)} collective-permute-done((bf16[80,768]{1,0:T(8,128)(2,1)S(1)}, bf16[80,768]{1,0:T(8,128)(2,1)S(1)}, u32[]{:S(2)}, u32[]{:S(2)}) %collective-permute-start.4) | collective-permute-done | bytes 122912 | tf_op jit(solution)/shard_map/combine/ppermute | solution.py:42
  116.9 0.3 combine.3
  117.2 24.4 %all_to_all.16 = bf16[16,48,128]{2,1,0:T(8,128)(2,1)S(1)} all-to-all(bf16[16,48,128]{2,1,0:T(8,128)(2,1)S(1)} %bitcast.18), channel_id=1, replica_groups={{0,2,16,18,32,34,48,50,72,74,88,90,104,106,120,122},{8,10,24,26,40,42,5..., dimensions={0} | all-to-all | bytes 393216 | tf_op jit(solution)/shard_map/to_tokens/all_to_all | solution.py:37
  141.6 4.0 %all-gather = f32[96,128]{1,0:T(8,128)S(1)} all-gather(f32[48,128]{1,0:T(8,128)S(1)} %convert_reduce_fusion), channel_id=2, replica_groups=mesh['y'=4,'zh'=8,'z0'=2,'xl'=2,'xh'=2,'c'=2] {'c'}, dimensions={0}, use_global_device_ids=true | all-gather | bytes 73728 | tf_op jit(solution)/shard_map/to_tokens/all_gather | solution.py:270
  145.6 0.1 reshape.26
  145.7 0.7 copy.15
  (7 shorter events, 0.1 us)
Async XLA Ops:
  67.0 1.1 copy-start
  68.1 12.6 %copy-start.3 = (bf16[640,64]{0,1:T(8,128)(2,1)S(1)}, bf16[640,64]{0,1:T(8,128)(2,1)}, u32[]{:S(2)}) copy-start(bf16[640,64]{0,1:T(8,128)(2,1)} %param.14) | copy-start | bytes 245764
  68.2 12.6 %copy-start.4 = (bf16[384,64]{0,1:T(8,128)(2,1)S(1)}, bf16[384,64]{0,1:T(8,128)(2,1)}, u32[]{:S(2)}) copy-start(bf16[384,64]{0,1:T(8,128)(2,1)} %param.15) | copy-start | bytes 147460
  68.2 24.1 %all-to-all-start.1 = ((bf16[32,2,96,128]{3,2,1,0:T(8,128)(2,1)}), bf16[32,2,96,128]{3,2,1,0:T(8,128)(2,1)S(1)}, u32[]{:S(2)}, u32[]{:S(2)}) async-start(bf16[32,2,96,128]{3,2,1,0:T(8,128)(2,1)} %bitcast.17), calls=%async_computation.1 | async-start | bytes 3145728 | tf_op jit(solution)/shard_map/gather/all_to_all | solution.py:37
  72.4 8.5 %collective-permute-start.2 = (bf16[768,128]{1,0:T(8,128)(2,1)S(1)}, bf16[768,128]{1,0:T(8,128)(2,1)S(1)}, u32[]{:S(2)}, u32[]{:S(2)}) collective-permute-start(bf16[768,128]{1,0:T(8,128)(2,1)S(1)} %get-tuple-element.7.refs_2_.refs_0_), channel_id=1, source_target_pairs={{0,132},{4,128},{128,4},{132,0},{256,388},{260,384},{384,260},{388... | collective-permute-start | bytes 589832 | tf_op jit(solution)/shard_map/gather/ppermute | solution.py:42
  76.0 9.4 %collective-permute-start.1 = (bf16[768,128]{1,0:T(8,128)(2,1)S(1)}, bf16[768,128]{1,0:T(8,128)(2,1)S(1)}, u32[]{:S(2)}, u32[]{:S(2)}) collective-permute-start(bf16[768,128]{1,0:T(8,128)(2,1)S(1)} %get-tuple-element.7.refs_2_.refs_0_), channel_id=1, source_target_pairs={{0,128},{4,132},{128,0},{132,4},{256,384},{260,388},{384,256},{388... | collective-permute-start | bytes 589832 | tf_op jit(solution)/shard_map/gather/ppermute | solution.py:42
  78.6 6.8 %collective-permute-start = (bf16[768,128]{1,0:T(8,128)(2,1)S(1)}, bf16[768,128]{1,0:T(8,128)(2,1)S(1)}, u32[]{:S(2)}, u32[]{:S(2)}) collective-permute-start(bf16[768,128]{1,0:T(8,128)(2,1)S(1)} %get-tuple-element.7.refs_2_.refs_0_), channel_id=1, source_target_pairs={{0,4},{4,0},{128,132},{132,128},{256,260},{260,256},{384,388},{388... | collective-permute-start | bytes 589832 | tf_op jit(solution)/shard_map/gather/ppermute | solution.py:42
  90.0 0.9 copy-start.1
  92.3 1.2 copy-start.2
  98.3 6.9 %collective-permute-start.3 = (bf16[2,80,768]{2,1,0:T(8,128)(2,1)S(1)}, bf16[2,80,768]{2,1,0:T(8,128)(2,1)S(1)}, u32[]{:S(2)}, u32[]{:S(2)}) collective-permute-start(bf16[2,80,768]{2,1,0:T(8,128)(2,1)S(1)} %attend.5), channel_id=1, source_target_pairs={{0,128},{4,132},{128,0},{132,4},{256,384},{260,388},{384,256},{388... | collective-permute-start | bytes 737288 | tf_op jit(solution)/shard_map/attend/ppermute | solution.py:42
  105.3 11.7 %collective-permute-start.4 = (bf16[80,768]{1,0:T(8,128)(2,1)S(1)}, bf16[80,768]{1,0:T(8,128)(2,1)S(1)}, u32[]{:S(2)}, u32[]{:S(2)}) collective-permute-start(bf16[80,768]{1,0:T(8,128)(2,1)S(1)} %combine.2), channel_id=1, source_target_pairs={{0,4},{4,0},{128,132},{132,128},{256,260},{260,256},{384,388},{388... | collective-permute-start | bytes 368648 | tf_op jit(solution)/shard_map/combine/ppermute | solution.py:42

commit v16 on v11

--- a/solution.py
+++ b/solution.py
@@ -24,10 +24,10 @@
 GRP = ("xh", "c")
 Z = ("zh", "z0")
 PLANE_SETS = ([0, 2, 4, 6, 9, 11, 13, 15], [1, 3, 5, 7, 8, 10, 12, 14])
-QUERY_AXES = ("y", "z0")
-Z0_STEP, Y_STEP = 1, 6
-KEY_AXES = ("y", "xl")
-KEY_STEPS = (1, 2, 3)
+QUERY_AXES = ("y", "xl")
+X_STEP, Y_STEP = 1, 2
+KEY_AXES = ("y", "z0")
+KEY_STEPS = (1, 6, 7)
 SIDES = 2
 PLANE_AXES = Z + ("xh",)
 SIDE_SETS = [[SIDES * z + x for z in planes for x in range(SIDES)] for planes in PLANE_SETS]
@@ -198,8 +198,8 @@
             compiler_params=SMALL,
         )(arrived)
         key_values = [kv] + [from_partner(kv, step, KEY_AXES) for step in KEY_STEPS]
-        beside = from_partner(q, Z0_STEP)
-        across = [from_partner(q, Y_STEP), from_partner(q, Y_STEP ^ Z0_STEP)]
+        beside = from_partner(q, X_STEP)
+        across = [from_partner(q, Y_STEP), from_partner(q, Y_STEP ^ X_STEP)]
     with jax.named_scope("attend"):
         there = from_partner(attend(across, key_values, map_t), Y_STEP)
         here = attend([q, beside], key_values, map_t)
@@ -217,7 +217,7 @@
             out_specs=VMEM,
             out_shape=jax.ShapeDtypeStruct((heads, SIDES, tokens_here // 2, 2 * CH), BF16),
             compiler_params=SMALL,
-        )(gain, here, there, from_partner(share, Z0_STEP))
+        )(gain, here, there, from_partner(share, X_STEP))
     with jax.named_scope("to_tokens"):
         velocity = velocity.reshape((heads * SIDES,) + velocity.shape[2:])
         velocity = exchange(velocity, PLANE_AXES, SIDE_SETS)

time: 135 us -> 129 us (0.956)
  blocking collectives: 82 us -> 76.6 us
  waiting for transfers between devices: 7.94 us -> 4.49 us
  starting transfers between devices: 29.3 us -> 31.7 us
    all_gather x1, blocking collectives: 10.2 us -> 4.67 us  [body(): velocity = jnp.sum(lax.all_gather(velocity, 'c', axis=0), axis=0)]
    ppermute x8, waiting for transfers between devices: 7.94 us -> 4.49 us  [from_partner(): lax.ppermute(x, axes, [(i, i ^ step) for i in range(lax.axis_size(axes))])]
    ppermute x8, starting transfers between devices: 29.3 us -> 31.7 us  [from_partner(): lax.ppermute(x, axes, [(i, i ^ step) for i in range(lax.axis_size(axes))])]
where the time goes in v16:
time: 129 us; the launch traced here: 128 us
  blocking collectives  76.6 us (59%)
  starting transfers between devices  31.7 us (25%)
  Pallas kernels  14.4 us (11%)
  waiting for transfers between devices  4.49 us (3%)
    all_to_all x2, blocking collectives, exchange(): return lax.all_to_all(x, axes, 0, 0, tiled=True, axis_index_groups=sets)  71.9 us
    ppermute x8, starting transfers between devices, from_partner(): lax.ppermute(x, axes, [(i, i ^ step) for i in range(lax.axis_size(axes))])  31.7 us
    pallas_call x2, Pallas kernels, attend(): pl.pallas_call(functools.partial(attend_kernel, blocks), in_specs=[VMEM]...  12 us
    all_gather x1, blocking collectives, body(): velocity = jnp.sum(lax.all_gather(velocity, 'c', axis=0), axis=0)  4.67 us
    ppermute x8, waiting for transfers between devices, from_partner(): lax.ppermute(x, axes, [(i, i ^ step) for i in range(lax.axis_size(axes))])  4.49 us
  transfers between devices with their start and end apart: 8, of which 3 were waited for; matrix products, arithmetic and copies ran while one was open for 0% of the time, Pallas kernels for 9%

profile of v16, /device:TPU:1, one launch (start us, length us, event | category | flops | bytes accessed | tf_op | source)
XLA Modules:
  0.0 128.2 jit_solution(7367516563989093803)
XLA Ops:
  0.0 2.1 %pack.1 = bf16[8,3,96,128]{3,2,1,0:T(8,128)(2,1)} custom-call(bf16[96,640]{1,0:T(8,128)(2,1)} %qm.1, bf16[96,640]{1,0:T(8,128)(2,1)} %km.1, bf16[96,640]{1,0:T(8,128)(2,1)} %vm.1, bf16[96,384]{1,0:T(8,128)(2,1)} %qg.1, bf16[96,384]{1,0:T(8,128)(2,1)} %kg.1, bf16[96,384]{1,0:T(8,128)(2,1)} %vg.1), custom_call_target="tpu_custom_call" | custom-call | tf_op jit(solution)/shard_map/pack/pallas_call | solution.py:181
  2.1 47.6 %all_to_all.10.in_ref = bf16[8,3,96,128]{3,2,1,0:T(8,128)(2,1)S(1)} all-to-all(bf16[8,3,96,128]{3,2,1,0:T(8,128)(2,1)} %pack.1), channel_id=1, replica_groups={{0,16,32,48,72,88,104,120},{8,24,40,56,64,80,96,112},{1,17,33,49,73,89,..., dimensions={0} | all-to-all | bytes 1179648 | tf_op jit(solution)/shard_map/to_heads/all_to_all | solution.py:37
  49.6 0.0 copy-start
  49.6 0.0 copy-start.1
  49.7 2.4 %collective-permute-start.1 = (bf16[8,2,96,128]{3,2,1,0:T(8,128)(2,1)S(1)}, bf16[8,2,96,128]{3,2,1,0:T(8,128)(2,1)S(1)}, u32[]{:S(2)}, u32[]{:S(2)}) collective-permute-start(bf16[8,2,96,128]{3,2,1,0:T(8,128)(2,1)S(1)} %get-tuple-element.8.refs_2_), channel_id=1, source_target_pairs={{0,8},{8,0},{128,136},{136,128},{256,264},{264,256},{384,392},{392... | collective-permute-start | bytes 1179656 | tf_op jit(solution)/shard_map/gather/ppermute | solution.py:41
  52.1 4.6 %collective-permute-start.2 = (bf16[8,2,96,128]{3,2,1,0:T(8,128)(2,1)S(1)}, bf16[8,2,96,128]{3,2,1,0:T(8,128)(2,1)S(1)}, u32[]{:S(2)}, u32[]{:S(2)}) collective-permute-start(bf16[8,2,96,128]{3,2,1,0:T(8,128)(2,1)S(1)} %get-tuple-element.8.refs_2_), channel_id=1, source_target_pairs={{0,384},{8,392},{128,256},{136,264},{256,128},{264,136},{384,0},{3... | collective-permute-start | bytes 1179656 | tf_op jit(solution)/shard_map/gather/ppermute | solution.py:41
  56.7 2.7 %collective-permute-start.3 = (bf16[8,2,96,128]{3,2,1,0:T(8,128)(2,1)S(1)}, bf16[8,2,96,128]{3,2,1,0:T(8,128)(2,1)S(1)}, u32[]{:S(2)}, u32[]{:S(2)}) collective-permute-start(bf16[8,2,96,128]{3,2,1,0:T(8,128)(2,1)S(1)} %get-tuple-element.8.refs_2_), channel_id=1, source_target_pairs={{0,392},{8,384},{128,264},{136,256},{256,136},{264,128},{384,8},{3... | collective-permute-start | bytes 1179656 | tf_op jit(solution)/shard_map/gather/ppermute | solution.py:41
  59.5 1.9 %collective-permute-start.4 = (bf16[768,128]{1,0:T(8,128)(2,1)S(1)}, bf16[768,128]{1,0:T(8,128)(2,1)S(1)}, u32[]{:S(2)}, u32[]{:S(2)}) collective-permute-start(bf16[768,128]{1,0:T(8,128)(2,1)S(1)} %get-tuple-element.7.refs_0_), channel_id=1, source_target_pairs={{0,128},{4,132},{128,0},{132,4},{256,384},{260,388},{384,256},{388... | collective-permute-start | bytes 589832 | tf_op jit(solution)/shard_map/gather/ppermute | solution.py:41
  61.4 4.3 %collective-permute-start.5 = (bf16[768,128]{1,0:T(8,128)(2,1)S(1)}, bf16[768,128]{1,0:T(8,128)(2,1)S(1)}, u32[]{:S(2)}, u32[]{:S(2)}) collective-permute-start(bf16[768,128]{1,0:T(8,128)(2,1)S(1)} %get-tuple-element.7.refs_0_), channel_id=1, source_target_pairs={{0,132},{4,128},{128,4},{132,0},{256,388},{260,384},{384,260},{388... | collective-permute-start | bytes 589832 | tf_op jit(solution)/shard_map/gather/ppermute | solution.py:41
  65.7 0.0 copy-done
  65.7 0.0 copy-done.1
  65.9 0.3 collective-permute-done.4.refs_0_
  66.2 3.1 %collective-permute-start = (bf16[768,128]{1,0:T(8,128)(2,1)S(1)}, bf16[768,128]{1,0:T(8,128)(2,1)S(1)}, u32[]{:S(2)}, u32[]{:S(2)}) collective-permute-start(bf16[768,128]{1,0:T(8,128)(2,1)S(1)} %get-tuple-element.7.refs_0_), channel_id=1, source_target_pairs={{0,4},{4,0},{128,132},{132,128},{256,260},{260,256},{384,388},{388... | collective-permute-start | bytes 589832 | tf_op jit(solution)/shard_map/gather/ppermute | solution.py:41
  69.3 0.0 collective-permute-done.5.refs_1_
  69.3 0.0 collective-permute-done.1.refs_3_
  69.3 0.0 collective-permute-done.2.refs_4_
  69.3 1.9 %collective-permute-done.3.refs_5_ = bf16[8,2,96,128]{3,2,1,0:T(8,128)(2,1)S(1)} collective-permute-done((bf16[8,2,96,128]{3,2,1,0:T(8,128)(2,1)S(1)}, bf16[8,2,96,128]{3,2,1,0:T(8,128)(2,1)S(1)}, u32[]{:S(2)}, u32[]{:S(2)}) %collective-permute-start.3) | collective-permute-done | bytes 393248 | tf_op jit(solution)/shard_map/gather/ppermute | solution.py:41
  71.2 6.0 %attend.3 = bf16[2,80,768]{2,1,0:T(8,128)(2,1)S(1)} custom-call(bf16[768,128]{1,0:T(8,128)(2,1)S(1)} %collective-permute-done.4.refs_0_, bf16[768,128]{1,0:T(8,128)(2,1)S(1)} %collective-permute-done.5.refs_1_, bf16[8,2,96,128]{3,2,1,0:T(8,128)(2,1)S(1)} %get-tuple-element.8.refs_2_, bf16[8,2,96,128]{3,2,1,0:T(8,128)(2,1)S(1)} %collective-permute-done.1.refs_3_, ...), custom_call_target="tpu_custom_call" | custom-call | flops 4831838208 | bytes 2097152 | tf_op jit(solution)/shard_map/attend/pallas_call | solution.py:124
  77.2 1.9 %collective-permute-start.6 = (bf16[2,80,768]{2,1,0:T(8,128)(2,1)S(1)}, bf16[2,80,768]{2,1,0:T(8,128)(2,1)S(1)}, u32[]{:S(2)}, u32[]{:S(2)}) collective-permute-start(bf16[2,80,768]{2,1,0:T(8,128)(2,1)S(1)} %attend.3), channel_id=1, source_target_pairs={{0,128},{4,132},{128,0},{132,4},{256,384},{260,388},{384,256},{388... | collective-permute-start | bytes 737288 | tf_op jit(solution)/shard_map/attend/ppermute | solution.py:41
  79.1 0.0 collective-permute-done.refs_1_
  79.1 6.0 %attend.2.here_ref = bf16[2,80,768]{2,1,0:T(8,128)(2,1)S(1)} custom-call(bf16[768,128]{1,0:T(8,128)(2,1)S(1)} %get-tuple-element.7.refs_0_, bf16[768,128]{1,0:T(8,128)(2,1)S(1)} %collective-permute-done.refs_1_, bf16[8,2,96,128]{3,2,1,0:T(8,128)(2,1)S(1)} %get-tuple-element.8.refs_2_, bf16[8,2,96,128]{3,2,1,0:T(8,128)(2,1)S(1)} %collective-permute-done.1.refs_3_, ...), custom_call_target="tpu_custom_call" | custom-call | flops 4831838208 | bytes 2097152 | tf_op jit(solution)/shard_map/attend/pallas_call | solution.py:124
  85.1 0.0 collective-permute-done.6.there_ref
  85.1 0.1 combine.2
  85.2 10.6 %collective-permute-start.7 = (bf16[80,768]{1,0:T(8,128)(2,1)S(1)}, bf16[80,768]{1,0:T(8,128)(2,1)S(1)}, u32[]{:S(2)}, u32[]{:S(2)}) collective-permute-start(bf16[80,768]{1,0:T(8,128)(2,1)S(1)} %combine.2), channel_id=1, source_target_pairs={{0,4},{4,0},{128,132},{132,128},{256,260},{260,256},{384,388},{388... | collective-permute-start | bytes 368648 | tf_op jit(solution)/shard_map/combine/ppermute | solution.py:41
  95.9 2.2 %collective-permute-done.7.beside_ref = bf16[80,768]{1,0:T(8,128)(2,1)S(1)} collective-permute-done((bf16[80,768]{1,0:T(8,128)(2,1)S(1)}, bf16[80,768]{1,0:T(8,128)(2,1)S(1)}, u32[]{:S(2)}, u32[]{:S(2)}) %collective-permute-start.7) | collective-permute-done | bytes 122912 | tf_op jit(solution)/shard_map/combine/ppermute | solution.py:41
  98.1 0.3 combine.3
  98.4 24.3 %all_to_all.11 = bf16[16,48,128]{2,1,0:T(8,128)(2,1)S(1)} all-to-all(bf16[16,48,128]{2,1,0:T(8,128)(2,1)S(1)} %bitcast.15), channel_id=1, replica_groups={{0,2,16,18,32,34,48,50,72,74,88,90,104,106,120,122},{8,10,24,26,40,42,5..., dimensions={0} | all-to-all | bytes 393216 | tf_op jit(solution)/shard_map/to_tokens/all_to_all | solution.py:37
  122.7 4.7 %all-gather = f32[96,128]{1,0:T(8,128)S(1)} all-gather(f32[48,128]{1,0:T(8,128)S(1)} %convert_reduce_fusion), channel_id=2, replica_groups=mesh['y'=4,'zh'=8,'z0'=2,'xl'=2,'xh'=2,'c'=2] {'c'}, dimensions={0}, use_global_device_ids=true | all-gather | bytes 73728 | tf_op jit(solution)/shard_map/to_tokens/all_gather | solution.py:225
  127.4 0.1 reshape.18
  127.5 0.7 copy.15
  (8 shorter events, 0.2 us)
Async XLA Ops:
  49.6 16.1 %copy-start = (bf16[640,64]{0,1:T(8,128)(2,1)S(1)}, bf16[640,64]{0,1:T(8,128)(2,1)}, u32[]{:S(2)}) copy-start(bf16[640,64]{0,1:T(8,128)(2,1)} %param.14) | copy-start | bytes 245764
  49.6 16.1 %copy-start.1 = (bf16[384,64]{0,1:T(8,128)(2,1)S(1)}, bf16[384,64]{0,1:T(8,128)(2,1)}, u32[]{:S(2)}) copy-start(bf16[384,64]{0,1:T(8,128)(2,1)} %param.15) | copy-start | bytes 147460
  49.7 19.7 %collective-permute-start.1 = (bf16[8,2,96,128]{3,2,1,0:T(8,128)(2,1)S(1)}, bf16[8,2,96,128]{3,2,1,0:T(8,128)(2,1)S(1)}, u32[]{:S(2)}, u32[]{:S(2)}) collective-permute-start(bf16[8,2,96,128]{3,2,1,0:T(8,128)(2,1)S(1)} %get-tuple-element.8.refs_2_), channel_id=1, source_target_pairs={{0,8},{8,0},{128,136},{136,128},{256,264},{264,256},{384,392},{392... | collective-permute-start | bytes 1179656 | tf_op jit(solution)/shard_map/gather/ppermute | solution.py:41
  52.1 17.3 %collective-permute-start.2 = (bf16[8,2,96,128]{3,2,1,0:T(8,128)(2,1)S(1)}, bf16[8,2,96,128]{3,2,1,0:T(8,128)(2,1)S(1)}, u32[]{:S(2)}, u32[]{:S(2)}) collective-permute-start(bf16[8,2,96,128]{3,2,1,0:T(8,128)(2,1)S(1)} %get-tuple-element.8.refs_2_), channel_id=1, source_target_pairs={{0,384},{8,392},{128,256},{136,264},{256,128},{264,136},{384,0},{3... | collective-permute-start | bytes 1179656 | tf_op jit(solution)/shard_map/gather/ppermute | solution.py:41
  56.7 14.5 %collective-permute-start.3 = (bf16[8,2,96,128]{3,2,1,0:T(8,128)(2,1)S(1)}, bf16[8,2,96,128]{3,2,1,0:T(8,128)(2,1)S(1)}, u32[]{:S(2)}, u32[]{:S(2)}) collective-permute-start(bf16[8,2,96,128]{3,2,1,0:T(8,128)(2,1)S(1)} %get-tuple-element.8.refs_2_), channel_id=1, source_target_pairs={{0,392},{8,384},{128,264},{136,256},{256,136},{264,128},{384,8},{3... | collective-permute-start | bytes 1179656 | tf_op jit(solution)/shard_map/gather/ppermute | solution.py:41
  59.5 6.7 %collective-permute-start.4 = (bf16[768,128]{1,0:T(8,128)(2,1)S(1)}, bf16[768,128]{1,0:T(8,128)(2,1)S(1)}, u32[]{:S(2)}, u32[]{:S(2)}) collective-permute-start(bf16[768,128]{1,0:T(8,128)(2,1)S(1)} %get-tuple-element.7.refs_0_), channel_id=1, source_target_pairs={{0,128},{4,132},{128,0},{132,4},{256,384},{260,388},{384,256},{388... | collective-permute-start | bytes 589832 | tf_op jit(solution)/shard_map/gather/ppermute | solution.py:41
  61.4 7.9 %collective-permute-start.5 = (bf16[768,128]{1,0:T(8,128)(2,1)S(1)}, bf16[768,128]{1,0:T(8,128)(2,1)S(1)}, u32[]{:S(2)}, u32[]{:S(2)}) collective-permute-start(bf16[768,128]{1,0:T(8,128)(2,1)S(1)} %get-tuple-element.7.refs_0_), channel_id=1, source_target_pairs={{0,132},{4,128},{128,4},{132,0},{256,388},{260,384},{384,260},{388... | collective-permute-start | bytes 589832 | tf_op jit(solution)/shard_map/gather/ppermute | solution.py:41
  66.2 12.9 %collective-permute-start = (bf16[768,128]{1,0:T(8,128)(2,1)S(1)}, bf16[768,128]{1,0:T(8,128)(2,1)S(1)}, u32[]{:S(2)}, u32[]{:S(2)}) collective-permute-start(bf16[768,128]{1,0:T(8,128)(2,1)S(1)} %get-tuple-element.7.refs_0_), channel_id=1, source_target_pairs={{0,4},{4,0},{128,132},{132,128},{256,260},{260,256},{384,388},{388... | collective-permute-start | bytes 589832 | tf_op jit(solution)/shard_map/gather/ppermute | solution.py:41
  77.2 7.9 %collective-permute-start.6 = (bf16[2,80,768]{2,1,0:T(8,128)(2,1)S(1)}, bf16[2,80,768]{2,1,0:T(8,128)(2,1)S(1)}, u32[]{:S(2)}, u32[]{:S(2)}) collective-permute-start(bf16[2,80,768]{2,1,0:T(8,128)(2,1)S(1)} %attend.3), channel_id=1, source_target_pairs={{0,128},{4,132},{128,0},{132,4},{256,384},{260,388},{384,256},{388... | collective-permute-start | bytes 737288 | tf_op jit(solution)/shard_map/attend/ppermute | solution.py:41
  85.2 12.9 %collective-permute-start.7 = (bf16[80,768]{1,0:T(8,128)(2,1)S(1)}, bf16[80,768]{1,0:T(8,128)(2,1)S(1)}, u32[]{:S(2)}, u32[]{:S(2)}) collective-permute-start(bf16[80,768]{1,0:T(8,128)(2,1)S(1)} %combine.2), channel_id=1, source_target_pairs={{0,4},{4,0},{128,132},{132,128},{256,260},{260,256},{384,388},{388... | collective-permute-start | bytes 368648 | tf_op jit(solution)/shard_map/combine/ppermute | solution.py:41
